TPU v7x, 32 devices: a whole 2x2x4 slice. The times are simulated.
32 devices in a mesh: prow: 8 (over y, x, core), pcol: 4 (over z).
Axes of the slice: x: 2, y: 2, z: 4, core: 2. Of those that a mesh axis runs over, the one named last changes fastest.
Arguments:
- slab: float32 [8192, 1024], P('prow', 'pcol'), may hold values from -6 to 6
- panel: float32 [8192, 256], P('prow', 'pcol'), may hold values from -0.1875 to 0.1875
- pivots: int32 [256], replicated, may hold values from 256 to 8191, as said below
Outputs:
- result: float32 [8192, 1024], P('prow', 'pcol')
Inputs may be any that keep to these rules, and one draw needn't show every extreme that they name: `pivots`: 256 distinct rows, none among the first 256; at most 32 of them lie in the 1024 rows of one process row, and some process row holds exactly 32.
All inputs are finite; a program needn't handle non-finite values.
Results may differ from a plain program's by a relative error of at most 0.00005.
Values sent between devices are 32-bit elements; how exact they have to be, the bound alone decides.
No kernel may reach another device: no remote copies, remote signals or barrier semaphores. Data moves between devices by JAX's collectives and lax.ppermute only.
A program may use at most 64 MiB of HBM per device.

v0:
```python
import jax
import jax.numpy as jnp
from jax import lax
from jax.sharding import PartitionSpec as P


def broadcast(value, axis, root):
    mine = lax.axis_index(axis) == root
    return lax.psum(jnp.where(mine, value, jnp.zeros_like(value)), axis)


def solve_block(diag_block, right_side):
    return jax.scipy.linalg.solve_triangular(diag_block, right_side, lower=True, unit_diagonal=True)


def local(slab, panel, pivots):
    row_count = slab.shape[0]
    panel_width = pivots.shape[0]
    row_index = lax.axis_index("prow")
    row_start = row_index * row_count
    held_here = pivots // row_count == row_index
    local_row = jnp.clip(pivots - row_start, 0, row_count - 1)
    picked = jnp.take(slab, local_row, axis=0)
    masked = jnp.where(held_here[:, None], picked, jnp.zeros_like(picked))
    leading, diag_piece = (
        broadcast(slab[:panel_width], "prow", 0),
        broadcast(panel[:panel_width], "prow", 0),
    )
    diag_block = lax.all_gather(diag_piece, "pcol", axis=1, tiled=True)
    pivot_rows = lax.psum(masked, "prow")
    upper_rows = solve_block(diag_block, pivot_rows)
    target_row = jnp.where(held_here, local_row, row_count)
    swapped = slab.at[target_row].set(leading, mode="drop")
    updated = swapped - jnp.dot(
        lax.all_gather(panel, "pcol", axis=1, tiled=True),
        upper_rows,
        precision=lax.Precision.HIGHEST,
        preferred_element_type=jnp.float32,
    )
    top_block = jnp.where(row_index == 0, upper_rows, updated[:panel_width])
    return updated.at[:panel_width].set(top_block)


def solution(mesh):
    return jax.shard_map(
        local,
        mesh=mesh,
        in_specs=(P("prow", "pcol"), P("prow", "pcol"), P()),
        out_specs=P("prow", "pcol"),
        check_vma=False,
    )
```

profile of v0, /device:TPU:0, one launch (start us, length us, event | category | flops | bytes accessed | tf_op | source)
XLA Modules:
  0.0 124.9 jit_solution(12217836227887618314)
XLA Ops:
  7.4 1.2 copy.23
  8.6 0.7 copy-done.2
  9.3 1.0 gather_fusion
  10.3 1.5 %slice_select_fusion.2 = f32[256,64]{0,1:T(8,128)} fusion(f32[1024,64]{0,1:T(8,128)} %param.6, pred[]{:T(512)S(6)} %eq.13), kind=kLoop, calls=%fused_computation.21 | loop fusion | flops 16384 | bytes 131073 | tf_op jit(solution)/shard_map/jit(_where)/select_n | solution.py:9
  11.8 0.9 select_select_fusion
  12.7 0.0 all-gather.2.cloned.1.call-start
  12.7 0.5 all-gather.2.cloned.1.call-update
  13.3 57.5 %all-reduce.3.cloned.1.call-done = (f32[256,256]{1,0:T(8,128)}, f32[256,256]{1,0:T(8,128)}, f32[256,64]{0,1:T(8,128)}) async-done(((f32[256,256]{1,0:T(8,128)}, f32[256,256]{1,0:T(8,128)}, f32[256,64]{0,1:T(8,128)}), (f32[256,256]{1,0:T(8,128)}, f32[256,256]{1,0:T(8,128)}, f32[256,64]{0,1:T(8,128)})) %all-reduce.3.cloned.1.call-update) | async-done | bytes 589840 | tf_op jit(solution)/shard_map/psum | solution.py:9
  70.8 14.1 %all_gather.6 = f32[256,256]{0,1:T(8,128)S(1)} all-gather(f32[256,64]{0,1:T(8,128)} %get-tuple-element.35), channel_id=1, replica_groups=mesh['prow'=8,'pcol'=4] {'pcol'}, dimensions={1}, use_global_device_ids=true | all-gather | bytes 327680 | tf_op jit(solution)/shard_map/all_gather | solution.py:29
  85.0 0.1 copy.6
  85.1 0.1 convert_add_fusion
  85.2 0.1 triangular_solve.72
  85.3 4.0 %while.2 = (s32[]{:T(128)}, f32[256,256]{1,0:T(8,128)S(1)}, s32[2,2]{1,0:T(2,128)S(1)}, f32[2,128,128]{2,1,0:T(8,128)S(1)}, s32[]{:T(128)}) while((s32[]{:T(128)}, f32[256,256]{1,0:T(8,128)S(1)}, s32[2,2]{1,0:T(2,128)S(1)}, f32[2,128,128]{2,1,0:T(8,128)S(1)}, s32[]{:T(128)}) %tuple.26), condition=%wide.while_cond.1, body=%wide.while_body.1.sunk | while | flops 2 | bytes 131181 | solution.py:13
  85.3 0.6 fusion.14
  85.9 1.4 %bitcast_dynamic-update-slice_fusion.2 = f32[2,128,128]{2,1,0:T(8,128)S(1)} fusion(f32[2,128,128]{2,1,0:T(8,128)S(1)} %get-tuple-element.81, s32[]{:T(128)} %get-tuple-element.78, f32[256,256]{1,0:T(8,128)S(1)} %get-tuple-element.84, s32[]{:T(128)} %bitcast.21, s32[]{:T(128)} %bitcast.22), kind=kLoop, calls=%fused_computation.2.clone.1 | loop fusion | bytes 131084 | tf_op jit(solution)/shard_map/jit(_solve_triangular)/triangular_solve
  87.3 0.6 fusion.14
  87.9 1.4 %bitcast_dynamic-update-slice_fusion.2 = f32[2,128,128]{2,1,0:T(8,128)S(1)} fusion(f32[2,128,128]{2,1,0:T(8,128)S(1)} %get-tuple-element.81, s32[]{:T(128)} %get-tuple-element.78, f32[256,256]{1,0:T(8,128)S(1)} %get-tuple-element.84, s32[]{:T(128)} %bitcast.21, s32[]{:T(128)} %bitcast.22), kind=kLoop, calls=%fused_computation.2.clone.1 | loop fusion | bytes 131084 | tf_op jit(solution)/shard_map/jit(_solve_triangular)/triangular_solve
  89.2 19.7 %custom-call.4 = f32[2,128,128]{1,2,0:T(8,128)S(1)} custom-call(f32[2,128,128]{2,1,0:T(8,128)S(1)} %get-tuple-element.24), custom_call_target="InvertDiagBlocksLowerTriangular" | custom-call | tf_op jit(solution)/shard_map/jit(_solve_triangular)/triangular_solve | solution.py:13
  109.0 1.8 %scatter_fusion = f32[1024,256]{1,0:T(8,128)S(1)} fusion(f32[1024,256]{1,0:T(8,128)S(1)} %copy.23, s32[256]{0:T(256)S(1)} %get-tuple-element.38, f32[256,256]{1,0:T(8,128)S(1)} %copy-done), kind=kCustom, calls=%fused_computation.1 | custom fusion | bytes 787456 | tf_op jit(solution)/shard_map/scatter | solution.py:33
  110.8 0.3 fusion.2
  111.1 0.3 convolution_subtract_fusion
  111.4 0.3 fusion.5
  111.7 4.0 %fusion = f32[1024,256]{1,0:T(8,128)} fusion(f32[1024,256]{1,0:T(8,128)S(1)} %scatter_fusion, f32[1024,256]{0,1:T(8,128)} %all-gather.2.cloned.1.call-done, f32[128,256]{1,0:T(8,128)S(1)} %fusion.5, f32[128,256]{1,0:T(8,128)S(1)} %fusion.2), kind=kOutput, calls=%fused_computation.5 | convolution fusion | flops 805634048 | bytes 3407872 | tf_op jit(solution)/shard_map/dot_general | solution.py:34
  115.8 1.7 %fusion.1 = f32[1024,256]{1,0:T(8,128)} fusion(f32[1024,256]{1,0:T(8,128)} %fusion, f32[128,256]{1,0:T(8,128)S(1)} %fusion.5, f32[128,256]{1,0:T(8,128)S(1)} %fusion.2, pred[]{:T(512)S(6)} %eq.13), kind=kLoop, calls=%fused_computation.8 | loop fusion | flops 131072 | bytes 786433 | tf_op jit(solution)/shard_map/scatter | solution.py:41
  (16 shorter events, 0.1 us)
Async XLA Ops:
  7.4 63.5 %all-reduce.3.cloned.1.call-start = ((), (), s32[]{:S(2)}) async-start(), calls=%async_computation.1 | async-start | bytes 1179648 | tf_op jit(solution)/shard_map/psum | solution.py:9
  8.6 0.7 copy-start.2
  12.7 99.1 %all-gather.2.cloned.1.call-start = ((), (), s32[]{:S(2)}) async-start(), calls=%async_computation | async-start | bytes 1310720 | tf_op jit(solution)/shard_map/all_gather | solution.py:35
  85.1 23.8 %copy-start = (f32[256,256]{1,0:T(8,128)S(1)}, f32[256,256]{1,0:T(8,128)}, u32[]{:S(2)}) copy-start(f32[256,256]{1,0:T(8,128)} %get-tuple-element.33) | copy-start | bytes 786436
  108.9 1.8 %copy-start.1 = (f32[256,256]{1,0:T(8,128)S(1)}, f32[256,256]{1,0:T(8,128)}, u32[]{:S(2)}) copy-start(f32[256,256]{1,0:T(8,128)} %get-tuple-element.34) | copy-start | bytes 786436
Sparse Core Ops, SparseCore 0:
  12.8 57.9 all-reduce.2
Sparse Core Ops, SparseCore 1:
  14.8 30.5 all-gather.1
where the time goes:
time: 125 us
  waiting for transfers between devices  58.1 us (46%)
  other arithmetic  23.8 us (19%)
  between operations  15 us (12%)
  blocking collectives  14.1 us (11%)
  local copies, waits for them, and re-layouts  8.84 us (7%)
  matrix products  4.89 us (4%)
    psum x1, waiting for transfers between devices, broadcast(): return lax.psum(jnp.where(mine, value, jnp.zeros_like(value)), axis)  57.5 us
    another operation x4, other arithmetic, solve_block(): jax.scipy.linalg.solve_triangular(diag_block, right_side, lower=True, uni...  19.8 us
    all_gather x1, blocking collectives, local(): diag_block = lax.all_gather(diag_piece, 'pcol', axis=1, tiled=True)  14.1 us
    dot_general x1, matrix products, local(): jnp.dot(lax.all_gather(panel, 'pcol', axis=1, tiled=True), upper_rows, pr...  4.01 us
    another operation x6, local copies, waits for them, and re-layouts  3.93 us
  transfers between devices with their start and end apart: 2, of which 1 were waited for; matrix products, arithmetic and copies ran while one was open for 21% of the time, Pallas kernels for 0%

commit v1 on v0

v1 whole, which is shorter than its diff:
```python
import functools

import jax
import jax.numpy as jnp
from jax import lax
from jax.experimental import pallas as pl
from jax.experimental.pallas import tpu as pltpu
from jax.sharding import PartitionSpec as P

CAP = 32
BLOCK = 32
F32 = jnp.float32
BF16 = jnp.bfloat16
VMEM = pl.BlockSpec(memory_space=pltpu.VMEM)
PARAMS = pltpu.CompilerParams(vmem_limit_bytes=24 * 1024 * 1024)


def split3(x):
    high = x.astype(BF16)
    rest = x - high.astype(F32)
    mid = rest.astype(BF16)
    low = (rest - mid.astype(F32)).astype(BF16)
    return high, mid, low


def split2(x):
    high = x.astype(BF16)
    return high, (x - high.astype(F32)).astype(BF16)


def select_rows(one_hot, x):
    return sum(jnp.dot(one_hot, part, preferred_element_type=F32) for part in split3(x))


def dot_full(a, b):
    return jnp.dot(a, b, precision=lax.Precision.HIGHEST, preferred_element_type=F32)


def tree_partner(r, span):
    if span == 1 or r % span > 1:
        return r ^ 1
    if r % 2 == 0:
        return r + 1 if r & span else r + span
    return r - span if r & span else r - 1


def lead_place(owner, n):
    bits = n.bit_length() - 1
    return sum((lax.shift_right_logical(owner, bit) & 1) * (1 << (bits - 1 - bit)) for bit in range(bits))


def slots(pivot_row, rows):
    width = pivot_row.shape[1]
    by_sublane = jnp.broadcast_to(pivot_row, (width, width)).T
    shift = rows.bit_length() - 1
    owner_row = jnp.broadcast_to(lax.shift_right_logical(pivot_row, shift), (width, width))
    owner_col = lax.shift_right_logical(by_sublane, shift)
    sub = lax.broadcasted_iota(jnp.int32, (width, width), 0)
    lane = lax.broadcasted_iota(jnp.int32, (width, width), 1)
    same = owner_row == owner_col
    rank_row = jnp.sum(jnp.where(same & (sub < lane), 1, 0), axis=0, keepdims=True)
    rank_col = jnp.sum(jnp.where(same & (lane < sub), 1, 0), axis=1, keepdims=True)
    return owner_row[:1], rank_row, owner_col[:, :1], rank_col


def pack_kernel(pivot_ref, slab_ref, packed_ref, lead_ref, local_ref):
    rows = slab_ref.shape[0]
    width = pivot_ref.shape[1]
    count = lead_ref.shape[0]
    lanes = local_ref.shape[1]
    me = lax.axis_index("prow")
    pivot_row = pivot_ref[...]
    owner_row, rank_row, owner_col, rank_col = slots(pivot_row, rows)
    pivot_col = jnp.broadcast_to(pivot_row, (lanes, width)).T
    slot = lax.broadcasted_iota(jnp.int32, (width, lanes), 1)
    mine = (owner_col == me) & (rank_col == slot)
    local = jnp.sum(jnp.where(mine, pivot_col - (me + 1) * rows, 0), axis=0, keepdims=True) + rows
    local_ref[...] = local
    slot = lax.broadcasted_iota(jnp.int32, (CAP, width), 0)
    mine = (owner_row == me) & (rank_row == slot)
    local = jnp.sum(jnp.where(mine, pivot_row - (me + 1) * rows, 0), axis=1, keepdims=True) + rows
    one_hot = (lax.broadcasted_iota(jnp.int32, (CAP, rows), 1) == local).astype(F32).astype(BF16)
    packed_ref[...] = select_rows(one_hot, slab_ref[...])
    slot = lax.broadcasted_iota(jnp.int32, (count, width), 0)
    one_hot = (slot == lead_place(owner_row, count // CAP) * CAP + rank_row).astype(F32).astype(BF16)
    lead_ref[...] = select_rows(one_hot, slab_ref[:width, :])


def block_inverses(lower):
    width = lower.shape[0]
    lane = lax.broadcasted_iota(jnp.int32, (BLOCK, width), 1)
    sub = lax.broadcasted_iota(jnp.int32, (BLOCK, width), 0)
    block = lane // BLOCK
    within = lane % BLOCK
    diag = jnp.zeros((BLOCK, width), F32)
    for b in range(width // BLOCK):
        diag = jnp.where(block == b, lower[b * BLOCK : (b + 1) * BLOCK], diag)
    diag = jnp.where(within < sub, diag, 0.0)
    inv = jnp.where(within == sub, 1.0, 0.0).astype(F32)
    half = 128
    first = (lax.broadcasted_iota(jnp.int32, (BLOCK, half), 1) // BLOCK) * BLOCK
    outs = []
    for h in range(0, width, half):
        d, x = diag[:, h : h + half], inv[:, h : h + half]
        for k in range(BLOCK - 1):
            column = jnp.take_along_axis(d, first + k, axis=1)
            x = x - column * x[k : k + 1, :]
        outs.append(x)
    return outs


def order_kernel(n, rows, pivot_ref, gathered_ref, out_ref, gathered):
    width = pivot_ref.shape[1]
    me = lax.axis_index("prow")
    for q in range(n):
        source = jnp.bitwise_xor(me, q)
        gathered[pl.ds(pl.multiple_of(source * CAP, CAP), CAP), :] = gathered_ref[q * CAP : (q + 1) * CAP, :]
    _, _, owner_col, rank_col = slots(pivot_ref[...], rows)
    slot = lax.broadcasted_iota(jnp.int32, (width, gathered.shape[0]), 1)
    one_hot = (slot == owner_col * CAP + rank_col).astype(F32).astype(BF16)
    out_ref[...] = select_rows(one_hot, gathered[...])


def top_order(m):
    return [0, 1, *range(m - 1, 1, -1)]


def cut_kernel(panel_ref, top_ref, rest_ref, sems):
    width = top_ref.shape[1]
    copies = []
    for c in range(sems.shape[0]):
        target = rest_ref.at[:, pl.ds((c - 1) * width, width)] if c else top_ref
        copies.append(pltpu.make_async_copy(panel_ref.at[:, pl.ds(c * width, width)], target, sems.at[c]))
        copies[-1].start()
    for copy in copies:
        copy.wait()


def assemble_kernel(m, *refs):
    *pieces, out_ref, lower_t = refs
    width = lower_t.shape[0]
    piece = width // m
    half = width // 2
    z = lax.axis_index("pcol")
    for d, ref in zip(top_order(m), pieces):
        lower_t[pl.ds(pl.multiple_of(jnp.bitwise_xor(z, d) * piece, piece), piece), :] = ref[...]
    out_ref[:half, :] = lower_t[:half, :]
    out_ref[half:, :half] = lower_t[half : half + half // 2, half:]
    out_ref[half:, half:] = lower_t[half + half // 2 :, half:]


def pick_kernel(span, moved_ref, held_ref, out_ref):
    child = lax.rem(lax.axis_index("prow"), 2 * span) == span

    @pl.when(child)
    def _():
        out_ref[...] = moved_ref[...]

    @pl.when(jnp.logical_not(child))
    def _():
        out_ref[...] = held_ref[...]


def invert_kernel(lower_ref, out_ref, lower_t):
    width = lower_t.shape[0]
    half = width // 2
    lower_t[:half, :] = lower_ref[:half, :]
    lower_t[half:, :half] = jnp.zeros((half, half), F32)
    lower_t[half : half + half // 2, half:] = lower_ref[half:, :half]
    lower_t[half + half // 2 :, half:] = lower_ref[half:, half:]
    lower = lower_t[...].T
    blocks = block_inverses(lower)
    row = lax.broadcasted_iota(jnp.int32, (half, half), 0)
    col = lax.broadcasted_iota(jnp.int32, (half, half), 1)
    for h, strip in enumerate(blocks):
        corner = lower[h * half : (h + 1) * half, h * half : (h + 1) * half]
        inv = jnp.where(row // BLOCK == col // BLOCK, jnp.concatenate([strip] * (half // BLOCK), axis=0), 0.0)
        size = BLOCK
        while size < half:
            off = (row // (2 * size) == col // (2 * size)) & (row // size > col // size)
            inv = inv - dot_full(dot_full(inv, jnp.where(off, corner, 0.0)), inv)
            size *= 2
        out_ref[:half, h * half : (h + 1) * half] = inv
    out_ref[half:, :half] = lower[half : half + half // 2, :half]
    out_ref[half:, half:] = lower[half + half // 2 :, :half]


def solve_kernel(inverse_ref, pivot_rows_ref, x_ref):
    half = pivot_rows_ref.shape[0] // 2
    quarter = jnp.concatenate([inverse_ref[half:, :half], inverse_ref[half:, half:]], axis=0)
    first = dot_full(inverse_ref[:half, :half], pivot_rows_ref[:half, :])
    x_ref[:half, :] = first
    x_ref[half:, :] = dot_full(inverse_ref[:half, half:], pivot_rows_ref[half:, :] - dot_full(quarter, first))


def product(piece, upper):
    high, low = split2(piece)
    upper_high, upper_low = split2(upper)
    left = jnp.concatenate([high, high, low], axis=0)
    right = jnp.concatenate([upper_high, upper_low, upper_high], axis=0)
    return lax.dot_general(left, right, (((0,), (0,)), ((), ())), preferred_element_type=F32)


def piece_rows(x_ref, m, d):
    piece = x_ref.shape[0] // m
    source = jnp.bitwise_xor(lax.axis_index("pcol"), d)
    return x_ref[pl.ds(pl.multiple_of(source * piece, piece), piece), :]


def update_kernel(m, local_ref, lead_ref, x_ref, slab_ref, *refs):
    *pieces, out_ref, result, sems = refs
    tops, rests = dict(zip(top_order(m), pieces[:m])), pieces[m:]
    rows, cols = slab_ref.shape
    width = x_ref.shape[0]
    result[:rows, :] = slab_ref[...]
    for s in range(CAP):
        result[pl.ds(local_ref[0, s], 1), :] = lead_ref[pl.ds(s, 1), :]
    uppers = [piece_rows(x_ref, m, d) for d in range(m)]
    copies = []
    for c in range(rows // width):
        part = pl.ds(c * width, width)
        total = result[part, :]
        for d, upper in enumerate(uppers):
            piece = rests[d][:, (c - 1) * width : c * width] if c else tops[d][...]
            total = total - product(piece, upper)
        result[part, :] = total
        if c == 0:

            @pl.when(lax.axis_index("prow") == 0)
            def _():
                result[part, :] = x_ref[...]

        copy = pltpu.make_async_copy(result.at[part], out_ref.at[part], sems.at[c])
        copy.start()
        copies.append(copy)
    for copy in copies:
        copy.wait()


def unit(held, steps, *operands):
    shapes = jax.eval_shape(steps, *operands)
    return lax.cond(held, steps, lambda *_: jax.tree.map(lambda s: jnp.zeros(s.shape, s.dtype), shapes), *operands)


def call(kernel, outs, operands, in_specs=None, out_specs=None, scratch=()):
    return pl.pallas_call(
        kernel,
        out_shape=outs,
        in_specs=in_specs or [VMEM] * len(operands),
        out_specs=out_specs or jax.tree.map(lambda _: VMEM, outs),
        scratch_shapes=list(scratch),
        compiler_params=PARAMS,
        cost_estimate=pl.CostEstimate(flops=1, bytes_accessed=1, transcendentals=0),
    )(*operands)


def local(n, m, slab, panel, pivots):
    rows, cols = slab.shape
    width = pivots.shape[0]
    piece = panel.shape[1]
    me = lax.axis_index("prow")
    panel_t = panel.T
    pivot_row = pivots.reshape(1, width)

    def spread(block, order):
        return [block] + [lax.ppermute(block, "pcol", [(c, c ^ d) for c in range(m)]) for d in order]

    top, rest = call(
        cut_kernel,
        (jax.ShapeDtypeStruct((piece, width), F32), jax.ShapeDtypeStruct((piece, rows - width), F32)),
        (panel_t,),
        in_specs=[pl.BlockSpec(memory_space=pl.ANY)],
        scratch=[pltpu.SemaphoreType.DMA((rows // width,))],
    )
    tops, rests = spread(top, top_order(m)[1:]), spread(rest, range(1, m))

    gathered, leading, local_rows = call(
        pack_kernel,
        (
            jax.ShapeDtypeStruct((CAP, cols), F32),
            jax.ShapeDtypeStruct((n * CAP, cols), F32),
            jax.ShapeDtypeStruct((1, 128), jnp.int32),
        ),
        (pivot_row, slab),
    )
    lower = call(
        functools.partial(assemble_kernel, m),
        jax.ShapeDtypeStruct((width * 3 // 4, width), F32),
        tops,
        scratch=[pltpu.VMEM((width, width), F32)],
    )

    def split(leading):
        blocks = leading.reshape(2, -1, cols)
        return blocks[0], blocks[1]

    def levels(lower, gathered, leading):
        kept, sent = split(leading)
        moved = lax.ppermute(sent, "prow", [(r, r ^ 1) for r in range(n)])
        leading = jnp.where(me & 1 != 0, moved, kept)
        span, other = n // 2, 2
        while span > 1:
            moved = lax.ppermute(lower, "prow", [(r, tree_partner(r, span)) for r in range(n)])
            lower = call(
                functools.partial(pick_kernel, span),
                jax.ShapeDtypeStruct(lower.shape, F32),
                (moved, lower),
            )
            kept, sent = split(leading)
            count = gathered.shape[0]
            message = jnp.concatenate([gathered, sent], axis=0)
            moved = lax.ppermute(message, "prow", [(r, r ^ other) for r in range(n)])
            gathered = jnp.concatenate([gathered, moved[:count]], axis=0)
            leading = jnp.where(me & other != 0, moved[count:], kept)
            span, other = span // 2, other * 2
        pivot_rows = call(
            functools.partial(order_kernel, n, rows),
            jax.ShapeDtypeStruct((width, cols), F32),
            (pivot_row, gathered),
            scratch=[pltpu.VMEM((n * CAP, cols), F32)],
        )
        inverse = call(
            invert_kernel,
            jax.ShapeDtypeStruct(lower.shape, F32),
            (lower,),
            scratch=[pltpu.VMEM((width, width), F32)],
        )
        moved = lax.ppermute(inverse, "prow", [(r, r ^ 1) for r in range(n)])
        inverse = jnp.where(me & 1 != 0, moved, inverse)
        return leading, call(solve_kernel, jax.ShapeDtypeStruct((width, cols), F32), (inverse, pivot_rows))

    gathered, lower = lax.optimization_barrier((gathered, lower))
    moved = lax.ppermute(jnp.concatenate([gathered, gathered], axis=0), "prow", [(r, r ^ 1) for r in range(n)])
    gathered = jnp.concatenate([gathered, moved[:CAP]], axis=0)
    leading, upper_rows = unit(me < n, levels, lower, gathered, leading)
    return call(
        functools.partial(update_kernel, m),
        jax.ShapeDtypeStruct((rows, cols), F32),
        (local_rows, leading, upper_rows, slab, *tops, *rests),
        in_specs=[pl.BlockSpec(memory_space=pltpu.SMEM)] + [VMEM] * (2 * m + 3),
        out_specs=pl.BlockSpec(memory_space=pl.ANY),
        scratch=[pltpu.VMEM((rows + 8, cols), F32), pltpu.SemaphoreType.DMA((rows // width,))],
    )


def solution(mesh):
    return jax.shard_map(
        functools.partial(local, mesh.shape["prow"], mesh.shape["pcol"]),
        mesh=mesh,
        in_specs=(P("prow", "pcol"), P("prow", "pcol"), P()),
        out_specs=P("prow", "pcol"),
        check_vma=False,
    )
```

time: 125 us -> 31.5 us (0.25)
  waiting for transfers between devices: 58.1 us -> 6.04 us
  other arithmetic: 23.8 us -> 0.13 us
  starting transfers between devices: 0.05 us -> 16.3 us
  between operations: 15 us -> 0.1 us
  blocking collectives: 14.1 us -> 0 us
  local copies, waits for them, and re-layouts: 8.84 us -> 2.22 us
  Pallas kernels: 0 us -> 6.39 us
  matrix products: 4.89 us -> 0 us
    psum x1 -> x0, waiting for transfers between devices: 57.5 us -> none  [broadcast(): return lax.psum(jnp.where(mine, value, jnp.zeros_like(value)), axis)]
    another operation x4 -> x0, other arithmetic: 19.8 us -> none  [solve_block(): jax.scipy.linalg.solve_triangular(diag_block, right_side, lower=True, uni...]
    ppermute x0 -> x13, starting transfers between devices: none -> 16.3 us  [the longest x6 10.1 us: spread(): lax.ppermute(block, 'pcol', [(c, c ^ d) for c in range(m)])]
    all_gather x1 -> x0, blocking collectives: 14.1 us -> none  [local(): diag_block = lax.all_gather(diag_piece, 'pcol', axis=1, tiled=True)]
    pallas_call x0 -> x9, Pallas kernels: none -> 6.39 us  [call(): pl.pallas_call(kernel, out_shape=outs, in_specs=in_specs or [VMEM] * len(...]
    ppermute x0 -> x13, waiting for transfers between devices: none -> 6.04 us  [the longest x2 2.75 us: levels(): moved = lax.ppermute(message, 'prow', [(r, r ^ other) for r in range(n)])]
    dot_general x1 -> x0, matrix products: 4.01 us -> none  [local(): jnp.dot(lax.all_gather(panel, 'pcol', axis=1, tiled=True), upper_rows, pr...]
    another operation x7 -> x0, local copies, waits for them, and re-layouts: 4 us -> none
  transfers between devices with their start and end apart: 2 -> 13, of which waited for: 1 -> 5; matrix products, arithmetic and copies ran while one was open for 21% -> 1% of each run, Pallas kernels for 0% -> 13%
where the time goes in v1:
time: 31.5 us; the launch traced here: 31.4 us
  starting transfers between devices  16.3 us (52%)
  Pallas kernels  6.39 us (20%)
  waiting for transfers between devices  6.04 us (19%)
  local copies, waits for them, and re-layouts  2.22 us (7%)
    ppermute x6, starting transfers between devices, spread(): lax.ppermute(block, 'pcol', [(c, c ^ d) for c in range(m)])  10.1 us
    pallas_call x9, Pallas kernels, call(): pl.pallas_call(kernel, out_shape=outs, in_specs=in_specs or [VMEM] * len(...  6.39 us
    ppermute x2, starting transfers between devices, levels(): moved = lax.ppermute(message, 'prow', [(r, r ^ other) for r in range(n)])  3.59 us
    ppermute x2, waiting for transfers between devices, levels(): moved = lax.ppermute(message, 'prow', [(r, r ^ other) for r in range(n)])  2.75 us
    unnamed x8, local copies, waits for them, and re-layouts  2.18 us
    ppermute x2, waiting for transfers between devices, levels(): lax.ppermute(lower, 'prow', [(r, tree_partner(r, span)) for r in range(n)])  1.91 us
    ppermute x2, starting transfers between devices, levels(): lax.ppermute(lower, 'prow', [(r, tree_partner(r, span)) for r in range(n)])  1.54 us
    ppermute x1, waiting for transfers between devices, local(): lax.ppermute(jnp.concatenate([gathered, gathered], axis=0), 'prow', [(r,...  1.24 us
  transfers between devices with their start and end apart: 13, of which 5 were waited for; matrix products, arithmetic and copies ran while one was open for 1% of the time, Pallas kernels for 13%

profile of v1, /device:TPU:0, one launch (start us, length us, event | category | flops | bytes accessed | tf_op | source)
XLA Modules:
  0.0 31.4 jit_solution(9233188921058871009)
XLA Ops:
  0.0 0.9 %copy-done.2 = f32[1024,64]{0,1:T(8,128)S(1)} copy-done((f32[1024,64]{0,1:T(8,128)S(1)}, f32[1024,64]{0,1:T(8,128)}, u32[]{:S(2)}) %copy-start.2) | copy-done | bytes 262168
  1.0 3.1 %collective-permute-start.6 = (f32[64,256]{1,0:T(8,128)S(1)}, f32[64,256]{1,0:T(8,128)S(1)}, u32[]{:S(2)}, u32[]{:S(2)}) collective-permute-start(f32[64,256]{1,0:T(8,128)S(1)} %get-tuple-element.32.refs_0_), channel_id=1, source_target_pairs={{0,1},{1,0},{2,3},{3,2},{4,5},{5,4},{6,7},{7,6},{8,9},{9,8},{10,11... | collective-permute-start | bytes 196616 | tf_op jit(solution)/shard_map/ppermute | solution.py:266
  4.1 2.5 %collective-permute-start.7 = (f32[64,256]{1,0:T(8,128)S(1)}, f32[64,256]{1,0:T(8,128)S(1)}, u32[]{:S(2)}, u32[]{:S(2)}) collective-permute-start(f32[64,256]{1,0:T(8,128)S(1)} %get-tuple-element.32.refs_0_), channel_id=1, source_target_pairs={{0,3},{1,2},{2,1},{3,0},{4,7},{5,6},{6,5},{7,4},{8,11},{9,10},{10,... | collective-permute-start | bytes 196616 | tf_op jit(solution)/shard_map/ppermute | solution.py:266
  6.6 0.1 collective-permute-start.8
  6.7 1.8 %collective-permute-start.10 = (f32[64,768]{1,0:T(8,128)S(1)}, f32[64,768]{1,0:T(8,128)S(1)}, u32[]{:S(2)}, u32[]{:S(2)}) collective-permute-start(f32[64,768]{1,0:T(8,128)S(1)} %get-tuple-element.37.refs_4_), channel_id=1, source_target_pairs={{0,1},{1,0},{2,3},{3,2},{4,5},{5,4},{6,7},{7,6},{8,9},{9,8},{10,11... | collective-permute-start | bytes 589832 | tf_op jit(solution)/shard_map/ppermute | solution.py:266
  8.5 1.7 %collective-permute-start.11 = (f32[64,768]{1,0:T(8,128)S(1)}, f32[64,768]{1,0:T(8,128)S(1)}, u32[]{:S(2)}, u32[]{:S(2)}) collective-permute-start(f32[64,768]{1,0:T(8,128)S(1)} %get-tuple-element.37.refs_4_), channel_id=1, source_target_pairs={{0,2},{1,3},{2,0},{3,1},{4,6},{5,7},{6,4},{7,5},{8,10},{9,11},{10,... | collective-permute-start | bytes 589832 | tf_op jit(solution)/shard_map/ppermute | solution.py:266
  10.2 1.2 %copy-done = f32[1024,256]{1,0:T(8,128)S(1)} copy-done((f32[1024,256]{1,0:T(8,128)S(1)}, f32[1024,256]{1,0:T(8,128)}, u32[]{:S(2)}) %copy-start) | copy-done | bytes 1048600
  11.4 0.7 %shard_map.37 = (f32[32,256]{1,0:T(8,128)S(1)}, f32[256,256]{1,0:T(8,128)S(1)}, s32[1,128]{1,0:T(1,128)S(1)}) custom-call(s32[1,256]{1,0:T(1,128)S(1)} %bitcast.3, f32[1024,256]{1,0:T(8,128)S(1)} %copy-done), custom_call_target="tpu_custom_call" | custom-call | flops 1 | bytes 1 | tf_op jit(solution)/shard_map/pallas_call | solution.py:246
  12.1 1.0 %collective-permute-start.12 = (f32[64,768]{1,0:T(8,128)S(1)}, f32[64,768]{1,0:T(8,128)S(1)}, u32[]{:S(2)}, u32[]{:S(2)}) collective-permute-start(f32[64,768]{1,0:T(8,128)S(1)} %get-tuple-element.37.refs_4_), channel_id=1, source_target_pairs={{0,3},{1,2},{2,1},{3,0},{4,7},{5,6},{6,5},{7,4},{8,11},{9,10},{10,... | collective-permute-start | bytes 589832 | tf_op jit(solution)/shard_map/ppermute | solution.py:266
  13.1 0.1 collective-permute-done.8.refs_3_
  13.4 1.2 %collective-permute-done.9 = f32[64,256]{1,0:T(8,128)S(1)} collective-permute-done((f32[64,256]{1,0:T(8,128)S(1)}, f32[64,256]{1,0:T(8,128)S(1)}, u32[]{:S(2)}, u32[]{:S(2)}) %collective-permute-start.9) | collective-permute-done | bytes 65568 | tf_op jit(solution)/shard_map/ppermute | solution.py:333
  14.6 14.4 %conditional.1 = (f32[32,256]{1,0:T(8,128)S(1)}, f32[256,256]{1,0:T(8,128)S(1)}) conditional(s32[]{:T(128)} %convert_element_type.3, () %tuple.14, (s32[]{:T(128)}, f32[256,256]{1,0:T(8,128)S(1)}, f32[64,256]{1,0:T(8,128)S(1)}, f32[192,256]{1,0:T(8,128)S(1)}, s32[1,256]{1,0:T(1,128)S(1)}) %tuple.20), branch_computations={%region_0.0_spmd, %region_1.2_spmd} | conditional | flops 352267 | bytes 7307592 | solution.py:242
  14.7 0.2 collective-permute-start
  14.9 1.5 %collective-permute-start.3 = (f32[192,256]{1,0:T(8,128)S(1)}, f32[192,256]{1,0:T(8,128)S(1)}, u32[]{:S(2)}, u32[]{:S(2)}) collective-permute-start(f32[192,256]{1,0:T(8,128)S(1)} %get-tuple-element.18.held_ref), channel_id=1, source_target_pairs={{0,16},{4,0},{8,12},{12,8},{16,20},{20,4},{24,28},{28,24},{1,17},{... | collective-permute-start | bytes 589832 | tf_op jit(solution)/shard_map/cond/branch_1_fun/ppermute | solution.py:303
  16.5 1.2 %collective-permute-start.1 = (f32[128,256]{1,0:T(8,128)S(1)}, f32[128,256]{1,0:T(8,128)S(1)}, u32[]{:S(2)}, u32[]{:S(2)}) collective-permute-start(f32[128,256]{1,0:T(8,128)S(1)} %pad_maximum_fusion.2), channel_id=1, source_target_pairs={{0,8},{4,12},{8,0},{12,4},{16,24},{20,28},{24,16},{28,20},{1,9},{5... | collective-permute-start | bytes 393224 | tf_op jit(solution)/shard_map/cond/branch_1_fun/ppermute | solution.py:312
  17.7 1.9 %collective-permute-done.3.moved_ref = f32[192,256]{1,0:T(8,128)S(1)} collective-permute-done((f32[192,256]{1,0:T(8,128)S(1)}, f32[192,256]{1,0:T(8,128)S(1)}, u32[]{:S(2)}, u32[]{:S(2)}) %collective-permute-start.3) | collective-permute-done | bytes 196640 | tf_op jit(solution)/shard_map/cond/branch_1_fun/ppermute | solution.py:303
  19.6 2.1 %collective-permute-done.1 = f32[128,256]{1,0:T(8,128)S(1)} collective-permute-done((f32[128,256]{1,0:T(8,128)S(1)}, f32[128,256]{1,0:T(8,128)S(1)}, u32[]{:S(2)}, u32[]{:S(2)}) %collective-permute-start.1) | collective-permute-done | bytes 131104 | tf_op jit(solution)/shard_map/cond/branch_1_fun/ppermute | solution.py:312
  21.8 2.4 %collective-permute-start.2 = (f32[160,256]{1,0:T(8,128)S(1)}, f32[160,256]{1,0:T(8,128)S(1)}, u32[]{:S(2)}, u32[]{:S(2)}) collective-permute-start(f32[160,256]{1,0:T(8,128)S(1)} %pad_maximum_fusion.1), channel_id=1, source_target_pairs={{0,16},{4,20},{8,24},{12,28},{16,0},{20,4},{24,8},{28,12},{1,17},{... | collective-permute-start | bytes 491528 | tf_op jit(solution)/shard_map/cond/branch_1_fun/ppermute | solution.py:312
  24.2 1.8 %branch_1_fun.7 = f32[192,256]{1,0:T(8,128)S(1)} custom-call(f32[192,256]{1,0:T(8,128)S(1)} %branch_1_fun.6.lower_ref), custom_call_target="tpu_custom_call" | custom-call | flops 1 | bytes 1 | tf_op jit(solution)/shard_map/cond/branch_1_fun/pallas_call | solution.py:246
  26.0 0.8 %collective-permute-start.5 = (f32[192,256]{1,0:T(8,128)S(1)}, f32[192,256]{1,0:T(8,128)S(1)}, u32[]{:S(2)}, u32[]{:S(2)}) collective-permute-start(f32[192,256]{1,0:T(8,128)S(1)} %branch_1_fun.7), channel_id=1, source_target_pairs={{0,4},{4,0},{8,12},{12,8},{16,20},{20,16},{24,28},{28,24},{1,5},{5... | collective-permute-start | bytes 589832 | tf_op jit(solution)/shard_map/cond/branch_1_fun/ppermute | solution.py:328
  26.8 0.6 %collective-permute-done.2 = f32[160,256]{1,0:T(8,128)S(1)} collective-permute-done((f32[160,256]{1,0:T(8,128)S(1)}, f32[160,256]{1,0:T(8,128)S(1)}, u32[]{:S(2)}, u32[]{:S(2)}) %collective-permute-start.2) | collective-permute-done | bytes 163872 | tf_op jit(solution)/shard_map/cond/branch_1_fun/ppermute | solution.py:312
  27.5 0.5 %branch_1_fun.8.pivot_rows_ref = f32[256,256]{1,0:T(8,128)S(1)} custom-call(s32[1,256]{1,0:T(1,128)S(1)} %get-tuple-element.19.pivot_ref, f32[256,256]{1,0:T(8,128)S(1)} %pad_maximum_fusion.gathered_ref), custom_call_target="tpu_custom_call" | custom-call | flops 1 | bytes 1 | tf_op jit(solution)/shard_map/cond/branch_1_fun/pallas_call | solution.py:246
  28.1 0.9 %branch_1_fun.9 = f32[256,256]{1,0:T(8,128)S(1)} custom-call(f32[192,256]{1,0:T(8,128)S(1)} %broadcast_select_fusion.inverse_ref, f32[256,256]{1,0:T(8,128)S(1)} %branch_1_fun.8.pivot_rows_ref), custom_call_target="tpu_custom_call" | custom-call | flops 1 | bytes 1 | tf_op jit(solution)/shard_map/cond/branch_1_fun/pallas_call | solution.py:246
  29.1 2.3 %shard_map.40 = f32[1024,256]{1,0:T(8,128)} custom-call(s32[1,128]{1,0:T(1,128)S(1)} %get-tuple-element.29.local_ref, f32[32,256]{1,0:T(8,128)S(1)} %get-tuple-element.35.lead_ref, f32[256,256]{1,0:T(8,128)S(1)} %get-tuple-element.36.x_ref, f32[1024,256]{1,0:T(8,128)S(1)} %copy-done.1, f32[64,256]{1,0:T(8,128)S(1)} %get-tuple-element.32.refs_0_, ...), custom_call_target="tpu_custom_call" | custom-call | flops 1 | bytes 1 | tf_op jit(solution)/shard_map/pallas_call | solution.py:246
  (34 shorter events, 0.4 us)
Async XLA Ops:
  0.0 0.9 %copy-start.2 = (f32[1024,64]{0,1:T(8,128)S(1)}, f32[1024,64]{0,1:T(8,128)}, u32[]{:S(2)}) copy-start(f32[1024,64]{0,1:T(8,128)} %param.6) | copy-start | bytes 786436
  1.0 11.1 %collective-permute-start.6 = (f32[64,256]{1,0:T(8,128)S(1)}, f32[64,256]{1,0:T(8,128)S(1)}, u32[]{:S(2)}, u32[]{:S(2)}) collective-permute-start(f32[64,256]{1,0:T(8,128)S(1)} %get-tuple-element.32.refs_0_), channel_id=1, source_target_pairs={{0,1},{1,0},{2,3},{3,2},{4,5},{5,4},{6,7},{7,6},{8,9},{9,8},{10,11... | collective-permute-start | bytes 196616 | tf_op jit(solution)/shard_map/ppermute | solution.py:266
  4.1 9.0 %collective-permute-start.7 = (f32[64,256]{1,0:T(8,128)S(1)}, f32[64,256]{1,0:T(8,128)S(1)}, u32[]{:S(2)}, u32[]{:S(2)}) collective-permute-start(f32[64,256]{1,0:T(8,128)S(1)} %get-tuple-element.32.refs_0_), channel_id=1, source_target_pairs={{0,3},{1,2},{2,1},{3,0},{4,7},{5,6},{6,5},{7,4},{8,11},{9,10},{10,... | collective-permute-start | bytes 196616 | tf_op jit(solution)/shard_map/ppermute | solution.py:266
  6.6 6.6 %collective-permute-start.8 = (f32[64,256]{1,0:T(8,128)S(1)}, f32[64,256]{1,0:T(8,128)S(1)}, u32[]{:S(2)}, u32[]{:S(2)}) collective-permute-start(f32[64,256]{1,0:T(8,128)S(1)} %get-tuple-element.32.refs_0_), channel_id=1, source_target_pairs={{0,2},{1,3},{2,0},{3,1},{4,6},{5,7},{6,4},{7,5},{8,10},{9,11},{10,... | collective-permute-start | bytes 196616 | tf_op jit(solution)/shard_map/ppermute | solution.py:266
  6.7 3.5 %copy-start.3 = (s32[256]{0:T(256)S(1)}, s32[256]{0:T(256)}, u32[]{:S(2)}) copy-start(s32[256]{0:T(256)} %param.7) | copy-start | bytes 3076
  6.7 22.3 %collective-permute-start.10 = (f32[64,768]{1,0:T(8,128)S(1)}, f32[64,768]{1,0:T(8,128)S(1)}, u32[]{:S(2)}, u32[]{:S(2)}) collective-permute-start(f32[64,768]{1,0:T(8,128)S(1)} %get-tuple-element.37.refs_4_), channel_id=1, source_target_pairs={{0,1},{1,0},{2,3},{3,2},{4,5},{5,4},{6,7},{7,6},{8,9},{9,8},{10,11... | collective-permute-start | bytes 589832 | tf_op jit(solution)/shard_map/ppermute | solution.py:266
  8.5 20.5 %collective-permute-start.11 = (f32[64,768]{1,0:T(8,128)S(1)}, f32[64,768]{1,0:T(8,128)S(1)}, u32[]{:S(2)}, u32[]{:S(2)}) collective-permute-start(f32[64,768]{1,0:T(8,128)S(1)} %get-tuple-element.37.refs_4_), channel_id=1, source_target_pairs={{0,2},{1,3},{2,0},{3,1},{4,6},{5,7},{6,4},{7,5},{8,10},{9,11},{10,... | collective-permute-start | bytes 589832 | tf_op jit(solution)/shard_map/ppermute | solution.py:266
  10.2 1.2 %copy-start = (f32[1024,256]{1,0:T(8,128)S(1)}, f32[1024,256]{1,0:T(8,128)}, u32[]{:S(2)}) copy-start(f32[1024,256]{1,0:T(8,128)} %slab_ref.3) | copy-start | bytes 3145732
  12.1 16.9 %collective-permute-start.12 = (f32[64,768]{1,0:T(8,128)S(1)}, f32[64,768]{1,0:T(8,128)S(1)}, u32[]{:S(2)}, u32[]{:S(2)}) collective-permute-start(f32[64,768]{1,0:T(8,128)S(1)} %get-tuple-element.37.refs_4_), channel_id=1, source_target_pairs={{0,3},{1,2},{2,1},{3,0},{4,7},{5,6},{6,5},{7,4},{8,11},{9,10},{10,... | collective-permute-start | bytes 589832 | tf_op jit(solution)/shard_map/ppermute | solution.py:266
  13.3 1.3 %collective-permute-start.9 = (f32[64,256]{1,0:T(8,128)S(1)}, f32[64,256]{1,0:T(8,128)S(1)}, u32[]{:S(2)}, u32[]{:S(2)}) collective-permute-start(f32[64,256]{1,0:T(8,128)S(1)} %pad_maximum_fusion.3), channel_id=1, source_target_pairs={{0,4},{4,0},{8,12},{12,8},{16,20},{20,16},{24,28},{28,24},{1,5},{5... | collective-permute-start | bytes 196616 | tf_op jit(solution)/shard_map/ppermute | solution.py:333
  14.6 14.4 %copy-start.1 = (f32[1024,256]{1,0:T(8,128)S(1)}, f32[1024,256]{1,0:T(8,128)}, u32[]{:S(2)}) copy-start(f32[1024,256]{1,0:T(8,128)} %slab_ref.3) | copy-start | bytes 3145732
  14.7 1.7 %collective-permute-start = (f32[128,256]{1,0:T(8,128)S(1)}, f32[128,256]{1,0:T(8,128)S(1)}, u32[]{:S(2)}, u32[]{:S(2)}) collective-permute-start(f32[128,256]{1,0:T(8,128)S(1)} %slice.28), channel_id=1, source_target_pairs={{0,4},{4,0},{8,12},{12,8},{16,20},{20,16},{24,28},{28,24},{1,5},{5... | collective-permute-start | bytes 393224 | tf_op jit(solution)/shard_map/cond/branch_1_fun/ppermute | solution.py:299
  14.9 4.7 %collective-permute-start.3 = (f32[192,256]{1,0:T(8,128)S(1)}, f32[192,256]{1,0:T(8,128)S(1)}, u32[]{:S(2)}, u32[]{:S(2)}) collective-permute-start(f32[192,256]{1,0:T(8,128)S(1)} %get-tuple-element.18.held_ref), channel_id=1, source_target_pairs={{0,16},{4,0},{8,12},{12,8},{16,20},{20,4},{24,28},{28,24},{1,17},{... | collective-permute-start | bytes 589832 | tf_op jit(solution)/shard_map/cond/branch_1_fun/ppermute | solution.py:303
  16.5 5.3 %collective-permute-start.1 = (f32[128,256]{1,0:T(8,128)S(1)}, f32[128,256]{1,0:T(8,128)S(1)}, u32[]{:S(2)}, u32[]{:S(2)}) collective-permute-start(f32[128,256]{1,0:T(8,128)S(1)} %pad_maximum_fusion.2), channel_id=1, source_target_pairs={{0,8},{4,12},{8,0},{12,4},{16,24},{20,28},{24,16},{28,20},{1,9},{5... | collective-permute-start | bytes 393224 | tf_op jit(solution)/shard_map/cond/branch_1_fun/ppermute | solution.py:312
  19.6 4.6 %collective-permute-start.4 = (f32[192,256]{1,0:T(8,128)S(1)}, f32[192,256]{1,0:T(8,128)S(1)}, u32[]{:S(2)}, u32[]{:S(2)}) collective-permute-start(f32[192,256]{1,0:T(8,128)S(1)} %branch_1_fun.5.held_ref), channel_id=1, source_target_pairs={{0,8},{4,0},{8,12},{12,4},{16,24},{20,16},{24,28},{28,20},{1,9},{5... | collective-permute-start | bytes 589832 | tf_op jit(solution)/shard_map/cond/branch_1_fun/ppermute | solution.py:303
  21.8 5.7 %collective-permute-start.2 = (f32[160,256]{1,0:T(8,128)S(1)}, f32[160,256]{1,0:T(8,128)S(1)}, u32[]{:S(2)}, u32[]{:S(2)}) collective-permute-start(f32[160,256]{1,0:T(8,128)S(1)} %pad_maximum_fusion.1), channel_id=1, source_target_pairs={{0,16},{4,20},{8,24},{12,28},{16,0},{20,4},{24,8},{28,12},{1,17},{... | collective-permute-start | bytes 491528 | tf_op jit(solution)/shard_map/cond/branch_1_fun/ppermute | solution.py:312
  26.0 2.0 %collective-permute-start.5 = (f32[192,256]{1,0:T(8,128)S(1)}, f32[192,256]{1,0:T(8,128)S(1)}, u32[]{:S(2)}, u32[]{:S(2)}) collective-permute-start(f32[192,256]{1,0:T(8,128)S(1)} %branch_1_fun.7), channel_id=1, source_target_pairs={{0,4},{4,0},{8,12},{12,8},{16,20},{20,16},{24,28},{28,24},{1,5},{5... | collective-permute-start | bytes 589832 | tf_op jit(solution)/shard_map/cond/branch_1_fun/ppermute | solution.py:328

commit v2 on v1

--- a/solution.py
+++ b/solution.py
@@ -63,7 +63,13 @@
     return owner_row[:1], rank_row, owner_col[:, :1], rank_col
 
 
-def pack_kernel(pivot_ref, slab_ref, packed_ref, lead_ref, local_ref):
+def pack_kernel(pivot_ref, slab_ref, packed_ref, lead_ref, local_ref, held, sems):
+    parts = sems.shape[0]
+    copies = []
+    for p in range(parts):
+        part = pl.ds(p * (slab_ref.shape[0] // parts), slab_ref.shape[0] // parts)
+        copies.append(pltpu.make_async_copy(slab_ref.at[part], held.at[part], sems.at[p]))
+        copies[-1].start()
     rows = slab_ref.shape[0]
     width = pivot_ref.shape[1]
     count = lead_ref.shape[0]
@@ -79,11 +85,13 @@
     slot = lax.broadcasted_iota(jnp.int32, (CAP, width), 0)
     mine = (owner_row == me) & (rank_row == slot)
     local = jnp.sum(jnp.where(mine, pivot_row - (me + 1) * rows, 0), axis=1, keepdims=True) + rows
-    one_hot = (lax.broadcasted_iota(jnp.int32, (CAP, rows), 1) == local).astype(F32).astype(BF16)
-    packed_ref[...] = select_rows(one_hot, slab_ref[...])
+    mine = (lax.broadcasted_iota(jnp.int32, (CAP, rows), 1) == local).astype(F32).astype(BF16)
     slot = lax.broadcasted_iota(jnp.int32, (count, width), 0)
-    one_hot = (slot == lead_place(owner_row, count // CAP) * CAP + rank_row).astype(F32).astype(BF16)
-    lead_ref[...] = select_rows(one_hot, slab_ref[:width, :])
+    lead = (slot == lead_place(owner_row, count // CAP) * CAP + rank_row).astype(F32).astype(BF16)
+    for copy in copies:
+        copy.wait()
+    packed_ref[...] = select_rows(mine, held[...])
+    lead_ref[...] = select_rows(lead, held[:width, :])
 
 
 def block_inverses(lower):
@@ -265,24 +273,32 @@
     def spread(block, order):
         return [block] + [lax.ppermute(block, "pcol", [(c, c ^ d) for c in range(m)]) for d in order]
 
-    top, rest = call(
-        cut_kernel,
-        (jax.ShapeDtypeStruct((piece, width), F32), jax.ShapeDtypeStruct((piece, rows - width), F32)),
-        (panel_t,),
-        in_specs=[pl.BlockSpec(memory_space=pl.ANY)],
-        scratch=[pltpu.SemaphoreType.DMA((rows // width,))],
-    )
+    def cut(panel_t):
+        return call(
+            cut_kernel,
+            (jax.ShapeDtypeStruct((piece, width), F32), jax.ShapeDtypeStruct((piece, rows - width), F32)),
+            (panel_t,),
+            in_specs=[pl.BlockSpec(memory_space=pl.ANY)],
+            scratch=[pltpu.SemaphoreType.DMA((rows // width,))],
+        )
+
+    top, rest = unit(me < n, cut, panel_t)
     tops, rests = spread(top, top_order(m)[1:]), spread(rest, range(1, m))
 
-    gathered, leading, local_rows = call(
-        pack_kernel,
-        (
-            jax.ShapeDtypeStruct((CAP, cols), F32),
-            jax.ShapeDtypeStruct((n * CAP, cols), F32),
-            jax.ShapeDtypeStruct((1, 128), jnp.int32),
-        ),
-        (pivot_row, slab),
-    )
+    def pack(pivot_row, slab):
+        return call(
+            pack_kernel,
+            (
+                jax.ShapeDtypeStruct((CAP, cols), F32),
+                jax.ShapeDtypeStruct((n * CAP, cols), F32),
+                jax.ShapeDtypeStruct((1, 128), jnp.int32),
+            ),
+            (pivot_row, slab),
+            in_specs=[VMEM, pl.BlockSpec(memory_space=pl.ANY)],
+            scratch=[pltpu.VMEM((rows, cols), F32), pltpu.SemaphoreType.DMA((8,))],
+        )
+
+    gathered, leading, local_rows = unit(me < n, pack, pivot_row, slab)
     lower = call(
         functools.partial(assemble_kernel, m),
         jax.ShapeDtypeStruct((width * 3 // 4, width), F32),

time: 31.5 us -> 32.2 us (1.022)
  Pallas kernels: 6.39 us -> 8.61 us
  local copies, waits for them, and re-layouts: 2.22 us -> 0.72 us
    pallas_call x9, Pallas kernels: 6.39 us -> 8.61 us  [call(): pl.pallas_call(kernel, out_shape=outs, in_specs=in_specs or [VMEM] * len(...]
    unnamed x8 -> x4, local copies, waits for them, and re-layouts: 2.18 us -> 0.68 us
  transfers between devices with their start and end apart: 13 -> 13, of which waited for: 5 -> 4; matrix products, arithmetic and copies ran while one was open for 1% -> 1% of each run, Pallas kernels for 13% -> 17%
where the time goes in v2:
time: 32.2 us; the launch traced here: 32 us
  starting transfers between devices  16.3 us (51%)
  Pallas kernels  8.61 us (27%)
  waiting for transfers between devices  5.92 us (18%)
  local copies, waits for them, and re-layouts  0.72 us (2%)
    ppermute x6, starting transfers between devices, spread(): lax.ppermute(block, 'pcol', [(c, c ^ d) for c in range(m)])  10.1 us
    pallas_call x9, Pallas kernels, call(): pl.pallas_call(kernel, out_shape=outs, in_specs=in_specs or [VMEM] * len(...  8.61 us
    ppermute x2, starting transfers between devices, levels(): moved = lax.ppermute(message, 'prow', [(r, r ^ other) for r in range(n)])  3.59 us
    ppermute x2, waiting for transfers between devices, levels(): moved = lax.ppermute(message, 'prow', [(r, r ^ other) for r in range(n)])  2.75 us
    ppermute x2, waiting for transfers between devices, levels(): lax.ppermute(lower, 'prow', [(r, tree_partner(r, span)) for r in range(n)])  1.91 us
    ppermute x2, starting transfers between devices, levels(): lax.ppermute(lower, 'prow', [(r, tree_partner(r, span)) for r in range(n)])  1.54 us
    ppermute x1, waiting for transfers between devices, local(): lax.ppermute(jnp.concatenate([gathered, gathered], axis=0), 'prow', [(r,...  1.24 us
    ppermute x1, starting transfers between devices, levels(): moved = lax.ppermute(inverse, 'prow', [(r, r ^ 1) for r in range(n)])  0.79 us
  transfers between devices with their start and end apart: 13, of which 4 were waited for; matrix products, arithmetic and copies ran while one was open for 1% of the time, Pallas kernels for 17%

profile of v2, /device:TPU:0, one launch (start us, length us, event | category | flops | bytes accessed | tf_op | source)
XLA Modules:
  0.0 32.0 jit_solution(5252300749777537104)
XLA Ops:
  0.0 1.0 %conditional.4 = ((f32[64,256]{1,0:T(8,128)S(1)}, f32[64,768]{1,0:T(8,128)S(1)})) conditional(s32[]{:T(128)} %convert_element_type.2, () %tuple.31, f32[64,1024]{1,0:T(8,128)} %bitcast.2), branch_computations={%region_2.0_spmd, %region_3.0_spmd} | conditional | flops 1 | bytes 262176 | solution.py:250
  0.0 1.0 %branch_1_fun.8 = (f32[64,256]{1,0:T(8,128)S(1)}, f32[64,768]{1,0:T(8,128)S(1)}) custom-call(f32[64,1024]{1,0:T(8,128)} %panel_ref), custom_call_target="tpu_custom_call" | custom-call | flops 1 | bytes 1 | tf_op jit(solution)/shard_map/cond/branch_1_fun/pallas_call | solution.py:254
  1.0 3.1 %collective-permute-start.6 = (f32[64,256]{1,0:T(8,128)S(1)}, f32[64,256]{1,0:T(8,128)S(1)}, u32[]{:S(2)}, u32[]{:S(2)}) collective-permute-start(f32[64,256]{1,0:T(8,128)S(1)} %get-tuple-element.39.refs_0_), channel_id=1, source_target_pairs={{0,1},{1,0},{2,3},{3,2},{4,5},{5,4},{6,7},{7,6},{8,9},{9,8},{10,11... | collective-permute-start | bytes 196616 | tf_op jit(solution)/shard_map/ppermute | solution.py:274
  4.1 2.5 %collective-permute-start.7 = (f32[64,256]{1,0:T(8,128)S(1)}, f32[64,256]{1,0:T(8,128)S(1)}, u32[]{:S(2)}, u32[]{:S(2)}) collective-permute-start(f32[64,256]{1,0:T(8,128)S(1)} %get-tuple-element.39.refs_0_), channel_id=1, source_target_pairs={{0,3},{1,2},{2,1},{3,0},{4,7},{5,6},{6,5},{7,4},{8,11},{9,10},{10,... | collective-permute-start | bytes 196616 | tf_op jit(solution)/shard_map/ppermute | solution.py:274
  6.7 1.8 %collective-permute-start.10 = (f32[64,768]{1,0:T(8,128)S(1)}, f32[64,768]{1,0:T(8,128)S(1)}, u32[]{:S(2)}, u32[]{:S(2)}) collective-permute-start(f32[64,768]{1,0:T(8,128)S(1)} %get-tuple-element.44.refs_4_), channel_id=1, source_target_pairs={{0,1},{1,0},{2,3},{3,2},{4,5},{5,4},{6,7},{7,6},{8,9},{9,8},{10,11... | collective-permute-start | bytes 589832 | tf_op jit(solution)/shard_map/ppermute | solution.py:274
  8.5 1.7 %collective-permute-start.11 = (f32[64,768]{1,0:T(8,128)S(1)}, f32[64,768]{1,0:T(8,128)S(1)}, u32[]{:S(2)}, u32[]{:S(2)}) collective-permute-start(f32[64,768]{1,0:T(8,128)S(1)} %get-tuple-element.44.refs_4_), channel_id=1, source_target_pairs={{0,2},{1,3},{2,0},{3,1},{4,6},{5,7},{6,4},{7,5},{8,10},{9,11},{10,... | collective-permute-start | bytes 589832 | tf_op jit(solution)/shard_map/ppermute | solution.py:274
  10.1 0.7 %copy-done.1 = s32[256]{0:T(256)S(1)} copy-done((s32[256]{0:T(256)S(1)}, s32[256]{0:T(256)}, u32[]{:S(2)}) %copy-start.1) | copy-done | bytes 1048
  10.8 2.0 %conditional.3 = ((f32[32,256]{1,0:T(8,128)S(1)}, f32[256,256]{1,0:T(8,128)S(1)}, s32[1,128]{1,0:T(1,128)S(1)})) conditional(s32[]{:T(128)} %convert_element_type.2, () %tuple.28, (s32[1,256]{1,0:T(1,128)S(1)}, f32[1024,256]{1,0:T(8,128)}) %tuple.45), branch_computations={%region_0.0_spmd, %region_1.0_spmd} | conditional | flops 1 | bytes 295468 | solution.py:250
  10.8 2.0 %branch_1_fun.7 = (f32[32,256]{1,0:T(8,128)S(1)}, f32[256,256]{1,0:T(8,128)S(1)}, s32[1,128]{1,0:T(1,128)S(1)}) custom-call(s32[1,256]{1,0:T(1,128)S(1)} %get-tuple-element.20.pivot_ref, f32[1024,256]{1,0:T(8,128)} %get-tuple-element.21.slab_ref), custom_call_target="tpu_custom_call" | custom-call | flops 1 | bytes 1 | tf_op jit(solution)/shard_map/cond/branch_1_fun/pallas_call | solution.py:254
  12.9 1.0 %collective-permute-start.12 = (f32[64,768]{1,0:T(8,128)S(1)}, f32[64,768]{1,0:T(8,128)S(1)}, u32[]{:S(2)}, u32[]{:S(2)}) collective-permute-start(f32[64,768]{1,0:T(8,128)S(1)} %get-tuple-element.44.refs_4_), channel_id=1, source_target_pairs={{0,3},{1,2},{2,1},{3,0},{4,7},{5,6},{6,5},{7,4},{8,11},{9,10},{10,... | collective-permute-start | bytes 589832 | tf_op jit(solution)/shard_map/ppermute | solution.py:274
  14.0 1.2 %collective-permute-done.9 = f32[64,256]{1,0:T(8,128)S(1)} collective-permute-done((f32[64,256]{1,0:T(8,128)S(1)}, f32[64,256]{1,0:T(8,128)S(1)}, u32[]{:S(2)}, u32[]{:S(2)}) %collective-permute-start.9) | collective-permute-done | bytes 65568 | tf_op jit(solution)/shard_map/ppermute | solution.py:349
  15.2 14.4 %conditional.5 = (f32[32,256]{1,0:T(8,128)S(1)}, f32[256,256]{1,0:T(8,128)S(1)}) conditional(s32[]{:T(128)} %convert_element_type.2, () %tuple.30, (s32[]{:T(128)}, f32[256,256]{1,0:T(8,128)S(1)}, f32[64,256]{1,0:T(8,128)S(1)}, f32[192,256]{1,0:T(8,128)S(1)}, s32[1,256]{1,0:T(1,128)S(1)}) %tuple.46), branch_computations={%region_4.0_spmd, %region_5.6_spmd} | conditional | flops 352267 | bytes 7307592 | solution.py:250
  15.3 0.2 collective-permute-start
  15.5 1.5 %collective-permute-start.3 = (f32[192,256]{1,0:T(8,128)S(1)}, f32[192,256]{1,0:T(8,128)S(1)}, u32[]{:S(2)}, u32[]{:S(2)}) collective-permute-start(f32[192,256]{1,0:T(8,128)S(1)} %get-tuple-element.25.held_ref), channel_id=1, source_target_pairs={{0,16},{4,0},{8,12},{12,8},{16,20},{20,4},{24,28},{28,24},{1,17},{... | collective-permute-start | bytes 589832 | tf_op jit(solution)/shard_map/cond/branch_1_fun/ppermute | solution.py:319
  17.1 1.2 %collective-permute-start.1 = (f32[128,256]{1,0:T(8,128)S(1)}, f32[128,256]{1,0:T(8,128)S(1)}, u32[]{:S(2)}, u32[]{:S(2)}) collective-permute-start(f32[128,256]{1,0:T(8,128)S(1)} %pad_maximum_fusion.2), channel_id=1, source_target_pairs={{0,8},{4,12},{8,0},{12,4},{16,24},{20,28},{24,16},{28,20},{1,9},{5... | collective-permute-start | bytes 393224 | tf_op jit(solution)/shard_map/cond/branch_1_fun/ppermute | solution.py:328
  18.3 1.9 %collective-permute-done.3.moved_ref = f32[192,256]{1,0:T(8,128)S(1)} collective-permute-done((f32[192,256]{1,0:T(8,128)S(1)}, f32[192,256]{1,0:T(8,128)S(1)}, u32[]{:S(2)}, u32[]{:S(2)}) %collective-permute-start.3) | collective-permute-done | bytes 196640 | tf_op jit(solution)/shard_map/cond/branch_1_fun/ppermute | solution.py:319
  20.3 2.1 %collective-permute-done.1 = f32[128,256]{1,0:T(8,128)S(1)} collective-permute-done((f32[128,256]{1,0:T(8,128)S(1)}, f32[128,256]{1,0:T(8,128)S(1)}, u32[]{:S(2)}, u32[]{:S(2)}) %collective-permute-start.1) | collective-permute-done | bytes 131104 | tf_op jit(solution)/shard_map/cond/branch_1_fun/ppermute | solution.py:328
  22.4 2.4 %collective-permute-start.2 = (f32[160,256]{1,0:T(8,128)S(1)}, f32[160,256]{1,0:T(8,128)S(1)}, u32[]{:S(2)}, u32[]{:S(2)}) collective-permute-start(f32[160,256]{1,0:T(8,128)S(1)} %pad_maximum_fusion.1), channel_id=1, source_target_pairs={{0,16},{4,20},{8,24},{12,28},{16,0},{20,4},{24,8},{28,12},{1,17},{... | collective-permute-start | bytes 491528 | tf_op jit(solution)/shard_map/cond/branch_1_fun/ppermute | solution.py:328
  24.8 1.8 %branch_1_fun.11 = f32[192,256]{1,0:T(8,128)S(1)} custom-call(f32[192,256]{1,0:T(8,128)S(1)} %branch_1_fun.10.lower_ref), custom_call_target="tpu_custom_call" | custom-call | flops 1 | bytes 1 | tf_op jit(solution)/shard_map/cond/branch_1_fun/pallas_call | solution.py:254
  26.7 0.8 %collective-permute-start.5 = (f32[192,256]{1,0:T(8,128)S(1)}, f32[192,256]{1,0:T(8,128)S(1)}, u32[]{:S(2)}, u32[]{:S(2)}) collective-permute-start(f32[192,256]{1,0:T(8,128)S(1)} %branch_1_fun.11), channel_id=1, source_target_pairs={{0,4},{4,0},{8,12},{12,8},{16,20},{20,16},{24,28},{28,24},{1,5},{5... | collective-permute-start | bytes 589832 | tf_op jit(solution)/shard_map/cond/branch_1_fun/ppermute | solution.py:344
  27.4 0.6 %collective-permute-done.2 = f32[160,256]{1,0:T(8,128)S(1)} collective-permute-done((f32[160,256]{1,0:T(8,128)S(1)}, f32[160,256]{1,0:T(8,128)S(1)}, u32[]{:S(2)}, u32[]{:S(2)}) %collective-permute-start.2) | collective-permute-done | bytes 163872 | tf_op jit(solution)/shard_map/cond/branch_1_fun/ppermute | solution.py:328
  28.1 0.5 %branch_1_fun.12.pivot_rows_ref = f32[256,256]{1,0:T(8,128)S(1)} custom-call(s32[1,256]{1,0:T(1,128)S(1)} %get-tuple-element.26.pivot_ref, f32[256,256]{1,0:T(8,128)S(1)} %pad_maximum_fusion.gathered_ref), custom_call_target="tpu_custom_call" | custom-call | flops 1 | bytes 1 | tf_op jit(solution)/shard_map/cond/branch_1_fun/pallas_call | solution.py:254
  28.7 0.9 %branch_1_fun.13 = f32[256,256]{1,0:T(8,128)S(1)} custom-call(f32[192,256]{1,0:T(8,128)S(1)} %broadcast_select_fusion.inverse_ref, f32[256,256]{1,0:T(8,128)S(1)} %branch_1_fun.12.pivot_rows_ref), custom_call_target="tpu_custom_call" | custom-call | flops 1 | bytes 1 | tf_op jit(solution)/shard_map/cond/branch_1_fun/pallas_call | solution.py:254
  29.7 2.3 %shard_map.38 = f32[1024,256]{1,0:T(8,128)} custom-call(s32[1,128]{1,0:T(1,128)S(1)} %get-tuple-element.36.local_ref, f32[32,256]{1,0:T(8,128)S(1)} %get-tuple-element.42.lead_ref, f32[256,256]{1,0:T(8,128)S(1)} %get-tuple-element.43.x_ref, f32[1024,256]{1,0:T(8,128)S(1)} %copy-done, f32[64,256]{1,0:T(8,128)S(1)} %get-tuple-element.39.refs_0_, ...), custom_call_target="tpu_custom_call" | custom-call | flops 1 | bytes 1 | tf_op jit(solution)/shard_map/pallas_call | solution.py:254
  (32 shorter events, 0.5 us)
Async XLA Ops:
  1.0 11.9 %collective-permute-start.6 = (f32[64,256]{1,0:T(8,128)S(1)}, f32[64,256]{1,0:T(8,128)S(1)}, u32[]{:S(2)}, u32[]{:S(2)}) collective-permute-start(f32[64,256]{1,0:T(8,128)S(1)} %get-tuple-element.39.refs_0_), channel_id=1, source_target_pairs={{0,1},{1,0},{2,3},{3,2},{4,5},{5,4},{6,7},{7,6},{8,9},{9,8},{10,11... | collective-permute-start | bytes 196616 | tf_op jit(solution)/shard_map/ppermute | solution.py:274
  4.1 9.8 %collective-permute-start.7 = (f32[64,256]{1,0:T(8,128)S(1)}, f32[64,256]{1,0:T(8,128)S(1)}, u32[]{:S(2)}, u32[]{:S(2)}) collective-permute-start(f32[64,256]{1,0:T(8,128)S(1)} %get-tuple-element.39.refs_0_), channel_id=1, source_target_pairs={{0,3},{1,2},{2,1},{3,0},{4,7},{5,6},{6,5},{7,4},{8,11},{9,10},{10,... | collective-permute-start | bytes 196616 | tf_op jit(solution)/shard_map/ppermute | solution.py:274
  6.5 7.3 %collective-permute-start.8 = (f32[64,256]{1,0:T(8,128)S(1)}, f32[64,256]{1,0:T(8,128)S(1)}, u32[]{:S(2)}, u32[]{:S(2)}) collective-permute-start(f32[64,256]{1,0:T(8,128)S(1)} %get-tuple-element.39.refs_0_), channel_id=1, source_target_pairs={{0,2},{1,3},{2,0},{3,1},{4,6},{5,7},{6,4},{7,5},{8,10},{9,11},{10,... | collective-permute-start | bytes 196616 | tf_op jit(solution)/shard_map/ppermute | solution.py:274
  6.7 23.0 %collective-permute-start.10 = (f32[64,768]{1,0:T(8,128)S(1)}, f32[64,768]{1,0:T(8,128)S(1)}, u32[]{:S(2)}, u32[]{:S(2)}) collective-permute-start(f32[64,768]{1,0:T(8,128)S(1)} %get-tuple-element.44.refs_4_), channel_id=1, source_target_pairs={{0,1},{1,0},{2,3},{3,2},{4,5},{5,4},{6,7},{7,6},{8,9},{9,8},{10,11... | collective-permute-start | bytes 589832 | tf_op jit(solution)/shard_map/ppermute | solution.py:274
  8.5 21.2 %collective-permute-start.11 = (f32[64,768]{1,0:T(8,128)S(1)}, f32[64,768]{1,0:T(8,128)S(1)}, u32[]{:S(2)}, u32[]{:S(2)}) collective-permute-start(f32[64,768]{1,0:T(8,128)S(1)} %get-tuple-element.44.refs_4_), channel_id=1, source_target_pairs={{0,2},{1,3},{2,0},{3,1},{4,6},{5,7},{6,4},{7,5},{8,10},{9,11},{10,... | collective-permute-start | bytes 589832 | tf_op jit(solution)/shard_map/ppermute | solution.py:274
  10.1 0.7 %copy-start.1 = (s32[256]{0:T(256)S(1)}, s32[256]{0:T(256)}, u32[]{:S(2)}) copy-start(s32[256]{0:T(256)} %param.11) | copy-start | bytes 3076
  12.9 16.8 %collective-permute-start.12 = (f32[64,768]{1,0:T(8,128)S(1)}, f32[64,768]{1,0:T(8,128)S(1)}, u32[]{:S(2)}, u32[]{:S(2)}) collective-permute-start(f32[64,768]{1,0:T(8,128)S(1)} %get-tuple-element.44.refs_4_), channel_id=1, source_target_pairs={{0,3},{1,2},{2,1},{3,0},{4,7},{5,6},{6,5},{7,4},{8,11},{9,10},{10,... | collective-permute-start | bytes 589832 | tf_op jit(solution)/shard_map/ppermute | solution.py:274
  13.9 1.3 %collective-permute-start.9 = (f32[64,256]{1,0:T(8,128)S(1)}, f32[64,256]{1,0:T(8,128)S(1)}, u32[]{:S(2)}, u32[]{:S(2)}) collective-permute-start(f32[64,256]{1,0:T(8,128)S(1)} %pad_maximum_fusion.3), channel_id=1, source_target_pairs={{0,4},{4,0},{8,12},{12,8},{16,20},{20,16},{24,28},{28,24},{1,5},{5... | collective-permute-start | bytes 196616 | tf_op jit(solution)/shard_map/ppermute | solution.py:349
  15.2 14.4 %copy-start = (f32[1024,256]{1,0:T(8,128)S(1)}, f32[1024,256]{1,0:T(8,128)}, u32[]{:S(2)}) copy-start(f32[1024,256]{1,0:T(8,128)} %slab_ref.1) | copy-start | bytes 3145732
  15.3 1.7 %collective-permute-start = (f32[128,256]{1,0:T(8,128)S(1)}, f32[128,256]{1,0:T(8,128)S(1)}, u32[]{:S(2)}, u32[]{:S(2)}) collective-permute-start(f32[128,256]{1,0:T(8,128)S(1)} %slice.28), channel_id=1, source_target_pairs={{0,4},{4,0},{8,12},{12,8},{16,20},{20,16},{24,28},{28,24},{1,5},{5... | collective-permute-start | bytes 393224 | tf_op jit(solution)/shard_map/cond/branch_1_fun/ppermute | solution.py:315
  15.5 4.7 %collective-permute-start.3 = (f32[192,256]{1,0:T(8,128)S(1)}, f32[192,256]{1,0:T(8,128)S(1)}, u32[]{:S(2)}, u32[]{:S(2)}) collective-permute-start(f32[192,256]{1,0:T(8,128)S(1)} %get-tuple-element.25.held_ref), channel_id=1, source_target_pairs={{0,16},{4,0},{8,12},{12,8},{16,20},{20,4},{24,28},{28,24},{1,17},{... | collective-permute-start | bytes 589832 | tf_op jit(solution)/shard_map/cond/branch_1_fun/ppermute | solution.py:319
  17.1 5.3 %collective-permute-start.1 = (f32[128,256]{1,0:T(8,128)S(1)}, f32[128,256]{1,0:T(8,128)S(1)}, u32[]{:S(2)}, u32[]{:S(2)}) collective-permute-start(f32[128,256]{1,0:T(8,128)S(1)} %pad_maximum_fusion.2), channel_id=1, source_target_pairs={{0,8},{4,12},{8,0},{12,4},{16,24},{20,28},{24,16},{28,20},{1,9},{5... | collective-permute-start | bytes 393224 | tf_op jit(solution)/shard_map/cond/branch_1_fun/ppermute | solution.py:328
  20.2 4.6 %collective-permute-start.4 = (f32[192,256]{1,0:T(8,128)S(1)}, f32[192,256]{1,0:T(8,128)S(1)}, u32[]{:S(2)}, u32[]{:S(2)}) collective-permute-start(f32[192,256]{1,0:T(8,128)S(1)} %branch_1_fun.9.held_ref), channel_id=1, source_target_pairs={{0,8},{4,0},{8,12},{12,4},{16,24},{20,16},{24,28},{28,20},{1,9},{5... | collective-permute-start | bytes 589832 | tf_op jit(solution)/shard_map/cond/branch_1_fun/ppermute | solution.py:319
  22.4 5.7 %collective-permute-start.2 = (f32[160,256]{1,0:T(8,128)S(1)}, f32[160,256]{1,0:T(8,128)S(1)}, u32[]{:S(2)}, u32[]{:S(2)}) collective-permute-start(f32[160,256]{1,0:T(8,128)S(1)} %pad_maximum_fusion.1), channel_id=1, source_target_pairs={{0,16},{4,20},{8,24},{12,28},{16,0},{20,4},{24,8},{28,12},{1,17},{... | collective-permute-start | bytes 491528 | tf_op jit(solution)/shard_map/cond/branch_1_fun/ppermute | solution.py:328
  26.7 2.0 %collective-permute-start.5 = (f32[192,256]{1,0:T(8,128)S(1)}, f32[192,256]{1,0:T(8,128)S(1)}, u32[]{:S(2)}, u32[]{:S(2)}) collective-permute-start(f32[192,256]{1,0:T(8,128)S(1)} %branch_1_fun.11), channel_id=1, source_target_pairs={{0,4},{4,0},{8,12},{12,8},{16,20},{20,16},{24,28},{28,24},{1,5},{5... | collective-permute-start | bytes 589832 | tf_op jit(solution)/shard_map/cond/branch_1_fun/ppermute | solution.py:344

commit v3 on v1

--- a/solution.py
+++ b/solution.py
@@ -33,7 +33,11 @@
 
 
 def dot_full(a, b):
-    return jnp.dot(a, b, precision=lax.Precision.HIGHEST, preferred_element_type=F32)
+    high, mid, low = split3(a)
+    left = jnp.concatenate([low, mid, high, mid, high, high], axis=1)
+    high, mid, low = split3(b)
+    right = jnp.concatenate([high, mid, low, high, mid, high], axis=0)
+    return jnp.dot(left, right, preferred_element_type=F32)
 
 
 def tree_partner(r, span):
@@ -193,37 +197,32 @@
     x_ref[half:, :] = dot_full(inverse_ref[:half, half:], pivot_rows_ref[half:, :] - dot_full(quarter, first))
 
 
-def product(piece, upper):
-    high, low = split2(piece)
-    upper_high, upper_low = split2(upper)
-    left = jnp.concatenate([high, high, low], axis=0)
-    right = jnp.concatenate([upper_high, upper_low, upper_high], axis=0)
-    return lax.dot_general(left, right, (((0,), (0,)), ((), ())), preferred_element_type=F32)
-
-
-def piece_rows(x_ref, m, d):
-    piece = x_ref.shape[0] // m
-    source = jnp.bitwise_xor(lax.axis_index("pcol"), d)
-    return x_ref[pl.ds(pl.multiple_of(source * piece, piece), piece), :]
-
-
 def update_kernel(m, local_ref, lead_ref, x_ref, slab_ref, *refs):
-    *pieces, out_ref, result, sems = refs
-    tops, rests = dict(zip(top_order(m), pieces[:m])), pieces[m:]
+    *pieces, out_ref, result, high_t, low_t, sems = refs
+    tops, rests = zip(top_order(m), pieces[:m]), zip(range(m), pieces[m:])
     rows, cols = slab_ref.shape
     width = x_ref.shape[0]
+    piece = width // m
+    z = lax.axis_index("pcol")
+    for blocks, columns in ((tops, pl.ds(0, width)), (rests, pl.ds(width, rows - width))):
+        for d, ref in blocks:
+            place = pl.ds(pl.multiple_of(jnp.bitwise_xor(z, d) * piece, piece), piece)
+            high_t[place, columns], low_t[place, columns] = split2(ref[...])
+    upper_high, upper_low = split2(x_ref[...])
+    upper = jnp.concatenate([upper_high, upper_low], axis=1)
     result[:rows, :] = slab_ref[...]
     for s in range(CAP):
         result[pl.ds(local_ref[0, s], 1), :] = lead_ref[pl.ds(s, 1), :]
-    uppers = [piece_rows(x_ref, m, d) for d in range(m)]
+
+    def product(part_t, factor):
+        return lax.dot_general(part_t, factor, (((0,), (0,)), ((), ())), preferred_element_type=F32)
+
     copies = []
     for c in range(rows // width):
         part = pl.ds(c * width, width)
-        total = result[part, :]
-        for d, upper in enumerate(uppers):
-            piece = rests[d][:, (c - 1) * width : c * width] if c else tops[d][...]
-            total = total - product(piece, upper)
-        result[part, :] = total
+        both = product(high_t[:, part], upper)
+        low = product(low_t[:, part], upper_high)
+        result[part, :] = result[part, :] - (both[:, :cols] + (both[:, cols:] + low))
         if c == 0:
 
             @pl.when(lax.axis_index("prow") == 0)
@@ -339,7 +338,12 @@
         (local_rows, leading, upper_rows, slab, *tops, *rests),
         in_specs=[pl.BlockSpec(memory_space=pltpu.SMEM)] + [VMEM] * (2 * m + 3),
         out_specs=pl.BlockSpec(memory_space=pl.ANY),
-        scratch=[pltpu.VMEM((rows + 8, cols), F32), pltpu.SemaphoreType.DMA((rows // width,))],
+        scratch=[
+            pltpu.VMEM((rows + 8, cols), F32),
+            pltpu.VMEM((width, rows), BF16),
+            pltpu.VMEM((width, rows), BF16),
+            pltpu.SemaphoreType.DMA((rows // width,)),
+        ],
     )
 
 

time: 31.5 us -> 31.5 us (level)
  transfers between devices with their start and end apart: 13 -> 13, of which waited for: 5 -> 5; matrix products, arithmetic and copies ran while one was open for 1% -> 1% of each run, Pallas kernels for 13% -> 12%
where the time goes in v3:
time: 31.5 us; the launch traced here: 31.3 us
  starting transfers between devices  16.3 us (52%)
  Pallas kernels  6.27 us (20%)
  waiting for transfers between devices  6.09 us (19%)
  local copies, waits for them, and re-layouts  2.22 us (7%)
    ppermute x6, starting transfers between devices, spread(): lax.ppermute(block, 'pcol', [(c, c ^ d) for c in range(m)])  10.1 us
    pallas_call x9, Pallas kernels, call(): pl.pallas_call(kernel, out_shape=outs, in_specs=in_specs or [VMEM] * len(...  6.27 us
    ppermute x2, starting transfers between devices, levels(): moved = lax.ppermute(message, 'prow', [(r, r ^ other) for r in range(n)])  3.59 us
    ppermute x2, waiting for transfers between devices, levels(): moved = lax.ppermute(message, 'prow', [(r, r ^ other) for r in range(n)])  2.8 us
    unnamed x8, local copies, waits for them, and re-layouts  2.18 us
    ppermute x2, waiting for transfers between devices, levels(): lax.ppermute(lower, 'prow', [(r, tree_partner(r, span)) for r in range(n)])  1.91 us
    ppermute x2, starting transfers between devices, levels(): lax.ppermute(lower, 'prow', [(r, tree_partner(r, span)) for r in range(n)])  1.54 us
    ppermute x1, waiting for transfers between devices, local(): lax.ppermute(jnp.concatenate([gathered, gathered], axis=0), 'prow', [(r,...  1.24 us
  transfers between devices with their start and end apart: 13, of which 5 were waited for; matrix products, arithmetic and copies ran while one was open for 1% of the time, Pallas kernels for 12%

profile of v3, /device:TPU:0, one launch (start us, length us, event | category | flops | bytes accessed | tf_op | source)
XLA Modules:
  0.0 31.3 jit_solution(11935042557239511007)
XLA Ops:
  0.0 0.9 %copy-done.2 = f32[1024,64]{0,1:T(8,128)S(1)} copy-done((f32[1024,64]{0,1:T(8,128)S(1)}, f32[1024,64]{0,1:T(8,128)}, u32[]{:S(2)}) %copy-start.2) | copy-done | bytes 262168
  1.0 3.1 %collective-permute-start.6 = (f32[64,256]{1,0:T(8,128)S(1)}, f32[64,256]{1,0:T(8,128)S(1)}, u32[]{:S(2)}, u32[]{:S(2)}) collective-permute-start(f32[64,256]{1,0:T(8,128)S(1)} %get-tuple-element.32.refs_0_), channel_id=1, source_target_pairs={{0,1},{1,0},{2,3},{3,2},{4,5},{5,4},{6,7},{7,6},{8,9},{9,8},{10,11... | collective-permute-start | bytes 196616 | tf_op jit(solution)/shard_map/ppermute | solution.py:265
  4.1 2.5 %collective-permute-start.7 = (f32[64,256]{1,0:T(8,128)S(1)}, f32[64,256]{1,0:T(8,128)S(1)}, u32[]{:S(2)}, u32[]{:S(2)}) collective-permute-start(f32[64,256]{1,0:T(8,128)S(1)} %get-tuple-element.32.refs_0_), channel_id=1, source_target_pairs={{0,3},{1,2},{2,1},{3,0},{4,7},{5,6},{6,5},{7,4},{8,11},{9,10},{10,... | collective-permute-start | bytes 196616 | tf_op jit(solution)/shard_map/ppermute | solution.py:265
  6.6 0.1 collective-permute-start.8
  6.7 1.8 %collective-permute-start.10 = (f32[64,768]{1,0:T(8,128)S(1)}, f32[64,768]{1,0:T(8,128)S(1)}, u32[]{:S(2)}, u32[]{:S(2)}) collective-permute-start(f32[64,768]{1,0:T(8,128)S(1)} %get-tuple-element.37.refs_4_), channel_id=1, source_target_pairs={{0,1},{1,0},{2,3},{3,2},{4,5},{5,4},{6,7},{7,6},{8,9},{9,8},{10,11... | collective-permute-start | bytes 589832 | tf_op jit(solution)/shard_map/ppermute | solution.py:265
  8.5 1.7 %collective-permute-start.11 = (f32[64,768]{1,0:T(8,128)S(1)}, f32[64,768]{1,0:T(8,128)S(1)}, u32[]{:S(2)}, u32[]{:S(2)}) collective-permute-start(f32[64,768]{1,0:T(8,128)S(1)} %get-tuple-element.37.refs_4_), channel_id=1, source_target_pairs={{0,2},{1,3},{2,0},{3,1},{4,6},{5,7},{6,4},{7,5},{8,10},{9,11},{10,... | collective-permute-start | bytes 589832 | tf_op jit(solution)/shard_map/ppermute | solution.py:265
  10.2 1.2 %copy-done = f32[1024,256]{1,0:T(8,128)S(1)} copy-done((f32[1024,256]{1,0:T(8,128)S(1)}, f32[1024,256]{1,0:T(8,128)}, u32[]{:S(2)}) %copy-start) | copy-done | bytes 1048600
  11.4 0.7 %shard_map.37 = (f32[32,256]{1,0:T(8,128)S(1)}, f32[256,256]{1,0:T(8,128)S(1)}, s32[1,128]{1,0:T(1,128)S(1)}) custom-call(s32[1,256]{1,0:T(1,128)S(1)} %bitcast.3, f32[1024,256]{1,0:T(8,128)S(1)} %copy-done), custom_call_target="tpu_custom_call" | custom-call | flops 1 | bytes 1 | tf_op jit(solution)/shard_map/pallas_call | solution.py:245
  12.1 1.0 %collective-permute-start.12 = (f32[64,768]{1,0:T(8,128)S(1)}, f32[64,768]{1,0:T(8,128)S(1)}, u32[]{:S(2)}, u32[]{:S(2)}) collective-permute-start(f32[64,768]{1,0:T(8,128)S(1)} %get-tuple-element.37.refs_4_), channel_id=1, source_target_pairs={{0,3},{1,2},{2,1},{3,0},{4,7},{5,6},{6,5},{7,4},{8,11},{9,10},{10,... | collective-permute-start | bytes 589832 | tf_op jit(solution)/shard_map/ppermute | solution.py:265
  13.1 0.1 collective-permute-done.8.refs_3_
  13.4 1.2 %collective-permute-done.9 = f32[64,256]{1,0:T(8,128)S(1)} collective-permute-done((f32[64,256]{1,0:T(8,128)S(1)}, f32[64,256]{1,0:T(8,128)S(1)}, u32[]{:S(2)}, u32[]{:S(2)}) %collective-permute-start.9) | collective-permute-done | bytes 65568 | tf_op jit(solution)/shard_map/ppermute | solution.py:332
  14.6 14.2 %conditional.1 = (f32[32,256]{1,0:T(8,128)S(1)}, f32[256,256]{1,0:T(8,128)S(1)}) conditional(s32[]{:T(128)} %convert_element_type.3, () %tuple.14, (s32[]{:T(128)}, f32[256,256]{1,0:T(8,128)S(1)}, f32[64,256]{1,0:T(8,128)S(1)}, f32[192,256]{1,0:T(8,128)S(1)}, s32[1,256]{1,0:T(1,128)S(1)}) %tuple.20), branch_computations={%region_0.0_spmd, %region_1.2_spmd} | conditional | flops 352267 | bytes 7307592 | solution.py:241
  14.7 0.2 collective-permute-start
  14.9 1.5 %collective-permute-start.3 = (f32[192,256]{1,0:T(8,128)S(1)}, f32[192,256]{1,0:T(8,128)S(1)}, u32[]{:S(2)}, u32[]{:S(2)}) collective-permute-start(f32[192,256]{1,0:T(8,128)S(1)} %get-tuple-element.18.held_ref), channel_id=1, source_target_pairs={{0,16},{4,0},{8,12},{12,8},{16,20},{20,4},{24,28},{28,24},{1,17},{... | collective-permute-start | bytes 589832 | tf_op jit(solution)/shard_map/cond/branch_1_fun/ppermute | solution.py:302
  16.5 1.2 %collective-permute-start.1 = (f32[128,256]{1,0:T(8,128)S(1)}, f32[128,256]{1,0:T(8,128)S(1)}, u32[]{:S(2)}, u32[]{:S(2)}) collective-permute-start(f32[128,256]{1,0:T(8,128)S(1)} %pad_maximum_fusion.2), channel_id=1, source_target_pairs={{0,8},{4,12},{8,0},{12,4},{16,24},{20,28},{24,16},{28,20},{1,9},{5... | collective-permute-start | bytes 393224 | tf_op jit(solution)/shard_map/cond/branch_1_fun/ppermute | solution.py:311
  17.7 1.9 %collective-permute-done.3.moved_ref = f32[192,256]{1,0:T(8,128)S(1)} collective-permute-done((f32[192,256]{1,0:T(8,128)S(1)}, f32[192,256]{1,0:T(8,128)S(1)}, u32[]{:S(2)}, u32[]{:S(2)}) %collective-permute-start.3) | collective-permute-done | bytes 196640 | tf_op jit(solution)/shard_map/cond/branch_1_fun/ppermute | solution.py:302
  19.6 2.1 %collective-permute-done.1 = f32[128,256]{1,0:T(8,128)S(1)} collective-permute-done((f32[128,256]{1,0:T(8,128)S(1)}, f32[128,256]{1,0:T(8,128)S(1)}, u32[]{:S(2)}, u32[]{:S(2)}) %collective-permute-start.1) | collective-permute-done | bytes 131104 | tf_op jit(solution)/shard_map/cond/branch_1_fun/ppermute | solution.py:311
  21.8 2.4 %collective-permute-start.2 = (f32[160,256]{1,0:T(8,128)S(1)}, f32[160,256]{1,0:T(8,128)S(1)}, u32[]{:S(2)}, u32[]{:S(2)}) collective-permute-start(f32[160,256]{1,0:T(8,128)S(1)} %pad_maximum_fusion.1), channel_id=1, source_target_pairs={{0,16},{4,20},{8,24},{12,28},{16,0},{20,4},{24,8},{28,12},{1,17},{... | collective-permute-start | bytes 491528 | tf_op jit(solution)/shard_map/cond/branch_1_fun/ppermute | solution.py:311
  24.2 1.8 %branch_1_fun.7 = f32[192,256]{1,0:T(8,128)S(1)} custom-call(f32[192,256]{1,0:T(8,128)S(1)} %branch_1_fun.6.lower_ref), custom_call_target="tpu_custom_call" | custom-call | flops 1 | bytes 1 | tf_op jit(solution)/shard_map/cond/branch_1_fun/pallas_call | solution.py:245
  26.0 0.8 %collective-permute-start.5 = (f32[192,256]{1,0:T(8,128)S(1)}, f32[192,256]{1,0:T(8,128)S(1)}, u32[]{:S(2)}, u32[]{:S(2)}) collective-permute-start(f32[192,256]{1,0:T(8,128)S(1)} %branch_1_fun.7), channel_id=1, source_target_pairs={{0,4},{4,0},{8,12},{12,8},{16,20},{20,16},{24,28},{28,24},{1,5},{5... | collective-permute-start | bytes 589832 | tf_op jit(solution)/shard_map/cond/branch_1_fun/ppermute | solution.py:327
  26.8 0.7 %collective-permute-done.2 = f32[160,256]{1,0:T(8,128)S(1)} collective-permute-done((f32[160,256]{1,0:T(8,128)S(1)}, f32[160,256]{1,0:T(8,128)S(1)}, u32[]{:S(2)}, u32[]{:S(2)}) %collective-permute-start.2) | collective-permute-done | bytes 163872 | tf_op jit(solution)/shard_map/cond/branch_1_fun/ppermute | solution.py:311
  27.5 0.5 %branch_1_fun.8.pivot_rows_ref = f32[256,256]{1,0:T(8,128)S(1)} custom-call(s32[1,256]{1,0:T(1,128)S(1)} %get-tuple-element.19.pivot_ref, f32[256,256]{1,0:T(8,128)S(1)} %pad_maximum_fusion.gathered_ref), custom_call_target="tpu_custom_call" | custom-call | flops 1 | bytes 1 | tf_op jit(solution)/shard_map/cond/branch_1_fun/pallas_call | solution.py:245
  28.1 0.7 %branch_1_fun.9 = f32[256,256]{1,0:T(8,128)S(1)} custom-call(f32[192,256]{1,0:T(8,128)S(1)} %broadcast_select_fusion.inverse_ref, f32[256,256]{1,0:T(8,128)S(1)} %branch_1_fun.8.pivot_rows_ref), custom_call_target="tpu_custom_call" | custom-call | flops 1 | bytes 1 | tf_op jit(solution)/shard_map/cond/branch_1_fun/pallas_call | solution.py:245
  28.9 2.4 %shard_map.40 = f32[1024,256]{1,0:T(8,128)} custom-call(s32[1,128]{1,0:T(1,128)S(1)} %get-tuple-element.29.local_ref, f32[32,256]{1,0:T(8,128)S(1)} %get-tuple-element.35.lead_ref, f32[256,256]{1,0:T(8,128)S(1)} %get-tuple-element.36.x_ref, f32[1024,256]{1,0:T(8,128)S(1)} %copy-done.1, f32[64,256]{1,0:T(8,128)S(1)} %get-tuple-element.32.refs_0_, ...), custom_call_target="tpu_custom_call" | custom-call | flops 1 | bytes 1 | tf_op jit(solution)/shard_map/pallas_call | solution.py:245
  (34 shorter events, 0.4 us)
Async XLA Ops:
  0.0 0.9 %copy-start.2 = (f32[1024,64]{0,1:T(8,128)S(1)}, f32[1024,64]{0,1:T(8,128)}, u32[]{:S(2)}) copy-start(f32[1024,64]{0,1:T(8,128)} %param.6) | copy-start | bytes 786436
  1.0 11.1 %collective-permute-start.6 = (f32[64,256]{1,0:T(8,128)S(1)}, f32[64,256]{1,0:T(8,128)S(1)}, u32[]{:S(2)}, u32[]{:S(2)}) collective-permute-start(f32[64,256]{1,0:T(8,128)S(1)} %get-tuple-element.32.refs_0_), channel_id=1, source_target_pairs={{0,1},{1,0},{2,3},{3,2},{4,5},{5,4},{6,7},{7,6},{8,9},{9,8},{10,11... | collective-permute-start | bytes 196616 | tf_op jit(solution)/shard_map/ppermute | solution.py:265
  4.1 9.0 %collective-permute-start.7 = (f32[64,256]{1,0:T(8,128)S(1)}, f32[64,256]{1,0:T(8,128)S(1)}, u32[]{:S(2)}, u32[]{:S(2)}) collective-permute-start(f32[64,256]{1,0:T(8,128)S(1)} %get-tuple-element.32.refs_0_), channel_id=1, source_target_pairs={{0,3},{1,2},{2,1},{3,0},{4,7},{5,6},{6,5},{7,4},{8,11},{9,10},{10,... | collective-permute-start | bytes 196616 | tf_op jit(solution)/shard_map/ppermute | solution.py:265
  6.6 6.6 %collective-permute-start.8 = (f32[64,256]{1,0:T(8,128)S(1)}, f32[64,256]{1,0:T(8,128)S(1)}, u32[]{:S(2)}, u32[]{:S(2)}) collective-permute-start(f32[64,256]{1,0:T(8,128)S(1)} %get-tuple-element.32.refs_0_), channel_id=1, source_target_pairs={{0,2},{1,3},{2,0},{3,1},{4,6},{5,7},{6,4},{7,5},{8,10},{9,11},{10,... | collective-permute-start | bytes 196616 | tf_op jit(solution)/shard_map/ppermute | solution.py:265
  6.7 3.5 %copy-start.3 = (s32[256]{0:T(256)S(1)}, s32[256]{0:T(256)}, u32[]{:S(2)}) copy-start(s32[256]{0:T(256)} %param.7) | copy-start | bytes 3076
  6.7 22.1 %collective-permute-start.10 = (f32[64,768]{1,0:T(8,128)S(1)}, f32[64,768]{1,0:T(8,128)S(1)}, u32[]{:S(2)}, u32[]{:S(2)}) collective-permute-start(f32[64,768]{1,0:T(8,128)S(1)} %get-tuple-element.37.refs_4_), channel_id=1, source_target_pairs={{0,1},{1,0},{2,3},{3,2},{4,5},{5,4},{6,7},{7,6},{8,9},{9,8},{10,11... | collective-permute-start | bytes 589832 | tf_op jit(solution)/shard_map/ppermute | solution.py:265
  8.5 20.3 %collective-permute-start.11 = (f32[64,768]{1,0:T(8,128)S(1)}, f32[64,768]{1,0:T(8,128)S(1)}, u32[]{:S(2)}, u32[]{:S(2)}) collective-permute-start(f32[64,768]{1,0:T(8,128)S(1)} %get-tuple-element.37.refs_4_), channel_id=1, source_target_pairs={{0,2},{1,3},{2,0},{3,1},{4,6},{5,7},{6,4},{7,5},{8,10},{9,11},{10,... | collective-permute-start | bytes 589832 | tf_op jit(solution)/shard_map/ppermute | solution.py:265
  10.2 1.2 %copy-start = (f32[1024,256]{1,0:T(8,128)S(1)}, f32[1024,256]{1,0:T(8,128)}, u32[]{:S(2)}) copy-start(f32[1024,256]{1,0:T(8,128)} %slab_ref.3) | copy-start | bytes 3145732
  12.1 16.7 %collective-permute-start.12 = (f32[64,768]{1,0:T(8,128)S(1)}, f32[64,768]{1,0:T(8,128)S(1)}, u32[]{:S(2)}, u32[]{:S(2)}) collective-permute-start(f32[64,768]{1,0:T(8,128)S(1)} %get-tuple-element.37.refs_4_), channel_id=1, source_target_pairs={{0,3},{1,2},{2,1},{3,0},{4,7},{5,6},{6,5},{7,4},{8,11},{9,10},{10,... | collective-permute-start | bytes 589832 | tf_op jit(solution)/shard_map/ppermute | solution.py:265
  13.3 1.3 %collective-permute-start.9 = (f32[64,256]{1,0:T(8,128)S(1)}, f32[64,256]{1,0:T(8,128)S(1)}, u32[]{:S(2)}, u32[]{:S(2)}) collective-permute-start(f32[64,256]{1,0:T(8,128)S(1)} %pad_maximum_fusion.3), channel_id=1, source_target_pairs={{0,4},{4,0},{8,12},{12,8},{16,20},{20,16},{24,28},{28,24},{1,5},{5... | collective-permute-start | bytes 196616 | tf_op jit(solution)/shard_map/ppermute | solution.py:332
  14.6 14.2 %copy-start.1 = (f32[1024,256]{1,0:T(8,128)S(1)}, f32[1024,256]{1,0:T(8,128)}, u32[]{:S(2)}) copy-start(f32[1024,256]{1,0:T(8,128)} %slab_ref.3) | copy-start | bytes 3145732
  14.7 1.7 %collective-permute-start = (f32[128,256]{1,0:T(8,128)S(1)}, f32[128,256]{1,0:T(8,128)S(1)}, u32[]{:S(2)}, u32[]{:S(2)}) collective-permute-start(f32[128,256]{1,0:T(8,128)S(1)} %slice.28), channel_id=1, source_target_pairs={{0,4},{4,0},{8,12},{12,8},{16,20},{20,16},{24,28},{28,24},{1,5},{5... | collective-permute-start | bytes 393224 | tf_op jit(solution)/shard_map/cond/branch_1_fun/ppermute | solution.py:298
  14.9 4.7 %collective-permute-start.3 = (f32[192,256]{1,0:T(8,128)S(1)}, f32[192,256]{1,0:T(8,128)S(1)}, u32[]{:S(2)}, u32[]{:S(2)}) collective-permute-start(f32[192,256]{1,0:T(8,128)S(1)} %get-tuple-element.18.held_ref), channel_id=1, source_target_pairs={{0,16},{4,0},{8,12},{12,8},{16,20},{20,4},{24,28},{28,24},{1,17},{... | collective-permute-start | bytes 589832 | tf_op jit(solution)/shard_map/cond/branch_1_fun/ppermute | solution.py:302
  16.5 5.3 %collective-permute-start.1 = (f32[128,256]{1,0:T(8,128)S(1)}, f32[128,256]{1,0:T(8,128)S(1)}, u32[]{:S(2)}, u32[]{:S(2)}) collective-permute-start(f32[128,256]{1,0:T(8,128)S(1)} %pad_maximum_fusion.2), channel_id=1, source_target_pairs={{0,8},{4,12},{8,0},{12,4},{16,24},{20,28},{24,16},{28,20},{1,9},{5... | collective-permute-start | bytes 393224 | tf_op jit(solution)/shard_map/cond/branch_1_fun/ppermute | solution.py:311
  19.6 4.6 %collective-permute-start.4 = (f32[192,256]{1,0:T(8,128)S(1)}, f32[192,256]{1,0:T(8,128)S(1)}, u32[]{:S(2)}, u32[]{:S(2)}) collective-permute-start(f32[192,256]{1,0:T(8,128)S(1)} %branch_1_fun.5.held_ref), channel_id=1, source_target_pairs={{0,8},{4,0},{8,12},{12,4},{16,24},{20,16},{24,28},{28,20},{1,9},{5... | collective-permute-start | bytes 589832 | tf_op jit(solution)/shard_map/cond/branch_1_fun/ppermute | solution.py:302
  21.8 5.7 %collective-permute-start.2 = (f32[160,256]{1,0:T(8,128)S(1)}, f32[160,256]{1,0:T(8,128)S(1)}, u32[]{:S(2)}, u32[]{:S(2)}) collective-permute-start(f32[160,256]{1,0:T(8,128)S(1)} %pad_maximum_fusion.1), channel_id=1, source_target_pairs={{0,16},{4,20},{8,24},{12,28},{16,0},{20,4},{24,8},{28,12},{1,17},{... | collective-permute-start | bytes 491528 | tf_op jit(solution)/shard_map/cond/branch_1_fun/ppermute | solution.py:311
  26.0 2.1 %collective-permute-start.5 = (f32[192,256]{1,0:T(8,128)S(1)}, f32[192,256]{1,0:T(8,128)S(1)}, u32[]{:S(2)}, u32[]{:S(2)}) collective-permute-start(f32[192,256]{1,0:T(8,128)S(1)} %branch_1_fun.7), channel_id=1, source_target_pairs={{0,4},{4,0},{8,12},{12,8},{16,20},{20,16},{24,28},{28,24},{1,5},{5... | collective-permute-start | bytes 589832 | tf_op jit(solution)/shard_map/cond/branch_1_fun/ppermute | solution.py:327

commit v4 on v1

--- a/solution.py
+++ b/solution.py
@@ -33,7 +33,11 @@
 
 
 def dot_full(a, b):
-    return jnp.dot(a, b, precision=lax.Precision.HIGHEST, preferred_element_type=F32)
+    high, mid, low = split3(a)
+    left = jnp.concatenate([low, mid, high, mid, high, high], axis=1)
+    high, mid, low = split3(b)
+    right = jnp.concatenate([high, mid, low, high, mid, high], axis=0)
+    return jnp.dot(left, right, preferred_element_type=F32)
 
 
 def tree_partner(r, span):
@@ -109,7 +113,7 @@
     return outs
 
 
-def order_kernel(n, rows, pivot_ref, gathered_ref, out_ref, gathered):
+def order_kernel(n, rows, pivot_ref, gathered_ref, mark_ref, out_ref, gathered):
     width = pivot_ref.shape[1]
     me = lax.axis_index("prow")
     for q in range(n):
@@ -125,13 +129,18 @@
     return [0, 1, *range(m - 1, 1, -1)]
 
 
-def cut_kernel(panel_ref, top_ref, rest_ref, sems):
+def cut_kernel(panel_ref, slab_ref, top_ref, rest_ref, held_ref, sems):
     width = top_ref.shape[1]
+    blocks = sems.shape[0] // 2
     copies = []
-    for c in range(sems.shape[0]):
+    for c in range(blocks):
         target = rest_ref.at[:, pl.ds((c - 1) * width, width)] if c else top_ref
         copies.append(pltpu.make_async_copy(panel_ref.at[:, pl.ds(c * width, width)], target, sems.at[c]))
-        copies[-1].start()
+    for c in range(blocks):
+        block = pl.ds(c * width, width)
+        copies.append(pltpu.make_async_copy(slab_ref.at[block], held_ref.at[block], sems.at[blocks + c]))
+    for copy in copies:
+        copy.start()
     for copy in copies:
         copy.wait()
 
@@ -265,24 +274,22 @@
     def spread(block, order):
         return [block] + [lax.ppermute(block, "pcol", [(c, c ^ d) for c in range(m)]) for d in order]
 
-    top, rest = call(
-        cut_kernel,
-        (jax.ShapeDtypeStruct((piece, width), F32), jax.ShapeDtypeStruct((piece, rows - width), F32)),
-        (panel_t,),
-        in_specs=[pl.BlockSpec(memory_space=pl.ANY)],
-        scratch=[pltpu.SemaphoreType.DMA((rows // width,))],
-    )
+    def cut(panel_t, slab):
+        return call(
+            cut_kernel,
+            (
+                jax.ShapeDtypeStruct((piece, width), F32),
+                jax.ShapeDtypeStruct((piece, rows - width), F32),
+                jax.ShapeDtypeStruct((rows, cols), F32),
+            ),
+            (panel_t, slab),
+            in_specs=[pl.BlockSpec(memory_space=pl.ANY)] * 2,
+            scratch=[pltpu.SemaphoreType.DMA((2 * (rows // width),))],
+        )
+
+    top, rest, slab = unit(me < n, cut, panel_t, slab)
     tops, rests = spread(top, top_order(m)[1:]), spread(rest, range(1, m))
 
-    gathered, leading, local_rows = call(
-        pack_kernel,
-        (
-            jax.ShapeDtypeStruct((CAP, cols), F32),
-            jax.ShapeDtypeStruct((n * CAP, cols), F32),
-            jax.ShapeDtypeStruct((1, 128), jnp.int32),
-        ),
-        (pivot_row, slab),
-    )
     lower = call(
         functools.partial(assemble_kernel, m),
         jax.ShapeDtypeStruct((width * 3 // 4, width), F32),
@@ -294,18 +301,16 @@
         blocks = leading.reshape(2, -1, cols)
         return blocks[0], blocks[1]
 
-    def levels(lower, gathered, leading):
-        kept, sent = split(leading)
-        moved = lax.ppermute(sent, "prow", [(r, r ^ 1) for r in range(n)])
-        leading = jnp.where(me & 1 != 0, moved, kept)
-        span, other = n // 2, 2
-        while span > 1:
-            moved = lax.ppermute(lower, "prow", [(r, tree_partner(r, span)) for r in range(n)])
-            lower = call(
-                functools.partial(pick_kernel, span),
-                jax.ShapeDtypeStruct(lower.shape, F32),
-                (moved, lower),
-            )
+    def levels(lower, gathered, leading, mark):
+        span, other = n // 2, 1
+        while other < n:
+            if span > 1:
+                moved = lax.ppermute(lower, "prow", [(r, tree_partner(r, span)) for r in range(n)])
+                lower = call(
+                    functools.partial(pick_kernel, span),
+                    jax.ShapeDtypeStruct(lower.shape, F32),
+                    (moved, lower),
+                )
             kept, sent = split(leading)
             count = gathered.shape[0]
             message = jnp.concatenate([gathered, sent], axis=0)
@@ -316,7 +321,7 @@
         pivot_rows = call(
             functools.partial(order_kernel, n, rows),
             jax.ShapeDtypeStruct((width, cols), F32),
-            (pivot_row, gathered),
+            (pivot_row, gathered, mark),
             scratch=[pltpu.VMEM((n * CAP, cols), F32)],
         )
         inverse = call(
@@ -329,10 +334,19 @@
         inverse = jnp.where(me & 1 != 0, moved, inverse)
         return leading, call(solve_kernel, jax.ShapeDtypeStruct((width, cols), F32), (inverse, pivot_rows))
 
-    gathered, lower = lax.optimization_barrier((gathered, lower))
-    moved = lax.ppermute(jnp.concatenate([gathered, gathered], axis=0), "prow", [(r, r ^ 1) for r in range(n)])
-    gathered = jnp.concatenate([gathered, moved[:CAP]], axis=0)
-    leading, upper_rows = unit(me < n, levels, lower, gathered, leading)
+    mark = lax.ppermute(lower[: 4 * CAP], "prow", [(r, r ^ 1) for r in range(n)])
+    pivot_row, lower = lax.optimization_barrier((pivot_row, lower))
+    gathered, leading, local_rows = call(
+        pack_kernel,
+        (
+            jax.ShapeDtypeStruct((CAP, cols), F32),
+            jax.ShapeDtypeStruct((n * CAP, cols), F32),
+            jax.ShapeDtypeStruct((1, 128), jnp.int32),
+        ),
+        (pivot_row, slab),
+    )
+
+    leading, upper_rows = unit(me < n, levels, lower, gathered, leading, mark)
     return call(
         functools.partial(update_kernel, m),
         jax.ShapeDtypeStruct((rows, cols), F32),

time: 31.5 us -> 32.1 us (1.019)
  local copies, waits for them, and re-layouts: 2.22 us -> 0.72 us
  waiting for transfers between devices: 6.04 us -> 7.22 us
  Pallas kernels: 6.39 us -> 7.48 us
    ppermute x6, waiting for transfers between devices: 0.13 us -> 2.13 us  [spread(): lax.ppermute(block, 'pcol', [(c, c ^ d) for c in range(m)])]
    unnamed x8 -> x2, local copies, waits for them, and re-layouts: 2.18 us -> 0.67 us
    ppermute x2 -> x1, waiting for transfers between devices: 1.24 us -> 0.01 us  [local(): mark = lax.ppermute(lower[:4 * CAP], 'prow', [(r, r ^ 1) for r in range(n)])]
    pallas_call x9, Pallas kernels: 6.39 us -> 7.48 us  [call(): pl.pallas_call(kernel, out_shape=outs, in_specs=in_specs or [VMEM] * len(...]
    ppermute x2 -> x3, waiting for transfers between devices: 2.75 us -> 3.03 us  [levels(): moved = lax.ppermute(message, 'prow', [(r, r ^ other) for r in range(n)])]
    ppermute x2 -> x3, starting transfers between devices: 3.59 us -> 3.78 us  [levels(): moved = lax.ppermute(message, 'prow', [(r, r ^ other) for r in range(n)])]
  transfers between devices with their start and end apart: 13 -> 13, of which waited for: 5 -> 4; matrix products, arithmetic and copies ran while one was open for 1% -> 1% of each run, Pallas kernels for 13% -> 12%
where the time goes in v4:
time: 32.1 us; the launch traced here: 31.9 us
  starting transfers between devices  16.1 us (50%)
  Pallas kernels  7.48 us (23%)
  waiting for transfers between devices  7.22 us (22%)
  local copies, waits for them, and re-layouts  0.72 us (2%)
    ppermute x6, starting transfers between devices, spread(): lax.ppermute(block, 'pcol', [(c, c ^ d) for c in range(m)])  10.1 us
    pallas_call x9, Pallas kernels, call(): pl.pallas_call(kernel, out_shape=outs, in_specs=in_specs or [VMEM] * len(...  7.48 us
    ppermute x3, starting transfers between devices, levels(): moved = lax.ppermute(message, 'prow', [(r, r ^ other) for r in range(n)])  3.78 us
    ppermute x3, waiting for transfers between devices, levels(): moved = lax.ppermute(message, 'prow', [(r, r ^ other) for r in range(n)])  3.03 us
    ppermute x6, waiting for transfers between devices, spread(): lax.ppermute(block, 'pcol', [(c, c ^ d) for c in range(m)])  2.13 us
    ppermute x2, waiting for transfers between devices, levels(): lax.ppermute(lower, 'prow', [(r, tree_partner(r, span)) for r in range(n)])  2.05 us
    ppermute x2, starting transfers between devices, levels(): lax.ppermute(lower, 'prow', [(r, tree_partner(r, span)) for r in range(n)])  1.54 us
    ppermute x1, starting transfers between devices, levels(): moved = lax.ppermute(inverse, 'prow', [(r, r ^ 1) for r in range(n)])  0.68 us
  transfers between devices with their start and end apart: 13, of which 4 were waited for; matrix products, arithmetic and copies ran while one was open for 1% of the time, Pallas kernels for 12%

profile of v4, /device:TPU:0, one launch (start us, length us, event | category | flops | bytes accessed | tf_op | source)
XLA Modules:
  0.0 31.9 jit_solution(8665991855404182789)
XLA Ops:
  0.0 1.4 %conditional.2 = ((f32[64,256]{1,0:T(8,128)S(1)}, f32[64,768]{1,0:T(8,128)S(1)}, f32[1024,256]{1,0:T(8,128)S(1)})) conditional(s32[]{:T(128)} %convert_element_type.4, () %tuple.21, (f32[64,1024]{1,0:T(8,128)}, f32[1024,256]{1,0:T(8,128)}) %tuple.33), branch_computations={%region_0.0_spmd, %region_1.0_spmd} | conditional | flops 1 | bytes 1310764 | solution.py:251
  0.0 1.4 %branch_1_fun.6 = (f32[64,256]{1,0:T(8,128)S(1)}, f32[64,768]{1,0:T(8,128)S(1)}, f32[1024,256]{1,0:T(8,128)S(1)}) custom-call(f32[64,1024]{1,0:T(8,128)} %get-tuple-element.21.panel_ref, f32[1024,256]{1,0:T(8,128)} %get-tuple-element.50.slab_ref), custom_call_target="tpu_custom_call" | custom-call | flops 1 | bytes 1 | tf_op jit(solution)/shard_map/cond/branch_1_fun/pallas_call | solution.py:255
  1.4 3.1 %collective-permute-start.6 = (f32[64,256]{1,0:T(8,128)S(1)}, f32[64,256]{1,0:T(8,128)S(1)}, u32[]{:S(2)}, u32[]{:S(2)}) collective-permute-start(f32[64,256]{1,0:T(8,128)S(1)} %get-tuple-element.39.refs_0_), channel_id=1, source_target_pairs={{0,1},{1,0},{2,3},{3,2},{4,5},{5,4},{6,7},{7,6},{8,9},{9,8},{10,11... | collective-permute-start | bytes 196616 | tf_op jit(solution)/shard_map/ppermute | solution.py:275
  4.5 2.5 %collective-permute-start.7 = (f32[64,256]{1,0:T(8,128)S(1)}, f32[64,256]{1,0:T(8,128)S(1)}, u32[]{:S(2)}, u32[]{:S(2)}) collective-permute-start(f32[64,256]{1,0:T(8,128)S(1)} %get-tuple-element.39.refs_0_), channel_id=1, source_target_pairs={{0,3},{1,2},{2,1},{3,0},{4,7},{5,6},{6,5},{7,4},{8,11},{9,10},{10,... | collective-permute-start | bytes 196616 | tf_op jit(solution)/shard_map/ppermute | solution.py:275
  7.0 0.1 collective-permute-start.8
  7.1 1.8 %collective-permute-start.10 = (f32[64,768]{1,0:T(8,128)S(1)}, f32[64,768]{1,0:T(8,128)S(1)}, u32[]{:S(2)}, u32[]{:S(2)}) collective-permute-start(f32[64,768]{1,0:T(8,128)S(1)} %get-tuple-element.48.refs_4_), channel_id=1, source_target_pairs={{0,1},{1,0},{2,3},{3,2},{4,5},{5,4},{6,7},{7,6},{8,9},{9,8},{10,11... | collective-permute-start | bytes 589832 | tf_op jit(solution)/shard_map/ppermute | solution.py:275
  8.9 1.7 %collective-permute-start.11 = (f32[64,768]{1,0:T(8,128)S(1)}, f32[64,768]{1,0:T(8,128)S(1)}, u32[]{:S(2)}, u32[]{:S(2)}) collective-permute-start(f32[64,768]{1,0:T(8,128)S(1)} %get-tuple-element.48.refs_4_), channel_id=1, source_target_pairs={{0,2},{1,3},{2,0},{3,1},{4,6},{5,7},{6,4},{7,5},{8,10},{9,11},{10,... | collective-permute-start | bytes 589832 | tf_op jit(solution)/shard_map/ppermute | solution.py:275
  10.6 0.9 %collective-permute-start.12 = (f32[64,768]{1,0:T(8,128)S(1)}, f32[64,768]{1,0:T(8,128)S(1)}, u32[]{:S(2)}, u32[]{:S(2)}) collective-permute-start(f32[64,768]{1,0:T(8,128)S(1)} %get-tuple-element.48.refs_4_), channel_id=1, source_target_pairs={{0,3},{1,2},{2,1},{3,0},{4,7},{5,6},{6,5},{7,4},{8,11},{9,10},{10,... | collective-permute-start | bytes 589832 | tf_op jit(solution)/shard_map/ppermute | solution.py:275
  11.5 2.1 %collective-permute-done.8.refs_3_ = f32[64,256]{1,0:T(8,128)S(1)} collective-permute-done((f32[64,256]{1,0:T(8,128)S(1)}, f32[64,256]{1,0:T(8,128)S(1)}, u32[]{:S(2)}, u32[]{:S(2)}) %collective-permute-start.8) | collective-permute-done | bytes 65568 | tf_op jit(solution)/shard_map/ppermute | solution.py:275
  13.8 0.7 %copy-done = s32[256]{0:T(256)S(1)} copy-done((s32[256]{0:T(256)S(1)}, s32[256]{0:T(256)}, u32[]{:S(2)}) %copy-start) | copy-done | bytes 1048
  14.4 0.7 %shard_map.39 = (f32[32,256]{1,0:T(8,128)S(1)}, f32[256,256]{1,0:T(8,128)S(1)}, s32[1,128]{1,0:T(1,128)S(1)}) custom-call(s32[1,256]{1,0:T(1,128)S(1)} %bitcast.3, f32[1024,256]{1,0:T(8,128)S(1)} %get-tuple-element.41.slab_ref), custom_call_target="tpu_custom_call" | custom-call | flops 1 | bytes 1 | tf_op jit(solution)/shard_map/pallas_call | solution.py:255
  15.1 14.4 %conditional.3 = (f32[32,256]{1,0:T(8,128)S(1)}, f32[256,256]{1,0:T(8,128)S(1)}) conditional(s32[]{:T(128)} %convert_element_type.4, () %tuple.24, (s32[]{:T(128)}, f32[256,256]{1,0:T(8,128)S(1)}, f32[32,256]{1,0:T(8,128)S(1)}, f32[192,256]{1,0:T(8,128)S(1)}, s32[1,256]{1,0:T(1,128)S(1)}, /*index=5*/f32[128,256]{1,0:T(8,128)S(1)}) %tuple.34), branch_computations={%region_2.0_spmd, %region_3.4_spmd} | conditional | flops 532491 | bytes 7831880 | solution.py:251
  15.2 0.6 %collective-permute-start = (f32[160,256]{1,0:T(8,128)S(1)}, f32[160,256]{1,0:T(8,128)S(1)}, u32[]{:S(2)}, u32[]{:S(2)}) collective-permute-start(f32[160,256]{1,0:T(8,128)S(1)} %pad_maximum_fusion.1), channel_id=1, source_target_pairs={{0,4},{4,0},{8,12},{12,8},{16,20},{20,16},{24,28},{28,24},{1,5},{5... | collective-permute-start | bytes 491528 | tf_op jit(solution)/shard_map/cond/branch_1_fun/ppermute | solution.py:317
  15.8 1.5 %collective-permute-start.3 = (f32[192,256]{1,0:T(8,128)S(1)}, f32[192,256]{1,0:T(8,128)S(1)}, u32[]{:S(2)}, u32[]{:S(2)}) collective-permute-start(f32[192,256]{1,0:T(8,128)S(1)} %get-tuple-element.26.held_ref), channel_id=1, source_target_pairs={{0,16},{4,0},{8,12},{12,8},{16,20},{20,4},{24,28},{28,24},{1,17},{... | collective-permute-start | bytes 589832 | tf_op jit(solution)/shard_map/cond/branch_1_fun/ppermute | solution.py:308
  17.3 1.1 %collective-permute-start.1 = (f32[128,256]{1,0:T(8,128)S(1)}, f32[128,256]{1,0:T(8,128)S(1)}, u32[]{:S(2)}, u32[]{:S(2)}) collective-permute-start(f32[128,256]{1,0:T(8,128)S(1)} %pad_maximum_fusion.3), channel_id=1, source_target_pairs={{0,8},{4,12},{8,0},{12,4},{16,24},{20,28},{24,16},{28,20},{1,9},{5... | collective-permute-start | bytes 393224 | tf_op jit(solution)/shard_map/cond/branch_1_fun/ppermute | solution.py:317
  18.4 2.0 %collective-permute-done.3.moved_ref = f32[192,256]{1,0:T(8,128)S(1)} collective-permute-done((f32[192,256]{1,0:T(8,128)S(1)}, f32[192,256]{1,0:T(8,128)S(1)}, u32[]{:S(2)}, u32[]{:S(2)}) %collective-permute-start.3) | collective-permute-done | bytes 196640 | tf_op jit(solution)/shard_map/cond/branch_1_fun/ppermute | solution.py:308
  20.5 2.2 %collective-permute-done.1 = f32[128,256]{1,0:T(8,128)S(1)} collective-permute-done((f32[128,256]{1,0:T(8,128)S(1)}, f32[128,256]{1,0:T(8,128)S(1)}, u32[]{:S(2)}, u32[]{:S(2)}) %collective-permute-start.1) | collective-permute-done | bytes 131104 | tf_op jit(solution)/shard_map/cond/branch_1_fun/ppermute | solution.py:317
  22.7 2.1 %collective-permute-start.2 = (f32[160,256]{1,0:T(8,128)S(1)}, f32[160,256]{1,0:T(8,128)S(1)}, u32[]{:S(2)}, u32[]{:S(2)}) collective-permute-start(f32[160,256]{1,0:T(8,128)S(1)} %fusion.1), channel_id=1, source_target_pairs={{0,16},{4,20},{8,24},{12,28},{16,0},{20,4},{24,8},{28,12},{1,17},{... | collective-permute-start | bytes 491528 | tf_op jit(solution)/shard_map/cond/branch_1_fun/ppermute | solution.py:317
  24.9 1.8 %branch_1_fun.9 = f32[192,256]{1,0:T(8,128)S(1)} custom-call(f32[192,256]{1,0:T(8,128)S(1)} %branch_1_fun.8.lower_ref), custom_call_target="tpu_custom_call" | custom-call | flops 1 | bytes 1 | tf_op jit(solution)/shard_map/cond/branch_1_fun/pallas_call | solution.py:255
  26.7 0.7 %collective-permute-start.5 = (f32[192,256]{1,0:T(8,128)S(1)}, f32[192,256]{1,0:T(8,128)S(1)}, u32[]{:S(2)}, u32[]{:S(2)}) collective-permute-start(f32[192,256]{1,0:T(8,128)S(1)} %branch_1_fun.9), channel_id=1, source_target_pairs={{0,4},{4,0},{8,12},{12,8},{16,20},{20,16},{24,28},{28,24},{1,5},{5... | collective-permute-start | bytes 589832 | tf_op jit(solution)/shard_map/cond/branch_1_fun/ppermute | solution.py:333
  27.4 0.9 %collective-permute-done.2 = f32[160,256]{1,0:T(8,128)S(1)} collective-permute-done((f32[160,256]{1,0:T(8,128)S(1)}, f32[160,256]{1,0:T(8,128)S(1)}, u32[]{:S(2)}, u32[]{:S(2)}) %collective-permute-start.2) | collective-permute-done | bytes 163872 | tf_op jit(solution)/shard_map/cond/branch_1_fun/ppermute | solution.py:317
  28.3 0.5 %branch_1_fun.10.pivot_rows_ref = f32[256,256]{1,0:T(8,128)S(1)} custom-call(s32[1,256]{1,0:T(1,128)S(1)} %get-tuple-element.27.pivot_ref, f32[256,256]{1,0:T(8,128)S(1)} %pad_maximum_fusion.gathered_ref, f32[128,256]{1,0:T(8,128)S(1)} %get-tuple-element.28.mark_ref), custom_call_target="tpu_custom_call" | custom-call | flops 1 | bytes 1 | tf_op jit(solution)/shard_map/cond/branch_1_fun/pallas_call | solution.py:255
  28.9 0.7 %branch_1_fun.11 = f32[256,256]{1,0:T(8,128)S(1)} custom-call(f32[192,256]{1,0:T(8,128)S(1)} %broadcast_select_fusion.inverse_ref, f32[256,256]{1,0:T(8,128)S(1)} %branch_1_fun.10.pivot_rows_ref), custom_call_target="tpu_custom_call" | custom-call | flops 1 | bytes 1 | tf_op jit(solution)/shard_map/cond/branch_1_fun/pallas_call | solution.py:255
  29.6 2.3 %shard_map.40 = f32[1024,256]{1,0:T(8,128)} custom-call(s32[1,128]{1,0:T(1,128)S(1)} %get-tuple-element.42.local_ref, f32[32,256]{1,0:T(8,128)S(1)} %get-tuple-element.46.lead_ref, f32[256,256]{1,0:T(8,128)S(1)} %get-tuple-element.47.x_ref, f32[1024,256]{1,0:T(8,128)S(1)} %get-tuple-element.41.slab_ref, f32[64,256]{1,0:T(8,128)S(1)} %get-tuple-element.39.refs_0_, ...), custom_call_target="tpu_custom_call" | custom-call | flops 1 | bytes 1 | tf_op jit(solution)/shard_map/pallas_call | solution.py:255
  (29 shorter events, 0.4 us)
Async XLA Ops:
  1.4 9.2 %collective-permute-start.6 = (f32[64,256]{1,0:T(8,128)S(1)}, f32[64,256]{1,0:T(8,128)S(1)}, u32[]{:S(2)}, u32[]{:S(2)}) collective-permute-start(f32[64,256]{1,0:T(8,128)S(1)} %get-tuple-element.39.refs_0_), channel_id=1, source_target_pairs={{0,1},{1,0},{2,3},{3,2},{4,5},{5,4},{6,7},{7,6},{8,9},{9,8},{10,11... | collective-permute-start | bytes 196616 | tf_op jit(solution)/shard_map/ppermute | solution.py:275
  4.5 7.0 %collective-permute-start.7 = (f32[64,256]{1,0:T(8,128)S(1)}, f32[64,256]{1,0:T(8,128)S(1)}, u32[]{:S(2)}, u32[]{:S(2)}) collective-permute-start(f32[64,256]{1,0:T(8,128)S(1)} %get-tuple-element.39.refs_0_), channel_id=1, source_target_pairs={{0,3},{1,2},{2,1},{3,0},{4,7},{5,6},{6,5},{7,4},{8,11},{9,10},{10,... | collective-permute-start | bytes 196616 | tf_op jit(solution)/shard_map/ppermute | solution.py:275
  7.0 6.6 %collective-permute-start.8 = (f32[64,256]{1,0:T(8,128)S(1)}, f32[64,256]{1,0:T(8,128)S(1)}, u32[]{:S(2)}, u32[]{:S(2)}) collective-permute-start(f32[64,256]{1,0:T(8,128)S(1)} %get-tuple-element.39.refs_0_), channel_id=1, source_target_pairs={{0,2},{1,3},{2,0},{3,1},{4,6},{5,7},{6,4},{7,5},{8,10},{9,11},{10,... | collective-permute-start | bytes 196616 | tf_op jit(solution)/shard_map/ppermute | solution.py:275
  7.1 22.5 %collective-permute-start.10 = (f32[64,768]{1,0:T(8,128)S(1)}, f32[64,768]{1,0:T(8,128)S(1)}, u32[]{:S(2)}, u32[]{:S(2)}) collective-permute-start(f32[64,768]{1,0:T(8,128)S(1)} %get-tuple-element.48.refs_4_), channel_id=1, source_target_pairs={{0,1},{1,0},{2,3},{3,2},{4,5},{5,4},{6,7},{7,6},{8,9},{9,8},{10,11... | collective-permute-start | bytes 589832 | tf_op jit(solution)/shard_map/ppermute | solution.py:275
  8.9 20.7 %collective-permute-start.11 = (f32[64,768]{1,0:T(8,128)S(1)}, f32[64,768]{1,0:T(8,128)S(1)}, u32[]{:S(2)}, u32[]{:S(2)}) collective-permute-start(f32[64,768]{1,0:T(8,128)S(1)} %get-tuple-element.48.refs_4_), channel_id=1, source_target_pairs={{0,2},{1,3},{2,0},{3,1},{4,6},{5,7},{6,4},{7,5},{8,10},{9,11},{10,... | collective-permute-start | bytes 589832 | tf_op jit(solution)/shard_map/ppermute | solution.py:275
  10.6 19.0 %collective-permute-start.12 = (f32[64,768]{1,0:T(8,128)S(1)}, f32[64,768]{1,0:T(8,128)S(1)}, u32[]{:S(2)}, u32[]{:S(2)}) collective-permute-start(f32[64,768]{1,0:T(8,128)S(1)} %get-tuple-element.48.refs_4_), channel_id=1, source_target_pairs={{0,3},{1,2},{2,1},{3,0},{4,7},{5,6},{6,5},{7,4},{8,11},{9,10},{10,... | collective-permute-start | bytes 589832 | tf_op jit(solution)/shard_map/ppermute | solution.py:275
  13.7 1.5 %collective-permute-start.9 = (f32[128,256]{1,0:T(8,128)S(1)}, f32[128,256]{1,0:T(8,128)S(1)}, u32[]{:S(2)}, u32[]{:S(2)}) collective-permute-start(f32[128,256]{1,0:T(8,128)S(1)} %slice.56), channel_id=1, source_target_pairs={{0,4},{4,0},{8,12},{12,8},{16,20},{20,16},{24,28},{28,24},{1,5},{5... | collective-permute-start | bytes 393224 | tf_op jit(solution)/shard_map/ppermute | solution.py:337
  13.7 0.7 %copy-start = (s32[256]{0:T(256)S(1)}, s32[256]{0:T(256)}, u32[]{:S(2)}) copy-start(s32[256]{0:T(256)} %param.9) | copy-start | bytes 3076
  15.2 2.1 %collective-permute-start = (f32[160,256]{1,0:T(8,128)S(1)}, f32[160,256]{1,0:T(8,128)S(1)}, u32[]{:S(2)}, u32[]{:S(2)}) collective-permute-start(f32[160,256]{1,0:T(8,128)S(1)} %pad_maximum_fusion.1), channel_id=1, source_target_pairs={{0,4},{4,0},{8,12},{12,8},{16,20},{20,16},{24,28},{28,24},{1,5},{5... | collective-permute-start | bytes 491528 | tf_op jit(solution)/shard_map/cond/branch_1_fun/ppermute | solution.py:317
  15.8 4.7 %collective-permute-start.3 = (f32[192,256]{1,0:T(8,128)S(1)}, f32[192,256]{1,0:T(8,128)S(1)}, u32[]{:S(2)}, u32[]{:S(2)}) collective-permute-start(f32[192,256]{1,0:T(8,128)S(1)} %get-tuple-element.26.held_ref), channel_id=1, source_target_pairs={{0,16},{4,0},{8,12},{12,8},{16,20},{20,4},{24,28},{28,24},{1,17},{... | collective-permute-start | bytes 589832 | tf_op jit(solution)/shard_map/cond/branch_1_fun/ppermute | solution.py:308
  17.3 5.3 %collective-permute-start.1 = (f32[128,256]{1,0:T(8,128)S(1)}, f32[128,256]{1,0:T(8,128)S(1)}, u32[]{:S(2)}, u32[]{:S(2)}) collective-permute-start(f32[128,256]{1,0:T(8,128)S(1)} %pad_maximum_fusion.3), channel_id=1, source_target_pairs={{0,8},{4,12},{8,0},{12,4},{16,24},{20,28},{24,16},{28,20},{1,9},{5... | collective-permute-start | bytes 393224 | tf_op jit(solution)/shard_map/cond/branch_1_fun/ppermute | solution.py:317
  20.5 4.4 %collective-permute-start.4 = (f32[192,256]{1,0:T(8,128)S(1)}, f32[192,256]{1,0:T(8,128)S(1)}, u32[]{:S(2)}, u32[]{:S(2)}) collective-permute-start(f32[192,256]{1,0:T(8,128)S(1)} %branch_1_fun.7.held_ref), channel_id=1, source_target_pairs={{0,8},{4,0},{8,12},{12,4},{16,24},{20,16},{24,28},{28,20},{1,9},{5... | collective-permute-start | bytes 589832 | tf_op jit(solution)/shard_map/cond/branch_1_fun/ppermute | solution.py:308
  22.7 5.5 %collective-permute-start.2 = (f32[160,256]{1,0:T(8,128)S(1)}, f32[160,256]{1,0:T(8,128)S(1)}, u32[]{:S(2)}, u32[]{:S(2)}) collective-permute-start(f32[160,256]{1,0:T(8,128)S(1)} %fusion.1), channel_id=1, source_target_pairs={{0,16},{4,20},{8,24},{12,28},{16,0},{20,4},{24,8},{28,12},{1,17},{... | collective-permute-start | bytes 491528 | tf_op jit(solution)/shard_map/cond/branch_1_fun/ppermute | solution.py:317
  26.7 2.1 %collective-permute-start.5 = (f32[192,256]{1,0:T(8,128)S(1)}, f32[192,256]{1,0:T(8,128)S(1)}, u32[]{:S(2)}, u32[]{:S(2)}) collective-permute-start(f32[192,256]{1,0:T(8,128)S(1)} %branch_1_fun.9), channel_id=1, source_target_pairs={{0,4},{4,0},{8,12},{12,8},{16,20},{20,16},{24,28},{28,24},{1,5},{5... | collective-permute-start | bytes 589832 | tf_op jit(solution)/shard_map/cond/branch_1_fun/ppermute | solution.py:333

commit v5 on v1

--- a/solution.py
+++ b/solution.py
@@ -9,6 +9,7 @@
 
 CAP = 32
 BLOCK = 32
+EXTRA = 32
 F32 = jnp.float32
 BF16 = jnp.bfloat16
 VMEM = pl.BlockSpec(memory_space=pltpu.VMEM)
@@ -33,15 +34,11 @@
 
 
 def dot_full(a, b):
-    return jnp.dot(a, b, precision=lax.Precision.HIGHEST, preferred_element_type=F32)
-
-
-def tree_partner(r, span):
-    if span == 1 or r % span > 1:
-        return r ^ 1
-    if r % 2 == 0:
-        return r + 1 if r & span else r + span
-    return r - span if r & span else r - 1
+    high, mid, low = split3(a)
+    left = jnp.concatenate([low, mid, high, mid, high, high], axis=1)
+    high, mid, low = split3(b)
+    right = jnp.concatenate([high, mid, low, high, mid, high], axis=0)
+    return jnp.dot(left, right, preferred_element_type=F32)
 
 
 def lead_place(owner, n):
@@ -150,24 +147,28 @@
 
 
 def pick_kernel(span, moved_ref, held_ref, out_ref):
-    child = lax.rem(lax.axis_index("prow"), 2 * span) == span
-
-    @pl.when(child)
+    reached = lax.rem(lax.axis_index("prow") // 2 * 2, 2 * span) == span
+
+    @pl.when(reached)
     def _():
         out_ref[...] = moved_ref[...]
 
-    @pl.when(jnp.logical_not(child))
+    @pl.when(jnp.logical_not(reached))
     def _():
         out_ref[...] = held_ref[...]
 
 
-def invert_kernel(lower_ref, out_ref, lower_t):
+def invert_kernel(own_ref, twin_ref, out_ref, packed, lower_t):
     width = lower_t.shape[0]
     half = width // 2
-    lower_t[:half, :] = lower_ref[:half, :]
+    count = own_ref.shape[0]
+    odd = lax.axis_index("prow") & 1
+    packed[pl.ds(pl.multiple_of(odd * count, count), count), :] = own_ref[...]
+    packed[pl.ds(pl.multiple_of((1 - odd) * count, count), count), :] = twin_ref[...]
+    lower_t[:half, :] = packed[:half, :]
     lower_t[half:, :half] = jnp.zeros((half, half), F32)
-    lower_t[half : half + half // 2, half:] = lower_ref[half:, :half]
-    lower_t[half + half // 2 :, half:] = lower_ref[half:, half:]
+    lower_t[half : half + half // 2, half:] = packed[half:, :half]
+    lower_t[half + half // 2 :, half:] = packed[half:, half:]
     lower = lower_t[...].T
     blocks = block_inverses(lower)
     row = lax.broadcasted_iota(jnp.int32, (half, half), 0)
@@ -208,22 +209,26 @@
 
 
 def update_kernel(m, local_ref, lead_ref, x_ref, slab_ref, *refs):
-    *pieces, out_ref, result, sems = refs
+    *pieces, out_ref, result, swaps, sems = refs
     tops, rests = dict(zip(top_order(m), pieces[:m])), pieces[m:]
-    rows, cols = slab_ref.shape
+    rows = slab_ref.shape[0]
     width = x_ref.shape[0]
+    blocks = rows // width
+    fetch = pltpu.make_async_copy(local_ref, swaps, sems.at[blocks])
+    fetch.start()
     result[:rows, :] = slab_ref[...]
-    for s in range(CAP):
-        result[pl.ds(local_ref[0, s], 1), :] = lead_ref[pl.ds(s, 1), :]
     uppers = [piece_rows(x_ref, m, d) for d in range(m)]
     copies = []
-    for c in range(rows // width):
+    for c in range(blocks):
         part = pl.ds(c * width, width)
-        total = result[part, :]
-        for d, upper in enumerate(uppers):
-            piece = rests[d][:, (c - 1) * width : c * width] if c else tops[d][...]
-            total = total - product(piece, upper)
-        result[part, :] = total
+        if c:
+            total = sum(product(rests[d][:, (c - 1) * width : c * width], uppers[d]) for d in range(m))
+        else:
+            total = sum(product(tops[d][...], uppers[d]) for d in range(m))
+            fetch.wait()
+            for s in range(CAP):
+                result[pl.ds(swaps[0, s], 1), :] = lead_ref[pl.ds(s, 1), :]
+        result[part, :] = result[part, :] - total
         if c == 0:
 
             @pl.when(lax.axis_index("prow") == 0)
@@ -294,17 +299,18 @@
         blocks = leading.reshape(2, -1, cols)
         return blocks[0], blocks[1]
 
-    def levels(lower, gathered, leading):
+    def levels(block, gathered, leading):
         kept, sent = split(leading)
-        moved = lax.ppermute(sent, "prow", [(r, r ^ 1) for r in range(n)])
-        leading = jnp.where(me & 1 != 0, moved, kept)
+        moved = lax.ppermute(jnp.concatenate([gathered, sent], axis=0), "prow", twins)
+        gathered = jnp.concatenate([gathered, moved[:CAP]], axis=0)
+        leading = jnp.where(me & 1 != 0, moved[CAP:], kept)
         span, other = n // 2, 2
         while span > 1:
-            moved = lax.ppermute(lower, "prow", [(r, tree_partner(r, span)) for r in range(n)])
-            lower = call(
+            moved = lax.ppermute(block, "prow", [(r, r ^ span) for r in range(n)])
+            block = call(
                 functools.partial(pick_kernel, span),
-                jax.ShapeDtypeStruct(lower.shape, F32),
-                (moved, lower),
+                jax.ShapeDtypeStruct(block.shape, F32),
+                (moved, block),
             )
             kept, sent = split(leading)
             count = gathered.shape[0]
@@ -313,33 +319,39 @@
             gathered = jnp.concatenate([gathered, moved[:count]], axis=0)
             leading = jnp.where(me & other != 0, moved[count:], kept)
             span, other = span // 2, other * 2
+        twin = lax.ppermute(block, "prow", [(r, r ^ 1) for r in range(n)])
+        inverse = call(
+            invert_kernel,
+            jax.ShapeDtypeStruct(lower.shape, F32),
+            (block, twin),
+            scratch=[pltpu.VMEM(lower.shape, F32), pltpu.VMEM((width, width), F32)],
+        )
+        gathered, inverse = lax.optimization_barrier((gathered, inverse))
         pivot_rows = call(
             functools.partial(order_kernel, n, rows),
             jax.ShapeDtypeStruct((width, cols), F32),
             (pivot_row, gathered),
             scratch=[pltpu.VMEM((n * CAP, cols), F32)],
         )
-        inverse = call(
-            invert_kernel,
-            jax.ShapeDtypeStruct(lower.shape, F32),
-            (lower,),
-            scratch=[pltpu.VMEM((width, width), F32)],
-        )
-        moved = lax.ppermute(inverse, "prow", [(r, r ^ 1) for r in range(n)])
-        inverse = jnp.where(me & 1 != 0, moved, inverse)
         return leading, call(solve_kernel, jax.ShapeDtypeStruct((width, cols), F32), (inverse, pivot_rows))
 
-    gathered, lower = lax.optimization_barrier((gathered, lower))
-    moved = lax.ppermute(jnp.concatenate([gathered, gathered], axis=0), "prow", [(r, r ^ 1) for r in range(n)])
-    gathered = jnp.concatenate([gathered, moved[:CAP]], axis=0)
-    leading, upper_rows = unit(me < n, levels, lower, gathered, leading)
+    half = lower.shape[0] // 2
+    twins = [(r, r ^ 1) for r in range(n)]
+    lower, gathered = lax.optimization_barrier((lower, gathered))
+    moved = lax.ppermute(lower[half - EXTRA :], "prow", twins)
+    block = jnp.where(me & 1 != 0, moved[EXTRA:], lower[:half])
+    leading, upper_rows = unit(me < n, levels, block, gathered, leading)
     return call(
         functools.partial(update_kernel, m),
         jax.ShapeDtypeStruct((rows, cols), F32),
         (local_rows, leading, upper_rows, slab, *tops, *rests),
-        in_specs=[pl.BlockSpec(memory_space=pltpu.SMEM)] + [VMEM] * (2 * m + 3),
+        in_specs=[VMEM] * (2 * m + 4),
         out_specs=pl.BlockSpec(memory_space=pl.ANY),
-        scratch=[pltpu.VMEM((rows + 8, cols), F32), pltpu.SemaphoreType.DMA((rows // width,))],
+        scratch=[
+            pltpu.VMEM((rows + 8, cols), F32),
+            pltpu.SMEM((1, 128), jnp.int32),
+            pltpu.SemaphoreType.DMA((rows // width + 1,)),
+        ],
     )
 
 

time: 31.5 us -> 34.1 us (1.083)
  waiting for transfers between devices: 6.04 us -> 9.6 us
  starting transfers between devices: 16.3 us -> 15.7 us
  Pallas kernels: 6.39 us -> 6.03 us
    ppermute x5, waiting for transfers between devices: 3.15 us -> 9.4 us  [the longest x2 5.54 us: levels(): moved = lax.ppermute(block, 'prow', [(r, r ^ span) for r in range(n)])]
    ppermute x2, waiting for transfers between devices: 2.75 us -> 0.01 us  [levels(): moved = lax.ppermute(message, 'prow', [(r, r ^ other) for r in range(n)])]
    ppermute x2, starting transfers between devices: 3.59 us -> 3.14 us  [levels(): moved = lax.ppermute(message, 'prow', [(r, r ^ other) for r in range(n)])]
    pallas_call x9, Pallas kernels: 6.39 us -> 6.03 us  [call(): pl.pallas_call(kernel, out_shape=outs, in_specs=in_specs or [VMEM] * len(...]
  transfers between devices with their start and end apart: 13 -> 13, of which waited for: 5 -> 6; matrix products, arithmetic and copies ran while one was open for 1% -> 0% of each run, Pallas kernels for 13% -> 11%
where the time goes in v5:
time: 34.1 us; the launch traced here: 33.9 us
  starting transfers between devices  15.7 us (46%)
  waiting for transfers between devices  9.6 us (28%)
  Pallas kernels  6.03 us (18%)
  local copies, waits for them, and re-layouts  2.23 us (7%)
    ppermute x6, starting transfers between devices, spread(): lax.ppermute(block, 'pcol', [(c, c ^ d) for c in range(m)])  10.1 us
    pallas_call x9, Pallas kernels, call(): pl.pallas_call(kernel, out_shape=outs, in_specs=in_specs or [VMEM] * len(...  6.03 us
    ppermute x2, waiting for transfers between devices, levels(): moved = lax.ppermute(block, 'prow', [(r, r ^ span) for r in range(n)])  5.54 us
    ppermute x2, starting transfers between devices, levels(): moved = lax.ppermute(message, 'prow', [(r, r ^ other) for r in range(n)])  3.14 us
    ppermute x2, starting transfers between devices, levels(): moved = lax.ppermute(block, 'prow', [(r, r ^ span) for r in range(n)])  2.18 us
    unnamed x8, local copies, waits for them, and re-layouts  2.18 us
    ppermute x1, waiting for transfers between devices, local(): moved = lax.ppermute(lower[half - EXTRA:], 'prow', twins)  1.33 us
    ppermute x1, waiting for transfers between devices, levels(): twin = lax.ppermute(block, 'prow', [(r, r ^ 1) for r in range(n)])  1.28 us
  transfers between devices with their start and end apart: 13, of which 6 were waited for; matrix products, arithmetic and copies ran while one was open for 0% of the time, Pallas kernels for 11%

profile of v5, /device:TPU:0, one launch (start us, length us, event | category | flops | bytes accessed | tf_op | source)
XLA Modules:
  0.0 33.9 jit_solution(17939305405317690450)
XLA Ops:
  0.0 0.9 %copy-done.2 = f32[1024,64]{0,1:T(8,128)S(1)} copy-done((f32[1024,64]{0,1:T(8,128)S(1)}, f32[1024,64]{0,1:T(8,128)}, u32[]{:S(2)}) %copy-start.2) | copy-done | bytes 262168
  1.0 3.1 %collective-permute-start.6 = (f32[64,256]{1,0:T(8,128)S(1)}, f32[64,256]{1,0:T(8,128)S(1)}, u32[]{:S(2)}, u32[]{:S(2)}) collective-permute-start(f32[64,256]{1,0:T(8,128)S(1)} %get-tuple-element.45.refs_0_), channel_id=1, source_target_pairs={{0,1},{1,0},{2,3},{3,2},{4,5},{5,4},{6,7},{7,6},{8,9},{9,8},{10,11... | collective-permute-start | bytes 196616 | tf_op jit(solution)/shard_map/ppermute | solution.py:271
  4.1 2.5 %collective-permute-start.7 = (f32[64,256]{1,0:T(8,128)S(1)}, f32[64,256]{1,0:T(8,128)S(1)}, u32[]{:S(2)}, u32[]{:S(2)}) collective-permute-start(f32[64,256]{1,0:T(8,128)S(1)} %get-tuple-element.45.refs_0_), channel_id=1, source_target_pairs={{0,3},{1,2},{2,1},{3,0},{4,7},{5,6},{6,5},{7,4},{8,11},{9,10},{10,... | collective-permute-start | bytes 196616 | tf_op jit(solution)/shard_map/ppermute | solution.py:271
  6.7 1.8 %collective-permute-start.10 = (f32[64,768]{1,0:T(8,128)S(1)}, f32[64,768]{1,0:T(8,128)S(1)}, u32[]{:S(2)}, u32[]{:S(2)}) collective-permute-start(f32[64,768]{1,0:T(8,128)S(1)} %get-tuple-element.51.refs_4_), channel_id=1, source_target_pairs={{0,1},{1,0},{2,3},{3,2},{4,5},{5,4},{6,7},{7,6},{8,9},{9,8},{10,11... | collective-permute-start | bytes 589832 | tf_op jit(solution)/shard_map/ppermute | solution.py:271
  8.5 1.7 %collective-permute-start.11 = (f32[64,768]{1,0:T(8,128)S(1)}, f32[64,768]{1,0:T(8,128)S(1)}, u32[]{:S(2)}, u32[]{:S(2)}) collective-permute-start(f32[64,768]{1,0:T(8,128)S(1)} %get-tuple-element.51.refs_4_), channel_id=1, source_target_pairs={{0,2},{1,3},{2,0},{3,1},{4,6},{5,7},{6,4},{7,5},{8,10},{9,11},{10,... | collective-permute-start | bytes 589832 | tf_op jit(solution)/shard_map/ppermute | solution.py:271
  10.2 0.9 %collective-permute-start.12 = (f32[64,768]{1,0:T(8,128)S(1)}, f32[64,768]{1,0:T(8,128)S(1)}, u32[]{:S(2)}, u32[]{:S(2)}) collective-permute-start(f32[64,768]{1,0:T(8,128)S(1)} %get-tuple-element.51.refs_4_), channel_id=1, source_target_pairs={{0,3},{1,2},{2,1},{3,0},{4,7},{5,6},{6,5},{7,4},{8,11},{9,10},{10,... | collective-permute-start | bytes 589832 | tf_op jit(solution)/shard_map/ppermute | solution.py:271
  11.1 1.2 %copy-done = f32[1024,256]{1,0:T(8,128)S(1)} copy-done((f32[1024,256]{1,0:T(8,128)S(1)}, f32[1024,256]{1,0:T(8,128)}, u32[]{:S(2)}) %copy-start) | copy-done | bytes 1048600
  12.3 0.7 %shard_map.37 = (f32[32,256]{1,0:T(8,128)S(1)}, f32[256,256]{1,0:T(8,128)S(1)}, s32[1,128]{1,0:T(1,128)S(1)}) custom-call(s32[1,256]{1,0:T(1,128)S(1)} %bitcast.3, f32[1024,256]{1,0:T(8,128)S(1)} %copy-done), custom_call_target="tpu_custom_call" | custom-call | flops 1 | bytes 1 | tf_op jit(solution)/shard_map/pallas_call | solution.py:251
  13.1 0.2 collective-permute-done.8.refs_3_
  13.4 1.3 %collective-permute-done.9 = f32[128,256]{1,0:T(8,128)S(1)} collective-permute-done((f32[128,256]{1,0:T(8,128)S(1)}, f32[128,256]{1,0:T(8,128)S(1)}, u32[]{:S(2)}, u32[]{:S(2)}) %collective-permute-start.9) | collective-permute-done | bytes 131104 | tf_op jit(solution)/shard_map/ppermute | solution.py:341
  14.7 17.0 %conditional.1 = (f32[32,256]{1,0:T(8,128)S(1)}, f32[256,256]{1,0:T(8,128)S(1)}) conditional(s32[]{:T(128)} %convert_element_type.3, () %tuple.18, (s32[]{:T(128)}, f32[256,256]{1,0:T(8,128)S(1)}, f32[32,256]{1,0:T(8,128)S(1)}, f32[128,256]{1,0:T(8,128)S(1)}, f32[192,256]{1,0:T(8,128)S(1)}, /*index=5*/s32[1,256]{1,0:T(1,128)S(1)}) %tuple.24), branch_computations={%region_0.1_spmd, %region_1.2_spmd} | conditional | flops 507915 | bytes 6357320 | solution.py:247
  14.7 0.2 collective-permute-start
  15.0 1.2 %collective-permute-done = f32[160,256]{1,0:T(8,128)S(1)} collective-permute-done((f32[160,256]{1,0:T(8,128)S(1)}, f32[160,256]{1,0:T(8,128)S(1)}, u32[]{:S(2)}, u32[]{:S(2)}) %collective-permute-start) | collective-permute-done | bytes 163872 | tf_op jit(solution)/shard_map/cond/branch_1_fun/ppermute | solution.py:304
  16.3 1.6 %collective-permute-start.1 = (f32[128,256]{1,0:T(8,128)S(1)}, f32[128,256]{1,0:T(8,128)S(1)}, u32[]{:S(2)}, u32[]{:S(2)}) collective-permute-start(f32[128,256]{1,0:T(8,128)S(1)} %pad_maximum_fusion.3), channel_id=1, source_target_pairs={{0,8},{4,12},{8,0},{12,4},{16,24},{20,28},{24,16},{28,20},{1,9},{5... | collective-permute-start | bytes 393224 | tf_op jit(solution)/shard_map/cond/branch_1_fun/ppermute | solution.py:318
  17.8 1.6 %collective-permute-start.3 = (f32[96,256]{1,0:T(8,128)S(1)}, f32[96,256]{1,0:T(8,128)S(1)}, u32[]{:S(2)}, u32[]{:S(2)}) collective-permute-start(f32[96,256]{1,0:T(8,128)S(1)} %slice_select_fusion.1.held_ref), channel_id=1, source_target_pairs={{0,16},{4,20},{8,24},{12,28},{16,0},{20,4},{24,8},{28,12},{1,17},{... | collective-permute-start | bytes 294920 | tf_op jit(solution)/shard_map/cond/branch_1_fun/ppermute | solution.py:309
  19.4 3.1 %collective-permute-done.3.moved_ref = f32[96,256]{1,0:T(8,128)S(1)} collective-permute-done((f32[96,256]{1,0:T(8,128)S(1)}, f32[96,256]{1,0:T(8,128)S(1)}, u32[]{:S(2)}, u32[]{:S(2)}) %collective-permute-start.3) | collective-permute-done | bytes 98336 | tf_op jit(solution)/shard_map/cond/branch_1_fun/ppermute | solution.py:309
  22.5 0.6 %collective-permute-start.4 = (f32[96,256]{1,0:T(8,128)S(1)}, f32[96,256]{1,0:T(8,128)S(1)}, u32[]{:S(2)}, u32[]{:S(2)}) collective-permute-start(f32[96,256]{1,0:T(8,128)S(1)} %branch_1_fun.5.held_ref), channel_id=1, source_target_pairs={{0,8},{4,12},{8,0},{12,4},{16,24},{20,28},{24,16},{28,20},{1,9},{5... | collective-permute-start | bytes 294920 | tf_op jit(solution)/shard_map/cond/branch_1_fun/ppermute | solution.py:309
  23.2 1.6 %collective-permute-start.2 = (f32[160,256]{1,0:T(8,128)S(1)}, f32[160,256]{1,0:T(8,128)S(1)}, u32[]{:S(2)}, u32[]{:S(2)}) collective-permute-start(f32[160,256]{1,0:T(8,128)S(1)} %fusion.1), channel_id=1, source_target_pairs={{0,16},{4,20},{8,24},{12,28},{16,0},{20,4},{24,8},{28,12},{1,17},{... | collective-permute-start | bytes 491528 | tf_op jit(solution)/shard_map/cond/branch_1_fun/ppermute | solution.py:318
  24.8 2.4 %collective-permute-done.4.moved_ref = f32[96,256]{1,0:T(8,128)S(1)} collective-permute-done((f32[96,256]{1,0:T(8,128)S(1)}, f32[96,256]{1,0:T(8,128)S(1)}, u32[]{:S(2)}, u32[]{:S(2)}) %collective-permute-start.4) | collective-permute-done | bytes 98336 | tf_op jit(solution)/shard_map/cond/branch_1_fun/ppermute | solution.py:309
  27.3 1.3 %collective-permute-done.5.twin_ref = f32[96,256]{1,0:T(8,128)S(1)} collective-permute-done((f32[96,256]{1,0:T(8,128)S(1)}, f32[96,256]{1,0:T(8,128)S(1)}, u32[]{:S(2)}, u32[]{:S(2)}) %collective-permute-start.5) | collective-permute-done | bytes 98336 | tf_op jit(solution)/shard_map/cond/branch_1_fun/ppermute | solution.py:322
  28.6 1.8 %branch_1_fun.7.inverse_ref = f32[192,256]{1,0:T(8,128)S(1)} custom-call(f32[96,256]{1,0:T(8,128)S(1)} %branch_1_fun.6.own_ref, f32[96,256]{1,0:T(8,128)S(1)} %collective-permute-done.5.twin_ref), custom_call_target="tpu_custom_call" | custom-call | flops 1 | bytes 1 | tf_op jit(solution)/shard_map/cond/branch_1_fun/pallas_call | solution.py:251
  30.5 0.5 %branch_1_fun.8.pivot_rows_ref = f32[256,256]{1,0:T(8,128)S(1)} custom-call(s32[1,256]{1,0:T(1,128)S(1)} %get-tuple-element.32.pivot_ref, f32[256,256]{1,0:T(8,128)S(1)} %pad_maximum_fusion.gathered_ref), custom_call_target="tpu_custom_call" | custom-call | flops 1 | bytes 1 | tf_op jit(solution)/shard_map/cond/branch_1_fun/pallas_call | solution.py:251
  31.0 0.7 %branch_1_fun.9 = f32[256,256]{1,0:T(8,128)S(1)} custom-call(f32[192,256]{1,0:T(8,128)S(1)} %branch_1_fun.7.inverse_ref, f32[256,256]{1,0:T(8,128)S(1)} %branch_1_fun.8.pivot_rows_ref), custom_call_target="tpu_custom_call" | custom-call | flops 1 | bytes 1 | tf_op jit(solution)/shard_map/cond/branch_1_fun/pallas_call | solution.py:251
  31.8 2.1 %shard_map.40 = f32[1024,256]{1,0:T(8,128)} custom-call(s32[1,128]{1,0:T(1,128)S(1)} %get-tuple-element.43.local_ref, f32[32,256]{1,0:T(8,128)S(1)} %get-tuple-element.49.lead_ref, f32[256,256]{1,0:T(8,128)S(1)} %get-tuple-element.50.x_ref, f32[1024,256]{1,0:T(8,128)S(1)} %copy-done.1, f32[64,256]{1,0:T(8,128)S(1)} %get-tuple-element.45.refs_0_, ...), custom_call_target="tpu_custom_call" | custom-call | flops 1 | bytes 1 | tf_op jit(solution)/shard_map/pallas_call | solution.py:251
  (34 shorter events, 0.6 us)
Async XLA Ops:
  0.0 0.9 %copy-start.2 = (f32[1024,64]{0,1:T(8,128)S(1)}, f32[1024,64]{0,1:T(8,128)}, u32[]{:S(2)}) copy-start(f32[1024,64]{0,1:T(8,128)} %param.6) | copy-start | bytes 786436
  1.0 9.2 %collective-permute-start.6 = (f32[64,256]{1,0:T(8,128)S(1)}, f32[64,256]{1,0:T(8,128)S(1)}, u32[]{:S(2)}, u32[]{:S(2)}) collective-permute-start(f32[64,256]{1,0:T(8,128)S(1)} %get-tuple-element.45.refs_0_), channel_id=1, source_target_pairs={{0,1},{1,0},{2,3},{3,2},{4,5},{5,4},{6,7},{7,6},{8,9},{9,8},{10,11... | collective-permute-start | bytes 196616 | tf_op jit(solution)/shard_map/ppermute | solution.py:271
  4.1 8.9 %collective-permute-start.7 = (f32[64,256]{1,0:T(8,128)S(1)}, f32[64,256]{1,0:T(8,128)S(1)}, u32[]{:S(2)}, u32[]{:S(2)}) collective-permute-start(f32[64,256]{1,0:T(8,128)S(1)} %get-tuple-element.45.refs_0_), channel_id=1, source_target_pairs={{0,3},{1,2},{2,1},{3,0},{4,7},{5,6},{6,5},{7,4},{8,11},{9,10},{10,... | collective-permute-start | bytes 196616 | tf_op jit(solution)/shard_map/ppermute | solution.py:271
  6.6 6.6 %collective-permute-start.8 = (f32[64,256]{1,0:T(8,128)S(1)}, f32[64,256]{1,0:T(8,128)S(1)}, u32[]{:S(2)}, u32[]{:S(2)}) collective-permute-start(f32[64,256]{1,0:T(8,128)S(1)} %get-tuple-element.45.refs_0_), channel_id=1, source_target_pairs={{0,2},{1,3},{2,0},{3,1},{4,6},{5,7},{6,4},{7,5},{8,10},{9,11},{10,... | collective-permute-start | bytes 196616 | tf_op jit(solution)/shard_map/ppermute | solution.py:271
  6.7 4.4 %copy-start.3 = (s32[256]{0:T(256)S(1)}, s32[256]{0:T(256)}, u32[]{:S(2)}) copy-start(s32[256]{0:T(256)} %param.7) | copy-start | bytes 3076
  6.7 25.0 %collective-permute-start.10 = (f32[64,768]{1,0:T(8,128)S(1)}, f32[64,768]{1,0:T(8,128)S(1)}, u32[]{:S(2)}, u32[]{:S(2)}) collective-permute-start(f32[64,768]{1,0:T(8,128)S(1)} %get-tuple-element.51.refs_4_), channel_id=1, source_target_pairs={{0,1},{1,0},{2,3},{3,2},{4,5},{5,4},{6,7},{7,6},{8,9},{9,8},{10,11... | collective-permute-start | bytes 589832 | tf_op jit(solution)/shard_map/ppermute | solution.py:271
  8.5 23.2 %collective-permute-start.11 = (f32[64,768]{1,0:T(8,128)S(1)}, f32[64,768]{1,0:T(8,128)S(1)}, u32[]{:S(2)}, u32[]{:S(2)}) collective-permute-start(f32[64,768]{1,0:T(8,128)S(1)} %get-tuple-element.51.refs_4_), channel_id=1, source_target_pairs={{0,2},{1,3},{2,0},{3,1},{4,6},{5,7},{6,4},{7,5},{8,10},{9,11},{10,... | collective-permute-start | bytes 589832 | tf_op jit(solution)/shard_map/ppermute | solution.py:271
  10.2 21.6 %collective-permute-start.12 = (f32[64,768]{1,0:T(8,128)S(1)}, f32[64,768]{1,0:T(8,128)S(1)}, u32[]{:S(2)}, u32[]{:S(2)}) collective-permute-start(f32[64,768]{1,0:T(8,128)S(1)} %get-tuple-element.51.refs_4_), channel_id=1, source_target_pairs={{0,3},{1,2},{2,1},{3,0},{4,7},{5,6},{6,5},{7,4},{8,11},{9,10},{10,... | collective-permute-start | bytes 589832 | tf_op jit(solution)/shard_map/ppermute | solution.py:271
  11.1 1.2 %copy-start = (f32[1024,256]{1,0:T(8,128)S(1)}, f32[1024,256]{1,0:T(8,128)}, u32[]{:S(2)}) copy-start(f32[1024,256]{1,0:T(8,128)} %slab_ref.3) | copy-start | bytes 3145732
  13.3 1.4 %collective-permute-start.9 = (f32[128,256]{1,0:T(8,128)S(1)}, f32[128,256]{1,0:T(8,128)S(1)}, u32[]{:S(2)}, u32[]{:S(2)}) collective-permute-start(f32[128,256]{1,0:T(8,128)S(1)} %slice.53), channel_id=1, source_target_pairs={{0,4},{4,0},{8,12},{12,8},{16,20},{20,16},{24,28},{28,24},{1,5},{5... | collective-permute-start | bytes 393224 | tf_op jit(solution)/shard_map/ppermute | solution.py:341
  14.7 17.1 %copy-start.1 = (f32[1024,256]{1,0:T(8,128)S(1)}, f32[1024,256]{1,0:T(8,128)}, u32[]{:S(2)}) copy-start(f32[1024,256]{1,0:T(8,128)} %slab_ref.3) | copy-start | bytes 3145732
  14.7 1.5 %collective-permute-start = (f32[160,256]{1,0:T(8,128)S(1)}, f32[160,256]{1,0:T(8,128)S(1)}, u32[]{:S(2)}, u32[]{:S(2)}) collective-permute-start(f32[160,256]{1,0:T(8,128)S(1)} %pad_maximum_fusion.1), channel_id=1, source_target_pairs={{0,4},{4,0},{8,12},{12,8},{16,20},{20,16},{24,28},{28,24},{1,5},{5... | collective-permute-start | bytes 491528 | tf_op jit(solution)/shard_map/cond/branch_1_fun/ppermute | solution.py:304
  16.3 6.9 %collective-permute-start.1 = (f32[128,256]{1,0:T(8,128)S(1)}, f32[128,256]{1,0:T(8,128)S(1)}, u32[]{:S(2)}, u32[]{:S(2)}) collective-permute-start(f32[128,256]{1,0:T(8,128)S(1)} %pad_maximum_fusion.3), channel_id=1, source_target_pairs={{0,8},{4,12},{8,0},{12,4},{16,24},{20,28},{24,16},{28,20},{1,9},{5... | collective-permute-start | bytes 393224 | tf_op jit(solution)/shard_map/cond/branch_1_fun/ppermute | solution.py:318
  17.8 4.7 %collective-permute-start.3 = (f32[96,256]{1,0:T(8,128)S(1)}, f32[96,256]{1,0:T(8,128)S(1)}, u32[]{:S(2)}, u32[]{:S(2)}) collective-permute-start(f32[96,256]{1,0:T(8,128)S(1)} %slice_select_fusion.1.held_ref), channel_id=1, source_target_pairs={{0,16},{4,20},{8,24},{12,28},{16,0},{20,4},{24,8},{28,12},{1,17},{... | collective-permute-start | bytes 294920 | tf_op jit(solution)/shard_map/cond/branch_1_fun/ppermute | solution.py:309
  22.5 4.7 %collective-permute-start.4 = (f32[96,256]{1,0:T(8,128)S(1)}, f32[96,256]{1,0:T(8,128)S(1)}, u32[]{:S(2)}, u32[]{:S(2)}) collective-permute-start(f32[96,256]{1,0:T(8,128)S(1)} %branch_1_fun.5.held_ref), channel_id=1, source_target_pairs={{0,8},{4,12},{8,0},{12,4},{16,24},{20,28},{24,16},{28,20},{1,9},{5... | collective-permute-start | bytes 294920 | tf_op jit(solution)/shard_map/cond/branch_1_fun/ppermute | solution.py:309
  23.2 7.2 %collective-permute-start.2 = (f32[160,256]{1,0:T(8,128)S(1)}, f32[160,256]{1,0:T(8,128)S(1)}, u32[]{:S(2)}, u32[]{:S(2)}) collective-permute-start(f32[160,256]{1,0:T(8,128)S(1)} %fusion.1), channel_id=1, source_target_pairs={{0,16},{4,20},{8,24},{12,28},{16,0},{20,4},{24,8},{28,12},{1,17},{... | collective-permute-start | bytes 491528 | tf_op jit(solution)/shard_map/cond/branch_1_fun/ppermute | solution.py:318
  27.2 1.4 %collective-permute-start.5 = (f32[96,256]{1,0:T(8,128)S(1)}, f32[96,256]{1,0:T(8,128)S(1)}, u32[]{:S(2)}, u32[]{:S(2)}) collective-permute-start(f32[96,256]{1,0:T(8,128)S(1)} %branch_1_fun.6.own_ref), channel_id=1, source_target_pairs={{0,4},{4,0},{8,12},{12,8},{16,20},{20,16},{24,28},{28,24},{1,5},{5... | collective-permute-start | bytes 294920 | tf_op jit(solution)/shard_map/cond/branch_1_fun/ppermute | solution.py:322

commit v6 on v1

--- a/solution.py
+++ b/solution.py
@@ -33,7 +33,11 @@
 
 
 def dot_full(a, b):
-    return jnp.dot(a, b, precision=lax.Precision.HIGHEST, preferred_element_type=F32)
+    high, mid, low = split3(a)
+    left = jnp.concatenate([low, mid, high, mid, high, high], axis=1)
+    high, mid, low = split3(b)
+    right = jnp.concatenate([high, mid, low, high, mid, high], axis=0)
+    return jnp.dot(left, right, preferred_element_type=F32)
 
 
 def tree_partner(r, span):
@@ -122,7 +126,7 @@
 
 
 def top_order(m):
-    return [0, 1, *range(m - 1, 1, -1)]
+    return [0, *range(m - 1, 0, -1)]
 
 
 def cut_kernel(panel_ref, top_ref, rest_ref, sems):
@@ -208,22 +212,26 @@
 
 
 def update_kernel(m, local_ref, lead_ref, x_ref, slab_ref, *refs):
-    *pieces, out_ref, result, sems = refs
+    *pieces, out_ref, result, swaps, sems = refs
     tops, rests = dict(zip(top_order(m), pieces[:m])), pieces[m:]
-    rows, cols = slab_ref.shape
+    rows = slab_ref.shape[0]
     width = x_ref.shape[0]
+    blocks = rows // width
+    fetch = pltpu.make_async_copy(local_ref, swaps, sems.at[blocks])
+    fetch.start()
     result[:rows, :] = slab_ref[...]
-    for s in range(CAP):
-        result[pl.ds(local_ref[0, s], 1), :] = lead_ref[pl.ds(s, 1), :]
     uppers = [piece_rows(x_ref, m, d) for d in range(m)]
     copies = []
-    for c in range(rows // width):
+    for c in range(blocks):
         part = pl.ds(c * width, width)
-        total = result[part, :]
-        for d, upper in enumerate(uppers):
-            piece = rests[d][:, (c - 1) * width : c * width] if c else tops[d][...]
-            total = total - product(piece, upper)
-        result[part, :] = total
+        if c:
+            total = sum(product(rests[d][:, (c - 1) * width : c * width], uppers[d]) for d in range(m))
+        else:
+            total = sum(product(tops[d][...], uppers[d]) for d in range(m))
+            fetch.wait()
+            for s in range(CAP):
+                result[pl.ds(swaps[0, s], 1), :] = lead_ref[pl.ds(s, 1), :]
+        result[part, :] = result[part, :] - total
         if c == 0:
 
             @pl.when(lax.axis_index("prow") == 0)
@@ -337,9 +345,13 @@
         functools.partial(update_kernel, m),
         jax.ShapeDtypeStruct((rows, cols), F32),
         (local_rows, leading, upper_rows, slab, *tops, *rests),
-        in_specs=[pl.BlockSpec(memory_space=pltpu.SMEM)] + [VMEM] * (2 * m + 3),
+        in_specs=[VMEM] * (2 * m + 4),
         out_specs=pl.BlockSpec(memory_space=pl.ANY),
-        scratch=[pltpu.VMEM((rows + 8, cols), F32), pltpu.SemaphoreType.DMA((rows // width,))],
+        scratch=[
+            pltpu.VMEM((rows + 8, cols), F32),
+            pltpu.SMEM((1, 128), jnp.int32),
+            pltpu.SemaphoreType.DMA((rows // width + 1,)),
+        ],
     )
 
 

time: 31.5 us -> 33.6 us (1.067)
  waiting for transfers between devices: 6.04 us -> 8.29 us
  Pallas kernels: 6.39 us -> 6.01 us
    ppermute x6, waiting for transfers between devices: 0.13 us -> 2.07 us  [spread(): lax.ppermute(block, 'pcol', [(c, c ^ d) for c in range(m)])]
    ppermute x1, starting transfers between devices: 0.79 us -> 0.27 us  [levels(): moved = lax.ppermute(inverse, 'prow', [(r, r ^ 1) for r in range(n)])]
    pallas_call x9, Pallas kernels: 6.39 us -> 6.01 us  [call(): pl.pallas_call(kernel, out_shape=outs, in_specs=in_specs or [VMEM] * len(...]
  transfers between devices with their start and end apart: 13 -> 13, of which waited for: 5 -> 5; matrix products, arithmetic and copies ran while one was open for 1% -> 0% of each run, Pallas kernels for 13% -> 11%
where the time goes in v6:
time: 33.6 us; the launch traced here: 33.4 us
  starting transfers between devices  16.5 us (49%)
  waiting for transfers between devices  8.29 us (25%)
  Pallas kernels  6.01 us (18%)
  local copies, waits for them, and re-layouts  2.22 us (7%)
    ppermute x6, starting transfers between devices, spread(): lax.ppermute(block, 'pcol', [(c, c ^ d) for c in range(m)])  10.2 us
    pallas_call x9, Pallas kernels, call(): pl.pallas_call(kernel, out_shape=outs, in_specs=in_specs or [VMEM] * len(...  6.01 us
    ppermute x2, starting transfers between devices, levels(): moved = lax.ppermute(message, 'prow', [(r, r ^ other) for r in range(n)])  3.84 us
    ppermute x2, waiting for transfers between devices, levels(): moved = lax.ppermute(message, 'prow', [(r, r ^ other) for r in range(n)])  3.07 us
    unnamed x8, local copies, waits for them, and re-layouts  2.18 us
    ppermute x6, waiting for transfers between devices, spread(): lax.ppermute(block, 'pcol', [(c, c ^ d) for c in range(m)])  2.07 us
    ppermute x2, waiting for transfers between devices, levels(): lax.ppermute(lower, 'prow', [(r, tree_partner(r, span)) for r in range(n)])  1.91 us
    ppermute x2, starting transfers between devices, levels(): lax.ppermute(lower, 'prow', [(r, tree_partner(r, span)) for r in range(n)])  1.87 us
  transfers between devices with their start and end apart: 13, of which 5 were waited for; matrix products, arithmetic and copies ran while one was open for 0% of the time, Pallas kernels for 11%

profile of v6, /device:TPU:0, one launch (start us, length us, event | category | flops | bytes accessed | tf_op | source)
XLA Modules:
  0.0 33.4 jit_solution(3129031436313162755)
XLA Ops:
  0.0 0.9 %copy-done.2 = f32[1024,64]{0,1:T(8,128)S(1)} copy-done((f32[1024,64]{0,1:T(8,128)S(1)}, f32[1024,64]{0,1:T(8,128)}, u32[]{:S(2)}) %copy-start.2) | copy-done | bytes 262168
  1.0 0.1 shard_map.38
  1.0 5.1 %collective-permute-start.6 = (f32[64,256]{1,0:T(8,128)S(1)}, f32[64,256]{1,0:T(8,128)S(1)}, u32[]{:S(2)}, u32[]{:S(2)}) collective-permute-start(f32[64,256]{1,0:T(8,128)S(1)} %get-tuple-element.32.refs_0_), channel_id=1, source_target_pairs={{0,3},{1,2},{2,1},{3,0},{4,7},{5,6},{6,5},{7,4},{8,11},{9,10},{10,... | collective-permute-start | bytes 196616 | tf_op jit(solution)/shard_map/ppermute | solution.py:274
  6.2 0.6 %collective-permute-start.8 = (f32[64,256]{1,0:T(8,128)S(1)}, f32[64,256]{1,0:T(8,128)S(1)}, u32[]{:S(2)}, u32[]{:S(2)}) collective-permute-start(f32[64,256]{1,0:T(8,128)S(1)} %get-tuple-element.32.refs_0_), channel_id=1, source_target_pairs={{0,1},{1,0},{2,3},{3,2},{4,5},{5,4},{6,7},{7,6},{8,9},{9,8},{10,11... | collective-permute-start | bytes 196616 | tf_op jit(solution)/shard_map/ppermute | solution.py:274
  6.8 1.4 %collective-permute-start.10 = (f32[64,768]{1,0:T(8,128)S(1)}, f32[64,768]{1,0:T(8,128)S(1)}, u32[]{:S(2)}, u32[]{:S(2)}) collective-permute-start(f32[64,768]{1,0:T(8,128)S(1)} %get-tuple-element.37.refs_4_), channel_id=1, source_target_pairs={{0,1},{1,0},{2,3},{3,2},{4,5},{5,4},{6,7},{7,6},{8,9},{9,8},{10,11... | collective-permute-start | bytes 589832 | tf_op jit(solution)/shard_map/ppermute | solution.py:274
  8.2 2.9 %collective-permute-start.11 = (f32[64,768]{1,0:T(8,128)S(1)}, f32[64,768]{1,0:T(8,128)S(1)}, u32[]{:S(2)}, u32[]{:S(2)}) collective-permute-start(f32[64,768]{1,0:T(8,128)S(1)} %get-tuple-element.37.refs_4_), channel_id=1, source_target_pairs={{0,2},{1,3},{2,0},{3,1},{4,6},{5,7},{6,4},{7,5},{8,10},{9,11},{10,... | collective-permute-start | bytes 589832 | tf_op jit(solution)/shard_map/ppermute | solution.py:274
  11.1 1.2 %copy-done = f32[1024,256]{1,0:T(8,128)S(1)} copy-done((f32[1024,256]{1,0:T(8,128)S(1)}, f32[1024,256]{1,0:T(8,128)}, u32[]{:S(2)}) %copy-start) | copy-done | bytes 1048600
  12.3 0.7 %shard_map.37 = (f32[32,256]{1,0:T(8,128)S(1)}, f32[256,256]{1,0:T(8,128)S(1)}, s32[1,128]{1,0:T(1,128)S(1)}) custom-call(s32[1,256]{1,0:T(1,128)S(1)} %bitcast.3, f32[1024,256]{1,0:T(8,128)S(1)} %copy-done), custom_call_target="tpu_custom_call" | custom-call | flops 1 | bytes 1 | tf_op jit(solution)/shard_map/pallas_call | solution.py:254
  13.0 0.2 collective-permute-start.12
  13.2 2.1 %collective-permute-done.8.refs_3_ = f32[64,256]{1,0:T(8,128)S(1)} collective-permute-done((f32[64,256]{1,0:T(8,128)S(1)}, f32[64,256]{1,0:T(8,128)S(1)}, u32[]{:S(2)}, u32[]{:S(2)}) %collective-permute-start.8) | collective-permute-done | bytes 65568 | tf_op jit(solution)/shard_map/ppermute | solution.py:274
  15.4 1.2 %collective-permute-done.9 = f32[64,256]{1,0:T(8,128)S(1)} collective-permute-done((f32[64,256]{1,0:T(8,128)S(1)}, f32[64,256]{1,0:T(8,128)S(1)}, u32[]{:S(2)}, u32[]{:S(2)}) %collective-permute-start.9) | collective-permute-done | bytes 65568 | tf_op jit(solution)/shard_map/ppermute | solution.py:341
  16.7 14.5 %conditional.1 = (f32[32,256]{1,0:T(8,128)S(1)}, f32[256,256]{1,0:T(8,128)S(1)}) conditional(s32[]{:T(128)} %convert_element_type.3, () %tuple.14, (s32[]{:T(128)}, f32[256,256]{1,0:T(8,128)S(1)}, f32[64,256]{1,0:T(8,128)S(1)}, f32[192,256]{1,0:T(8,128)S(1)}, s32[1,256]{1,0:T(1,128)S(1)}) %tuple.20), branch_computations={%region_0.0_spmd, %region_1.2_spmd} | conditional | flops 352267 | bytes 7307592 | solution.py:250
  16.7 0.2 collective-permute-start
  16.9 1.8 %collective-permute-start.3 = (f32[192,256]{1,0:T(8,128)S(1)}, f32[192,256]{1,0:T(8,128)S(1)}, u32[]{:S(2)}, u32[]{:S(2)}) collective-permute-start(f32[192,256]{1,0:T(8,128)S(1)} %get-tuple-element.18.held_ref), channel_id=1, source_target_pairs={{0,16},{4,0},{8,12},{12,8},{16,20},{20,4},{24,28},{28,24},{1,17},{... | collective-permute-start | bytes 589832 | tf_op jit(solution)/shard_map/cond/branch_1_fun/ppermute | solution.py:311
  18.8 1.2 %collective-permute-start.1 = (f32[128,256]{1,0:T(8,128)S(1)}, f32[128,256]{1,0:T(8,128)S(1)}, u32[]{:S(2)}, u32[]{:S(2)}) collective-permute-start(f32[128,256]{1,0:T(8,128)S(1)} %pad_maximum_fusion.2), channel_id=1, source_target_pairs={{0,8},{4,12},{8,0},{12,4},{16,24},{20,28},{24,16},{28,20},{1,9},{5... | collective-permute-start | bytes 393224 | tf_op jit(solution)/shard_map/cond/branch_1_fun/ppermute | solution.py:320
  20.1 1.9 %collective-permute-done.3.moved_ref = f32[192,256]{1,0:T(8,128)S(1)} collective-permute-done((f32[192,256]{1,0:T(8,128)S(1)}, f32[192,256]{1,0:T(8,128)S(1)}, u32[]{:S(2)}, u32[]{:S(2)}) %collective-permute-start.3) | collective-permute-done | bytes 196640 | tf_op jit(solution)/shard_map/cond/branch_1_fun/ppermute | solution.py:311
  22.0 1.9 %collective-permute-done.1 = f32[128,256]{1,0:T(8,128)S(1)} collective-permute-done((f32[128,256]{1,0:T(8,128)S(1)}, f32[128,256]{1,0:T(8,128)S(1)}, u32[]{:S(2)}, u32[]{:S(2)}) %collective-permute-start.1) | collective-permute-done | bytes 131104 | tf_op jit(solution)/shard_map/cond/branch_1_fun/ppermute | solution.py:320
  23.9 2.6 %collective-permute-start.2 = (f32[160,256]{1,0:T(8,128)S(1)}, f32[160,256]{1,0:T(8,128)S(1)}, u32[]{:S(2)}, u32[]{:S(2)}) collective-permute-start(f32[160,256]{1,0:T(8,128)S(1)} %pad_maximum_fusion.1), channel_id=1, source_target_pairs={{0,16},{4,20},{8,24},{12,28},{16,0},{20,4},{24,8},{28,12},{1,17},{... | collective-permute-start | bytes 491528 | tf_op jit(solution)/shard_map/cond/branch_1_fun/ppermute | solution.py:320
  26.6 1.8 %branch_1_fun.7 = f32[192,256]{1,0:T(8,128)S(1)} custom-call(f32[192,256]{1,0:T(8,128)S(1)} %branch_1_fun.6.lower_ref), custom_call_target="tpu_custom_call" | custom-call | flops 1 | bytes 1 | tf_op jit(solution)/shard_map/cond/branch_1_fun/pallas_call | solution.py:254
  28.4 0.3 collective-permute-start.5
  28.6 1.2 %collective-permute-done.2 = f32[160,256]{1,0:T(8,128)S(1)} collective-permute-done((f32[160,256]{1,0:T(8,128)S(1)}, f32[160,256]{1,0:T(8,128)S(1)}, u32[]{:S(2)}, u32[]{:S(2)}) %collective-permute-start.2) | collective-permute-done | bytes 163872 | tf_op jit(solution)/shard_map/cond/branch_1_fun/ppermute | solution.py:320
  29.9 0.5 %branch_1_fun.8.pivot_rows_ref = f32[256,256]{1,0:T(8,128)S(1)} custom-call(s32[1,256]{1,0:T(1,128)S(1)} %get-tuple-element.19.pivot_ref, f32[256,256]{1,0:T(8,128)S(1)} %pad_maximum_fusion.gathered_ref), custom_call_target="tpu_custom_call" | custom-call | flops 1 | bytes 1 | tf_op jit(solution)/shard_map/cond/branch_1_fun/pallas_call | solution.py:254
  30.5 0.7 %branch_1_fun.9 = f32[256,256]{1,0:T(8,128)S(1)} custom-call(f32[192,256]{1,0:T(8,128)S(1)} %broadcast_select_fusion.inverse_ref, f32[256,256]{1,0:T(8,128)S(1)} %branch_1_fun.8.pivot_rows_ref), custom_call_target="tpu_custom_call" | custom-call | flops 1 | bytes 1 | tf_op jit(solution)/shard_map/cond/branch_1_fun/pallas_call | solution.py:254
  31.2 2.1 %shard_map.40 = f32[1024,256]{1,0:T(8,128)} custom-call(s32[1,128]{1,0:T(1,128)S(1)} %get-tuple-element.29.local_ref, f32[32,256]{1,0:T(8,128)S(1)} %get-tuple-element.35.lead_ref, f32[256,256]{1,0:T(8,128)S(1)} %get-tuple-element.36.x_ref, f32[1024,256]{1,0:T(8,128)S(1)} %copy-done.1, f32[64,256]{1,0:T(8,128)S(1)} %get-tuple-element.32.refs_0_, ...), custom_call_target="tpu_custom_call" | custom-call | flops 1 | bytes 1 | tf_op jit(solution)/shard_map/pallas_call | solution.py:254
  (34 shorter events, 0.4 us)
Async XLA Ops:
  0.0 0.9 %copy-start.2 = (f32[1024,64]{0,1:T(8,128)S(1)}, f32[1024,64]{0,1:T(8,128)}, u32[]{:S(2)}) copy-start(f32[1024,64]{0,1:T(8,128)} %param.6) | copy-start | bytes 786436
  1.0 12.0 %collective-permute-start.6 = (f32[64,256]{1,0:T(8,128)S(1)}, f32[64,256]{1,0:T(8,128)S(1)}, u32[]{:S(2)}, u32[]{:S(2)}) collective-permute-start(f32[64,256]{1,0:T(8,128)S(1)} %get-tuple-element.32.refs_0_), channel_id=1, source_target_pairs={{0,3},{1,2},{2,1},{3,0},{4,7},{5,6},{6,5},{7,4},{8,11},{9,10},{10,... | collective-permute-start | bytes 196616 | tf_op jit(solution)/shard_map/ppermute | solution.py:274
  6.2 7.1 %collective-permute-start.7 = (f32[64,256]{1,0:T(8,128)S(1)}, f32[64,256]{1,0:T(8,128)S(1)}, u32[]{:S(2)}, u32[]{:S(2)}) collective-permute-start(f32[64,256]{1,0:T(8,128)S(1)} %get-tuple-element.32.refs_0_), channel_id=1, source_target_pairs={{0,2},{1,3},{2,0},{3,1},{4,6},{5,7},{6,4},{7,5},{8,10},{9,11},{10,... | collective-permute-start | bytes 196616 | tf_op jit(solution)/shard_map/ppermute | solution.py:274
  6.2 9.1 %collective-permute-start.8 = (f32[64,256]{1,0:T(8,128)S(1)}, f32[64,256]{1,0:T(8,128)S(1)}, u32[]{:S(2)}, u32[]{:S(2)}) collective-permute-start(f32[64,256]{1,0:T(8,128)S(1)} %get-tuple-element.32.refs_0_), channel_id=1, source_target_pairs={{0,1},{1,0},{2,3},{3,2},{4,5},{5,4},{6,7},{7,6},{8,9},{9,8},{10,11... | collective-permute-start | bytes 196616 | tf_op jit(solution)/shard_map/ppermute | solution.py:274
  6.8 4.3 %copy-start.3 = (s32[256]{0:T(256)S(1)}, s32[256]{0:T(256)}, u32[]{:S(2)}) copy-start(s32[256]{0:T(256)} %param.7) | copy-start | bytes 3076
  6.8 24.4 %collective-permute-start.10 = (f32[64,768]{1,0:T(8,128)S(1)}, f32[64,768]{1,0:T(8,128)S(1)}, u32[]{:S(2)}, u32[]{:S(2)}) collective-permute-start(f32[64,768]{1,0:T(8,128)S(1)} %get-tuple-element.37.refs_4_), channel_id=1, source_target_pairs={{0,1},{1,0},{2,3},{3,2},{4,5},{5,4},{6,7},{7,6},{8,9},{9,8},{10,11... | collective-permute-start | bytes 589832 | tf_op jit(solution)/shard_map/ppermute | solution.py:274
  8.2 23.0 %collective-permute-start.11 = (f32[64,768]{1,0:T(8,128)S(1)}, f32[64,768]{1,0:T(8,128)S(1)}, u32[]{:S(2)}, u32[]{:S(2)}) collective-permute-start(f32[64,768]{1,0:T(8,128)S(1)} %get-tuple-element.37.refs_4_), channel_id=1, source_target_pairs={{0,2},{1,3},{2,0},{3,1},{4,6},{5,7},{6,4},{7,5},{8,10},{9,11},{10,... | collective-permute-start | bytes 589832 | tf_op jit(solution)/shard_map/ppermute | solution.py:274
  11.1 1.2 %copy-start = (f32[1024,256]{1,0:T(8,128)S(1)}, f32[1024,256]{1,0:T(8,128)}, u32[]{:S(2)}) copy-start(f32[1024,256]{1,0:T(8,128)} %slab_ref.3) | copy-start | bytes 3145732
  13.0 18.2 %collective-permute-start.12 = (f32[64,768]{1,0:T(8,128)S(1)}, f32[64,768]{1,0:T(8,128)S(1)}, u32[]{:S(2)}, u32[]{:S(2)}) collective-permute-start(f32[64,768]{1,0:T(8,128)S(1)} %get-tuple-element.37.refs_4_), channel_id=1, source_target_pairs={{0,3},{1,2},{2,1},{3,0},{4,7},{5,6},{6,5},{7,4},{8,11},{9,10},{10,... | collective-permute-start | bytes 589832 | tf_op jit(solution)/shard_map/ppermute | solution.py:274
  15.3 1.3 %collective-permute-start.9 = (f32[64,256]{1,0:T(8,128)S(1)}, f32[64,256]{1,0:T(8,128)S(1)}, u32[]{:S(2)}, u32[]{:S(2)}) collective-permute-start(f32[64,256]{1,0:T(8,128)S(1)} %pad_maximum_fusion.3), channel_id=1, source_target_pairs={{0,4},{4,0},{8,12},{12,8},{16,20},{20,16},{24,28},{28,24},{1,5},{5... | collective-permute-start | bytes 196616 | tf_op jit(solution)/shard_map/ppermute | solution.py:341
  16.7 14.6 %copy-start.1 = (f32[1024,256]{1,0:T(8,128)S(1)}, f32[1024,256]{1,0:T(8,128)}, u32[]{:S(2)}) copy-start(f32[1024,256]{1,0:T(8,128)} %slab_ref.3) | copy-start | bytes 3145732
  16.7 2.1 %collective-permute-start = (f32[128,256]{1,0:T(8,128)S(1)}, f32[128,256]{1,0:T(8,128)S(1)}, u32[]{:S(2)}, u32[]{:S(2)}) collective-permute-start(f32[128,256]{1,0:T(8,128)S(1)} %slice.28), channel_id=1, source_target_pairs={{0,4},{4,0},{8,12},{12,8},{16,20},{20,16},{24,28},{28,24},{1,5},{5... | collective-permute-start | bytes 393224 | tf_op jit(solution)/shard_map/cond/branch_1_fun/ppermute | solution.py:307
  16.9 5.0 %collective-permute-start.3 = (f32[192,256]{1,0:T(8,128)S(1)}, f32[192,256]{1,0:T(8,128)S(1)}, u32[]{:S(2)}, u32[]{:S(2)}) collective-permute-start(f32[192,256]{1,0:T(8,128)S(1)} %get-tuple-element.18.held_ref), channel_id=1, source_target_pairs={{0,16},{4,0},{8,12},{12,8},{16,20},{20,4},{24,28},{28,24},{1,17},{... | collective-permute-start | bytes 589832 | tf_op jit(solution)/shard_map/cond/branch_1_fun/ppermute | solution.py:311
  18.8 5.0 %collective-permute-start.1 = (f32[128,256]{1,0:T(8,128)S(1)}, f32[128,256]{1,0:T(8,128)S(1)}, u32[]{:S(2)}, u32[]{:S(2)}) collective-permute-start(f32[128,256]{1,0:T(8,128)S(1)} %pad_maximum_fusion.2), channel_id=1, source_target_pairs={{0,8},{4,12},{8,0},{12,4},{16,24},{20,28},{24,16},{28,20},{1,9},{5... | collective-permute-start | bytes 393224 | tf_op jit(solution)/shard_map/cond/branch_1_fun/ppermute | solution.py:320
  22.0 4.6 %collective-permute-start.4 = (f32[192,256]{1,0:T(8,128)S(1)}, f32[192,256]{1,0:T(8,128)S(1)}, u32[]{:S(2)}, u32[]{:S(2)}) collective-permute-start(f32[192,256]{1,0:T(8,128)S(1)} %branch_1_fun.5.held_ref), channel_id=1, source_target_pairs={{0,8},{4,0},{8,12},{12,4},{16,24},{20,16},{24,28},{28,20},{1,9},{5... | collective-permute-start | bytes 589832 | tf_op jit(solution)/shard_map/cond/branch_1_fun/ppermute | solution.py:311
  23.9 5.9 %collective-permute-start.2 = (f32[160,256]{1,0:T(8,128)S(1)}, f32[160,256]{1,0:T(8,128)S(1)}, u32[]{:S(2)}, u32[]{:S(2)}) collective-permute-start(f32[160,256]{1,0:T(8,128)S(1)} %pad_maximum_fusion.1), channel_id=1, source_target_pairs={{0,16},{4,20},{8,24},{12,28},{16,0},{20,4},{24,8},{28,12},{1,17},{... | collective-permute-start | bytes 491528 | tf_op jit(solution)/shard_map/cond/branch_1_fun/ppermute | solution.py:320
  28.4 2.1 %collective-permute-start.5 = (f32[192,256]{1,0:T(8,128)S(1)}, f32[192,256]{1,0:T(8,128)S(1)}, u32[]{:S(2)}, u32[]{:S(2)}) collective-permute-start(f32[192,256]{1,0:T(8,128)S(1)} %branch_1_fun.7), channel_id=1, source_target_pairs={{0,4},{4,0},{8,12},{12,8},{16,20},{20,16},{24,28},{28,24},{1,5},{5... | collective-permute-start | bytes 589832 | tf_op jit(solution)/shard_map/cond/branch_1_fun/ppermute | solution.py:336

commit v7 on v6

--- a/solution.py
+++ b/solution.py
@@ -126,7 +126,7 @@
 
 
 def top_order(m):
-    return [0, *range(m - 1, 0, -1)]
+    return [0, 1, *range(m - 1, 1, -1)]
 
 
 def cut_kernel(panel_ref, top_ref, rest_ref, sems):

time: 33.6 us -> 31.2 us (0.929)
  waiting for transfers between devices: 8.29 us -> 6.09 us
    ppermute x6, waiting for transfers between devices: 2.07 us -> 0.13 us  [spread(): lax.ppermute(block, 'pcol', [(c, c ^ d) for c in range(m)])]
    ppermute x1, starting transfers between devices: 0.27 us -> 0.79 us  [levels(): moved = lax.ppermute(inverse, 'prow', [(r, r ^ 1) for r in range(n)])]
  transfers between devices with their start and end apart: 13 -> 13, of which waited for: 5 -> 5; matrix products, arithmetic and copies ran while one was open for 0% -> 1% of each run, Pallas kernels for 11% -> 12%
where the time goes in v7:
time: 31.2 us; the launch traced here: 31 us
  starting transfers between devices  16.3 us (52%)
  waiting for transfers between devices  6.09 us (20%)
  Pallas kernels  6.02 us (19%)
  local copies, waits for them, and re-layouts  2.22 us (7%)
    ppermute x6, starting transfers between devices, spread(): lax.ppermute(block, 'pcol', [(c, c ^ d) for c in range(m)])  10.1 us
    pallas_call x9, Pallas kernels, call(): pl.pallas_call(kernel, out_shape=outs, in_specs=in_specs or [VMEM] * len(...  6.02 us
    ppermute x2, starting transfers between devices, levels(): moved = lax.ppermute(message, 'prow', [(r, r ^ other) for r in range(n)])  3.59 us
    ppermute x2, waiting for transfers between devices, levels(): moved = lax.ppermute(message, 'prow', [(r, r ^ other) for r in range(n)])  2.8 us
    unnamed x8, local copies, waits for them, and re-layouts  2.18 us
    ppermute x2, waiting for transfers between devices, levels(): lax.ppermute(lower, 'prow', [(r, tree_partner(r, span)) for r in range(n)])  1.91 us
    ppermute x2, starting transfers between devices, levels(): lax.ppermute(lower, 'prow', [(r, tree_partner(r, span)) for r in range(n)])  1.54 us
    ppermute x1, waiting for transfers between devices, local(): lax.ppermute(jnp.concatenate([gathered, gathered], axis=0), 'prow', [(r,...  1.24 us
  transfers between devices with their start and end apart: 13, of which 5 were waited for; matrix products, arithmetic and copies ran while one was open for 1% of the time, Pallas kernels for 12%

profile of v7, /device:TPU:0, one launch (start us, length us, event | category | flops | bytes accessed | tf_op | source)
XLA Modules:
  0.0 31.0 jit_solution(15869786652965017241)
XLA Ops:
  0.0 0.9 %copy-done.2 = f32[1024,64]{0,1:T(8,128)S(1)} copy-done((f32[1024,64]{0,1:T(8,128)S(1)}, f32[1024,64]{0,1:T(8,128)}, u32[]{:S(2)}) %copy-start.2) | copy-done | bytes 262168
  1.0 3.1 %collective-permute-start.6 = (f32[64,256]{1,0:T(8,128)S(1)}, f32[64,256]{1,0:T(8,128)S(1)}, u32[]{:S(2)}, u32[]{:S(2)}) collective-permute-start(f32[64,256]{1,0:T(8,128)S(1)} %get-tuple-element.32.refs_0_), channel_id=1, source_target_pairs={{0,1},{1,0},{2,3},{3,2},{4,5},{5,4},{6,7},{7,6},{8,9},{9,8},{10,11... | collective-permute-start | bytes 196616 | tf_op jit(solution)/shard_map/ppermute | solution.py:274
  4.1 2.5 %collective-permute-start.7 = (f32[64,256]{1,0:T(8,128)S(1)}, f32[64,256]{1,0:T(8,128)S(1)}, u32[]{:S(2)}, u32[]{:S(2)}) collective-permute-start(f32[64,256]{1,0:T(8,128)S(1)} %get-tuple-element.32.refs_0_), channel_id=1, source_target_pairs={{0,3},{1,2},{2,1},{3,0},{4,7},{5,6},{6,5},{7,4},{8,11},{9,10},{10,... | collective-permute-start | bytes 196616 | tf_op jit(solution)/shard_map/ppermute | solution.py:274
  6.6 0.1 collective-permute-start.8
  6.7 1.8 %collective-permute-start.10 = (f32[64,768]{1,0:T(8,128)S(1)}, f32[64,768]{1,0:T(8,128)S(1)}, u32[]{:S(2)}, u32[]{:S(2)}) collective-permute-start(f32[64,768]{1,0:T(8,128)S(1)} %get-tuple-element.37.refs_4_), channel_id=1, source_target_pairs={{0,1},{1,0},{2,3},{3,2},{4,5},{5,4},{6,7},{7,6},{8,9},{9,8},{10,11... | collective-permute-start | bytes 589832 | tf_op jit(solution)/shard_map/ppermute | solution.py:274
  8.5 1.7 %collective-permute-start.11 = (f32[64,768]{1,0:T(8,128)S(1)}, f32[64,768]{1,0:T(8,128)S(1)}, u32[]{:S(2)}, u32[]{:S(2)}) collective-permute-start(f32[64,768]{1,0:T(8,128)S(1)} %get-tuple-element.37.refs_4_), channel_id=1, source_target_pairs={{0,2},{1,3},{2,0},{3,1},{4,6},{5,7},{6,4},{7,5},{8,10},{9,11},{10,... | collective-permute-start | bytes 589832 | tf_op jit(solution)/shard_map/ppermute | solution.py:274
  10.2 1.2 %copy-done = f32[1024,256]{1,0:T(8,128)S(1)} copy-done((f32[1024,256]{1,0:T(8,128)S(1)}, f32[1024,256]{1,0:T(8,128)}, u32[]{:S(2)}) %copy-start) | copy-done | bytes 1048600
  11.4 0.7 %shard_map.37 = (f32[32,256]{1,0:T(8,128)S(1)}, f32[256,256]{1,0:T(8,128)S(1)}, s32[1,128]{1,0:T(1,128)S(1)}) custom-call(s32[1,256]{1,0:T(1,128)S(1)} %bitcast.3, f32[1024,256]{1,0:T(8,128)S(1)} %copy-done), custom_call_target="tpu_custom_call" | custom-call | flops 1 | bytes 1 | tf_op jit(solution)/shard_map/pallas_call | solution.py:254
  12.1 1.0 %collective-permute-start.12 = (f32[64,768]{1,0:T(8,128)S(1)}, f32[64,768]{1,0:T(8,128)S(1)}, u32[]{:S(2)}, u32[]{:S(2)}) collective-permute-start(f32[64,768]{1,0:T(8,128)S(1)} %get-tuple-element.37.refs_4_), channel_id=1, source_target_pairs={{0,3},{1,2},{2,1},{3,0},{4,7},{5,6},{6,5},{7,4},{8,11},{9,10},{10,... | collective-permute-start | bytes 589832 | tf_op jit(solution)/shard_map/ppermute | solution.py:274
  13.1 0.1 collective-permute-done.8.refs_3_
  13.4 1.2 %collective-permute-done.9 = f32[64,256]{1,0:T(8,128)S(1)} collective-permute-done((f32[64,256]{1,0:T(8,128)S(1)}, f32[64,256]{1,0:T(8,128)S(1)}, u32[]{:S(2)}, u32[]{:S(2)}) %collective-permute-start.9) | collective-permute-done | bytes 65568 | tf_op jit(solution)/shard_map/ppermute | solution.py:341
  14.6 14.2 %conditional.1 = (f32[32,256]{1,0:T(8,128)S(1)}, f32[256,256]{1,0:T(8,128)S(1)}) conditional(s32[]{:T(128)} %convert_element_type.3, () %tuple.14, (s32[]{:T(128)}, f32[256,256]{1,0:T(8,128)S(1)}, f32[64,256]{1,0:T(8,128)S(1)}, f32[192,256]{1,0:T(8,128)S(1)}, s32[1,256]{1,0:T(1,128)S(1)}) %tuple.20), branch_computations={%region_0.0_spmd, %region_1.2_spmd} | conditional | flops 352267 | bytes 7307592 | solution.py:250
  14.7 0.2 collective-permute-start
  14.9 1.5 %collective-permute-start.3 = (f32[192,256]{1,0:T(8,128)S(1)}, f32[192,256]{1,0:T(8,128)S(1)}, u32[]{:S(2)}, u32[]{:S(2)}) collective-permute-start(f32[192,256]{1,0:T(8,128)S(1)} %get-tuple-element.18.held_ref), channel_id=1, source_target_pairs={{0,16},{4,0},{8,12},{12,8},{16,20},{20,4},{24,28},{28,24},{1,17},{... | collective-permute-start | bytes 589832 | tf_op jit(solution)/shard_map/cond/branch_1_fun/ppermute | solution.py:311
  16.5 1.2 %collective-permute-start.1 = (f32[128,256]{1,0:T(8,128)S(1)}, f32[128,256]{1,0:T(8,128)S(1)}, u32[]{:S(2)}, u32[]{:S(2)}) collective-permute-start(f32[128,256]{1,0:T(8,128)S(1)} %pad_maximum_fusion.2), channel_id=1, source_target_pairs={{0,8},{4,12},{8,0},{12,4},{16,24},{20,28},{24,16},{28,20},{1,9},{5... | collective-permute-start | bytes 393224 | tf_op jit(solution)/shard_map/cond/branch_1_fun/ppermute | solution.py:320
  17.7 1.9 %collective-permute-done.3.moved_ref = f32[192,256]{1,0:T(8,128)S(1)} collective-permute-done((f32[192,256]{1,0:T(8,128)S(1)}, f32[192,256]{1,0:T(8,128)S(1)}, u32[]{:S(2)}, u32[]{:S(2)}) %collective-permute-start.3) | collective-permute-done | bytes 196640 | tf_op jit(solution)/shard_map/cond/branch_1_fun/ppermute | solution.py:311
  19.6 2.1 %collective-permute-done.1 = f32[128,256]{1,0:T(8,128)S(1)} collective-permute-done((f32[128,256]{1,0:T(8,128)S(1)}, f32[128,256]{1,0:T(8,128)S(1)}, u32[]{:S(2)}, u32[]{:S(2)}) %collective-permute-start.1) | collective-permute-done | bytes 131104 | tf_op jit(solution)/shard_map/cond/branch_1_fun/ppermute | solution.py:320
  21.8 2.4 %collective-permute-start.2 = (f32[160,256]{1,0:T(8,128)S(1)}, f32[160,256]{1,0:T(8,128)S(1)}, u32[]{:S(2)}, u32[]{:S(2)}) collective-permute-start(f32[160,256]{1,0:T(8,128)S(1)} %pad_maximum_fusion.1), channel_id=1, source_target_pairs={{0,16},{4,20},{8,24},{12,28},{16,0},{20,4},{24,8},{28,12},{1,17},{... | collective-permute-start | bytes 491528 | tf_op jit(solution)/shard_map/cond/branch_1_fun/ppermute | solution.py:320
  24.2 1.8 %branch_1_fun.7 = f32[192,256]{1,0:T(8,128)S(1)} custom-call(f32[192,256]{1,0:T(8,128)S(1)} %branch_1_fun.6.lower_ref), custom_call_target="tpu_custom_call" | custom-call | flops 1 | bytes 1 | tf_op jit(solution)/shard_map/cond/branch_1_fun/pallas_call | solution.py:254
  26.0 0.8 %collective-permute-start.5 = (f32[192,256]{1,0:T(8,128)S(1)}, f32[192,256]{1,0:T(8,128)S(1)}, u32[]{:S(2)}, u32[]{:S(2)}) collective-permute-start(f32[192,256]{1,0:T(8,128)S(1)} %branch_1_fun.7), channel_id=1, source_target_pairs={{0,4},{4,0},{8,12},{12,8},{16,20},{20,16},{24,28},{28,24},{1,5},{5... | collective-permute-start | bytes 589832 | tf_op jit(solution)/shard_map/cond/branch_1_fun/ppermute | solution.py:336
  26.8 0.7 %collective-permute-done.2 = f32[160,256]{1,0:T(8,128)S(1)} collective-permute-done((f32[160,256]{1,0:T(8,128)S(1)}, f32[160,256]{1,0:T(8,128)S(1)}, u32[]{:S(2)}, u32[]{:S(2)}) %collective-permute-start.2) | collective-permute-done | bytes 163872 | tf_op jit(solution)/shard_map/cond/branch_1_fun/ppermute | solution.py:320
  27.5 0.5 %branch_1_fun.8.pivot_rows_ref = f32[256,256]{1,0:T(8,128)S(1)} custom-call(s32[1,256]{1,0:T(1,128)S(1)} %get-tuple-element.19.pivot_ref, f32[256,256]{1,0:T(8,128)S(1)} %pad_maximum_fusion.gathered_ref), custom_call_target="tpu_custom_call" | custom-call | flops 1 | bytes 1 | tf_op jit(solution)/shard_map/cond/branch_1_fun/pallas_call | solution.py:254
  28.1 0.7 %branch_1_fun.9 = f32[256,256]{1,0:T(8,128)S(1)} custom-call(f32[192,256]{1,0:T(8,128)S(1)} %broadcast_select_fusion.inverse_ref, f32[256,256]{1,0:T(8,128)S(1)} %branch_1_fun.8.pivot_rows_ref), custom_call_target="tpu_custom_call" | custom-call | flops 1 | bytes 1 | tf_op jit(solution)/shard_map/cond/branch_1_fun/pallas_call | solution.py:254
  28.9 2.2 %shard_map.40 = f32[1024,256]{1,0:T(8,128)} custom-call(s32[1,128]{1,0:T(1,128)S(1)} %get-tuple-element.29.local_ref, f32[32,256]{1,0:T(8,128)S(1)} %get-tuple-element.35.lead_ref, f32[256,256]{1,0:T(8,128)S(1)} %get-tuple-element.36.x_ref, f32[1024,256]{1,0:T(8,128)S(1)} %copy-done.1, f32[64,256]{1,0:T(8,128)S(1)} %get-tuple-element.32.refs_0_, ...), custom_call_target="tpu_custom_call" | custom-call | flops 1 | bytes 1 | tf_op jit(solution)/shard_map/pallas_call | solution.py:254
  (34 shorter events, 0.4 us)
Async XLA Ops:
  0.0 0.9 %copy-start.2 = (f32[1024,64]{0,1:T(8,128)S(1)}, f32[1024,64]{0,1:T(8,128)}, u32[]{:S(2)}) copy-start(f32[1024,64]{0,1:T(8,128)} %param.6) | copy-start | bytes 786436
  1.0 11.1 %collective-permute-start.6 = (f32[64,256]{1,0:T(8,128)S(1)}, f32[64,256]{1,0:T(8,128)S(1)}, u32[]{:S(2)}, u32[]{:S(2)}) collective-permute-start(f32[64,256]{1,0:T(8,128)S(1)} %get-tuple-element.32.refs_0_), channel_id=1, source_target_pairs={{0,1},{1,0},{2,3},{3,2},{4,5},{5,4},{6,7},{7,6},{8,9},{9,8},{10,11... | collective-permute-start | bytes 196616 | tf_op jit(solution)/shard_map/ppermute | solution.py:274
  4.1 9.0 %collective-permute-start.7 = (f32[64,256]{1,0:T(8,128)S(1)}, f32[64,256]{1,0:T(8,128)S(1)}, u32[]{:S(2)}, u32[]{:S(2)}) collective-permute-start(f32[64,256]{1,0:T(8,128)S(1)} %get-tuple-element.32.refs_0_), channel_id=1, source_target_pairs={{0,3},{1,2},{2,1},{3,0},{4,7},{5,6},{6,5},{7,4},{8,11},{9,10},{10,... | collective-permute-start | bytes 196616 | tf_op jit(solution)/shard_map/ppermute | solution.py:274
  6.6 6.6 %collective-permute-start.8 = (f32[64,256]{1,0:T(8,128)S(1)}, f32[64,256]{1,0:T(8,128)S(1)}, u32[]{:S(2)}, u32[]{:S(2)}) collective-permute-start(f32[64,256]{1,0:T(8,128)S(1)} %get-tuple-element.32.refs_0_), channel_id=1, source_target_pairs={{0,2},{1,3},{2,0},{3,1},{4,6},{5,7},{6,4},{7,5},{8,10},{9,11},{10,... | collective-permute-start | bytes 196616 | tf_op jit(solution)/shard_map/ppermute | solution.py:274
  6.7 3.5 %copy-start.3 = (s32[256]{0:T(256)S(1)}, s32[256]{0:T(256)}, u32[]{:S(2)}) copy-start(s32[256]{0:T(256)} %param.7) | copy-start | bytes 3076
  6.7 22.1 %collective-permute-start.10 = (f32[64,768]{1,0:T(8,128)S(1)}, f32[64,768]{1,0:T(8,128)S(1)}, u32[]{:S(2)}, u32[]{:S(2)}) collective-permute-start(f32[64,768]{1,0:T(8,128)S(1)} %get-tuple-element.37.refs_4_), channel_id=1, source_target_pairs={{0,1},{1,0},{2,3},{3,2},{4,5},{5,4},{6,7},{7,6},{8,9},{9,8},{10,11... | collective-permute-start | bytes 589832 | tf_op jit(solution)/shard_map/ppermute | solution.py:274
  8.5 20.3 %collective-permute-start.11 = (f32[64,768]{1,0:T(8,128)S(1)}, f32[64,768]{1,0:T(8,128)S(1)}, u32[]{:S(2)}, u32[]{:S(2)}) collective-permute-start(f32[64,768]{1,0:T(8,128)S(1)} %get-tuple-element.37.refs_4_), channel_id=1, source_target_pairs={{0,2},{1,3},{2,0},{3,1},{4,6},{5,7},{6,4},{7,5},{8,10},{9,11},{10,... | collective-permute-start | bytes 589832 | tf_op jit(solution)/shard_map/ppermute | solution.py:274
  10.2 1.2 %copy-start = (f32[1024,256]{1,0:T(8,128)S(1)}, f32[1024,256]{1,0:T(8,128)}, u32[]{:S(2)}) copy-start(f32[1024,256]{1,0:T(8,128)} %slab_ref.3) | copy-start | bytes 3145732
  12.1 16.7 %collective-permute-start.12 = (f32[64,768]{1,0:T(8,128)S(1)}, f32[64,768]{1,0:T(8,128)S(1)}, u32[]{:S(2)}, u32[]{:S(2)}) collective-permute-start(f32[64,768]{1,0:T(8,128)S(1)} %get-tuple-element.37.refs_4_), channel_id=1, source_target_pairs={{0,3},{1,2},{2,1},{3,0},{4,7},{5,6},{6,5},{7,4},{8,11},{9,10},{10,... | collective-permute-start | bytes 589832 | tf_op jit(solution)/shard_map/ppermute | solution.py:274
  13.3 1.3 %collective-permute-start.9 = (f32[64,256]{1,0:T(8,128)S(1)}, f32[64,256]{1,0:T(8,128)S(1)}, u32[]{:S(2)}, u32[]{:S(2)}) collective-permute-start(f32[64,256]{1,0:T(8,128)S(1)} %pad_maximum_fusion.3), channel_id=1, source_target_pairs={{0,4},{4,0},{8,12},{12,8},{16,20},{20,16},{24,28},{28,24},{1,5},{5... | collective-permute-start | bytes 196616 | tf_op jit(solution)/shard_map/ppermute | solution.py:341
  14.6 14.2 %copy-start.1 = (f32[1024,256]{1,0:T(8,128)S(1)}, f32[1024,256]{1,0:T(8,128)}, u32[]{:S(2)}) copy-start(f32[1024,256]{1,0:T(8,128)} %slab_ref.3) | copy-start | bytes 3145732
  14.7 1.7 %collective-permute-start = (f32[128,256]{1,0:T(8,128)S(1)}, f32[128,256]{1,0:T(8,128)S(1)}, u32[]{:S(2)}, u32[]{:S(2)}) collective-permute-start(f32[128,256]{1,0:T(8,128)S(1)} %slice.28), channel_id=1, source_target_pairs={{0,4},{4,0},{8,12},{12,8},{16,20},{20,16},{24,28},{28,24},{1,5},{5... | collective-permute-start | bytes 393224 | tf_op jit(solution)/shard_map/cond/branch_1_fun/ppermute | solution.py:307
  14.9 4.7 %collective-permute-start.3 = (f32[192,256]{1,0:T(8,128)S(1)}, f32[192,256]{1,0:T(8,128)S(1)}, u32[]{:S(2)}, u32[]{:S(2)}) collective-permute-start(f32[192,256]{1,0:T(8,128)S(1)} %get-tuple-element.18.held_ref), channel_id=1, source_target_pairs={{0,16},{4,0},{8,12},{12,8},{16,20},{20,4},{24,28},{28,24},{1,17},{... | collective-permute-start | bytes 589832 | tf_op jit(solution)/shard_map/cond/branch_1_fun/ppermute | solution.py:311
  16.5 5.3 %collective-permute-start.1 = (f32[128,256]{1,0:T(8,128)S(1)}, f32[128,256]{1,0:T(8,128)S(1)}, u32[]{:S(2)}, u32[]{:S(2)}) collective-permute-start(f32[128,256]{1,0:T(8,128)S(1)} %pad_maximum_fusion.2), channel_id=1, source_target_pairs={{0,8},{4,12},{8,0},{12,4},{16,24},{20,28},{24,16},{28,20},{1,9},{5... | collective-permute-start | bytes 393224 | tf_op jit(solution)/shard_map/cond/branch_1_fun/ppermute | solution.py:320
  19.6 4.6 %collective-permute-start.4 = (f32[192,256]{1,0:T(8,128)S(1)}, f32[192,256]{1,0:T(8,128)S(1)}, u32[]{:S(2)}, u32[]{:S(2)}) collective-permute-start(f32[192,256]{1,0:T(8,128)S(1)} %branch_1_fun.5.held_ref), channel_id=1, source_target_pairs={{0,8},{4,0},{8,12},{12,4},{16,24},{20,16},{24,28},{28,20},{1,9},{5... | collective-permute-start | bytes 589832 | tf_op jit(solution)/shard_map/cond/branch_1_fun/ppermute | solution.py:311
  21.8 5.7 %collective-permute-start.2 = (f32[160,256]{1,0:T(8,128)S(1)}, f32[160,256]{1,0:T(8,128)S(1)}, u32[]{:S(2)}, u32[]{:S(2)}) collective-permute-start(f32[160,256]{1,0:T(8,128)S(1)} %pad_maximum_fusion.1), channel_id=1, source_target_pairs={{0,16},{4,20},{8,24},{12,28},{16,0},{20,4},{24,8},{28,12},{1,17},{... | collective-permute-start | bytes 491528 | tf_op jit(solution)/shard_map/cond/branch_1_fun/ppermute | solution.py:320
  26.0 2.1 %collective-permute-start.5 = (f32[192,256]{1,0:T(8,128)S(1)}, f32[192,256]{1,0:T(8,128)S(1)}, u32[]{:S(2)}, u32[]{:S(2)}) collective-permute-start(f32[192,256]{1,0:T(8,128)S(1)} %branch_1_fun.7), channel_id=1, source_target_pairs={{0,4},{4,0},{8,12},{12,8},{16,20},{20,16},{24,28},{28,24},{1,5},{5... | collective-permute-start | bytes 589832 | tf_op jit(solution)/shard_map/cond/branch_1_fun/ppermute | solution.py:336

commit v8 on v7

--- a/solution.py
+++ b/solution.py
@@ -270,8 +270,8 @@
     panel_t = panel.T
     pivot_row = pivots.reshape(1, width)
 
-    def spread(block, order):
-        return [block] + [lax.ppermute(block, "pcol", [(c, c ^ d) for c in range(m)]) for d in order]
+    def exchange(block, d):
+        return lax.ppermute(block, "pcol", [(c, c ^ d) for c in range(m)])
 
     top, rest = call(
         cut_kernel,
@@ -280,7 +280,8 @@
         in_specs=[pl.BlockSpec(memory_space=pl.ANY)],
         scratch=[pltpu.SemaphoreType.DMA((rows // width,))],
     )
-    tops, rests = spread(top, top_order(m)[1:]), spread(rest, range(1, m))
+    tops = [top] + [exchange(top, d) for d in top_order(m)[1:]]
+    rests = [rest] + [exchange(rest, d) for d in range(1, m)]
 
     gathered, leading, local_rows = call(
         pack_kernel,
@@ -303,9 +304,6 @@
         return blocks[0], blocks[1]
 
     def levels(lower, gathered, leading):
-        kept, sent = split(leading)
-        moved = lax.ppermute(sent, "prow", [(r, r ^ 1) for r in range(n)])
-        leading = jnp.where(me & 1 != 0, moved, kept)
         span, other = n // 2, 2
         while span > 1:
             moved = lax.ppermute(lower, "prow", [(r, tree_partner(r, span)) for r in range(n)])
@@ -338,8 +336,11 @@
         return leading, call(solve_kernel, jax.ShapeDtypeStruct((width, cols), F32), (inverse, pivot_rows))
 
     gathered, lower = lax.optimization_barrier((gathered, lower))
-    moved = lax.ppermute(jnp.concatenate([gathered, gathered], axis=0), "prow", [(r, r ^ 1) for r in range(n)])
-    gathered = jnp.concatenate([gathered, moved[:CAP]], axis=0)
+    twins = [(r, r ^ 1) for r in range(n)]
+    moved = lax.ppermute(gathered, "prow", twins)
+    gathered = jnp.concatenate([gathered, moved], axis=0)
+    kept, sent = split(leading)
+    leading = jnp.where(me & 1 != 0, lax.ppermute(sent, "prow", twins), kept)
     leading, upper_rows = unit(me < n, levels, lower, gathered, leading)
     return call(
         functools.partial(update_kernel, m),

time: 31.2 us -> 32.4 us (1.038)
  starting transfers between devices: 16.3 us -> 17.3 us
  waiting for transfers between devices: 6.09 us -> 6.48 us
    ppermute x2, starting transfers between devices: 1.54 us -> 2.64 us  [levels(): lax.ppermute(lower, 'prow', [(r, tree_partner(r, span)) for r in range(n)])]
    ppermute x2, waiting for transfers between devices: 2.8 us -> 3.31 us  [levels(): moved = lax.ppermute(message, 'prow', [(r, r ^ other) for r in range(n)])]
    ppermute x2, starting transfers between devices: 3.59 us -> 3.17 us  [levels(): moved = lax.ppermute(message, 'prow', [(r, r ^ other) for r in range(n)])]
  transfers between devices with their start and end apart: 13 -> 13, of which waited for: 5 -> 7; matrix products, arithmetic and copies ran while one was open for 1% -> 0% of each run, Pallas kernels for 12% -> 12%
where the time goes in v8:
time: 32.4 us; the launch traced here: 32.3 us
  starting transfers between devices  17.3 us (53%)
  waiting for transfers between devices  6.48 us (20%)
  Pallas kernels  6.01 us (19%)
  local copies, waits for them, and re-layouts  2.21 us (7%)
    ppermute x6, starting transfers between devices, exchange(): return lax.ppermute(block, 'pcol', [(c, c ^ d) for c in range(m)])  10.1 us
    pallas_call x9, Pallas kernels, call(): pl.pallas_call(kernel, out_shape=outs, in_specs=in_specs or [VMEM] * len(...  6.01 us
    ppermute x2, waiting for transfers between devices, levels(): moved = lax.ppermute(message, 'prow', [(r, r ^ other) for r in range(n)])  3.31 us
    ppermute x2, starting transfers between devices, levels(): moved = lax.ppermute(message, 'prow', [(r, r ^ other) for r in range(n)])  3.17 us
    ppermute x2, starting transfers between devices, levels(): lax.ppermute(lower, 'prow', [(r, tree_partner(r, span)) for r in range(n)])  2.64 us
    unnamed x8, local copies, waits for them, and re-layouts  2.18 us
    ppermute x2, waiting for transfers between devices, levels(): lax.ppermute(lower, 'prow', [(r, tree_partner(r, span)) for r in range(n)])  1.99 us
    ppermute x1, starting transfers between devices, levels(): moved = lax.ppermute(inverse, 'prow', [(r, r ^ 1) for r in range(n)])  0.76 us
  transfers between devices with their start and end apart: 13, of which 7 were waited for; matrix products, arithmetic and copies ran while one was open for 0% of the time, Pallas kernels for 12%

profile of v8, /device:TPU:0, one launch (start us, length us, event | category | flops | bytes accessed | tf_op | source)
XLA Modules:
  0.0 32.3 jit_solution(2814489077786510589)
XLA Ops:
  0.0 0.9 %copy-done.2 = f32[1024,64]{0,1:T(8,128)S(1)} copy-done((f32[1024,64]{0,1:T(8,128)S(1)}, f32[1024,64]{0,1:T(8,128)}, u32[]{:S(2)}) %copy-start.2) | copy-done | bytes 262168
  1.0 3.1 %collective-permute-start.6 = (f32[64,256]{1,0:T(8,128)S(1)}, f32[64,256]{1,0:T(8,128)S(1)}, u32[]{:S(2)}, u32[]{:S(2)}) collective-permute-start(f32[64,256]{1,0:T(8,128)S(1)} %get-tuple-element.43.refs_0_), channel_id=1, source_target_pairs={{0,1},{1,0},{2,3},{3,2},{4,5},{5,4},{6,7},{7,6},{8,9},{9,8},{10,11... | collective-permute-start | bytes 196616 | tf_op jit(solution)/shard_map/ppermute | solution.py:274
  4.1 2.5 %collective-permute-start.7 = (f32[64,256]{1,0:T(8,128)S(1)}, f32[64,256]{1,0:T(8,128)S(1)}, u32[]{:S(2)}, u32[]{:S(2)}) collective-permute-start(f32[64,256]{1,0:T(8,128)S(1)} %get-tuple-element.43.refs_0_), channel_id=1, source_target_pairs={{0,3},{1,2},{2,1},{3,0},{4,7},{5,6},{6,5},{7,4},{8,11},{9,10},{10,... | collective-permute-start | bytes 196616 | tf_op jit(solution)/shard_map/ppermute | solution.py:274
  6.7 1.8 %collective-permute-start.10 = (f32[64,768]{1,0:T(8,128)S(1)}, f32[64,768]{1,0:T(8,128)S(1)}, u32[]{:S(2)}, u32[]{:S(2)}) collective-permute-start(f32[64,768]{1,0:T(8,128)S(1)} %get-tuple-element.48.refs_4_), channel_id=1, source_target_pairs={{0,1},{1,0},{2,3},{3,2},{4,5},{5,4},{6,7},{7,6},{8,9},{9,8},{10,11... | collective-permute-start | bytes 589832 | tf_op jit(solution)/shard_map/ppermute | solution.py:274
  8.5 1.7 %collective-permute-start.11 = (f32[64,768]{1,0:T(8,128)S(1)}, f32[64,768]{1,0:T(8,128)S(1)}, u32[]{:S(2)}, u32[]{:S(2)}) collective-permute-start(f32[64,768]{1,0:T(8,128)S(1)} %get-tuple-element.48.refs_4_), channel_id=1, source_target_pairs={{0,2},{1,3},{2,0},{3,1},{4,6},{5,7},{6,4},{7,5},{8,10},{9,11},{10,... | collective-permute-start | bytes 589832 | tf_op jit(solution)/shard_map/ppermute | solution.py:274
  10.2 0.9 %collective-permute-start.12 = (f32[64,768]{1,0:T(8,128)S(1)}, f32[64,768]{1,0:T(8,128)S(1)}, u32[]{:S(2)}, u32[]{:S(2)}) collective-permute-start(f32[64,768]{1,0:T(8,128)S(1)} %get-tuple-element.48.refs_4_), channel_id=1, source_target_pairs={{0,3},{1,2},{2,1},{3,0},{4,7},{5,6},{6,5},{7,4},{8,11},{9,10},{10,... | collective-permute-start | bytes 589832 | tf_op jit(solution)/shard_map/ppermute | solution.py:274
  11.1 1.2 %copy-done = f32[1024,256]{1,0:T(8,128)S(1)} copy-done((f32[1024,256]{1,0:T(8,128)S(1)}, f32[1024,256]{1,0:T(8,128)}, u32[]{:S(2)}) %copy-start) | copy-done | bytes 1048600
  12.3 0.7 %shard_map.37 = (f32[32,256]{1,0:T(8,128)S(1)}, f32[256,256]{1,0:T(8,128)S(1)}, s32[1,128]{1,0:T(1,128)S(1)}) custom-call(s32[1,256]{1,0:T(1,128)S(1)} %bitcast.3, f32[1024,256]{1,0:T(8,128)S(1)} %copy-done), custom_call_target="tpu_custom_call" | custom-call | flops 1 | bytes 1 | tf_op jit(solution)/shard_map/pallas_call | solution.py:254
  13.4 0.6 %collective-permute-start.5 = (f32[128,256]{1,0:T(8,128)S(1)}, f32[128,256]{1,0:T(8,128)S(1)}, u32[]{:S(2)}, u32[]{:S(2)}) collective-permute-start(f32[128,256]{1,0:T(8,128)S(1)} %slice.37), channel_id=1, source_target_pairs={{0,4},{4,0},{8,12},{12,8},{16,20},{20,16},{24,28},{28,24},{1,5},{5... | collective-permute-start | bytes 393224 | tf_op jit(solution)/shard_map/ppermute | solution.py:343
  13.9 0.6 %collective-permute-done.9 = f32[32,256]{1,0:T(8,128)S(1)} collective-permute-done((f32[32,256]{1,0:T(8,128)S(1)}, f32[32,256]{1,0:T(8,128)S(1)}, u32[]{:S(2)}, u32[]{:S(2)}) %collective-permute-start.9) | collective-permute-done | bytes 32800 | tf_op jit(solution)/shard_map/ppermute | solution.py:340
  14.9 15.2 %conditional.1 = (f32[32,256]{1,0:T(8,128)S(1)}, f32[256,256]{1,0:T(8,128)S(1)}) conditional(s32[]{:T(128)} %convert_element_type.3, () %tuple.17, (s32[]{:T(128)}, f32[256,256]{1,0:T(8,128)S(1)}, f32[128,256]{1,0:T(8,128)S(1)}, f32[64,256]{1,0:T(8,128)S(1)}, f32[192,256]{1,0:T(8,128)S(1)}, /*index=5*/s32[1,256]{1,0:T(1,128)S(1)}) %tuple.23), branch_computations={%region_0.1_spmd, %region_1.2_spmd} | conditional | flops 352267 | bytes 6521120 | solution.py:250
  15.0 1.6 %collective-permute-start = (f32[128,256]{1,0:T(8,128)S(1)}, f32[128,256]{1,0:T(8,128)S(1)}, u32[]{:S(2)}, u32[]{:S(2)}) collective-permute-start(f32[128,256]{1,0:T(8,128)S(1)} %pad_maximum_fusion.2), channel_id=1, source_target_pairs={{0,8},{4,12},{8,0},{12,4},{16,24},{20,28},{24,16},{28,20},{1,9},{5... | collective-permute-start | bytes 393224 | tf_op jit(solution)/shard_map/cond/branch_1_fun/ppermute | solution.py:318
  16.5 1.5 %collective-permute-start.2 = (f32[192,256]{1,0:T(8,128)S(1)}, f32[192,256]{1,0:T(8,128)S(1)}, u32[]{:S(2)}, u32[]{:S(2)}) collective-permute-start(f32[192,256]{1,0:T(8,128)S(1)} %get-tuple-element.29.held_ref), channel_id=1, source_target_pairs={{0,16},{4,0},{8,12},{12,8},{16,20},{20,4},{24,28},{28,24},{1,17},{... | collective-permute-start | bytes 589832 | tf_op jit(solution)/shard_map/cond/branch_1_fun/ppermute | solution.py:309
  18.1 2.7 %collective-permute-done = f32[128,256]{1,0:T(8,128)S(1)} collective-permute-done((f32[128,256]{1,0:T(8,128)S(1)}, f32[128,256]{1,0:T(8,128)S(1)}, u32[]{:S(2)}, u32[]{:S(2)}) %collective-permute-start) | collective-permute-done | bytes 131104 | tf_op jit(solution)/shard_map/cond/branch_1_fun/ppermute | solution.py:318
  20.8 0.4 %collective-permute-done.2.moved_ref = f32[192,256]{1,0:T(8,128)S(1)} collective-permute-done((f32[192,256]{1,0:T(8,128)S(1)}, f32[192,256]{1,0:T(8,128)S(1)}, u32[]{:S(2)}, u32[]{:S(2)}) %collective-permute-start.2) | collective-permute-done | bytes 196640 | tf_op jit(solution)/shard_map/cond/branch_1_fun/ppermute | solution.py:309
  21.3 1.1 %collective-permute-start.3 = (f32[192,256]{1,0:T(8,128)S(1)}, f32[192,256]{1,0:T(8,128)S(1)}, u32[]{:S(2)}, u32[]{:S(2)}) collective-permute-start(f32[192,256]{1,0:T(8,128)S(1)} %branch_1_fun.5.held_ref), channel_id=1, source_target_pairs={{0,8},{4,0},{8,12},{12,4},{16,24},{20,16},{24,28},{28,20},{1,9},{5... | collective-permute-start | bytes 589832 | tf_op jit(solution)/shard_map/cond/branch_1_fun/ppermute | solution.py:309
  22.4 1.6 %collective-permute-start.1 = (f32[160,256]{1,0:T(8,128)S(1)}, f32[160,256]{1,0:T(8,128)S(1)}, u32[]{:S(2)}, u32[]{:S(2)}) collective-permute-start(f32[160,256]{1,0:T(8,128)S(1)} %pad_maximum_fusion.1), channel_id=1, source_target_pairs={{0,16},{4,20},{8,24},{12,28},{16,0},{20,4},{24,8},{28,12},{1,17},{... | collective-permute-start | bytes 491528 | tf_op jit(solution)/shard_map/cond/branch_1_fun/ppermute | solution.py:318
  24.0 1.6 %collective-permute-done.3.moved_ref = f32[192,256]{1,0:T(8,128)S(1)} collective-permute-done((f32[192,256]{1,0:T(8,128)S(1)}, f32[192,256]{1,0:T(8,128)S(1)}, u32[]{:S(2)}, u32[]{:S(2)}) %collective-permute-start.3) | collective-permute-done | bytes 196640 | tf_op jit(solution)/shard_map/cond/branch_1_fun/ppermute | solution.py:309
  25.6 1.8 %branch_1_fun.7 = f32[192,256]{1,0:T(8,128)S(1)} custom-call(f32[192,256]{1,0:T(8,128)S(1)} %branch_1_fun.6.lower_ref), custom_call_target="tpu_custom_call" | custom-call | flops 1 | bytes 1 | tf_op jit(solution)/shard_map/cond/branch_1_fun/pallas_call | solution.py:254
  27.4 0.8 %collective-permute-start.4 = (f32[192,256]{1,0:T(8,128)S(1)}, f32[192,256]{1,0:T(8,128)S(1)}, u32[]{:S(2)}, u32[]{:S(2)}) collective-permute-start(f32[192,256]{1,0:T(8,128)S(1)} %branch_1_fun.7), channel_id=1, source_target_pairs={{0,4},{4,0},{8,12},{12,8},{16,20},{20,16},{24,28},{28,24},{1,5},{5... | collective-permute-start | bytes 589832 | tf_op jit(solution)/shard_map/cond/branch_1_fun/ppermute | solution.py:334
  28.2 0.6 %collective-permute-done.1 = f32[160,256]{1,0:T(8,128)S(1)} collective-permute-done((f32[160,256]{1,0:T(8,128)S(1)}, f32[160,256]{1,0:T(8,128)S(1)}, u32[]{:S(2)}, u32[]{:S(2)}) %collective-permute-start.1) | collective-permute-done | bytes 163872 | tf_op jit(solution)/shard_map/cond/branch_1_fun/ppermute | solution.py:318
  28.8 0.5 %branch_1_fun.8.pivot_rows_ref = f32[256,256]{1,0:T(8,128)S(1)} custom-call(s32[1,256]{1,0:T(1,128)S(1)} %get-tuple-element.30.pivot_ref, f32[256,256]{1,0:T(8,128)S(1)} %pad_maximum_fusion.gathered_ref), custom_call_target="tpu_custom_call" | custom-call | flops 1 | bytes 1 | tf_op jit(solution)/shard_map/cond/branch_1_fun/pallas_call | solution.py:254
  29.4 0.7 %branch_1_fun.9 = f32[256,256]{1,0:T(8,128)S(1)} custom-call(f32[192,256]{1,0:T(8,128)S(1)} %broadcast_select_fusion.inverse_ref, f32[256,256]{1,0:T(8,128)S(1)} %branch_1_fun.8.pivot_rows_ref), custom_call_target="tpu_custom_call" | custom-call | flops 1 | bytes 1 | tf_op jit(solution)/shard_map/cond/branch_1_fun/pallas_call | solution.py:254
  30.1 2.1 %shard_map.40 = f32[1024,256]{1,0:T(8,128)} custom-call(s32[1,128]{1,0:T(1,128)S(1)} %get-tuple-element.40.local_ref, f32[32,256]{1,0:T(8,128)S(1)} %get-tuple-element.46.lead_ref, f32[256,256]{1,0:T(8,128)S(1)} %get-tuple-element.47.x_ref, f32[1024,256]{1,0:T(8,128)S(1)} %copy-done.1, f32[64,256]{1,0:T(8,128)S(1)} %get-tuple-element.43.refs_0_, ...), custom_call_target="tpu_custom_call" | custom-call | flops 1 | bytes 1 | tf_op jit(solution)/shard_map/pallas_call | solution.py:254
  (32 shorter events, 1.1 us)
Async XLA Ops:
  0.0 0.9 %copy-start.2 = (f32[1024,64]{0,1:T(8,128)S(1)}, f32[1024,64]{0,1:T(8,128)}, u32[]{:S(2)}) copy-start(f32[1024,64]{0,1:T(8,128)} %param.6) | copy-start | bytes 786436
  1.0 9.2 %collective-permute-start.6 = (f32[64,256]{1,0:T(8,128)S(1)}, f32[64,256]{1,0:T(8,128)S(1)}, u32[]{:S(2)}, u32[]{:S(2)}) collective-permute-start(f32[64,256]{1,0:T(8,128)S(1)} %get-tuple-element.43.refs_0_), channel_id=1, source_target_pairs={{0,1},{1,0},{2,3},{3,2},{4,5},{5,4},{6,7},{7,6},{8,9},{9,8},{10,11... | collective-permute-start | bytes 196616 | tf_op jit(solution)/shard_map/ppermute | solution.py:274
  4.1 8.9 %collective-permute-start.7 = (f32[64,256]{1,0:T(8,128)S(1)}, f32[64,256]{1,0:T(8,128)S(1)}, u32[]{:S(2)}, u32[]{:S(2)}) collective-permute-start(f32[64,256]{1,0:T(8,128)S(1)} %get-tuple-element.43.refs_0_), channel_id=1, source_target_pairs={{0,3},{1,2},{2,1},{3,0},{4,7},{5,6},{6,5},{7,4},{8,11},{9,10},{10,... | collective-permute-start | bytes 196616 | tf_op jit(solution)/shard_map/ppermute | solution.py:274
  6.6 6.6 %collective-permute-start.8 = (f32[64,256]{1,0:T(8,128)S(1)}, f32[64,256]{1,0:T(8,128)S(1)}, u32[]{:S(2)}, u32[]{:S(2)}) collective-permute-start(f32[64,256]{1,0:T(8,128)S(1)} %get-tuple-element.43.refs_0_), channel_id=1, source_target_pairs={{0,2},{1,3},{2,0},{3,1},{4,6},{5,7},{6,4},{7,5},{8,10},{9,11},{10,... | collective-permute-start | bytes 196616 | tf_op jit(solution)/shard_map/ppermute | solution.py:274
  6.7 4.4 %copy-start.3 = (s32[256]{0:T(256)S(1)}, s32[256]{0:T(256)}, u32[]{:S(2)}) copy-start(s32[256]{0:T(256)} %param.7) | copy-start | bytes 3076
  6.7 23.4 %collective-permute-start.10 = (f32[64,768]{1,0:T(8,128)S(1)}, f32[64,768]{1,0:T(8,128)S(1)}, u32[]{:S(2)}, u32[]{:S(2)}) collective-permute-start(f32[64,768]{1,0:T(8,128)S(1)} %get-tuple-element.48.refs_4_), channel_id=1, source_target_pairs={{0,1},{1,0},{2,3},{3,2},{4,5},{5,4},{6,7},{7,6},{8,9},{9,8},{10,11... | collective-permute-start | bytes 589832 | tf_op jit(solution)/shard_map/ppermute | solution.py:274
  8.5 21.6 %collective-permute-start.11 = (f32[64,768]{1,0:T(8,128)S(1)}, f32[64,768]{1,0:T(8,128)S(1)}, u32[]{:S(2)}, u32[]{:S(2)}) collective-permute-start(f32[64,768]{1,0:T(8,128)S(1)} %get-tuple-element.48.refs_4_), channel_id=1, source_target_pairs={{0,2},{1,3},{2,0},{3,1},{4,6},{5,7},{6,4},{7,5},{8,10},{9,11},{10,... | collective-permute-start | bytes 589832 | tf_op jit(solution)/shard_map/ppermute | solution.py:274
  10.2 19.9 %collective-permute-start.12 = (f32[64,768]{1,0:T(8,128)S(1)}, f32[64,768]{1,0:T(8,128)S(1)}, u32[]{:S(2)}, u32[]{:S(2)}) collective-permute-start(f32[64,768]{1,0:T(8,128)S(1)} %get-tuple-element.48.refs_4_), channel_id=1, source_target_pairs={{0,3},{1,2},{2,1},{3,0},{4,7},{5,6},{6,5},{7,4},{8,11},{9,10},{10,... | collective-permute-start | bytes 589832 | tf_op jit(solution)/shard_map/ppermute | solution.py:274
  11.1 1.2 %copy-start = (f32[1024,256]{1,0:T(8,128)S(1)}, f32[1024,256]{1,0:T(8,128)}, u32[]{:S(2)}) copy-start(f32[1024,256]{1,0:T(8,128)} %slab_ref.3) | copy-start | bytes 3145732
  13.3 1.3 %collective-permute-start.9 = (f32[32,256]{1,0:T(8,128)S(1)}, f32[32,256]{1,0:T(8,128)S(1)}, u32[]{:S(2)}, u32[]{:S(2)}) collective-permute-start(f32[32,256]{1,0:T(8,128)S(1)} %get-tuple-element.44), channel_id=1, source_target_pairs={{0,4},{4,0},{8,12},{12,8},{16,20},{20,16},{24,28},{28,24},{1,5},{5... | collective-permute-start | bytes 98312 | tf_op jit(solution)/shard_map/ppermute | solution.py:340
  13.4 1.5 %collective-permute-start.5 = (f32[128,256]{1,0:T(8,128)S(1)}, f32[128,256]{1,0:T(8,128)S(1)}, u32[]{:S(2)}, u32[]{:S(2)}) collective-permute-start(f32[128,256]{1,0:T(8,128)S(1)} %slice.37), channel_id=1, source_target_pairs={{0,4},{4,0},{8,12},{12,8},{16,20},{20,16},{24,28},{28,24},{1,5},{5... | collective-permute-start | bytes 393224 | tf_op jit(solution)/shard_map/ppermute | solution.py:343
  14.9 15.2 %copy-start.1 = (f32[1024,256]{1,0:T(8,128)S(1)}, f32[1024,256]{1,0:T(8,128)}, u32[]{:S(2)}) copy-start(f32[1024,256]{1,0:T(8,128)} %slab_ref.3) | copy-start | bytes 3145732
  15.0 5.8 %collective-permute-start = (f32[128,256]{1,0:T(8,128)S(1)}, f32[128,256]{1,0:T(8,128)S(1)}, u32[]{:S(2)}, u32[]{:S(2)}) collective-permute-start(f32[128,256]{1,0:T(8,128)S(1)} %pad_maximum_fusion.2), channel_id=1, source_target_pairs={{0,8},{4,12},{8,0},{12,4},{16,24},{20,28},{24,16},{28,20},{1,9},{5... | collective-permute-start | bytes 393224 | tf_op jit(solution)/shard_map/cond/branch_1_fun/ppermute | solution.py:318
  16.5 4.7 %collective-permute-start.2 = (f32[192,256]{1,0:T(8,128)S(1)}, f32[192,256]{1,0:T(8,128)S(1)}, u32[]{:S(2)}, u32[]{:S(2)}) collective-permute-start(f32[192,256]{1,0:T(8,128)S(1)} %get-tuple-element.29.held_ref), channel_id=1, source_target_pairs={{0,16},{4,0},{8,12},{12,8},{16,20},{20,4},{24,28},{28,24},{1,17},{... | collective-permute-start | bytes 589832 | tf_op jit(solution)/shard_map/cond/branch_1_fun/ppermute | solution.py:309
  21.3 4.3 %collective-permute-start.3 = (f32[192,256]{1,0:T(8,128)S(1)}, f32[192,256]{1,0:T(8,128)S(1)}, u32[]{:S(2)}, u32[]{:S(2)}) collective-permute-start(f32[192,256]{1,0:T(8,128)S(1)} %branch_1_fun.5.held_ref), channel_id=1, source_target_pairs={{0,8},{4,0},{8,12},{12,4},{16,24},{20,16},{24,28},{28,20},{1,9},{5... | collective-permute-start | bytes 589832 | tf_op jit(solution)/shard_map/cond/branch_1_fun/ppermute | solution.py:309
  22.4 6.3 %collective-permute-start.1 = (f32[160,256]{1,0:T(8,128)S(1)}, f32[160,256]{1,0:T(8,128)S(1)}, u32[]{:S(2)}, u32[]{:S(2)}) collective-permute-start(f32[160,256]{1,0:T(8,128)S(1)} %pad_maximum_fusion.1), channel_id=1, source_target_pairs={{0,16},{4,20},{8,24},{12,28},{16,0},{20,4},{24,8},{28,12},{1,17},{... | collective-permute-start | bytes 491528 | tf_op jit(solution)/shard_map/cond/branch_1_fun/ppermute | solution.py:318
  27.4 1.9 %collective-permute-start.4 = (f32[192,256]{1,0:T(8,128)S(1)}, f32[192,256]{1,0:T(8,128)S(1)}, u32[]{:S(2)}, u32[]{:S(2)}) collective-permute-start(f32[192,256]{1,0:T(8,128)S(1)} %branch_1_fun.7), channel_id=1, source_target_pairs={{0,4},{4,0},{8,12},{12,8},{16,20},{20,16},{24,28},{28,24},{1,5},{5... | collective-permute-start | bytes 589832 | tf_op jit(solution)/shard_map/cond/branch_1_fun/ppermute | solution.py:334

commit v9 on v8

--- a/solution.py
+++ b/solution.py
@@ -304,18 +304,19 @@
         return blocks[0], blocks[1]
 
     def levels(lower, gathered, leading):
-        span, other = n // 2, 2
+        span, other, held = n // 2, 2, lower
         while span > 1:
             moved = lax.ppermute(lower, "prow", [(r, tree_partner(r, span)) for r in range(n)])
             lower = call(
                 functools.partial(pick_kernel, span),
                 jax.ShapeDtypeStruct(lower.shape, F32),
-                (moved, lower),
+                (moved, held),
             )
             kept, sent = split(leading)
             count = gathered.shape[0]
             message = jnp.concatenate([gathered, sent], axis=0)
             moved = lax.ppermute(message, "prow", [(r, r ^ other) for r in range(n)])
+            moved, held = lax.optimization_barrier((moved, lower))
             gathered = jnp.concatenate([gathered, moved[:count]], axis=0)
             leading = jnp.where(me & other != 0, moved[count:], kept)
             span, other = span // 2, other * 2

time: 32.4 us -> 31 us (0.957)
  starting transfers between devices: 17.3 us -> 16.1 us
    ppermute x2, starting transfers between devices: 3.17 us -> 1.69 us  [levels(): moved = lax.ppermute(message, 'prow', [(r, r ^ other) for r in range(n)])]
    ppermute x1, starting transfers between devices: 0.76 us -> 2.13 us  [levels(): moved = lax.ppermute(inverse, 'prow', [(r, r ^ 1) for r in range(n)])]
    ppermute x2, waiting for transfers between devices: 3.31 us -> 2.16 us  [levels(): moved = lax.ppermute(message, 'prow', [(r, r ^ other) for r in range(n)])]
    ppermute x2, starting transfers between devices: 2.64 us -> 1.54 us  [levels(): lax.ppermute(lower, 'prow', [(r, tree_partner(r, span)) for r in range(n)])]
    ppermute x2, waiting for transfers between devices: 1.99 us -> 2.74 us  [levels(): lax.ppermute(lower, 'prow', [(r, tree_partner(r, span)) for r in range(n)])]
where the time goes in v9:
time: 31 us; the launch traced here: 30.8 us
  starting transfers between devices  16.1 us (52%)
  waiting for transfers between devices  6.26 us (20%)
  Pallas kernels  6.01 us (19%)
  local copies, waits for them, and re-layouts  2.21 us (7%)
    ppermute x6, starting transfers between devices, exchange(): return lax.ppermute(block, 'pcol', [(c, c ^ d) for c in range(m)])  10.1 us
    pallas_call x9, Pallas kernels, call(): pl.pallas_call(kernel, out_shape=outs, in_specs=in_specs or [VMEM] * len(...  6.01 us
    ppermute x2, waiting for transfers between devices, levels(): lax.ppermute(lower, 'prow', [(r, tree_partner(r, span)) for r in range(n)])  2.74 us
    unnamed x8, local copies, waits for them, and re-layouts  2.18 us
    ppermute x2, waiting for transfers between devices, levels(): moved = lax.ppermute(message, 'prow', [(r, r ^ other) for r in range(n)])  2.16 us
    ppermute x1, starting transfers between devices, levels(): moved = lax.ppermute(inverse, 'prow', [(r, r ^ 1) for r in range(n)])  2.13 us
    ppermute x2, starting transfers between devices, levels(): moved = lax.ppermute(message, 'prow', [(r, r ^ other) for r in range(n)])  1.69 us
    ppermute x2, starting transfers between devices, levels(): lax.ppermute(lower, 'prow', [(r, tree_partner(r, span)) for r in range(n)])  1.54 us
  transfers between devices with their start and end apart: 13, of which 7 were waited for; matrix products, arithmetic and copies ran while one was open for 0% of the time, Pallas kernels for 12%

profile of v9, /device:TPU:0, one launch (start us, length us, event | category | flops | bytes accessed | tf_op | source)
XLA Modules:
  0.0 30.8 jit_solution(8796102174864619417)
XLA Ops:
  0.0 0.9 %copy-done.2 = f32[1024,64]{0,1:T(8,128)S(1)} copy-done((f32[1024,64]{0,1:T(8,128)S(1)}, f32[1024,64]{0,1:T(8,128)}, u32[]{:S(2)}) %copy-start.2) | copy-done | bytes 262168
  1.0 3.1 %collective-permute-start.6 = (f32[64,256]{1,0:T(8,128)S(1)}, f32[64,256]{1,0:T(8,128)S(1)}, u32[]{:S(2)}, u32[]{:S(2)}) collective-permute-start(f32[64,256]{1,0:T(8,128)S(1)} %get-tuple-element.46.refs_0_), channel_id=1, source_target_pairs={{0,1},{1,0},{2,3},{3,2},{4,5},{5,4},{6,7},{7,6},{8,9},{9,8},{10,11... | collective-permute-start | bytes 196616 | tf_op jit(solution)/shard_map/ppermute | solution.py:274
  4.1 2.5 %collective-permute-start.7 = (f32[64,256]{1,0:T(8,128)S(1)}, f32[64,256]{1,0:T(8,128)S(1)}, u32[]{:S(2)}, u32[]{:S(2)}) collective-permute-start(f32[64,256]{1,0:T(8,128)S(1)} %get-tuple-element.46.refs_0_), channel_id=1, source_target_pairs={{0,3},{1,2},{2,1},{3,0},{4,7},{5,6},{6,5},{7,4},{8,11},{9,10},{10,... | collective-permute-start | bytes 196616 | tf_op jit(solution)/shard_map/ppermute | solution.py:274
  6.7 1.8 %collective-permute-start.10 = (f32[64,768]{1,0:T(8,128)S(1)}, f32[64,768]{1,0:T(8,128)S(1)}, u32[]{:S(2)}, u32[]{:S(2)}) collective-permute-start(f32[64,768]{1,0:T(8,128)S(1)} %get-tuple-element.51.refs_4_), channel_id=1, source_target_pairs={{0,1},{1,0},{2,3},{3,2},{4,5},{5,4},{6,7},{7,6},{8,9},{9,8},{10,11... | collective-permute-start | bytes 589832 | tf_op jit(solution)/shard_map/ppermute | solution.py:274
  8.5 1.7 %collective-permute-start.11 = (f32[64,768]{1,0:T(8,128)S(1)}, f32[64,768]{1,0:T(8,128)S(1)}, u32[]{:S(2)}, u32[]{:S(2)}) collective-permute-start(f32[64,768]{1,0:T(8,128)S(1)} %get-tuple-element.51.refs_4_), channel_id=1, source_target_pairs={{0,2},{1,3},{2,0},{3,1},{4,6},{5,7},{6,4},{7,5},{8,10},{9,11},{10,... | collective-permute-start | bytes 589832 | tf_op jit(solution)/shard_map/ppermute | solution.py:274
  10.2 0.9 %collective-permute-start.12 = (f32[64,768]{1,0:T(8,128)S(1)}, f32[64,768]{1,0:T(8,128)S(1)}, u32[]{:S(2)}, u32[]{:S(2)}) collective-permute-start(f32[64,768]{1,0:T(8,128)S(1)} %get-tuple-element.51.refs_4_), channel_id=1, source_target_pairs={{0,3},{1,2},{2,1},{3,0},{4,7},{5,6},{6,5},{7,4},{8,11},{9,10},{10,... | collective-permute-start | bytes 589832 | tf_op jit(solution)/shard_map/ppermute | solution.py:274
  11.1 1.2 %copy-done = f32[1024,256]{1,0:T(8,128)S(1)} copy-done((f32[1024,256]{1,0:T(8,128)S(1)}, f32[1024,256]{1,0:T(8,128)}, u32[]{:S(2)}) %copy-start) | copy-done | bytes 1048600
  12.3 0.7 %shard_map.37 = (f32[32,256]{1,0:T(8,128)S(1)}, f32[256,256]{1,0:T(8,128)S(1)}, s32[1,128]{1,0:T(1,128)S(1)}) custom-call(s32[1,256]{1,0:T(1,128)S(1)} %bitcast.3, f32[1024,256]{1,0:T(8,128)S(1)} %copy-done), custom_call_target="tpu_custom_call" | custom-call | flops 1 | bytes 1 | tf_op jit(solution)/shard_map/pallas_call | solution.py:254
  13.1 0.2 collective-permute-done.8.refs_3_
  13.4 0.6 %collective-permute-start.5 = (f32[128,256]{1,0:T(8,128)S(1)}, f32[128,256]{1,0:T(8,128)S(1)}, u32[]{:S(2)}, u32[]{:S(2)}) collective-permute-start(f32[128,256]{1,0:T(8,128)S(1)} %slice.37), channel_id=1, source_target_pairs={{0,4},{4,0},{8,12},{12,8},{16,20},{20,16},{24,28},{28,24},{1,5},{5... | collective-permute-start | bytes 393224 | tf_op jit(solution)/shard_map/ppermute | solution.py:344
  13.9 0.6 %collective-permute-done.9 = f32[32,256]{1,0:T(8,128)S(1)} collective-permute-done((f32[32,256]{1,0:T(8,128)S(1)}, f32[32,256]{1,0:T(8,128)S(1)}, u32[]{:S(2)}, u32[]{:S(2)}) %collective-permute-start.9) | collective-permute-done | bytes 32800 | tf_op jit(solution)/shard_map/ppermute | solution.py:341
  14.6 0.4 %collective-permute-done.5 = f32[128,256]{1,0:T(8,128)S(1)} collective-permute-done((f32[128,256]{1,0:T(8,128)S(1)}, f32[128,256]{1,0:T(8,128)S(1)}, u32[]{:S(2)}, u32[]{:S(2)}) %collective-permute-start.5) | collective-permute-done | bytes 131104 | tf_op jit(solution)/shard_map/ppermute | solution.py:344
  14.9 13.7 %conditional.1 = (f32[32,256]{1,0:T(8,128)S(1)}, f32[256,256]{1,0:T(8,128)S(1)}) conditional(s32[]{:T(128)} %convert_element_type.3, () %tuple.19, (s32[]{:T(128)}, f32[256,256]{1,0:T(8,128)S(1)}, f32[128,256]{1,0:T(8,128)S(1)}, f32[64,256]{1,0:T(8,128)S(1)}, f32[192,256]{1,0:T(8,128)S(1)}, /*index=5*/s32[1,256]{1,0:T(1,128)S(1)}) %tuple.25), branch_computations={%region_0.1_spmd, %region_1.2_spmd} | conditional | flops 352267 | bytes 6521120 | solution.py:250
  14.9 1.5 %collective-permute-start.1 = (f32[192,256]{1,0:T(8,128)S(1)}, f32[192,256]{1,0:T(8,128)S(1)}, u32[]{:S(2)}, u32[]{:S(2)}) collective-permute-start(f32[192,256]{1,0:T(8,128)S(1)} %get-tuple-element.29.held_ref), channel_id=1, source_target_pairs={{0,16},{4,0},{8,12},{12,8},{16,20},{20,4},{24,28},{28,24},{1,17},{... | collective-permute-start | bytes 589832 | tf_op jit(solution)/shard_map/cond/branch_1_fun/ppermute | solution.py:309
  16.5 0.4 %collective-permute-start = (f32[128,256]{1,0:T(8,128)S(1)}, f32[128,256]{1,0:T(8,128)S(1)}, u32[]{:S(2)}, u32[]{:S(2)}) collective-permute-start(f32[128,256]{1,0:T(8,128)S(1)} %pad_maximum_fusion.2), channel_id=1, source_target_pairs={{0,8},{4,12},{8,0},{12,4},{16,24},{20,28},{24,16},{28,20},{1,9},{5... | collective-permute-start | bytes 393224 | tf_op jit(solution)/shard_map/cond/branch_1_fun/ppermute | solution.py:318
  16.9 2.7 %collective-permute-done.1.moved_ref = f32[192,256]{1,0:T(8,128)S(1)} collective-permute-done((f32[192,256]{1,0:T(8,128)S(1)}, f32[192,256]{1,0:T(8,128)S(1)}, u32[]{:S(2)}, u32[]{:S(2)}) %collective-permute-start.1) | collective-permute-done | bytes 196640 | tf_op jit(solution)/shard_map/cond/branch_1_fun/ppermute | solution.py:309
  19.7 1.9 %collective-permute-done = f32[128,256]{1,0:T(8,128)S(1)} collective-permute-done((f32[128,256]{1,0:T(8,128)S(1)}, f32[128,256]{1,0:T(8,128)S(1)}, u32[]{:S(2)}, u32[]{:S(2)}) %collective-permute-start) | collective-permute-done | bytes 131104 | tf_op jit(solution)/shard_map/cond/branch_1_fun/ppermute | solution.py:318
  21.6 1.3 %collective-permute-start.2 = (f32[160,256]{1,0:T(8,128)S(1)}, f32[160,256]{1,0:T(8,128)S(1)}, u32[]{:S(2)}, u32[]{:S(2)}) collective-permute-start(f32[160,256]{1,0:T(8,128)S(1)} %pad_maximum_fusion.1), channel_id=1, source_target_pairs={{0,16},{4,20},{8,24},{12,28},{16,0},{20,4},{24,8},{28,12},{1,17},{... | collective-permute-start | bytes 491528 | tf_op jit(solution)/shard_map/cond/branch_1_fun/ppermute | solution.py:318
  22.9 1.8 %branch_1_fun.7 = f32[192,256]{1,0:T(8,128)S(1)} custom-call(f32[192,256]{1,0:T(8,128)S(1)} %branch_1_fun.6.lower_ref), custom_call_target="tpu_custom_call" | custom-call | flops 1 | bytes 1 | tf_op jit(solution)/shard_map/cond/branch_1_fun/pallas_call | solution.py:254
  24.7 2.1 %collective-permute-start.4 = (f32[192,256]{1,0:T(8,128)S(1)}, f32[192,256]{1,0:T(8,128)S(1)}, u32[]{:S(2)}, u32[]{:S(2)}) collective-permute-start(f32[192,256]{1,0:T(8,128)S(1)} %branch_1_fun.7), channel_id=1, source_target_pairs={{0,4},{4,0},{8,12},{12,8},{16,20},{20,16},{24,28},{28,24},{1,5},{5... | collective-permute-start | bytes 589832 | tf_op jit(solution)/shard_map/cond/branch_1_fun/ppermute | solution.py:335
  26.8 0.3 %collective-permute-done.2 = f32[160,256]{1,0:T(8,128)S(1)} collective-permute-done((f32[160,256]{1,0:T(8,128)S(1)}, f32[160,256]{1,0:T(8,128)S(1)}, u32[]{:S(2)}, u32[]{:S(2)}) %collective-permute-start.2) | collective-permute-done | bytes 163872 | tf_op jit(solution)/shard_map/cond/branch_1_fun/ppermute | solution.py:318
  27.2 0.5 %branch_1_fun.8.pivot_rows_ref = f32[256,256]{1,0:T(8,128)S(1)} custom-call(s32[1,256]{1,0:T(1,128)S(1)} %get-tuple-element.33.pivot_ref, f32[256,256]{1,0:T(8,128)S(1)} %pad_maximum_fusion.gathered_ref), custom_call_target="tpu_custom_call" | custom-call | flops 1 | bytes 1 | tf_op jit(solution)/shard_map/cond/branch_1_fun/pallas_call | solution.py:254
  28.0 0.7 %branch_1_fun.9 = f32[256,256]{1,0:T(8,128)S(1)} custom-call(f32[192,256]{1,0:T(8,128)S(1)} %broadcast_select_fusion.inverse_ref, f32[256,256]{1,0:T(8,128)S(1)} %branch_1_fun.8.pivot_rows_ref), custom_call_target="tpu_custom_call" | custom-call | flops 1 | bytes 1 | tf_op jit(solution)/shard_map/cond/branch_1_fun/pallas_call | solution.py:254
  28.7 2.1 %shard_map.40 = f32[1024,256]{1,0:T(8,128)} custom-call(s32[1,128]{1,0:T(1,128)S(1)} %get-tuple-element.43.local_ref, f32[32,256]{1,0:T(8,128)S(1)} %get-tuple-element.49.lead_ref, f32[256,256]{1,0:T(8,128)S(1)} %get-tuple-element.50.x_ref, f32[1024,256]{1,0:T(8,128)S(1)} %copy-done.1, f32[64,256]{1,0:T(8,128)S(1)} %get-tuple-element.46.refs_0_, ...), custom_call_target="tpu_custom_call" | custom-call | flops 1 | bytes 1 | tf_op jit(solution)/shard_map/pallas_call | solution.py:254
  (32 shorter events, 0.7 us)
Async XLA Ops:
  0.0 0.9 %copy-start.2 = (f32[1024,64]{0,1:T(8,128)S(1)}, f32[1024,64]{0,1:T(8,128)}, u32[]{:S(2)}) copy-start(f32[1024,64]{0,1:T(8,128)} %param.6) | copy-start | bytes 786436
  1.0 9.2 %collective-permute-start.6 = (f32[64,256]{1,0:T(8,128)S(1)}, f32[64,256]{1,0:T(8,128)S(1)}, u32[]{:S(2)}, u32[]{:S(2)}) collective-permute-start(f32[64,256]{1,0:T(8,128)S(1)} %get-tuple-element.46.refs_0_), channel_id=1, source_target_pairs={{0,1},{1,0},{2,3},{3,2},{4,5},{5,4},{6,7},{7,6},{8,9},{9,8},{10,11... | collective-permute-start | bytes 196616 | tf_op jit(solution)/shard_map/ppermute | solution.py:274
  4.1 8.9 %collective-permute-start.7 = (f32[64,256]{1,0:T(8,128)S(1)}, f32[64,256]{1,0:T(8,128)S(1)}, u32[]{:S(2)}, u32[]{:S(2)}) collective-permute-start(f32[64,256]{1,0:T(8,128)S(1)} %get-tuple-element.46.refs_0_), channel_id=1, source_target_pairs={{0,3},{1,2},{2,1},{3,0},{4,7},{5,6},{6,5},{7,4},{8,11},{9,10},{10,... | collective-permute-start | bytes 196616 | tf_op jit(solution)/shard_map/ppermute | solution.py:274
  6.6 6.6 %collective-permute-start.8 = (f32[64,256]{1,0:T(8,128)S(1)}, f32[64,256]{1,0:T(8,128)S(1)}, u32[]{:S(2)}, u32[]{:S(2)}) collective-permute-start(f32[64,256]{1,0:T(8,128)S(1)} %get-tuple-element.46.refs_0_), channel_id=1, source_target_pairs={{0,2},{1,3},{2,0},{3,1},{4,6},{5,7},{6,4},{7,5},{8,10},{9,11},{10,... | collective-permute-start | bytes 196616 | tf_op jit(solution)/shard_map/ppermute | solution.py:274
  6.7 4.4 %copy-start.3 = (s32[256]{0:T(256)S(1)}, s32[256]{0:T(256)}, u32[]{:S(2)}) copy-start(s32[256]{0:T(256)} %param.7) | copy-start | bytes 3076
  6.7 21.9 %collective-permute-start.10 = (f32[64,768]{1,0:T(8,128)S(1)}, f32[64,768]{1,0:T(8,128)S(1)}, u32[]{:S(2)}, u32[]{:S(2)}) collective-permute-start(f32[64,768]{1,0:T(8,128)S(1)} %get-tuple-element.51.refs_4_), channel_id=1, source_target_pairs={{0,1},{1,0},{2,3},{3,2},{4,5},{5,4},{6,7},{7,6},{8,9},{9,8},{10,11... | collective-permute-start | bytes 589832 | tf_op jit(solution)/shard_map/ppermute | solution.py:274
  8.5 20.1 %collective-permute-start.11 = (f32[64,768]{1,0:T(8,128)S(1)}, f32[64,768]{1,0:T(8,128)S(1)}, u32[]{:S(2)}, u32[]{:S(2)}) collective-permute-start(f32[64,768]{1,0:T(8,128)S(1)} %get-tuple-element.51.refs_4_), channel_id=1, source_target_pairs={{0,2},{1,3},{2,0},{3,1},{4,6},{5,7},{6,4},{7,5},{8,10},{9,11},{10,... | collective-permute-start | bytes 589832 | tf_op jit(solution)/shard_map/ppermute | solution.py:274
  10.2 18.5 %collective-permute-start.12 = (f32[64,768]{1,0:T(8,128)S(1)}, f32[64,768]{1,0:T(8,128)S(1)}, u32[]{:S(2)}, u32[]{:S(2)}) collective-permute-start(f32[64,768]{1,0:T(8,128)S(1)} %get-tuple-element.51.refs_4_), channel_id=1, source_target_pairs={{0,3},{1,2},{2,1},{3,0},{4,7},{5,6},{6,5},{7,4},{8,11},{9,10},{10,... | collective-permute-start | bytes 589832 | tf_op jit(solution)/shard_map/ppermute | solution.py:274
  11.1 1.2 %copy-start = (f32[1024,256]{1,0:T(8,128)S(1)}, f32[1024,256]{1,0:T(8,128)}, u32[]{:S(2)}) copy-start(f32[1024,256]{1,0:T(8,128)} %slab_ref.3) | copy-start | bytes 3145732
  13.3 1.3 %collective-permute-start.9 = (f32[32,256]{1,0:T(8,128)S(1)}, f32[32,256]{1,0:T(8,128)S(1)}, u32[]{:S(2)}, u32[]{:S(2)}) collective-permute-start(f32[32,256]{1,0:T(8,128)S(1)} %get-tuple-element.47), channel_id=1, source_target_pairs={{0,4},{4,0},{8,12},{12,8},{16,20},{20,16},{24,28},{28,24},{1,5},{5... | collective-permute-start | bytes 98312 | tf_op jit(solution)/shard_map/ppermute | solution.py:341
  13.4 1.5 %collective-permute-start.5 = (f32[128,256]{1,0:T(8,128)S(1)}, f32[128,256]{1,0:T(8,128)S(1)}, u32[]{:S(2)}, u32[]{:S(2)}) collective-permute-start(f32[128,256]{1,0:T(8,128)S(1)} %slice.37), channel_id=1, source_target_pairs={{0,4},{4,0},{8,12},{12,8},{16,20},{20,16},{24,28},{28,24},{1,5},{5... | collective-permute-start | bytes 393224 | tf_op jit(solution)/shard_map/ppermute | solution.py:344
  14.9 13.8 %copy-start.1 = (f32[1024,256]{1,0:T(8,128)S(1)}, f32[1024,256]{1,0:T(8,128)}, u32[]{:S(2)}) copy-start(f32[1024,256]{1,0:T(8,128)} %slab_ref.3) | copy-start | bytes 3145732
  14.9 4.7 %collective-permute-start.1 = (f32[192,256]{1,0:T(8,128)S(1)}, f32[192,256]{1,0:T(8,128)S(1)}, u32[]{:S(2)}, u32[]{:S(2)}) collective-permute-start(f32[192,256]{1,0:T(8,128)S(1)} %get-tuple-element.29.held_ref), channel_id=1, source_target_pairs={{0,16},{4,0},{8,12},{12,8},{16,20},{20,4},{24,28},{28,24},{1,17},{... | collective-permute-start | bytes 589832 | tf_op jit(solution)/shard_map/cond/branch_1_fun/ppermute | solution.py:309
  16.5 5.0 %collective-permute-start = (f32[128,256]{1,0:T(8,128)S(1)}, f32[128,256]{1,0:T(8,128)S(1)}, u32[]{:S(2)}, u32[]{:S(2)}) collective-permute-start(f32[128,256]{1,0:T(8,128)S(1)} %pad_maximum_fusion.2), channel_id=1, source_target_pairs={{0,8},{4,12},{8,0},{12,4},{16,24},{20,28},{24,16},{28,20},{1,9},{5... | collective-permute-start | bytes 393224 | tf_op jit(solution)/shard_map/cond/branch_1_fun/ppermute | solution.py:318
  19.6 3.2 %collective-permute-start.3 = (f32[192,256]{1,0:T(8,128)S(1)}, f32[192,256]{1,0:T(8,128)S(1)}, u32[]{:S(2)}, u32[]{:S(2)}) collective-permute-start(f32[192,256]{1,0:T(8,128)S(1)} %branch_1_fun.5.held_ref), channel_id=1, source_target_pairs={{0,8},{4,0},{8,12},{12,4},{16,24},{20,16},{24,28},{28,20},{1,9},{5... | collective-permute-start | bytes 589832 | tf_op jit(solution)/shard_map/cond/branch_1_fun/ppermute | solution.py:309
  21.6 5.6 %collective-permute-start.2 = (f32[160,256]{1,0:T(8,128)S(1)}, f32[160,256]{1,0:T(8,128)S(1)}, u32[]{:S(2)}, u32[]{:S(2)}) collective-permute-start(f32[160,256]{1,0:T(8,128)S(1)} %pad_maximum_fusion.1), channel_id=1, source_target_pairs={{0,16},{4,20},{8,24},{12,28},{16,0},{20,4},{24,8},{28,12},{1,17},{... | collective-permute-start | bytes 491528 | tf_op jit(solution)/shard_map/cond/branch_1_fun/ppermute | solution.py:318
  24.7 3.2 %collective-permute-start.4 = (f32[192,256]{1,0:T(8,128)S(1)}, f32[192,256]{1,0:T(8,128)S(1)}, u32[]{:S(2)}, u32[]{:S(2)}) collective-permute-start(f32[192,256]{1,0:T(8,128)S(1)} %branch_1_fun.7), channel_id=1, source_target_pairs={{0,4},{4,0},{8,12},{12,8},{16,20},{20,16},{24,28},{28,24},{1,5},{5... | collective-permute-start | bytes 589832 | tf_op jit(solution)/shard_map/cond/branch_1_fun/ppermute | solution.py:335

commit v10 on v9

--- a/solution.py
+++ b/solution.py
@@ -197,12 +197,17 @@
     x_ref[half:, :] = dot_full(inverse_ref[:half, half:], pivot_rows_ref[half:, :] - dot_full(quarter, first))
 
 
-def product(piece, upper):
-    high, low = split2(piece)
-    upper_high, upper_low = split2(upper)
-    left = jnp.concatenate([high, high, low], axis=0)
-    right = jnp.concatenate([upper_high, upper_low, upper_high], axis=0)
-    return lax.dot_general(left, right, (((0,), (0,)), ((), ())), preferred_element_type=F32)
+def product(pieces, upper):
+    high, low = zip(*(split2(piece) for piece in pieces))
+    high, low = jnp.concatenate(high, axis=0), jnp.concatenate(low, axis=0)
+    upper_high, upper_low = upper
+    width = upper_high.shape[1]
+
+    def dot(a, b):
+        return lax.dot_general(a, b, (((0,), (0,)), ((), ())), preferred_element_type=F32)
+
+    both = dot(high, jnp.concatenate([upper_high, upper_low], axis=1))
+    return both[:, :width] + (both[:, width:] + dot(low, upper_high))
 
 
 def piece_rows(x_ref, m, d):
@@ -213,21 +218,22 @@
 
 def update_kernel(m, local_ref, lead_ref, x_ref, slab_ref, *refs):
     *pieces, out_ref, result, swaps, sems = refs
-    tops, rests = dict(zip(top_order(m), pieces[:m])), pieces[m:]
+    tops, rests = pieces[:m], pieces[m:]
     rows = slab_ref.shape[0]
     width = x_ref.shape[0]
     blocks = rows // width
     fetch = pltpu.make_async_copy(local_ref, swaps, sems.at[blocks])
     fetch.start()
     result[:rows, :] = slab_ref[...]
-    uppers = [piece_rows(x_ref, m, d) for d in range(m)]
+    top_upper = split2(jnp.concatenate([piece_rows(x_ref, m, d) for d in top_order(m)], axis=0))
+    upper = split2(jnp.concatenate([piece_rows(x_ref, m, d) for d in range(m)], axis=0))
     copies = []
     for c in range(blocks):
         part = pl.ds(c * width, width)
         if c:
-            total = sum(product(rests[d][:, (c - 1) * width : c * width], uppers[d]) for d in range(m))
+            total = product([rest[:, (c - 1) * width : c * width] for rest in rests], upper)
         else:
-            total = sum(product(tops[d][...], uppers[d]) for d in range(m))
+            total = product([top[...] for top in tops], top_upper)
             fetch.wait()
             for s in range(CAP):
                 result[pl.ds(swaps[0, s], 1), :] = lead_ref[pl.ds(s, 1), :]

time: 31 us -> 30.9 us (level)
  no operation moved by 1% of the time
where the time goes in v10:
time: 30.9 us; the launch traced here: 30.7 us
  starting transfers between devices  16.1 us (52%)
  waiting for transfers between devices  6.26 us (20%)
  Pallas kernels  5.85 us (19%)
  local copies, waits for them, and re-layouts  2.21 us (7%)
    ppermute x6, starting transfers between devices, exchange(): return lax.ppermute(block, 'pcol', [(c, c ^ d) for c in range(m)])  10.1 us
    pallas_call x9, Pallas kernels, call(): pl.pallas_call(kernel, out_shape=outs, in_specs=in_specs or [VMEM] * len(...  5.85 us
    ppermute x2, waiting for transfers between devices, levels(): lax.ppermute(lower, 'prow', [(r, tree_partner(r, span)) for r in range(n)])  2.74 us
    unnamed x8, local copies, waits for them, and re-layouts  2.18 us
    ppermute x2, waiting for transfers between devices, levels(): moved = lax.ppermute(message, 'prow', [(r, r ^ other) for r in range(n)])  2.16 us
    ppermute x1, starting transfers between devices, levels(): moved = lax.ppermute(inverse, 'prow', [(r, r ^ 1) for r in range(n)])  2.13 us
    ppermute x2, starting transfers between devices, levels(): moved = lax.ppermute(message, 'prow', [(r, r ^ other) for r in range(n)])  1.69 us
    ppermute x2, starting transfers between devices, levels(): lax.ppermute(lower, 'prow', [(r, tree_partner(r, span)) for r in range(n)])  1.54 us
  transfers between devices with their start and end apart: 13, of which 7 were waited for; matrix products, arithmetic and copies ran while one was open for 0% of the time, Pallas kernels for 12%

profile of v10, /device:TPU:0, one launch (start us, length us, event | category | flops | bytes accessed | tf_op | source)
XLA Modules:
  0.0 30.7 jit_solution(13578980228851107816)
XLA Ops:
  0.0 0.9 %copy-done.2 = f32[1024,64]{0,1:T(8,128)S(1)} copy-done((f32[1024,64]{0,1:T(8,128)S(1)}, f32[1024,64]{0,1:T(8,128)}, u32[]{:S(2)}) %copy-start.2) | copy-done | bytes 262168
  1.0 3.1 %collective-permute-start.6 = (f32[64,256]{1,0:T(8,128)S(1)}, f32[64,256]{1,0:T(8,128)S(1)}, u32[]{:S(2)}, u32[]{:S(2)}) collective-permute-start(f32[64,256]{1,0:T(8,128)S(1)} %get-tuple-element.46.refs_0_), channel_id=1, source_target_pairs={{0,1},{1,0},{2,3},{3,2},{4,5},{5,4},{6,7},{7,6},{8,9},{9,8},{10,11... | collective-permute-start | bytes 196616 | tf_op jit(solution)/shard_map/ppermute | solution.py:280
  4.1 2.5 %collective-permute-start.7 = (f32[64,256]{1,0:T(8,128)S(1)}, f32[64,256]{1,0:T(8,128)S(1)}, u32[]{:S(2)}, u32[]{:S(2)}) collective-permute-start(f32[64,256]{1,0:T(8,128)S(1)} %get-tuple-element.46.refs_0_), channel_id=1, source_target_pairs={{0,3},{1,2},{2,1},{3,0},{4,7},{5,6},{6,5},{7,4},{8,11},{9,10},{10,... | collective-permute-start | bytes 196616 | tf_op jit(solution)/shard_map/ppermute | solution.py:280
  6.7 1.8 %collective-permute-start.10 = (f32[64,768]{1,0:T(8,128)S(1)}, f32[64,768]{1,0:T(8,128)S(1)}, u32[]{:S(2)}, u32[]{:S(2)}) collective-permute-start(f32[64,768]{1,0:T(8,128)S(1)} %get-tuple-element.51.refs_4_), channel_id=1, source_target_pairs={{0,1},{1,0},{2,3},{3,2},{4,5},{5,4},{6,7},{7,6},{8,9},{9,8},{10,11... | collective-permute-start | bytes 589832 | tf_op jit(solution)/shard_map/ppermute | solution.py:280
  8.5 1.7 %collective-permute-start.11 = (f32[64,768]{1,0:T(8,128)S(1)}, f32[64,768]{1,0:T(8,128)S(1)}, u32[]{:S(2)}, u32[]{:S(2)}) collective-permute-start(f32[64,768]{1,0:T(8,128)S(1)} %get-tuple-element.51.refs_4_), channel_id=1, source_target_pairs={{0,2},{1,3},{2,0},{3,1},{4,6},{5,7},{6,4},{7,5},{8,10},{9,11},{10,... | collective-permute-start | bytes 589832 | tf_op jit(solution)/shard_map/ppermute | solution.py:280
  10.2 0.9 %collective-permute-start.12 = (f32[64,768]{1,0:T(8,128)S(1)}, f32[64,768]{1,0:T(8,128)S(1)}, u32[]{:S(2)}, u32[]{:S(2)}) collective-permute-start(f32[64,768]{1,0:T(8,128)S(1)} %get-tuple-element.51.refs_4_), channel_id=1, source_target_pairs={{0,3},{1,2},{2,1},{3,0},{4,7},{5,6},{6,5},{7,4},{8,11},{9,10},{10,... | collective-permute-start | bytes 589832 | tf_op jit(solution)/shard_map/ppermute | solution.py:280
  11.1 1.2 %copy-done = f32[1024,256]{1,0:T(8,128)S(1)} copy-done((f32[1024,256]{1,0:T(8,128)S(1)}, f32[1024,256]{1,0:T(8,128)}, u32[]{:S(2)}) %copy-start) | copy-done | bytes 1048600
  12.3 0.7 %shard_map.37 = (f32[32,256]{1,0:T(8,128)S(1)}, f32[256,256]{1,0:T(8,128)S(1)}, s32[1,128]{1,0:T(1,128)S(1)}) custom-call(s32[1,256]{1,0:T(1,128)S(1)} %bitcast.3, f32[1024,256]{1,0:T(8,128)S(1)} %copy-done), custom_call_target="tpu_custom_call" | custom-call | flops 1 | bytes 1 | tf_op jit(solution)/shard_map/pallas_call | solution.py:260
  13.1 0.2 collective-permute-done.8.refs_3_
  13.4 0.6 %collective-permute-start.5 = (f32[128,256]{1,0:T(8,128)S(1)}, f32[128,256]{1,0:T(8,128)S(1)}, u32[]{:S(2)}, u32[]{:S(2)}) collective-permute-start(f32[128,256]{1,0:T(8,128)S(1)} %slice.37), channel_id=1, source_target_pairs={{0,4},{4,0},{8,12},{12,8},{16,20},{20,16},{24,28},{28,24},{1,5},{5... | collective-permute-start | bytes 393224 | tf_op jit(solution)/shard_map/ppermute | solution.py:350
  13.9 0.6 %collective-permute-done.9 = f32[32,256]{1,0:T(8,128)S(1)} collective-permute-done((f32[32,256]{1,0:T(8,128)S(1)}, f32[32,256]{1,0:T(8,128)S(1)}, u32[]{:S(2)}, u32[]{:S(2)}) %collective-permute-start.9) | collective-permute-done | bytes 32800 | tf_op jit(solution)/shard_map/ppermute | solution.py:347
  14.6 0.4 %collective-permute-done.5 = f32[128,256]{1,0:T(8,128)S(1)} collective-permute-done((f32[128,256]{1,0:T(8,128)S(1)}, f32[128,256]{1,0:T(8,128)S(1)}, u32[]{:S(2)}, u32[]{:S(2)}) %collective-permute-start.5) | collective-permute-done | bytes 131104 | tf_op jit(solution)/shard_map/ppermute | solution.py:350
  14.9 13.7 %conditional.1 = (f32[32,256]{1,0:T(8,128)S(1)}, f32[256,256]{1,0:T(8,128)S(1)}) conditional(s32[]{:T(128)} %convert_element_type.3, () %tuple.19, (s32[]{:T(128)}, f32[256,256]{1,0:T(8,128)S(1)}, f32[128,256]{1,0:T(8,128)S(1)}, f32[64,256]{1,0:T(8,128)S(1)}, f32[192,256]{1,0:T(8,128)S(1)}, /*index=5*/s32[1,256]{1,0:T(1,128)S(1)}) %tuple.25), branch_computations={%region_0.1_spmd, %region_1.2_spmd} | conditional | flops 352267 | bytes 6521120 | solution.py:256
  14.9 1.5 %collective-permute-start.1 = (f32[192,256]{1,0:T(8,128)S(1)}, f32[192,256]{1,0:T(8,128)S(1)}, u32[]{:S(2)}, u32[]{:S(2)}) collective-permute-start(f32[192,256]{1,0:T(8,128)S(1)} %get-tuple-element.29.held_ref), channel_id=1, source_target_pairs={{0,16},{4,0},{8,12},{12,8},{16,20},{20,4},{24,28},{28,24},{1,17},{... | collective-permute-start | bytes 589832 | tf_op jit(solution)/shard_map/cond/branch_1_fun/ppermute | solution.py:315
  16.5 0.4 %collective-permute-start = (f32[128,256]{1,0:T(8,128)S(1)}, f32[128,256]{1,0:T(8,128)S(1)}, u32[]{:S(2)}, u32[]{:S(2)}) collective-permute-start(f32[128,256]{1,0:T(8,128)S(1)} %pad_maximum_fusion.2), channel_id=1, source_target_pairs={{0,8},{4,12},{8,0},{12,4},{16,24},{20,28},{24,16},{28,20},{1,9},{5... | collective-permute-start | bytes 393224 | tf_op jit(solution)/shard_map/cond/branch_1_fun/ppermute | solution.py:324
  16.9 2.7 %collective-permute-done.1.moved_ref = f32[192,256]{1,0:T(8,128)S(1)} collective-permute-done((f32[192,256]{1,0:T(8,128)S(1)}, f32[192,256]{1,0:T(8,128)S(1)}, u32[]{:S(2)}, u32[]{:S(2)}) %collective-permute-start.1) | collective-permute-done | bytes 196640 | tf_op jit(solution)/shard_map/cond/branch_1_fun/ppermute | solution.py:315
  19.7 1.9 %collective-permute-done = f32[128,256]{1,0:T(8,128)S(1)} collective-permute-done((f32[128,256]{1,0:T(8,128)S(1)}, f32[128,256]{1,0:T(8,128)S(1)}, u32[]{:S(2)}, u32[]{:S(2)}) %collective-permute-start) | collective-permute-done | bytes 131104 | tf_op jit(solution)/shard_map/cond/branch_1_fun/ppermute | solution.py:324
  21.6 1.3 %collective-permute-start.2 = (f32[160,256]{1,0:T(8,128)S(1)}, f32[160,256]{1,0:T(8,128)S(1)}, u32[]{:S(2)}, u32[]{:S(2)}) collective-permute-start(f32[160,256]{1,0:T(8,128)S(1)} %pad_maximum_fusion.1), channel_id=1, source_target_pairs={{0,16},{4,20},{8,24},{12,28},{16,0},{20,4},{24,8},{28,12},{1,17},{... | collective-permute-start | bytes 491528 | tf_op jit(solution)/shard_map/cond/branch_1_fun/ppermute | solution.py:324
  22.9 1.8 %branch_1_fun.7 = f32[192,256]{1,0:T(8,128)S(1)} custom-call(f32[192,256]{1,0:T(8,128)S(1)} %branch_1_fun.6.lower_ref), custom_call_target="tpu_custom_call" | custom-call | flops 1 | bytes 1 | tf_op jit(solution)/shard_map/cond/branch_1_fun/pallas_call | solution.py:260
  24.7 2.1 %collective-permute-start.4 = (f32[192,256]{1,0:T(8,128)S(1)}, f32[192,256]{1,0:T(8,128)S(1)}, u32[]{:S(2)}, u32[]{:S(2)}) collective-permute-start(f32[192,256]{1,0:T(8,128)S(1)} %branch_1_fun.7), channel_id=1, source_target_pairs={{0,4},{4,0},{8,12},{12,8},{16,20},{20,16},{24,28},{28,24},{1,5},{5... | collective-permute-start | bytes 589832 | tf_op jit(solution)/shard_map/cond/branch_1_fun/ppermute | solution.py:341
  26.8 0.3 %collective-permute-done.2 = f32[160,256]{1,0:T(8,128)S(1)} collective-permute-done((f32[160,256]{1,0:T(8,128)S(1)}, f32[160,256]{1,0:T(8,128)S(1)}, u32[]{:S(2)}, u32[]{:S(2)}) %collective-permute-start.2) | collective-permute-done | bytes 163872 | tf_op jit(solution)/shard_map/cond/branch_1_fun/ppermute | solution.py:324
  27.2 0.5 %branch_1_fun.8.pivot_rows_ref = f32[256,256]{1,0:T(8,128)S(1)} custom-call(s32[1,256]{1,0:T(1,128)S(1)} %get-tuple-element.33.pivot_ref, f32[256,256]{1,0:T(8,128)S(1)} %pad_maximum_fusion.gathered_ref), custom_call_target="tpu_custom_call" | custom-call | flops 1 | bytes 1 | tf_op jit(solution)/shard_map/cond/branch_1_fun/pallas_call | solution.py:260
  28.0 0.7 %branch_1_fun.9 = f32[256,256]{1,0:T(8,128)S(1)} custom-call(f32[192,256]{1,0:T(8,128)S(1)} %broadcast_select_fusion.inverse_ref, f32[256,256]{1,0:T(8,128)S(1)} %branch_1_fun.8.pivot_rows_ref), custom_call_target="tpu_custom_call" | custom-call | flops 1 | bytes 1 | tf_op jit(solution)/shard_map/cond/branch_1_fun/pallas_call | solution.py:260
  28.7 2.0 %shard_map.40 = f32[1024,256]{1,0:T(8,128)} custom-call(s32[1,128]{1,0:T(1,128)S(1)} %get-tuple-element.43.local_ref, f32[32,256]{1,0:T(8,128)S(1)} %get-tuple-element.49.lead_ref, f32[256,256]{1,0:T(8,128)S(1)} %get-tuple-element.50.x_ref, f32[1024,256]{1,0:T(8,128)S(1)} %copy-done.1, f32[64,256]{1,0:T(8,128)S(1)} %get-tuple-element.46.refs_0_, ...), custom_call_target="tpu_custom_call" | custom-call | flops 1 | bytes 1 | tf_op jit(solution)/shard_map/pallas_call | solution.py:260
  (32 shorter events, 0.7 us)
Async XLA Ops:
  0.0 0.9 %copy-start.2 = (f32[1024,64]{0,1:T(8,128)S(1)}, f32[1024,64]{0,1:T(8,128)}, u32[]{:S(2)}) copy-start(f32[1024,64]{0,1:T(8,128)} %param.6) | copy-start | bytes 786436
  1.0 9.2 %collective-permute-start.6 = (f32[64,256]{1,0:T(8,128)S(1)}, f32[64,256]{1,0:T(8,128)S(1)}, u32[]{:S(2)}, u32[]{:S(2)}) collective-permute-start(f32[64,256]{1,0:T(8,128)S(1)} %get-tuple-element.46.refs_0_), channel_id=1, source_target_pairs={{0,1},{1,0},{2,3},{3,2},{4,5},{5,4},{6,7},{7,6},{8,9},{9,8},{10,11... | collective-permute-start | bytes 196616 | tf_op jit(solution)/shard_map/ppermute | solution.py:280
  4.1 8.9 %collective-permute-start.7 = (f32[64,256]{1,0:T(8,128)S(1)}, f32[64,256]{1,0:T(8,128)S(1)}, u32[]{:S(2)}, u32[]{:S(2)}) collective-permute-start(f32[64,256]{1,0:T(8,128)S(1)} %get-tuple-element.46.refs_0_), channel_id=1, source_target_pairs={{0,3},{1,2},{2,1},{3,0},{4,7},{5,6},{6,5},{7,4},{8,11},{9,10},{10,... | collective-permute-start | bytes 196616 | tf_op jit(solution)/shard_map/ppermute | solution.py:280
  6.6 6.6 %collective-permute-start.8 = (f32[64,256]{1,0:T(8,128)S(1)}, f32[64,256]{1,0:T(8,128)S(1)}, u32[]{:S(2)}, u32[]{:S(2)}) collective-permute-start(f32[64,256]{1,0:T(8,128)S(1)} %get-tuple-element.46.refs_0_), channel_id=1, source_target_pairs={{0,2},{1,3},{2,0},{3,1},{4,6},{5,7},{6,4},{7,5},{8,10},{9,11},{10,... | collective-permute-start | bytes 196616 | tf_op jit(solution)/shard_map/ppermute | solution.py:280
  6.7 4.4 %copy-start.3 = (s32[256]{0:T(256)S(1)}, s32[256]{0:T(256)}, u32[]{:S(2)}) copy-start(s32[256]{0:T(256)} %param.7) | copy-start | bytes 3076
  6.7 21.9 %collective-permute-start.10 = (f32[64,768]{1,0:T(8,128)S(1)}, f32[64,768]{1,0:T(8,128)S(1)}, u32[]{:S(2)}, u32[]{:S(2)}) collective-permute-start(f32[64,768]{1,0:T(8,128)S(1)} %get-tuple-element.51.refs_4_), channel_id=1, source_target_pairs={{0,1},{1,0},{2,3},{3,2},{4,5},{5,4},{6,7},{7,6},{8,9},{9,8},{10,11... | collective-permute-start | bytes 589832 | tf_op jit(solution)/shard_map/ppermute | solution.py:280
  8.5 20.1 %collective-permute-start.11 = (f32[64,768]{1,0:T(8,128)S(1)}, f32[64,768]{1,0:T(8,128)S(1)}, u32[]{:S(2)}, u32[]{:S(2)}) collective-permute-start(f32[64,768]{1,0:T(8,128)S(1)} %get-tuple-element.51.refs_4_), channel_id=1, source_target_pairs={{0,2},{1,3},{2,0},{3,1},{4,6},{5,7},{6,4},{7,5},{8,10},{9,11},{10,... | collective-permute-start | bytes 589832 | tf_op jit(solution)/shard_map/ppermute | solution.py:280
  10.2 18.5 %collective-permute-start.12 = (f32[64,768]{1,0:T(8,128)S(1)}, f32[64,768]{1,0:T(8,128)S(1)}, u32[]{:S(2)}, u32[]{:S(2)}) collective-permute-start(f32[64,768]{1,0:T(8,128)S(1)} %get-tuple-element.51.refs_4_), channel_id=1, source_target_pairs={{0,3},{1,2},{2,1},{3,0},{4,7},{5,6},{6,5},{7,4},{8,11},{9,10},{10,... | collective-permute-start | bytes 589832 | tf_op jit(solution)/shard_map/ppermute | solution.py:280
  11.1 1.2 %copy-start = (f32[1024,256]{1,0:T(8,128)S(1)}, f32[1024,256]{1,0:T(8,128)}, u32[]{:S(2)}) copy-start(f32[1024,256]{1,0:T(8,128)} %slab_ref.3) | copy-start | bytes 3145732
  13.3 1.3 %collective-permute-start.9 = (f32[32,256]{1,0:T(8,128)S(1)}, f32[32,256]{1,0:T(8,128)S(1)}, u32[]{:S(2)}, u32[]{:S(2)}) collective-permute-start(f32[32,256]{1,0:T(8,128)S(1)} %get-tuple-element.47), channel_id=1, source_target_pairs={{0,4},{4,0},{8,12},{12,8},{16,20},{20,16},{24,28},{28,24},{1,5},{5... | collective-permute-start | bytes 98312 | tf_op jit(solution)/shard_map/ppermute | solution.py:347
  13.4 1.5 %collective-permute-start.5 = (f32[128,256]{1,0:T(8,128)S(1)}, f32[128,256]{1,0:T(8,128)S(1)}, u32[]{:S(2)}, u32[]{:S(2)}) collective-permute-start(f32[128,256]{1,0:T(8,128)S(1)} %slice.37), channel_id=1, source_target_pairs={{0,4},{4,0},{8,12},{12,8},{16,20},{20,16},{24,28},{28,24},{1,5},{5... | collective-permute-start | bytes 393224 | tf_op jit(solution)/shard_map/ppermute | solution.py:350
  14.9 13.8 %copy-start.1 = (f32[1024,256]{1,0:T(8,128)S(1)}, f32[1024,256]{1,0:T(8,128)}, u32[]{:S(2)}) copy-start(f32[1024,256]{1,0:T(8,128)} %slab_ref.3) | copy-start | bytes 3145732
  14.9 4.7 %collective-permute-start.1 = (f32[192,256]{1,0:T(8,128)S(1)}, f32[192,256]{1,0:T(8,128)S(1)}, u32[]{:S(2)}, u32[]{:S(2)}) collective-permute-start(f32[192,256]{1,0:T(8,128)S(1)} %get-tuple-element.29.held_ref), channel_id=1, source_target_pairs={{0,16},{4,0},{8,12},{12,8},{16,20},{20,4},{24,28},{28,24},{1,17},{... | collective-permute-start | bytes 589832 | tf_op jit(solution)/shard_map/cond/branch_1_fun/ppermute | solution.py:315
  16.5 5.0 %collective-permute-start = (f32[128,256]{1,0:T(8,128)S(1)}, f32[128,256]{1,0:T(8,128)S(1)}, u32[]{:S(2)}, u32[]{:S(2)}) collective-permute-start(f32[128,256]{1,0:T(8,128)S(1)} %pad_maximum_fusion.2), channel_id=1, source_target_pairs={{0,8},{4,12},{8,0},{12,4},{16,24},{20,28},{24,16},{28,20},{1,9},{5... | collective-permute-start | bytes 393224 | tf_op jit(solution)/shard_map/cond/branch_1_fun/ppermute | solution.py:324
  19.6 3.2 %collective-permute-start.3 = (f32[192,256]{1,0:T(8,128)S(1)}, f32[192,256]{1,0:T(8,128)S(1)}, u32[]{:S(2)}, u32[]{:S(2)}) collective-permute-start(f32[192,256]{1,0:T(8,128)S(1)} %branch_1_fun.5.held_ref), channel_id=1, source_target_pairs={{0,8},{4,0},{8,12},{12,4},{16,24},{20,16},{24,28},{28,20},{1,9},{5... | collective-permute-start | bytes 589832 | tf_op jit(solution)/shard_map/cond/branch_1_fun/ppermute | solution.py:315
  21.6 5.6 %collective-permute-start.2 = (f32[160,256]{1,0:T(8,128)S(1)}, f32[160,256]{1,0:T(8,128)S(1)}, u32[]{:S(2)}, u32[]{:S(2)}) collective-permute-start(f32[160,256]{1,0:T(8,128)S(1)} %pad_maximum_fusion.1), channel_id=1, source_target_pairs={{0,16},{4,20},{8,24},{12,28},{16,0},{20,4},{24,8},{28,12},{1,17},{... | collective-permute-start | bytes 491528 | tf_op jit(solution)/shard_map/cond/branch_1_fun/ppermute | solution.py:324
  24.7 3.2 %collective-permute-start.4 = (f32[192,256]{1,0:T(8,128)S(1)}, f32[192,256]{1,0:T(8,128)S(1)}, u32[]{:S(2)}, u32[]{:S(2)}) collective-permute-start(f32[192,256]{1,0:T(8,128)S(1)} %branch_1_fun.7), channel_id=1, source_target_pairs={{0,4},{4,0},{8,12},{12,8},{16,20},{20,16},{24,28},{28,24},{1,5},{5... | collective-permute-start | bytes 589832 | tf_op jit(solution)/shard_map/cond/branch_1_fun/ppermute | solution.py:341

commit v11 on v10

--- a/solution.py
+++ b/solution.py
@@ -8,7 +8,7 @@
 from jax.sharding import PartitionSpec as P
 
 CAP = 32
-BLOCK = 32
+BLOCK = 64
 F32 = jnp.float32
 BF16 = jnp.bfloat16
 VMEM = pl.BlockSpec(memory_space=pltpu.VMEM)
@@ -101,16 +101,19 @@
         diag = jnp.where(block == b, lower[b * BLOCK : (b + 1) * BLOCK], diag)
     diag = jnp.where(within < sub, diag, 0.0)
     inv = jnp.where(within == sub, 1.0, 0.0).astype(F32)
-    half = 128
-    first = (lax.broadcasted_iota(jnp.int32, (BLOCK, half), 1) // BLOCK) * BLOCK
-    outs = []
-    for h in range(0, width, half):
-        d, x = diag[:, h : h + half], inv[:, h : h + half]
-        for k in range(BLOCK - 1):
-            column = jnp.take_along_axis(d, first + k, axis=1)
-            x = x - column * x[k : k + 1, :]
-        outs.append(x)
-    return outs
+    half, tile = 128, 8
+    first = (lax.broadcasted_iota(jnp.int32, (tile, half), 1) // BLOCK) * BLOCK
+    starts = range(0, width, half)
+    tops = range(0, BLOCK, tile)
+    d = [[diag[t : t + tile, h : h + half] for t in tops] for h in starts]
+    x = [[inv[t : t + tile, h : h + half] for t in tops] for h in starts]
+    for k in range(BLOCK - 1):
+        for h in range(len(starts)):
+            row = x[h][k // tile][k % tile : k % tile + 1, :]
+            for t in range((k + 1) // tile, len(tops)):
+                column = jnp.take_along_axis(d[h][t], first + k, axis=1)
+                x[h][t] = x[h][t] - column * row
+    return [jnp.concatenate(tiles, axis=0) for tiles in x]
 
 
 def order_kernel(n, rows, pivot_ref, gathered_ref, out_ref, gathered):

time: 30.9 us -> 30.9 us (level)
  transfers between devices with their start and end apart: 13 -> 13, of which waited for: 7 -> 7; matrix products, arithmetic and copies ran while one was open for 0% -> 0% of each run, Pallas kernels for 12% -> 13%
where the time goes in v11:
time: 30.9 us; the launch traced here: 30.8 us
  starting transfers between devices  16.1 us (52%)
  waiting for transfers between devices  6.26 us (20%)
  Pallas kernels  5.93 us (19%)
  local copies, waits for them, and re-layouts  2.21 us (7%)
    ppermute x6, starting transfers between devices, exchange(): return lax.ppermute(block, 'pcol', [(c, c ^ d) for c in range(m)])  10.1 us
    pallas_call x9, Pallas kernels, call(): pl.pallas_call(kernel, out_shape=outs, in_specs=in_specs or [VMEM] * len(...  5.93 us
    ppermute x2, waiting for transfers between devices, levels(): lax.ppermute(lower, 'prow', [(r, tree_partner(r, span)) for r in range(n)])  2.74 us
    unnamed x8, local copies, waits for them, and re-layouts  2.18 us
    ppermute x1, starting transfers between devices, levels(): moved = lax.ppermute(inverse, 'prow', [(r, r ^ 1) for r in range(n)])  2.13 us
    ppermute x2, waiting for transfers between devices, levels(): moved = lax.ppermute(message, 'prow', [(r, r ^ other) for r in range(n)])  2.08 us
    ppermute x2, starting transfers between devices, levels(): moved = lax.ppermute(message, 'prow', [(r, r ^ other) for r in range(n)])  1.69 us
    ppermute x2, starting transfers between devices, levels(): lax.ppermute(lower, 'prow', [(r, tree_partner(r, span)) for r in range(n)])  1.54 us
  transfers between devices with their start and end apart: 13, of which 7 were waited for; matrix products, arithmetic and copies ran while one was open for 0% of the time, Pallas kernels for 13%

profile of v11, /device:TPU:0, one launch (start us, length us, event | category | flops | bytes accessed | tf_op | source)
XLA Modules:
  0.0 30.8 jit_solution(12415985424090055195)
XLA Ops:
  0.0 0.9 %copy-done.2 = f32[1024,64]{0,1:T(8,128)S(1)} copy-done((f32[1024,64]{0,1:T(8,128)S(1)}, f32[1024,64]{0,1:T(8,128)}, u32[]{:S(2)}) %copy-start.2) | copy-done | bytes 262168
  1.0 3.1 %collective-permute-start.6 = (f32[64,256]{1,0:T(8,128)S(1)}, f32[64,256]{1,0:T(8,128)S(1)}, u32[]{:S(2)}, u32[]{:S(2)}) collective-permute-start(f32[64,256]{1,0:T(8,128)S(1)} %get-tuple-element.46.refs_0_), channel_id=1, source_target_pairs={{0,1},{1,0},{2,3},{3,2},{4,5},{5,4},{6,7},{7,6},{8,9},{9,8},{10,11... | collective-permute-start | bytes 196616 | tf_op jit(solution)/shard_map/ppermute | solution.py:283
  4.1 2.5 %collective-permute-start.7 = (f32[64,256]{1,0:T(8,128)S(1)}, f32[64,256]{1,0:T(8,128)S(1)}, u32[]{:S(2)}, u32[]{:S(2)}) collective-permute-start(f32[64,256]{1,0:T(8,128)S(1)} %get-tuple-element.46.refs_0_), channel_id=1, source_target_pairs={{0,3},{1,2},{2,1},{3,0},{4,7},{5,6},{6,5},{7,4},{8,11},{9,10},{10,... | collective-permute-start | bytes 196616 | tf_op jit(solution)/shard_map/ppermute | solution.py:283
  6.7 1.8 %collective-permute-start.10 = (f32[64,768]{1,0:T(8,128)S(1)}, f32[64,768]{1,0:T(8,128)S(1)}, u32[]{:S(2)}, u32[]{:S(2)}) collective-permute-start(f32[64,768]{1,0:T(8,128)S(1)} %get-tuple-element.51.refs_4_), channel_id=1, source_target_pairs={{0,1},{1,0},{2,3},{3,2},{4,5},{5,4},{6,7},{7,6},{8,9},{9,8},{10,11... | collective-permute-start | bytes 589832 | tf_op jit(solution)/shard_map/ppermute | solution.py:283
  8.5 1.7 %collective-permute-start.11 = (f32[64,768]{1,0:T(8,128)S(1)}, f32[64,768]{1,0:T(8,128)S(1)}, u32[]{:S(2)}, u32[]{:S(2)}) collective-permute-start(f32[64,768]{1,0:T(8,128)S(1)} %get-tuple-element.51.refs_4_), channel_id=1, source_target_pairs={{0,2},{1,3},{2,0},{3,1},{4,6},{5,7},{6,4},{7,5},{8,10},{9,11},{10,... | collective-permute-start | bytes 589832 | tf_op jit(solution)/shard_map/ppermute | solution.py:283
  10.2 0.9 %collective-permute-start.12 = (f32[64,768]{1,0:T(8,128)S(1)}, f32[64,768]{1,0:T(8,128)S(1)}, u32[]{:S(2)}, u32[]{:S(2)}) collective-permute-start(f32[64,768]{1,0:T(8,128)S(1)} %get-tuple-element.51.refs_4_), channel_id=1, source_target_pairs={{0,3},{1,2},{2,1},{3,0},{4,7},{5,6},{6,5},{7,4},{8,11},{9,10},{10,... | collective-permute-start | bytes 589832 | tf_op jit(solution)/shard_map/ppermute | solution.py:283
  11.1 1.2 %copy-done = f32[1024,256]{1,0:T(8,128)S(1)} copy-done((f32[1024,256]{1,0:T(8,128)S(1)}, f32[1024,256]{1,0:T(8,128)}, u32[]{:S(2)}) %copy-start) | copy-done | bytes 1048600
  12.3 0.7 %shard_map.37 = (f32[32,256]{1,0:T(8,128)S(1)}, f32[256,256]{1,0:T(8,128)S(1)}, s32[1,128]{1,0:T(1,128)S(1)}) custom-call(s32[1,256]{1,0:T(1,128)S(1)} %bitcast.3, f32[1024,256]{1,0:T(8,128)S(1)} %copy-done), custom_call_target="tpu_custom_call" | custom-call | flops 1 | bytes 1 | tf_op jit(solution)/shard_map/pallas_call | solution.py:263
  13.4 0.6 %collective-permute-start.5 = (f32[128,256]{1,0:T(8,128)S(1)}, f32[128,256]{1,0:T(8,128)S(1)}, u32[]{:S(2)}, u32[]{:S(2)}) collective-permute-start(f32[128,256]{1,0:T(8,128)S(1)} %slice.37), channel_id=1, source_target_pairs={{0,4},{4,0},{8,12},{12,8},{16,20},{20,16},{24,28},{28,24},{1,5},{5... | collective-permute-start | bytes 393224 | tf_op jit(solution)/shard_map/ppermute | solution.py:353
  13.9 0.6 %collective-permute-done.9 = f32[32,256]{1,0:T(8,128)S(1)} collective-permute-done((f32[32,256]{1,0:T(8,128)S(1)}, f32[32,256]{1,0:T(8,128)S(1)}, u32[]{:S(2)}, u32[]{:S(2)}) %collective-permute-start.9) | collective-permute-done | bytes 32800 | tf_op jit(solution)/shard_map/ppermute | solution.py:350
  14.6 0.4 %collective-permute-done.5 = f32[128,256]{1,0:T(8,128)S(1)} collective-permute-done((f32[128,256]{1,0:T(8,128)S(1)}, f32[128,256]{1,0:T(8,128)S(1)}, u32[]{:S(2)}, u32[]{:S(2)}) %collective-permute-start.5) | collective-permute-done | bytes 131104 | tf_op jit(solution)/shard_map/ppermute | solution.py:353
  14.9 13.8 %conditional.1 = (f32[32,256]{1,0:T(8,128)S(1)}, f32[256,256]{1,0:T(8,128)S(1)}) conditional(s32[]{:T(128)} %convert_element_type.3, () %tuple.19, (s32[]{:T(128)}, f32[256,256]{1,0:T(8,128)S(1)}, f32[128,256]{1,0:T(8,128)S(1)}, f32[64,256]{1,0:T(8,128)S(1)}, f32[192,256]{1,0:T(8,128)S(1)}, /*index=5*/s32[1,256]{1,0:T(1,128)S(1)}) %tuple.25), branch_computations={%region_0.1_spmd, %region_1.2_spmd} | conditional | flops 352267 | bytes 6521120 | solution.py:259
  14.9 1.5 %collective-permute-start.1 = (f32[192,256]{1,0:T(8,128)S(1)}, f32[192,256]{1,0:T(8,128)S(1)}, u32[]{:S(2)}, u32[]{:S(2)}) collective-permute-start(f32[192,256]{1,0:T(8,128)S(1)} %get-tuple-element.29.held_ref), channel_id=1, source_target_pairs={{0,16},{4,0},{8,12},{12,8},{16,20},{20,4},{24,28},{28,24},{1,17},{... | collective-permute-start | bytes 589832 | tf_op jit(solution)/shard_map/cond/branch_1_fun/ppermute | solution.py:318
  16.5 0.4 %collective-permute-start = (f32[128,256]{1,0:T(8,128)S(1)}, f32[128,256]{1,0:T(8,128)S(1)}, u32[]{:S(2)}, u32[]{:S(2)}) collective-permute-start(f32[128,256]{1,0:T(8,128)S(1)} %pad_maximum_fusion.2), channel_id=1, source_target_pairs={{0,8},{4,12},{8,0},{12,4},{16,24},{20,28},{24,16},{28,20},{1,9},{5... | collective-permute-start | bytes 393224 | tf_op jit(solution)/shard_map/cond/branch_1_fun/ppermute | solution.py:327
  16.9 2.7 %collective-permute-done.1.moved_ref = f32[192,256]{1,0:T(8,128)S(1)} collective-permute-done((f32[192,256]{1,0:T(8,128)S(1)}, f32[192,256]{1,0:T(8,128)S(1)}, u32[]{:S(2)}, u32[]{:S(2)}) %collective-permute-start.1) | collective-permute-done | bytes 196640 | tf_op jit(solution)/shard_map/cond/branch_1_fun/ppermute | solution.py:318
  19.7 1.9 %collective-permute-done = f32[128,256]{1,0:T(8,128)S(1)} collective-permute-done((f32[128,256]{1,0:T(8,128)S(1)}, f32[128,256]{1,0:T(8,128)S(1)}, u32[]{:S(2)}, u32[]{:S(2)}) %collective-permute-start) | collective-permute-done | bytes 131104 | tf_op jit(solution)/shard_map/cond/branch_1_fun/ppermute | solution.py:327
  21.6 1.3 %collective-permute-start.2 = (f32[160,256]{1,0:T(8,128)S(1)}, f32[160,256]{1,0:T(8,128)S(1)}, u32[]{:S(2)}, u32[]{:S(2)}) collective-permute-start(f32[160,256]{1,0:T(8,128)S(1)} %pad_maximum_fusion.1), channel_id=1, source_target_pairs={{0,16},{4,20},{8,24},{12,28},{16,0},{20,4},{24,8},{28,12},{1,17},{... | collective-permute-start | bytes 491528 | tf_op jit(solution)/shard_map/cond/branch_1_fun/ppermute | solution.py:327
  22.9 1.9 %branch_1_fun.7 = f32[192,256]{1,0:T(8,128)S(1)} custom-call(f32[192,256]{1,0:T(8,128)S(1)} %branch_1_fun.6.lower_ref), custom_call_target="tpu_custom_call" | custom-call | flops 1 | bytes 1 | tf_op jit(solution)/shard_map/cond/branch_1_fun/pallas_call | solution.py:263
  24.8 2.1 %collective-permute-start.4 = (f32[192,256]{1,0:T(8,128)S(1)}, f32[192,256]{1,0:T(8,128)S(1)}, u32[]{:S(2)}, u32[]{:S(2)}) collective-permute-start(f32[192,256]{1,0:T(8,128)S(1)} %branch_1_fun.7), channel_id=1, source_target_pairs={{0,4},{4,0},{8,12},{12,8},{16,20},{20,16},{24,28},{28,24},{1,5},{5... | collective-permute-start | bytes 589832 | tf_op jit(solution)/shard_map/cond/branch_1_fun/ppermute | solution.py:344
  26.9 0.2 collective-permute-done.2
  27.2 0.5 %branch_1_fun.8.pivot_rows_ref = f32[256,256]{1,0:T(8,128)S(1)} custom-call(s32[1,256]{1,0:T(1,128)S(1)} %get-tuple-element.33.pivot_ref, f32[256,256]{1,0:T(8,128)S(1)} %pad_maximum_fusion.gathered_ref), custom_call_target="tpu_custom_call" | custom-call | flops 1 | bytes 1 | tf_op jit(solution)/shard_map/cond/branch_1_fun/pallas_call | solution.py:263
  27.7 0.3 collective-permute-done.4
  28.0 0.7 %branch_1_fun.9 = f32[256,256]{1,0:T(8,128)S(1)} custom-call(f32[192,256]{1,0:T(8,128)S(1)} %broadcast_select_fusion.inverse_ref, f32[256,256]{1,0:T(8,128)S(1)} %branch_1_fun.8.pivot_rows_ref), custom_call_target="tpu_custom_call" | custom-call | flops 1 | bytes 1 | tf_op jit(solution)/shard_map/cond/branch_1_fun/pallas_call | solution.py:263
  28.8 2.0 %shard_map.40 = f32[1024,256]{1,0:T(8,128)} custom-call(s32[1,128]{1,0:T(1,128)S(1)} %get-tuple-element.43.local_ref, f32[32,256]{1,0:T(8,128)S(1)} %get-tuple-element.49.lead_ref, f32[256,256]{1,0:T(8,128)S(1)} %get-tuple-element.50.x_ref, f32[1024,256]{1,0:T(8,128)S(1)} %copy-done.1, f32[64,256]{1,0:T(8,128)S(1)} %get-tuple-element.46.refs_0_, ...), custom_call_target="tpu_custom_call" | custom-call | flops 1 | bytes 1 | tf_op jit(solution)/shard_map/pallas_call | solution.py:263
  (32 shorter events, 0.7 us)
Async XLA Ops:
  0.0 0.9 %copy-start.2 = (f32[1024,64]{0,1:T(8,128)S(1)}, f32[1024,64]{0,1:T(8,128)}, u32[]{:S(2)}) copy-start(f32[1024,64]{0,1:T(8,128)} %param.6) | copy-start | bytes 786436
  1.0 9.2 %collective-permute-start.6 = (f32[64,256]{1,0:T(8,128)S(1)}, f32[64,256]{1,0:T(8,128)S(1)}, u32[]{:S(2)}, u32[]{:S(2)}) collective-permute-start(f32[64,256]{1,0:T(8,128)S(1)} %get-tuple-element.46.refs_0_), channel_id=1, source_target_pairs={{0,1},{1,0},{2,3},{3,2},{4,5},{5,4},{6,7},{7,6},{8,9},{9,8},{10,11... | collective-permute-start | bytes 196616 | tf_op jit(solution)/shard_map/ppermute | solution.py:283
  4.1 8.9 %collective-permute-start.7 = (f32[64,256]{1,0:T(8,128)S(1)}, f32[64,256]{1,0:T(8,128)S(1)}, u32[]{:S(2)}, u32[]{:S(2)}) collective-permute-start(f32[64,256]{1,0:T(8,128)S(1)} %get-tuple-element.46.refs_0_), channel_id=1, source_target_pairs={{0,3},{1,2},{2,1},{3,0},{4,7},{5,6},{6,5},{7,4},{8,11},{9,10},{10,... | collective-permute-start | bytes 196616 | tf_op jit(solution)/shard_map/ppermute | solution.py:283
  6.6 6.6 %collective-permute-start.8 = (f32[64,256]{1,0:T(8,128)S(1)}, f32[64,256]{1,0:T(8,128)S(1)}, u32[]{:S(2)}, u32[]{:S(2)}) collective-permute-start(f32[64,256]{1,0:T(8,128)S(1)} %get-tuple-element.46.refs_0_), channel_id=1, source_target_pairs={{0,2},{1,3},{2,0},{3,1},{4,6},{5,7},{6,4},{7,5},{8,10},{9,11},{10,... | collective-permute-start | bytes 196616 | tf_op jit(solution)/shard_map/ppermute | solution.py:283
  6.7 4.4 %copy-start.3 = (s32[256]{0:T(256)S(1)}, s32[256]{0:T(256)}, u32[]{:S(2)}) copy-start(s32[256]{0:T(256)} %param.7) | copy-start | bytes 3076
  6.7 22.0 %collective-permute-start.10 = (f32[64,768]{1,0:T(8,128)S(1)}, f32[64,768]{1,0:T(8,128)S(1)}, u32[]{:S(2)}, u32[]{:S(2)}) collective-permute-start(f32[64,768]{1,0:T(8,128)S(1)} %get-tuple-element.51.refs_4_), channel_id=1, source_target_pairs={{0,1},{1,0},{2,3},{3,2},{4,5},{5,4},{6,7},{7,6},{8,9},{9,8},{10,11... | collective-permute-start | bytes 589832 | tf_op jit(solution)/shard_map/ppermute | solution.py:283
  8.5 20.2 %collective-permute-start.11 = (f32[64,768]{1,0:T(8,128)S(1)}, f32[64,768]{1,0:T(8,128)S(1)}, u32[]{:S(2)}, u32[]{:S(2)}) collective-permute-start(f32[64,768]{1,0:T(8,128)S(1)} %get-tuple-element.51.refs_4_), channel_id=1, source_target_pairs={{0,2},{1,3},{2,0},{3,1},{4,6},{5,7},{6,4},{7,5},{8,10},{9,11},{10,... | collective-permute-start | bytes 589832 | tf_op jit(solution)/shard_map/ppermute | solution.py:283
  10.2 18.5 %collective-permute-start.12 = (f32[64,768]{1,0:T(8,128)S(1)}, f32[64,768]{1,0:T(8,128)S(1)}, u32[]{:S(2)}, u32[]{:S(2)}) collective-permute-start(f32[64,768]{1,0:T(8,128)S(1)} %get-tuple-element.51.refs_4_), channel_id=1, source_target_pairs={{0,3},{1,2},{2,1},{3,0},{4,7},{5,6},{6,5},{7,4},{8,11},{9,10},{10,... | collective-permute-start | bytes 589832 | tf_op jit(solution)/shard_map/ppermute | solution.py:283
  11.1 1.2 %copy-start = (f32[1024,256]{1,0:T(8,128)S(1)}, f32[1024,256]{1,0:T(8,128)}, u32[]{:S(2)}) copy-start(f32[1024,256]{1,0:T(8,128)} %slab_ref.3) | copy-start | bytes 3145732
  13.3 1.3 %collective-permute-start.9 = (f32[32,256]{1,0:T(8,128)S(1)}, f32[32,256]{1,0:T(8,128)S(1)}, u32[]{:S(2)}, u32[]{:S(2)}) collective-permute-start(f32[32,256]{1,0:T(8,128)S(1)} %get-tuple-element.47), channel_id=1, source_target_pairs={{0,4},{4,0},{8,12},{12,8},{16,20},{20,16},{24,28},{28,24},{1,5},{5... | collective-permute-start | bytes 98312 | tf_op jit(solution)/shard_map/ppermute | solution.py:350
  13.4 1.5 %collective-permute-start.5 = (f32[128,256]{1,0:T(8,128)S(1)}, f32[128,256]{1,0:T(8,128)S(1)}, u32[]{:S(2)}, u32[]{:S(2)}) collective-permute-start(f32[128,256]{1,0:T(8,128)S(1)} %slice.37), channel_id=1, source_target_pairs={{0,4},{4,0},{8,12},{12,8},{16,20},{20,16},{24,28},{28,24},{1,5},{5... | collective-permute-start | bytes 393224 | tf_op jit(solution)/shard_map/ppermute | solution.py:353
  14.9 13.9 %copy-start.1 = (f32[1024,256]{1,0:T(8,128)S(1)}, f32[1024,256]{1,0:T(8,128)}, u32[]{:S(2)}) copy-start(f32[1024,256]{1,0:T(8,128)} %slab_ref.3) | copy-start | bytes 3145732
  14.9 4.7 %collective-permute-start.1 = (f32[192,256]{1,0:T(8,128)S(1)}, f32[192,256]{1,0:T(8,128)S(1)}, u32[]{:S(2)}, u32[]{:S(2)}) collective-permute-start(f32[192,256]{1,0:T(8,128)S(1)} %get-tuple-element.29.held_ref), channel_id=1, source_target_pairs={{0,16},{4,0},{8,12},{12,8},{16,20},{20,4},{24,28},{28,24},{1,17},{... | collective-permute-start | bytes 589832 | tf_op jit(solution)/shard_map/cond/branch_1_fun/ppermute | solution.py:318
  16.5 5.0 %collective-permute-start = (f32[128,256]{1,0:T(8,128)S(1)}, f32[128,256]{1,0:T(8,128)S(1)}, u32[]{:S(2)}, u32[]{:S(2)}) collective-permute-start(f32[128,256]{1,0:T(8,128)S(1)} %pad_maximum_fusion.2), channel_id=1, source_target_pairs={{0,8},{4,12},{8,0},{12,4},{16,24},{20,28},{24,16},{28,20},{1,9},{5... | collective-permute-start | bytes 393224 | tf_op jit(solution)/shard_map/cond/branch_1_fun/ppermute | solution.py:327
  19.6 3.2 %collective-permute-start.3 = (f32[192,256]{1,0:T(8,128)S(1)}, f32[192,256]{1,0:T(8,128)S(1)}, u32[]{:S(2)}, u32[]{:S(2)}) collective-permute-start(f32[192,256]{1,0:T(8,128)S(1)} %branch_1_fun.5.held_ref), channel_id=1, source_target_pairs={{0,8},{4,0},{8,12},{12,4},{16,24},{20,16},{24,28},{28,20},{1,9},{5... | collective-permute-start | bytes 589832 | tf_op jit(solution)/shard_map/cond/branch_1_fun/ppermute | solution.py:318
  21.6 5.6 %collective-permute-start.2 = (f32[160,256]{1,0:T(8,128)S(1)}, f32[160,256]{1,0:T(8,128)S(1)}, u32[]{:S(2)}, u32[]{:S(2)}) collective-permute-start(f32[160,256]{1,0:T(8,128)S(1)} %pad_maximum_fusion.1), channel_id=1, source_target_pairs={{0,16},{4,20},{8,24},{12,28},{16,0},{20,4},{24,8},{28,12},{1,17},{... | collective-permute-start | bytes 491528 | tf_op jit(solution)/shard_map/cond/branch_1_fun/ppermute | solution.py:327
  24.8 3.2 %collective-permute-start.4 = (f32[192,256]{1,0:T(8,128)S(1)}, f32[192,256]{1,0:T(8,128)S(1)}, u32[]{:S(2)}, u32[]{:S(2)}) collective-permute-start(f32[192,256]{1,0:T(8,128)S(1)} %branch_1_fun.7), channel_id=1, source_target_pairs={{0,4},{4,0},{8,12},{12,8},{16,20},{20,16},{24,28},{28,24},{1,5},{5... | collective-permute-start | bytes 589832 | tf_op jit(solution)/shard_map/cond/branch_1_fun/ppermute | solution.py:344

commit v12 on v10

--- a/solution.py
+++ b/solution.py
@@ -166,27 +166,35 @@
 
 
 def invert_kernel(lower_ref, out_ref, lower_t):
-    width = lower_t.shape[0]
-    half = width // 2
-    lower_t[:half, :] = lower_ref[:half, :]
-    lower_t[half:, :half] = jnp.zeros((half, half), F32)
-    lower_t[half : half + half // 2, half:] = lower_ref[half:, :half]
-    lower_t[half + half // 2 :, half:] = lower_ref[half:, half:]
-    lower = lower_t[...].T
-    blocks = block_inverses(lower)
-    row = lax.broadcasted_iota(jnp.int32, (half, half), 0)
-    col = lax.broadcasted_iota(jnp.int32, (half, half), 1)
-    for h, strip in enumerate(blocks):
-        corner = lower[h * half : (h + 1) * half, h * half : (h + 1) * half]
-        inv = jnp.where(row // BLOCK == col // BLOCK, jnp.concatenate([strip] * (half // BLOCK), axis=0), 0.0)
-        size = BLOCK
-        while size < half:
-            off = (row // (2 * size) == col // (2 * size)) & (row // size > col // size)
-            inv = inv - dot_full(dot_full(inv, jnp.where(off, corner, 0.0)), inv)
-            size *= 2
-        out_ref[:half, h * half : (h + 1) * half] = inv
-    out_ref[half:, :half] = lower[half : half + half // 2, :half]
-    out_ref[half:, half:] = lower[half + half // 2 :, :half]
+    holds = lax.axis_index("prow") & 1 == 0
+
+    @pl.when(jnp.logical_not(holds))
+    def _():
+        out_ref[...] = jnp.zeros_like(out_ref)
+
+    @pl.when(holds)
+    def _():
+        width = lower_t.shape[0]
+        half = width // 2
+        lower_t[:half, :] = lower_ref[:half, :]
+        lower_t[half:, :half] = jnp.zeros((half, half), F32)
+        lower_t[half : half + half // 2, half:] = lower_ref[half:, :half]
+        lower_t[half + half // 2 :, half:] = lower_ref[half:, half:]
+        lower = lower_t[...].T
+        blocks = block_inverses(lower)
+        row = lax.broadcasted_iota(jnp.int32, (half, half), 0)
+        col = lax.broadcasted_iota(jnp.int32, (half, half), 1)
+        for h, strip in enumerate(blocks):
+            corner = lower[h * half : (h + 1) * half, h * half : (h + 1) * half]
+            inv = jnp.where(row // BLOCK == col // BLOCK, jnp.concatenate([strip] * (half // BLOCK), axis=0), 0.0)
+            size = BLOCK
+            while size < half:
+                off = (row // (2 * size) == col // (2 * size)) & (row // size > col // size)
+                inv = inv - dot_full(dot_full(inv, jnp.where(off, corner, 0.0)), inv)
+                size *= 2
+            out_ref[:half, h * half : (h + 1) * half] = inv
+        out_ref[half:, :half] = lower[half : half + half // 2, :half]
+        out_ref[half:, half:] = lower[half + half // 2 :, :half]
 
 
 def solve_kernel(inverse_ref, pivot_rows_ref, x_ref):

time: 30.9 us -> 30.7 us (level)
  starting transfers between devices: 16.1 us -> 14.3 us
  waiting for transfers between devices: 6.26 us -> 7.84 us
    ppermute x1, starting transfers between devices: 2.13 us -> 0.35 us  [levels(): moved = lax.ppermute(inverse, 'prow', [(r, r ^ 1) for r in range(n)])]
    ppermute x2, waiting for transfers between devices: 2.16 us -> 3.93 us  [levels(): moved = lax.ppermute(message, 'prow', [(r, r ^ other) for r in range(n)])]
  transfers between devices with their start and end apart: 13 -> 13, of which waited for: 7 -> 6; matrix products, arithmetic and copies ran while one was open for 0% -> 0% of each run, Pallas kernels for 12% -> 12%
where the time goes in v12:
time: 30.7 us; the launch traced here: 30.5 us
  starting transfers between devices  14.3 us (47%)
  waiting for transfers between devices  7.84 us (26%)
  Pallas kernels  5.87 us (19%)
  local copies, waits for them, and re-layouts  2.21 us (7%)
    ppermute x6, starting transfers between devices, exchange(): return lax.ppermute(block, 'pcol', [(c, c ^ d) for c in range(m)])  10.1 us
    pallas_call x9, Pallas kernels, call(): pl.pallas_call(kernel, out_shape=outs, in_specs=in_specs or [VMEM] * len(...  5.87 us
    ppermute x2, waiting for transfers between devices, levels(): moved = lax.ppermute(message, 'prow', [(r, r ^ other) for r in range(n)])  3.93 us
    ppermute x2, waiting for transfers between devices, levels(): lax.ppermute(lower, 'prow', [(r, tree_partner(r, span)) for r in range(n)])  2.74 us
    unnamed x8, local copies, waits for them, and re-layouts  2.18 us
    ppermute x2, starting transfers between devices, levels(): moved = lax.ppermute(message, 'prow', [(r, r ^ other) for r in range(n)])  1.69 us
    ppermute x2, starting transfers between devices, levels(): lax.ppermute(lower, 'prow', [(r, tree_partner(r, span)) for r in range(n)])  1.54 us
    ppermute x1, waiting for transfers between devices, local(): moved = lax.ppermute(gathered, 'prow', twins)  0.62 us
  transfers between devices with their start and end apart: 13, of which 6 were waited for; matrix products, arithmetic and copies ran while one was open for 0% of the time, Pallas kernels for 12%

profile of v12, /device:TPU:0, one launch (start us, length us, event | category | flops | bytes accessed | tf_op | source)
XLA Modules:
  0.0 30.5 jit_solution(4728306499480469945)
XLA Ops:
  0.0 0.9 %copy-done.2 = f32[1024,64]{0,1:T(8,128)S(1)} copy-done((f32[1024,64]{0,1:T(8,128)S(1)}, f32[1024,64]{0,1:T(8,128)}, u32[]{:S(2)}) %copy-start.2) | copy-done | bytes 262168
  1.0 3.1 %collective-permute-start.6 = (f32[64,256]{1,0:T(8,128)S(1)}, f32[64,256]{1,0:T(8,128)S(1)}, u32[]{:S(2)}, u32[]{:S(2)}) collective-permute-start(f32[64,256]{1,0:T(8,128)S(1)} %get-tuple-element.46.refs_0_), channel_id=1, source_target_pairs={{0,1},{1,0},{2,3},{3,2},{4,5},{5,4},{6,7},{7,6},{8,9},{9,8},{10,11... | collective-permute-start | bytes 196616 | tf_op jit(solution)/shard_map/ppermute | solution.py:288
  4.1 2.5 %collective-permute-start.7 = (f32[64,256]{1,0:T(8,128)S(1)}, f32[64,256]{1,0:T(8,128)S(1)}, u32[]{:S(2)}, u32[]{:S(2)}) collective-permute-start(f32[64,256]{1,0:T(8,128)S(1)} %get-tuple-element.46.refs_0_), channel_id=1, source_target_pairs={{0,3},{1,2},{2,1},{3,0},{4,7},{5,6},{6,5},{7,4},{8,11},{9,10},{10,... | collective-permute-start | bytes 196616 | tf_op jit(solution)/shard_map/ppermute | solution.py:288
  6.7 1.8 %collective-permute-start.10 = (f32[64,768]{1,0:T(8,128)S(1)}, f32[64,768]{1,0:T(8,128)S(1)}, u32[]{:S(2)}, u32[]{:S(2)}) collective-permute-start(f32[64,768]{1,0:T(8,128)S(1)} %get-tuple-element.51.refs_4_), channel_id=1, source_target_pairs={{0,1},{1,0},{2,3},{3,2},{4,5},{5,4},{6,7},{7,6},{8,9},{9,8},{10,11... | collective-permute-start | bytes 589832 | tf_op jit(solution)/shard_map/ppermute | solution.py:288
  8.5 1.7 %collective-permute-start.11 = (f32[64,768]{1,0:T(8,128)S(1)}, f32[64,768]{1,0:T(8,128)S(1)}, u32[]{:S(2)}, u32[]{:S(2)}) collective-permute-start(f32[64,768]{1,0:T(8,128)S(1)} %get-tuple-element.51.refs_4_), channel_id=1, source_target_pairs={{0,2},{1,3},{2,0},{3,1},{4,6},{5,7},{6,4},{7,5},{8,10},{9,11},{10,... | collective-permute-start | bytes 589832 | tf_op jit(solution)/shard_map/ppermute | solution.py:288
  10.2 0.9 %collective-permute-start.12 = (f32[64,768]{1,0:T(8,128)S(1)}, f32[64,768]{1,0:T(8,128)S(1)}, u32[]{:S(2)}, u32[]{:S(2)}) collective-permute-start(f32[64,768]{1,0:T(8,128)S(1)} %get-tuple-element.51.refs_4_), channel_id=1, source_target_pairs={{0,3},{1,2},{2,1},{3,0},{4,7},{5,6},{6,5},{7,4},{8,11},{9,10},{10,... | collective-permute-start | bytes 589832 | tf_op jit(solution)/shard_map/ppermute | solution.py:288
  11.1 1.2 %copy-done = f32[1024,256]{1,0:T(8,128)S(1)} copy-done((f32[1024,256]{1,0:T(8,128)S(1)}, f32[1024,256]{1,0:T(8,128)}, u32[]{:S(2)}) %copy-start) | copy-done | bytes 1048600
  12.3 0.7 %shard_map.37 = (f32[32,256]{1,0:T(8,128)S(1)}, f32[256,256]{1,0:T(8,128)S(1)}, s32[1,128]{1,0:T(1,128)S(1)}) custom-call(s32[1,256]{1,0:T(1,128)S(1)} %bitcast.3, f32[1024,256]{1,0:T(8,128)S(1)} %copy-done), custom_call_target="tpu_custom_call" | custom-call | flops 1 | bytes 1 | tf_op jit(solution)/shard_map/pallas_call | solution.py:268
  13.1 0.2 collective-permute-done.8.refs_3_
  13.4 0.6 %collective-permute-start.5 = (f32[128,256]{1,0:T(8,128)S(1)}, f32[128,256]{1,0:T(8,128)S(1)}, u32[]{:S(2)}, u32[]{:S(2)}) collective-permute-start(f32[128,256]{1,0:T(8,128)S(1)} %slice.37), channel_id=1, source_target_pairs={{0,4},{4,0},{8,12},{12,8},{16,20},{20,16},{24,28},{28,24},{1,5},{5... | collective-permute-start | bytes 393224 | tf_op jit(solution)/shard_map/ppermute | solution.py:358
  13.9 0.6 %collective-permute-done.9 = f32[32,256]{1,0:T(8,128)S(1)} collective-permute-done((f32[32,256]{1,0:T(8,128)S(1)}, f32[32,256]{1,0:T(8,128)S(1)}, u32[]{:S(2)}, u32[]{:S(2)}) %collective-permute-start.9) | collective-permute-done | bytes 32800 | tf_op jit(solution)/shard_map/ppermute | solution.py:355
  14.6 0.4 %collective-permute-done.5 = f32[128,256]{1,0:T(8,128)S(1)} collective-permute-done((f32[128,256]{1,0:T(8,128)S(1)}, f32[128,256]{1,0:T(8,128)S(1)}, u32[]{:S(2)}, u32[]{:S(2)}) %collective-permute-start.5) | collective-permute-done | bytes 131104 | tf_op jit(solution)/shard_map/ppermute | solution.py:358
  14.9 13.6 %conditional.1 = (f32[32,256]{1,0:T(8,128)S(1)}, f32[256,256]{1,0:T(8,128)S(1)}) conditional(s32[]{:T(128)} %convert_element_type.3, () %tuple.19, (s32[]{:T(128)}, f32[256,256]{1,0:T(8,128)S(1)}, f32[128,256]{1,0:T(8,128)S(1)}, f32[64,256]{1,0:T(8,128)S(1)}, f32[192,256]{1,0:T(8,128)S(1)}, /*index=5*/s32[1,256]{1,0:T(1,128)S(1)}) %tuple.25), branch_computations={%region_0.1_spmd, %region_1.2_spmd} | conditional | flops 352267 | bytes 6521120 | solution.py:264
  14.9 1.5 %collective-permute-start.1 = (f32[192,256]{1,0:T(8,128)S(1)}, f32[192,256]{1,0:T(8,128)S(1)}, u32[]{:S(2)}, u32[]{:S(2)}) collective-permute-start(f32[192,256]{1,0:T(8,128)S(1)} %get-tuple-element.29.held_ref), channel_id=1, source_target_pairs={{0,16},{4,0},{8,12},{12,8},{16,20},{20,4},{24,28},{28,24},{1,17},{... | collective-permute-start | bytes 589832 | tf_op jit(solution)/shard_map/cond/branch_1_fun/ppermute | solution.py:323
  16.5 0.4 %collective-permute-start = (f32[128,256]{1,0:T(8,128)S(1)}, f32[128,256]{1,0:T(8,128)S(1)}, u32[]{:S(2)}, u32[]{:S(2)}) collective-permute-start(f32[128,256]{1,0:T(8,128)S(1)} %pad_maximum_fusion.2), channel_id=1, source_target_pairs={{0,8},{4,12},{8,0},{12,4},{16,24},{20,28},{24,16},{28,20},{1,9},{5... | collective-permute-start | bytes 393224 | tf_op jit(solution)/shard_map/cond/branch_1_fun/ppermute | solution.py:332
  16.9 2.7 %collective-permute-done.1.moved_ref = f32[192,256]{1,0:T(8,128)S(1)} collective-permute-done((f32[192,256]{1,0:T(8,128)S(1)}, f32[192,256]{1,0:T(8,128)S(1)}, u32[]{:S(2)}, u32[]{:S(2)}) %collective-permute-start.1) | collective-permute-done | bytes 196640 | tf_op jit(solution)/shard_map/cond/branch_1_fun/ppermute | solution.py:323
  19.7 1.9 %collective-permute-done = f32[128,256]{1,0:T(8,128)S(1)} collective-permute-done((f32[128,256]{1,0:T(8,128)S(1)}, f32[128,256]{1,0:T(8,128)S(1)}, u32[]{:S(2)}, u32[]{:S(2)}) %collective-permute-start) | collective-permute-done | bytes 131104 | tf_op jit(solution)/shard_map/cond/branch_1_fun/ppermute | solution.py:332
  21.6 1.3 %collective-permute-start.2 = (f32[160,256]{1,0:T(8,128)S(1)}, f32[160,256]{1,0:T(8,128)S(1)}, u32[]{:S(2)}, u32[]{:S(2)}) collective-permute-start(f32[160,256]{1,0:T(8,128)S(1)} %pad_maximum_fusion.1), channel_id=1, source_target_pairs={{0,16},{4,20},{8,24},{12,28},{16,0},{20,4},{24,8},{28,12},{1,17},{... | collective-permute-start | bytes 491528 | tf_op jit(solution)/shard_map/cond/branch_1_fun/ppermute | solution.py:332
  22.9 1.8 %branch_1_fun.7 = f32[192,256]{1,0:T(8,128)S(1)} custom-call(f32[192,256]{1,0:T(8,128)S(1)} %branch_1_fun.6.lower_ref), custom_call_target="tpu_custom_call" | custom-call | flops 1 | bytes 1 | tf_op jit(solution)/shard_map/cond/branch_1_fun/pallas_call | solution.py:268
  24.7 0.4 %collective-permute-start.4 = (f32[192,256]{1,0:T(8,128)S(1)}, f32[192,256]{1,0:T(8,128)S(1)}, u32[]{:S(2)}, u32[]{:S(2)}) collective-permute-start(f32[192,256]{1,0:T(8,128)S(1)} %branch_1_fun.7), channel_id=1, source_target_pairs={{0,4},{4,0},{8,12},{12,8},{16,20},{20,16},{24,28},{28,24},{1,5},{5... | collective-permute-start | bytes 589832 | tf_op jit(solution)/shard_map/cond/branch_1_fun/ppermute | solution.py:349
  25.1 2.1 %collective-permute-done.2 = f32[160,256]{1,0:T(8,128)S(1)} collective-permute-done((f32[160,256]{1,0:T(8,128)S(1)}, f32[160,256]{1,0:T(8,128)S(1)}, u32[]{:S(2)}, u32[]{:S(2)}) %collective-permute-start.2) | collective-permute-done | bytes 163872 | tf_op jit(solution)/shard_map/cond/branch_1_fun/ppermute | solution.py:332
  27.2 0.5 %branch_1_fun.8.pivot_rows_ref = f32[256,256]{1,0:T(8,128)S(1)} custom-call(s32[1,256]{1,0:T(1,128)S(1)} %get-tuple-element.33.pivot_ref, f32[256,256]{1,0:T(8,128)S(1)} %pad_maximum_fusion.gathered_ref), custom_call_target="tpu_custom_call" | custom-call | flops 1 | bytes 1 | tf_op jit(solution)/shard_map/cond/branch_1_fun/pallas_call | solution.py:268
  27.8 0.7 %branch_1_fun.9 = f32[256,256]{1,0:T(8,128)S(1)} custom-call(f32[192,256]{1,0:T(8,128)S(1)} %broadcast_select_fusion.inverse_ref, f32[256,256]{1,0:T(8,128)S(1)} %branch_1_fun.8.pivot_rows_ref), custom_call_target="tpu_custom_call" | custom-call | flops 1 | bytes 1 | tf_op jit(solution)/shard_map/cond/branch_1_fun/pallas_call | solution.py:268
  28.5 2.0 %shard_map.40 = f32[1024,256]{1,0:T(8,128)} custom-call(s32[1,128]{1,0:T(1,128)S(1)} %get-tuple-element.43.local_ref, f32[32,256]{1,0:T(8,128)S(1)} %get-tuple-element.49.lead_ref, f32[256,256]{1,0:T(8,128)S(1)} %get-tuple-element.50.x_ref, f32[1024,256]{1,0:T(8,128)S(1)} %copy-done.1, f32[64,256]{1,0:T(8,128)S(1)} %get-tuple-element.46.refs_0_, ...), custom_call_target="tpu_custom_call" | custom-call | flops 1 | bytes 1 | tf_op jit(solution)/shard_map/pallas_call | solution.py:268
  (32 shorter events, 0.5 us)
Async XLA Ops:
  0.0 0.9 %copy-start.2 = (f32[1024,64]{0,1:T(8,128)S(1)}, f32[1024,64]{0,1:T(8,128)}, u32[]{:S(2)}) copy-start(f32[1024,64]{0,1:T(8,128)} %param.6) | copy-start | bytes 786436
  1.0 9.2 %collective-permute-start.6 = (f32[64,256]{1,0:T(8,128)S(1)}, f32[64,256]{1,0:T(8,128)S(1)}, u32[]{:S(2)}, u32[]{:S(2)}) collective-permute-start(f32[64,256]{1,0:T(8,128)S(1)} %get-tuple-element.46.refs_0_), channel_id=1, source_target_pairs={{0,1},{1,0},{2,3},{3,2},{4,5},{5,4},{6,7},{7,6},{8,9},{9,8},{10,11... | collective-permute-start | bytes 196616 | tf_op jit(solution)/shard_map/ppermute | solution.py:288
  4.1 8.9 %collective-permute-start.7 = (f32[64,256]{1,0:T(8,128)S(1)}, f32[64,256]{1,0:T(8,128)S(1)}, u32[]{:S(2)}, u32[]{:S(2)}) collective-permute-start(f32[64,256]{1,0:T(8,128)S(1)} %get-tuple-element.46.refs_0_), channel_id=1, source_target_pairs={{0,3},{1,2},{2,1},{3,0},{4,7},{5,6},{6,5},{7,4},{8,11},{9,10},{10,... | collective-permute-start | bytes 196616 | tf_op jit(solution)/shard_map/ppermute | solution.py:288
  6.6 6.6 %collective-permute-start.8 = (f32[64,256]{1,0:T(8,128)S(1)}, f32[64,256]{1,0:T(8,128)S(1)}, u32[]{:S(2)}, u32[]{:S(2)}) collective-permute-start(f32[64,256]{1,0:T(8,128)S(1)} %get-tuple-element.46.refs_0_), channel_id=1, source_target_pairs={{0,2},{1,3},{2,0},{3,1},{4,6},{5,7},{6,4},{7,5},{8,10},{9,11},{10,... | collective-permute-start | bytes 196616 | tf_op jit(solution)/shard_map/ppermute | solution.py:288
  6.7 4.4 %copy-start.3 = (s32[256]{0:T(256)S(1)}, s32[256]{0:T(256)}, u32[]{:S(2)}) copy-start(s32[256]{0:T(256)} %param.7) | copy-start | bytes 3076
  6.7 21.8 %collective-permute-start.10 = (f32[64,768]{1,0:T(8,128)S(1)}, f32[64,768]{1,0:T(8,128)S(1)}, u32[]{:S(2)}, u32[]{:S(2)}) collective-permute-start(f32[64,768]{1,0:T(8,128)S(1)} %get-tuple-element.51.refs_4_), channel_id=1, source_target_pairs={{0,1},{1,0},{2,3},{3,2},{4,5},{5,4},{6,7},{7,6},{8,9},{9,8},{10,11... | collective-permute-start | bytes 589832 | tf_op jit(solution)/shard_map/ppermute | solution.py:288
  8.5 20.0 %collective-permute-start.11 = (f32[64,768]{1,0:T(8,128)S(1)}, f32[64,768]{1,0:T(8,128)S(1)}, u32[]{:S(2)}, u32[]{:S(2)}) collective-permute-start(f32[64,768]{1,0:T(8,128)S(1)} %get-tuple-element.51.refs_4_), channel_id=1, source_target_pairs={{0,2},{1,3},{2,0},{3,1},{4,6},{5,7},{6,4},{7,5},{8,10},{9,11},{10,... | collective-permute-start | bytes 589832 | tf_op jit(solution)/shard_map/ppermute | solution.py:288
  10.2 18.3 %collective-permute-start.12 = (f32[64,768]{1,0:T(8,128)S(1)}, f32[64,768]{1,0:T(8,128)S(1)}, u32[]{:S(2)}, u32[]{:S(2)}) collective-permute-start(f32[64,768]{1,0:T(8,128)S(1)} %get-tuple-element.51.refs_4_), channel_id=1, source_target_pairs={{0,3},{1,2},{2,1},{3,0},{4,7},{5,6},{6,5},{7,4},{8,11},{9,10},{10,... | collective-permute-start | bytes 589832 | tf_op jit(solution)/shard_map/ppermute | solution.py:288
  11.1 1.2 %copy-start = (f32[1024,256]{1,0:T(8,128)S(1)}, f32[1024,256]{1,0:T(8,128)}, u32[]{:S(2)}) copy-start(f32[1024,256]{1,0:T(8,128)} %slab_ref.3) | copy-start | bytes 3145732
  13.3 1.3 %collective-permute-start.9 = (f32[32,256]{1,0:T(8,128)S(1)}, f32[32,256]{1,0:T(8,128)S(1)}, u32[]{:S(2)}, u32[]{:S(2)}) collective-permute-start(f32[32,256]{1,0:T(8,128)S(1)} %get-tuple-element.47), channel_id=1, source_target_pairs={{0,4},{4,0},{8,12},{12,8},{16,20},{20,16},{24,28},{28,24},{1,5},{5... | collective-permute-start | bytes 98312 | tf_op jit(solution)/shard_map/ppermute | solution.py:355
  13.4 1.5 %collective-permute-start.5 = (f32[128,256]{1,0:T(8,128)S(1)}, f32[128,256]{1,0:T(8,128)S(1)}, u32[]{:S(2)}, u32[]{:S(2)}) collective-permute-start(f32[128,256]{1,0:T(8,128)S(1)} %slice.37), channel_id=1, source_target_pairs={{0,4},{4,0},{8,12},{12,8},{16,20},{20,16},{24,28},{28,24},{1,5},{5... | collective-permute-start | bytes 393224 | tf_op jit(solution)/shard_map/ppermute | solution.py:358
  14.9 13.6 %copy-start.1 = (f32[1024,256]{1,0:T(8,128)S(1)}, f32[1024,256]{1,0:T(8,128)}, u32[]{:S(2)}) copy-start(f32[1024,256]{1,0:T(8,128)} %slab_ref.3) | copy-start | bytes 3145732
  14.9 4.7 %collective-permute-start.1 = (f32[192,256]{1,0:T(8,128)S(1)}, f32[192,256]{1,0:T(8,128)S(1)}, u32[]{:S(2)}, u32[]{:S(2)}) collective-permute-start(f32[192,256]{1,0:T(8,128)S(1)} %get-tuple-element.29.held_ref), channel_id=1, source_target_pairs={{0,16},{4,0},{8,12},{12,8},{16,20},{20,4},{24,28},{28,24},{1,17},{... | collective-permute-start | bytes 589832 | tf_op jit(solution)/shard_map/cond/branch_1_fun/ppermute | solution.py:323
  16.5 5.0 %collective-permute-start = (f32[128,256]{1,0:T(8,128)S(1)}, f32[128,256]{1,0:T(8,128)S(1)}, u32[]{:S(2)}, u32[]{:S(2)}) collective-permute-start(f32[128,256]{1,0:T(8,128)S(1)} %pad_maximum_fusion.2), channel_id=1, source_target_pairs={{0,8},{4,12},{8,0},{12,4},{16,24},{20,28},{24,16},{28,20},{1,9},{5... | collective-permute-start | bytes 393224 | tf_op jit(solution)/shard_map/cond/branch_1_fun/ppermute | solution.py:332
  19.6 3.2 %collective-permute-start.3 = (f32[192,256]{1,0:T(8,128)S(1)}, f32[192,256]{1,0:T(8,128)S(1)}, u32[]{:S(2)}, u32[]{:S(2)}) collective-permute-start(f32[192,256]{1,0:T(8,128)S(1)} %branch_1_fun.5.held_ref), channel_id=1, source_target_pairs={{0,8},{4,0},{8,12},{12,4},{16,24},{20,16},{24,28},{28,20},{1,9},{5... | collective-permute-start | bytes 589832 | tf_op jit(solution)/shard_map/cond/branch_1_fun/ppermute | solution.py:323
  21.6 5.6 %collective-permute-start.2 = (f32[160,256]{1,0:T(8,128)S(1)}, f32[160,256]{1,0:T(8,128)S(1)}, u32[]{:S(2)}, u32[]{:S(2)}) collective-permute-start(f32[160,256]{1,0:T(8,128)S(1)} %pad_maximum_fusion.1), channel_id=1, source_target_pairs={{0,16},{4,20},{8,24},{12,28},{16,0},{20,4},{24,8},{28,12},{1,17},{... | collective-permute-start | bytes 491528 | tf_op jit(solution)/shard_map/cond/branch_1_fun/ppermute | solution.py:332
  24.7 3.0 %collective-permute-start.4 = (f32[192,256]{1,0:T(8,128)S(1)}, f32[192,256]{1,0:T(8,128)S(1)}, u32[]{:S(2)}, u32[]{:S(2)}) collective-permute-start(f32[192,256]{1,0:T(8,128)S(1)} %branch_1_fun.7), channel_id=1, source_target_pairs={{0,4},{4,0},{8,12},{12,8},{16,20},{20,16},{24,28},{28,24},{1,5},{5... | collective-permute-start | bytes 589832 | tf_op jit(solution)/shard_map/cond/branch_1_fun/ppermute | solution.py:349

commit v13 on v12

--- a/solution.py
+++ b/solution.py
@@ -113,16 +113,14 @@
     return outs
 
 
-def order_kernel(n, rows, pivot_ref, gathered_ref, out_ref, gathered):
-    width = pivot_ref.shape[1]
-    me = lax.axis_index("prow")
-    for q in range(n):
-        source = jnp.bitwise_xor(me, q)
-        gathered[pl.ds(pl.multiple_of(source * CAP, CAP), CAP), :] = gathered_ref[q * CAP : (q + 1) * CAP, :]
+def choice_kernel(n, rows, pivot_ref, out_ref):
     _, _, owner_col, rank_col = slots(pivot_ref[...], rows)
-    slot = lax.broadcasted_iota(jnp.int32, (width, gathered.shape[0]), 1)
-    one_hot = (slot == owner_col * CAP + rank_col).astype(F32).astype(BF16)
-    out_ref[...] = select_rows(one_hot, gathered[...])
+    place = jnp.bitwise_xor(owner_col, lax.axis_index("prow")) * CAP + rank_col
+    out_ref[...] = (lax.broadcasted_iota(jnp.int32, out_ref.shape, 1) == place).astype(F32).astype(BF16)
+
+
+def order_kernel(choice_ref, gathered_ref, out_ref):
+    out_ref[...] = select_rows(choice_ref[...], gathered_ref[...])
 
 
 def top_order(m):
@@ -334,12 +332,10 @@
             gathered = jnp.concatenate([gathered, moved[:count]], axis=0)
             leading = jnp.where(me & other != 0, moved[count:], kept)
             span, other = span // 2, other * 2
-        pivot_rows = call(
-            functools.partial(order_kernel, n, rows),
-            jax.ShapeDtypeStruct((width, cols), F32),
-            (pivot_row, gathered),
-            scratch=[pltpu.VMEM((n * CAP, cols), F32)],
+        choice = call(
+            functools.partial(choice_kernel, n, rows), jax.ShapeDtypeStruct((width, n * CAP), BF16), (pivot_row,)
         )
+        pivot_rows = call(order_kernel, jax.ShapeDtypeStruct((width, cols), F32), (choice, gathered))
         inverse = call(
             invert_kernel,
             jax.ShapeDtypeStruct(lower.shape, F32),

time: 30.7 us -> 31.9 us (1.039)
  Pallas kernels: 5.87 us -> 6.65 us
  other arithmetic: 0.12 us -> 0.73 us
    pallas_call x9 -> x10, Pallas kernels: 5.87 us -> 6.65 us  [call(): pl.pallas_call(kernel, out_shape=outs, in_specs=in_specs or [VMEM] * len(...]
    select_n x1, other arithmetic: 0.01 us -> 0.62 us  [levels(): leading = jnp.where(me & other != 0, moved[count:], kept)]
  transfers between devices with their start and end apart: 13 -> 13, of which waited for: 6 -> 6; matrix products, arithmetic and copies ran while one was open for 0% -> 2% of each run, Pallas kernels for 12% -> 12%
where the time goes in v13:
time: 31.9 us; the launch traced here: 31.6 us
  starting transfers between devices  14.3 us (45%)
  waiting for transfers between devices  7.55 us (24%)
  Pallas kernels  6.65 us (21%)
  local copies, waits for them, and re-layouts  2.21 us (7%)
  other arithmetic  0.73 us (2%)
    ppermute x6, starting transfers between devices, exchange(): return lax.ppermute(block, 'pcol', [(c, c ^ d) for c in range(m)])  10.1 us
    pallas_call x10, Pallas kernels, call(): pl.pallas_call(kernel, out_shape=outs, in_specs=in_specs or [VMEM] * len(...  6.65 us
    ppermute x2, waiting for transfers between devices, levels(): moved = lax.ppermute(message, 'prow', [(r, r ^ other) for r in range(n)])  3.63 us
    ppermute x2, waiting for transfers between devices, levels(): lax.ppermute(lower, 'prow', [(r, tree_partner(r, span)) for r in range(n)])  2.74 us
    unnamed x8, local copies, waits for them, and re-layouts  2.18 us
    ppermute x2, starting transfers between devices, levels(): moved = lax.ppermute(message, 'prow', [(r, r ^ other) for r in range(n)])  1.7 us
    ppermute x2, starting transfers between devices, levels(): lax.ppermute(lower, 'prow', [(r, tree_partner(r, span)) for r in range(n)])  1.54 us
  transfers between devices with their start and end apart: 13, of which 6 were waited for; matrix products, arithmetic and copies ran while one was open for 2% of the time, Pallas kernels for 12%

profile of v13, /device:TPU:0, one launch (start us, length us, event | category | flops | bytes accessed | tf_op | source)
XLA Modules:
  0.0 31.6 jit_solution(18034018232414200487)
XLA Ops:
  0.0 0.9 %copy-done.2 = f32[1024,64]{0,1:T(8,128)S(1)} copy-done((f32[1024,64]{0,1:T(8,128)S(1)}, f32[1024,64]{0,1:T(8,128)}, u32[]{:S(2)}) %copy-start.2) | copy-done | bytes 262168
  1.0 3.1 %collective-permute-start.6 = (f32[64,256]{1,0:T(8,128)S(1)}, f32[64,256]{1,0:T(8,128)S(1)}, u32[]{:S(2)}, u32[]{:S(2)}) collective-permute-start(f32[64,256]{1,0:T(8,128)S(1)} %get-tuple-element.46.refs_0_), channel_id=1, source_target_pairs={{0,1},{1,0},{2,3},{3,2},{4,5},{5,4},{6,7},{7,6},{8,9},{9,8},{10,11... | collective-permute-start | bytes 196616 | tf_op jit(solution)/shard_map/ppermute | solution.py:286
  4.1 2.5 %collective-permute-start.7 = (f32[64,256]{1,0:T(8,128)S(1)}, f32[64,256]{1,0:T(8,128)S(1)}, u32[]{:S(2)}, u32[]{:S(2)}) collective-permute-start(f32[64,256]{1,0:T(8,128)S(1)} %get-tuple-element.46.refs_0_), channel_id=1, source_target_pairs={{0,3},{1,2},{2,1},{3,0},{4,7},{5,6},{6,5},{7,4},{8,11},{9,10},{10,... | collective-permute-start | bytes 196616 | tf_op jit(solution)/shard_map/ppermute | solution.py:286
  6.7 1.8 %collective-permute-start.10 = (f32[64,768]{1,0:T(8,128)S(1)}, f32[64,768]{1,0:T(8,128)S(1)}, u32[]{:S(2)}, u32[]{:S(2)}) collective-permute-start(f32[64,768]{1,0:T(8,128)S(1)} %get-tuple-element.51.refs_4_), channel_id=1, source_target_pairs={{0,1},{1,0},{2,3},{3,2},{4,5},{5,4},{6,7},{7,6},{8,9},{9,8},{10,11... | collective-permute-start | bytes 589832 | tf_op jit(solution)/shard_map/ppermute | solution.py:286
  8.5 1.7 %collective-permute-start.11 = (f32[64,768]{1,0:T(8,128)S(1)}, f32[64,768]{1,0:T(8,128)S(1)}, u32[]{:S(2)}, u32[]{:S(2)}) collective-permute-start(f32[64,768]{1,0:T(8,128)S(1)} %get-tuple-element.51.refs_4_), channel_id=1, source_target_pairs={{0,2},{1,3},{2,0},{3,1},{4,6},{5,7},{6,4},{7,5},{8,10},{9,11},{10,... | collective-permute-start | bytes 589832 | tf_op jit(solution)/shard_map/ppermute | solution.py:286
  10.2 0.9 %collective-permute-start.12 = (f32[64,768]{1,0:T(8,128)S(1)}, f32[64,768]{1,0:T(8,128)S(1)}, u32[]{:S(2)}, u32[]{:S(2)}) collective-permute-start(f32[64,768]{1,0:T(8,128)S(1)} %get-tuple-element.51.refs_4_), channel_id=1, source_target_pairs={{0,3},{1,2},{2,1},{3,0},{4,7},{5,6},{6,5},{7,4},{8,11},{9,10},{10,... | collective-permute-start | bytes 589832 | tf_op jit(solution)/shard_map/ppermute | solution.py:286
  11.1 1.2 %copy-done = f32[1024,256]{1,0:T(8,128)S(1)} copy-done((f32[1024,256]{1,0:T(8,128)S(1)}, f32[1024,256]{1,0:T(8,128)}, u32[]{:S(2)}) %copy-start) | copy-done | bytes 1048600
  12.3 0.7 %shard_map.37 = (f32[32,256]{1,0:T(8,128)S(1)}, f32[256,256]{1,0:T(8,128)S(1)}, s32[1,128]{1,0:T(1,128)S(1)}) custom-call(s32[1,256]{1,0:T(1,128)S(1)} %bitcast.3, f32[1024,256]{1,0:T(8,128)S(1)} %copy-done), custom_call_target="tpu_custom_call" | custom-call | flops 1 | bytes 1 | tf_op jit(solution)/shard_map/pallas_call | solution.py:266
  13.4 0.6 %collective-permute-start.5 = (f32[128,256]{1,0:T(8,128)S(1)}, f32[128,256]{1,0:T(8,128)S(1)}, u32[]{:S(2)}, u32[]{:S(2)}) collective-permute-start(f32[128,256]{1,0:T(8,128)S(1)} %slice.37), channel_id=1, source_target_pairs={{0,4},{4,0},{8,12},{12,8},{16,20},{20,16},{24,28},{28,24},{1,5},{5... | collective-permute-start | bytes 393224 | tf_op jit(solution)/shard_map/ppermute | solution.py:354
  13.9 0.6 %collective-permute-done.9 = f32[32,256]{1,0:T(8,128)S(1)} collective-permute-done((f32[32,256]{1,0:T(8,128)S(1)}, f32[32,256]{1,0:T(8,128)S(1)}, u32[]{:S(2)}, u32[]{:S(2)}) %collective-permute-start.9) | collective-permute-done | bytes 32800 | tf_op jit(solution)/shard_map/ppermute | solution.py:351
  14.6 0.4 %collective-permute-done.5 = f32[128,256]{1,0:T(8,128)S(1)} collective-permute-done((f32[128,256]{1,0:T(8,128)S(1)}, f32[128,256]{1,0:T(8,128)S(1)}, u32[]{:S(2)}, u32[]{:S(2)}) %collective-permute-start.5) | collective-permute-done | bytes 131104 | tf_op jit(solution)/shard_map/ppermute | solution.py:354
  14.9 13.9 %conditional.1 = (f32[32,256]{1,0:T(8,128)}, f32[256,256]{1,0:T(8,128)S(1)}) conditional(s32[]{:T(128)} %convert_element_type.3, () %tuple.19, (s32[]{:T(128)}, f32[256,256]{1,0:T(8,128)S(1)}, f32[128,256]{1,0:T(8,128)S(1)}, f32[64,256]{1,0:T(8,128)S(1)}, f32[192,256]{1,0:T(8,128)S(1)}, /*index=5*/s32[1,256]{1,0:T(1,128)S(1)}) %tuple.25), branch_computations={%region_0.1_spmd, %region_1.2_spmd} | conditional | flops 352268 | bytes 6521121 | solution.py:262
  14.9 1.5 %collective-permute-start.1 = (f32[192,256]{1,0:T(8,128)S(1)}, f32[192,256]{1,0:T(8,128)S(1)}, u32[]{:S(2)}, u32[]{:S(2)}) collective-permute-start(f32[192,256]{1,0:T(8,128)S(1)} %get-tuple-element.29.held_ref), channel_id=1, source_target_pairs={{0,16},{4,0},{8,12},{12,8},{16,20},{20,4},{24,28},{28,24},{1,17},{... | collective-permute-start | bytes 589832 | tf_op jit(solution)/shard_map/cond/branch_1_fun/ppermute | solution.py:321
  16.5 0.4 %collective-permute-start = (f32[128,256]{1,0:T(8,128)S(1)}, f32[128,256]{1,0:T(8,128)S(1)}, u32[]{:S(2)}, u32[]{:S(2)}) collective-permute-start(f32[128,256]{1,0:T(8,128)S(1)} %pad_maximum_fusion.2), channel_id=1, source_target_pairs={{0,8},{4,12},{8,0},{12,4},{16,24},{20,28},{24,16},{28,20},{1,9},{5... | collective-permute-start | bytes 393224 | tf_op jit(solution)/shard_map/cond/branch_1_fun/ppermute | solution.py:330
  16.9 2.7 %collective-permute-done.1.moved_ref = f32[192,256]{1,0:T(8,128)S(1)} collective-permute-done((f32[192,256]{1,0:T(8,128)S(1)}, f32[192,256]{1,0:T(8,128)S(1)}, u32[]{:S(2)}, u32[]{:S(2)}) %collective-permute-start.1) | collective-permute-done | bytes 196640 | tf_op jit(solution)/shard_map/cond/branch_1_fun/ppermute | solution.py:321
  19.7 1.9 %collective-permute-done = f32[128,256]{1,0:T(8,128)S(1)} collective-permute-done((f32[128,256]{1,0:T(8,128)S(1)}, f32[128,256]{1,0:T(8,128)S(1)}, u32[]{:S(2)}, u32[]{:S(2)}) %collective-permute-start) | collective-permute-done | bytes 131104 | tf_op jit(solution)/shard_map/cond/branch_1_fun/ppermute | solution.py:330
  21.6 1.3 %collective-permute-start.2 = (f32[160,256]{1,0:T(8,128)S(1)}, f32[160,256]{1,0:T(8,128)S(1)}, u32[]{:S(2)}, u32[]{:S(2)}) collective-permute-start(f32[160,256]{1,0:T(8,128)S(1)} %pad_maximum_fusion.1), channel_id=1, source_target_pairs={{0,16},{4,20},{8,24},{12,28},{16,0},{20,4},{24,8},{28,12},{1,17},{... | collective-permute-start | bytes 491528 | tf_op jit(solution)/shard_map/cond/branch_1_fun/ppermute | solution.py:330
  22.9 1.8 %branch_1_fun.8 = f32[192,256]{1,0:T(8,128)S(1)} custom-call(f32[192,256]{1,0:T(8,128)S(1)} %branch_1_fun.7.lower_ref), custom_call_target="tpu_custom_call" | custom-call | flops 1 | bytes 1 | tf_op jit(solution)/shard_map/cond/branch_1_fun/pallas_call | solution.py:266
  24.7 0.3 %collective-permute-start.4 = (f32[192,256]{1,0:T(8,128)S(1)}, f32[192,256]{1,0:T(8,128)S(1)}, u32[]{:S(2)}, u32[]{:S(2)}) collective-permute-start(f32[192,256]{1,0:T(8,128)S(1)} %branch_1_fun.8), channel_id=1, source_target_pairs={{0,4},{4,0},{8,12},{12,8},{16,20},{20,16},{24,28},{28,24},{1,5},{5... | collective-permute-start | bytes 589832 | tf_op jit(solution)/shard_map/cond/branch_1_fun/ppermute | solution.py:345
  25.1 0.3 branch_1_fun.9.choice_ref
  25.4 1.8 %collective-permute-done.2 = f32[160,256]{1,0:T(8,128)S(1)} collective-permute-done((f32[160,256]{1,0:T(8,128)S(1)}, f32[160,256]{1,0:T(8,128)S(1)}, u32[]{:S(2)}, u32[]{:S(2)}) %collective-permute-start.2) | collective-permute-done | bytes 163872 | tf_op jit(solution)/shard_map/cond/branch_1_fun/ppermute | solution.py:330
  27.5 0.6 %slice_select_fusion.2 = f32[32,256]{1,0:T(8,128)} fusion(f32[64,256]{1,0:T(8,128)S(1)} %get-tuple-element.53, f32[160,256]{1,0:T(8,128)S(1)} %collective-permute-done.2, pred[]{:T(512)S(6)} %ne.9), kind=kLoop, calls=%fused_computation.6 | loop fusion | flops 8192 | bytes 98305 | tf_op jit(solution)/shard_map/cond/branch_1_fun/jit(_where)/select_n | solution.py:333
  28.1 0.7 %branch_1_fun.11 = f32[256,256]{1,0:T(8,128)S(1)} custom-call(f32[192,256]{1,0:T(8,128)S(1)} %broadcast_select_fusion.inverse_ref, f32[256,256]{1,0:T(8,128)S(1)} %branch_1_fun.10.pivot_rows_ref), custom_call_target="tpu_custom_call" | custom-call | flops 1 | bytes 1 | tf_op jit(solution)/shard_map/cond/branch_1_fun/pallas_call | solution.py:266
  28.9 2.7 %shard_map.40 = f32[1024,256]{1,0:T(8,128)} custom-call(s32[1,128]{1,0:T(1,128)S(1)} %get-tuple-element.43.local_ref, f32[32,256]{1,0:T(8,128)} %get-tuple-element.49.lead_ref, f32[256,256]{1,0:T(8,128)S(1)} %get-tuple-element.50.x_ref, f32[1024,256]{1,0:T(8,128)S(1)} %copy-done.1, f32[64,256]{1,0:T(8,128)S(1)} %get-tuple-element.46.refs_0_, ...), custom_call_target="tpu_custom_call" | custom-call | flops 1 | bytes 1 | tf_op jit(solution)/shard_map/pallas_call | solution.py:266
  (33 shorter events, 1.0 us)
Async XLA Ops:
  0.0 0.9 %copy-start.2 = (f32[1024,64]{0,1:T(8,128)S(1)}, f32[1024,64]{0,1:T(8,128)}, u32[]{:S(2)}) copy-start(f32[1024,64]{0,1:T(8,128)} %param.6) | copy-start | bytes 786436
  1.0 9.2 %collective-permute-start.6 = (f32[64,256]{1,0:T(8,128)S(1)}, f32[64,256]{1,0:T(8,128)S(1)}, u32[]{:S(2)}, u32[]{:S(2)}) collective-permute-start(f32[64,256]{1,0:T(8,128)S(1)} %get-tuple-element.46.refs_0_), channel_id=1, source_target_pairs={{0,1},{1,0},{2,3},{3,2},{4,5},{5,4},{6,7},{7,6},{8,9},{9,8},{10,11... | collective-permute-start | bytes 196616 | tf_op jit(solution)/shard_map/ppermute | solution.py:286
  4.1 8.9 %collective-permute-start.7 = (f32[64,256]{1,0:T(8,128)S(1)}, f32[64,256]{1,0:T(8,128)S(1)}, u32[]{:S(2)}, u32[]{:S(2)}) collective-permute-start(f32[64,256]{1,0:T(8,128)S(1)} %get-tuple-element.46.refs_0_), channel_id=1, source_target_pairs={{0,3},{1,2},{2,1},{3,0},{4,7},{5,6},{6,5},{7,4},{8,11},{9,10},{10,... | collective-permute-start | bytes 196616 | tf_op jit(solution)/shard_map/ppermute | solution.py:286
  6.6 6.6 %collective-permute-start.8 = (f32[64,256]{1,0:T(8,128)S(1)}, f32[64,256]{1,0:T(8,128)S(1)}, u32[]{:S(2)}, u32[]{:S(2)}) collective-permute-start(f32[64,256]{1,0:T(8,128)S(1)} %get-tuple-element.46.refs_0_), channel_id=1, source_target_pairs={{0,2},{1,3},{2,0},{3,1},{4,6},{5,7},{6,4},{7,5},{8,10},{9,11},{10,... | collective-permute-start | bytes 196616 | tf_op jit(solution)/shard_map/ppermute | solution.py:286
  6.7 4.4 %copy-start.3 = (s32[256]{0:T(256)S(1)}, s32[256]{0:T(256)}, u32[]{:S(2)}) copy-start(s32[256]{0:T(256)} %param.7) | copy-start | bytes 3076
  6.7 22.1 %collective-permute-start.10 = (f32[64,768]{1,0:T(8,128)S(1)}, f32[64,768]{1,0:T(8,128)S(1)}, u32[]{:S(2)}, u32[]{:S(2)}) collective-permute-start(f32[64,768]{1,0:T(8,128)S(1)} %get-tuple-element.51.refs_4_), channel_id=1, source_target_pairs={{0,1},{1,0},{2,3},{3,2},{4,5},{5,4},{6,7},{7,6},{8,9},{9,8},{10,11... | collective-permute-start | bytes 589832 | tf_op jit(solution)/shard_map/ppermute | solution.py:286
  8.5 20.3 %collective-permute-start.11 = (f32[64,768]{1,0:T(8,128)S(1)}, f32[64,768]{1,0:T(8,128)S(1)}, u32[]{:S(2)}, u32[]{:S(2)}) collective-permute-start(f32[64,768]{1,0:T(8,128)S(1)} %get-tuple-element.51.refs_4_), channel_id=1, source_target_pairs={{0,2},{1,3},{2,0},{3,1},{4,6},{5,7},{6,4},{7,5},{8,10},{9,11},{10,... | collective-permute-start | bytes 589832 | tf_op jit(solution)/shard_map/ppermute | solution.py:286
  10.2 18.6 %collective-permute-start.12 = (f32[64,768]{1,0:T(8,128)S(1)}, f32[64,768]{1,0:T(8,128)S(1)}, u32[]{:S(2)}, u32[]{:S(2)}) collective-permute-start(f32[64,768]{1,0:T(8,128)S(1)} %get-tuple-element.51.refs_4_), channel_id=1, source_target_pairs={{0,3},{1,2},{2,1},{3,0},{4,7},{5,6},{6,5},{7,4},{8,11},{9,10},{10,... | collective-permute-start | bytes 589832 | tf_op jit(solution)/shard_map/ppermute | solution.py:286
  11.1 1.2 %copy-start = (f32[1024,256]{1,0:T(8,128)S(1)}, f32[1024,256]{1,0:T(8,128)}, u32[]{:S(2)}) copy-start(f32[1024,256]{1,0:T(8,128)} %slab_ref.3) | copy-start | bytes 3145732
  13.3 1.3 %collective-permute-start.9 = (f32[32,256]{1,0:T(8,128)S(1)}, f32[32,256]{1,0:T(8,128)S(1)}, u32[]{:S(2)}, u32[]{:S(2)}) collective-permute-start(f32[32,256]{1,0:T(8,128)S(1)} %get-tuple-element.47), channel_id=1, source_target_pairs={{0,4},{4,0},{8,12},{12,8},{16,20},{20,16},{24,28},{28,24},{1,5},{5... | collective-permute-start | bytes 98312 | tf_op jit(solution)/shard_map/ppermute | solution.py:351
  13.4 1.5 %collective-permute-start.5 = (f32[128,256]{1,0:T(8,128)S(1)}, f32[128,256]{1,0:T(8,128)S(1)}, u32[]{:S(2)}, u32[]{:S(2)}) collective-permute-start(f32[128,256]{1,0:T(8,128)S(1)} %slice.37), channel_id=1, source_target_pairs={{0,4},{4,0},{8,12},{12,8},{16,20},{20,16},{24,28},{28,24},{1,5},{5... | collective-permute-start | bytes 393224 | tf_op jit(solution)/shard_map/ppermute | solution.py:354
  14.9 14.0 %copy-start.1 = (f32[1024,256]{1,0:T(8,128)S(1)}, f32[1024,256]{1,0:T(8,128)}, u32[]{:S(2)}) copy-start(f32[1024,256]{1,0:T(8,128)} %slab_ref.3) | copy-start | bytes 3145732
  14.9 4.7 %collective-permute-start.1 = (f32[192,256]{1,0:T(8,128)S(1)}, f32[192,256]{1,0:T(8,128)S(1)}, u32[]{:S(2)}, u32[]{:S(2)}) collective-permute-start(f32[192,256]{1,0:T(8,128)S(1)} %get-tuple-element.29.held_ref), channel_id=1, source_target_pairs={{0,16},{4,0},{8,12},{12,8},{16,20},{20,4},{24,28},{28,24},{1,17},{... | collective-permute-start | bytes 589832 | tf_op jit(solution)/shard_map/cond/branch_1_fun/ppermute | solution.py:321
  16.5 5.0 %collective-permute-start = (f32[128,256]{1,0:T(8,128)S(1)}, f32[128,256]{1,0:T(8,128)S(1)}, u32[]{:S(2)}, u32[]{:S(2)}) collective-permute-start(f32[128,256]{1,0:T(8,128)S(1)} %pad_maximum_fusion.2), channel_id=1, source_target_pairs={{0,8},{4,12},{8,0},{12,4},{16,24},{20,28},{24,16},{28,20},{1,9},{5... | collective-permute-start | bytes 393224 | tf_op jit(solution)/shard_map/cond/branch_1_fun/ppermute | solution.py:330
  19.6 3.2 %collective-permute-start.3 = (f32[192,256]{1,0:T(8,128)S(1)}, f32[192,256]{1,0:T(8,128)S(1)}, u32[]{:S(2)}, u32[]{:S(2)}) collective-permute-start(f32[192,256]{1,0:T(8,128)S(1)} %branch_1_fun.6.held_ref), channel_id=1, source_target_pairs={{0,8},{4,0},{8,12},{12,4},{16,24},{20,16},{24,28},{28,20},{1,9},{5... | collective-permute-start | bytes 589832 | tf_op jit(solution)/shard_map/cond/branch_1_fun/ppermute | solution.py:321
  21.6 5.6 %collective-permute-start.2 = (f32[160,256]{1,0:T(8,128)S(1)}, f32[160,256]{1,0:T(8,128)S(1)}, u32[]{:S(2)}, u32[]{:S(2)}) collective-permute-start(f32[160,256]{1,0:T(8,128)S(1)} %pad_maximum_fusion.1), channel_id=1, source_target_pairs={{0,16},{4,20},{8,24},{12,28},{16,0},{20,4},{24,8},{28,12},{1,17},{... | collective-permute-start | bytes 491528 | tf_op jit(solution)/shard_map/cond/branch_1_fun/ppermute | solution.py:330
  24.7 2.8 %collective-permute-start.4 = (f32[192,256]{1,0:T(8,128)S(1)}, f32[192,256]{1,0:T(8,128)S(1)}, u32[]{:S(2)}, u32[]{:S(2)}) collective-permute-start(f32[192,256]{1,0:T(8,128)S(1)} %branch_1_fun.8), channel_id=1, source_target_pairs={{0,4},{4,0},{8,12},{12,8},{16,20},{20,16},{24,28},{28,24},{1,5},{5... | collective-permute-start | bytes 589832 | tf_op jit(solution)/shard_map/cond/branch_1_fun/ppermute | solution.py:345

commit v14 on v13

--- a/solution.py
+++ b/solution.py
@@ -217,16 +217,16 @@
 
 
 def piece_rows(x_ref, m, d):
-    piece = x_ref.shape[0] // m
+    piece = (x_ref.shape[0] - CAP) // m
     source = jnp.bitwise_xor(lax.axis_index("pcol"), d)
     return x_ref[pl.ds(pl.multiple_of(source * piece, piece), piece), :]
 
 
-def update_kernel(m, local_ref, lead_ref, x_ref, slab_ref, *refs):
+def update_kernel(m, local_ref, x_ref, slab_ref, *refs):
     *pieces, out_ref, result, swaps, sems = refs
     tops, rests = pieces[:m], pieces[m:]
     rows = slab_ref.shape[0]
-    width = x_ref.shape[0]
+    width = x_ref.shape[0] - CAP
     blocks = rows // width
     fetch = pltpu.make_async_copy(local_ref, swaps, sems.at[blocks])
     fetch.start()
@@ -242,13 +242,13 @@
             total = product([top[...] for top in tops], top_upper)
             fetch.wait()
             for s in range(CAP):
-                result[pl.ds(swaps[0, s], 1), :] = lead_ref[pl.ds(s, 1), :]
+                result[pl.ds(swaps[0, s], 1), :] = x_ref[pl.ds(width + s, 1), :]
         result[part, :] = result[part, :] - total
         if c == 0:
 
             @pl.when(lax.axis_index("prow") == 0)
             def _():
-                result[part, :] = x_ref[...]
+                result[part, :] = x_ref[:width, :]
 
         copy = pltpu.make_async_copy(result.at[part], out_ref.at[part], sems.at[c])
         copy.start()
@@ -344,7 +344,8 @@
         )
         moved = lax.ppermute(inverse, "prow", [(r, r ^ 1) for r in range(n)])
         inverse = jnp.where(me & 1 != 0, moved, inverse)
-        return leading, call(solve_kernel, jax.ShapeDtypeStruct((width, cols), F32), (inverse, pivot_rows))
+        upper_rows = call(solve_kernel, jax.ShapeDtypeStruct((width, cols), F32), (inverse, pivot_rows))
+        return jnp.concatenate([upper_rows, leading], axis=0)
 
     gathered, lower = lax.optimization_barrier((gathered, lower))
     twins = [(r, r ^ 1) for r in range(n)]
@@ -352,12 +353,12 @@
     gathered = jnp.concatenate([gathered, moved], axis=0)
     kept, sent = split(leading)
     leading = jnp.where(me & 1 != 0, lax.ppermute(sent, "prow", twins), kept)
-    leading, upper_rows = unit(me < n, levels, lower, gathered, leading)
+    upper_rows = unit(me < n, levels, lower, gathered, leading)
     return call(
         functools.partial(update_kernel, m),
         jax.ShapeDtypeStruct((rows, cols), F32),
-        (local_rows, leading, upper_rows, slab, *tops, *rests),
-        in_specs=[VMEM] * (2 * m + 4),
+        (local_rows, upper_rows, slab, *tops, *rests),
+        in_specs=[VMEM] * (2 * m + 3),
         out_specs=pl.BlockSpec(memory_space=pl.ANY),
         scratch=[
             pltpu.VMEM((rows + 8, cols), F32),

time: 31.9 us -> 31.3 us (0.981)
  Pallas kernels: 6.65 us -> 5.9 us
  waiting for transfers between devices: 7.55 us -> 8.03 us
  starting transfers between devices: 14.3 us -> 13.9 us
    pallas_call x10, Pallas kernels: 6.65 us -> 5.9 us  [call(): pl.pallas_call(kernel, out_shape=outs, in_specs=in_specs or [VMEM] * len(...]
    concatenate x2, other arithmetic: 0.02 us -> 0.69 us  [levels(): message = jnp.concatenate([gathered, sent], axis=0)]
    select_n x1, other arithmetic: 0.62 us -> 0.01 us  [levels(): leading = jnp.where(me & other != 0, moved[count:], kept)]
    ppermute x2, waiting for transfers between devices: 3.63 us -> 4.11 us  [levels(): moved = lax.ppermute(message, 'prow', [(r, r ^ other) for r in range(n)])]
  transfers between devices with their start and end apart: 13 -> 13, of which waited for: 6 -> 6; matrix products, arithmetic and copies ran while one was open for 2% -> 3% of each run, Pallas kernels for 12% -> 12%
where the time goes in v14:
time: 31.3 us; the launch traced here: 31.1 us
  starting transfers between devices  13.9 us (44%)
  waiting for transfers between devices  8.03 us (26%)
  Pallas kernels  5.9 us (19%)
  local copies, waits for them, and re-layouts  2.21 us (7%)
  other arithmetic  0.81 us (3%)
    ppermute x6, starting transfers between devices, exchange(): return lax.ppermute(block, 'pcol', [(c, c ^ d) for c in range(m)])  10.1 us
    pallas_call x10, Pallas kernels, call(): pl.pallas_call(kernel, out_shape=outs, in_specs=in_specs or [VMEM] * len(...  5.9 us
    ppermute x2, waiting for transfers between devices, levels(): moved = lax.ppermute(message, 'prow', [(r, r ^ other) for r in range(n)])  4.11 us
    ppermute x2, waiting for transfers between devices, levels(): lax.ppermute(lower, 'prow', [(r, tree_partner(r, span)) for r in range(n)])  2.74 us
    unnamed x8, local copies, waits for them, and re-layouts  2.18 us
    ppermute x2, starting transfers between devices, levels(): moved = lax.ppermute(message, 'prow', [(r, r ^ other) for r in range(n)])  1.63 us
    ppermute x2, starting transfers between devices, levels(): lax.ppermute(lower, 'prow', [(r, tree_partner(r, span)) for r in range(n)])  1.54 us
    concatenate x2, other arithmetic, levels(): message = jnp.concatenate([gathered, sent], axis=0)  0.69 us
  transfers between devices with their start and end apart: 13, of which 6 were waited for; matrix products, arithmetic and copies ran while one was open for 3% of the time, Pallas kernels for 12%

profile of v14, /device:TPU:0, one launch (start us, length us, event | category | flops | bytes accessed | tf_op | source)
XLA Modules:
  0.0 31.1 jit_solution(10249139164030721938)
XLA Ops:
  0.0 0.9 %copy-done.2 = f32[1024,64]{0,1:T(8,128)S(1)} copy-done((f32[1024,64]{0,1:T(8,128)S(1)}, f32[1024,64]{0,1:T(8,128)}, u32[]{:S(2)}) %copy-start.2) | copy-done | bytes 262168
  1.0 3.1 %collective-permute-start.5 = (f32[64,256]{1,0:T(8,128)S(1)}, f32[64,256]{1,0:T(8,128)S(1)}, u32[]{:S(2)}, u32[]{:S(2)}) collective-permute-start(f32[64,256]{1,0:T(8,128)S(1)} %get-tuple-element.46.refs_0_), channel_id=1, source_target_pairs={{0,1},{1,0},{2,3},{3,2},{4,5},{5,4},{6,7},{7,6},{8,9},{9,8},{10,11... | collective-permute-start | bytes 196616 | tf_op jit(solution)/shard_map/ppermute | solution.py:286
  4.1 2.5 %collective-permute-start.6 = (f32[64,256]{1,0:T(8,128)S(1)}, f32[64,256]{1,0:T(8,128)S(1)}, u32[]{:S(2)}, u32[]{:S(2)}) collective-permute-start(f32[64,256]{1,0:T(8,128)S(1)} %get-tuple-element.46.refs_0_), channel_id=1, source_target_pairs={{0,3},{1,2},{2,1},{3,0},{4,7},{5,6},{6,5},{7,4},{8,11},{9,10},{10,... | collective-permute-start | bytes 196616 | tf_op jit(solution)/shard_map/ppermute | solution.py:286
  6.7 1.8 %collective-permute-start.10 = (f32[64,768]{1,0:T(8,128)S(1)}, f32[64,768]{1,0:T(8,128)S(1)}, u32[]{:S(2)}, u32[]{:S(2)}) collective-permute-start(f32[64,768]{1,0:T(8,128)S(1)} %get-tuple-element.50.refs_4_), channel_id=1, source_target_pairs={{0,1},{1,0},{2,3},{3,2},{4,5},{5,4},{6,7},{7,6},{8,9},{9,8},{10,11... | collective-permute-start | bytes 589832 | tf_op jit(solution)/shard_map/ppermute | solution.py:286
  8.5 1.7 %collective-permute-start.11 = (f32[64,768]{1,0:T(8,128)S(1)}, f32[64,768]{1,0:T(8,128)S(1)}, u32[]{:S(2)}, u32[]{:S(2)}) collective-permute-start(f32[64,768]{1,0:T(8,128)S(1)} %get-tuple-element.50.refs_4_), channel_id=1, source_target_pairs={{0,2},{1,3},{2,0},{3,1},{4,6},{5,7},{6,4},{7,5},{8,10},{9,11},{10,... | collective-permute-start | bytes 589832 | tf_op jit(solution)/shard_map/ppermute | solution.py:286
  10.2 0.9 %collective-permute-start.12 = (f32[64,768]{1,0:T(8,128)S(1)}, f32[64,768]{1,0:T(8,128)S(1)}, u32[]{:S(2)}, u32[]{:S(2)}) collective-permute-start(f32[64,768]{1,0:T(8,128)S(1)} %get-tuple-element.50.refs_4_), channel_id=1, source_target_pairs={{0,3},{1,2},{2,1},{3,0},{4,7},{5,6},{6,5},{7,4},{8,11},{9,10},{10,... | collective-permute-start | bytes 589832 | tf_op jit(solution)/shard_map/ppermute | solution.py:286
  11.1 1.2 %copy-done = f32[1024,256]{1,0:T(8,128)S(1)} copy-done((f32[1024,256]{1,0:T(8,128)S(1)}, f32[1024,256]{1,0:T(8,128)}, u32[]{:S(2)}) %copy-start) | copy-done | bytes 1048600
  12.3 0.7 %shard_map.37 = (f32[32,256]{1,0:T(8,128)S(1)}, f32[256,256]{1,0:T(8,128)S(1)}, s32[1,128]{1,0:T(1,128)S(1)}) custom-call(s32[1,256]{1,0:T(1,128)S(1)} %bitcast.3, f32[1024,256]{1,0:T(8,128)S(1)} %copy-done), custom_call_target="tpu_custom_call" | custom-call | flops 1 | bytes 1 | tf_op jit(solution)/shard_map/pallas_call | solution.py:266
  13.4 0.6 %collective-permute-start.8 = (f32[128,256]{1,0:T(8,128)S(1)}, f32[128,256]{1,0:T(8,128)S(1)}, u32[]{:S(2)}, u32[]{:S(2)}) collective-permute-start(f32[128,256]{1,0:T(8,128)S(1)} %slice.37), channel_id=1, source_target_pairs={{0,4},{4,0},{8,12},{12,8},{16,20},{20,16},{24,28},{28,24},{1,5},{5... | collective-permute-start | bytes 393224 | tf_op jit(solution)/shard_map/ppermute | solution.py:355
  13.9 0.6 %collective-permute-done.9 = f32[32,256]{1,0:T(8,128)S(1)} collective-permute-done((f32[32,256]{1,0:T(8,128)S(1)}, f32[32,256]{1,0:T(8,128)S(1)}, u32[]{:S(2)}, u32[]{:S(2)}) %collective-permute-start.9) | collective-permute-done | bytes 32800 | tf_op jit(solution)/shard_map/ppermute | solution.py:352
  14.6 0.4 %collective-permute-done.8 = f32[128,256]{1,0:T(8,128)S(1)} collective-permute-done((f32[128,256]{1,0:T(8,128)S(1)}, f32[128,256]{1,0:T(8,128)S(1)}, u32[]{:S(2)}, u32[]{:S(2)}) %collective-permute-start.8) | collective-permute-done | bytes 131104 | tf_op jit(solution)/shard_map/ppermute | solution.py:355
  14.9 14.1 %conditional.1 = (f32[288,256]{1,0:T(8,128)S(1)}) conditional(s32[]{:T(128)} %convert_element_type.3, () %tuple.17, (s32[]{:T(128)}, f32[192,256]{1,0:T(8,128)S(1)}, f32[256,256]{1,0:T(8,128)S(1)}, f32[128,256]{1,0:T(8,128)S(1)}, f32[64,256]{1,0:T(8,128)S(1)}, /*index=5*/s32[1,256]{1,0:T(1,128)S(1)}) %tuple.23), branch_computations={%region_0.1_spmd, %region_1.2_spmd} | conditional | flops 425996 | bytes 7110937 | solution.py:262
  14.9 1.5 %collective-permute-start = (f32[192,256]{1,0:T(8,128)S(1)}, f32[192,256]{1,0:T(8,128)S(1)}, u32[]{:S(2)}, u32[]{:S(2)}) collective-permute-start(f32[192,256]{1,0:T(8,128)S(1)} %get-tuple-element.29.held_ref), channel_id=1, source_target_pairs={{0,16},{4,0},{8,12},{12,8},{16,20},{20,4},{24,28},{28,24},{1,17},{... | collective-permute-start | bytes 589832 | tf_op jit(solution)/shard_map/cond/branch_1_fun/ppermute | solution.py:321
  16.5 0.4 %collective-permute-start.2 = (f32[128,256]{1,0:T(8,128)S(1)}, f32[128,256]{1,0:T(8,128)S(1)}, u32[]{:S(2)}, u32[]{:S(2)}) collective-permute-start(f32[128,256]{1,0:T(8,128)S(1)} %pad_maximum_fusion.3), channel_id=1, source_target_pairs={{0,8},{4,12},{8,0},{12,4},{16,24},{20,28},{24,16},{28,20},{1,9},{5... | collective-permute-start | bytes 393224 | tf_op jit(solution)/shard_map/cond/branch_1_fun/ppermute | solution.py:330
  16.9 2.7 %collective-permute-done.moved_ref = f32[192,256]{1,0:T(8,128)S(1)} collective-permute-done((f32[192,256]{1,0:T(8,128)S(1)}, f32[192,256]{1,0:T(8,128)S(1)}, u32[]{:S(2)}, u32[]{:S(2)}) %collective-permute-start) | collective-permute-done | bytes 196640 | tf_op jit(solution)/shard_map/cond/branch_1_fun/ppermute | solution.py:321
  19.7 1.9 %collective-permute-done.2 = f32[128,256]{1,0:T(8,128)S(1)} collective-permute-done((f32[128,256]{1,0:T(8,128)S(1)}, f32[128,256]{1,0:T(8,128)S(1)}, u32[]{:S(2)}, u32[]{:S(2)}) %collective-permute-start.2) | collective-permute-done | bytes 131104 | tf_op jit(solution)/shard_map/cond/branch_1_fun/ppermute | solution.py:330
  21.6 0.7 %pad_maximum_fusion.2 = f32[160,256]{1,0:T(8,128)} fusion(f32[32,256]{1,0:T(8,128)S(1)} %slice.40, f32[64,256]{1,0:T(8,128)S(1)} %get-tuple-element.51, f32[64,256]{1,0:T(8,128)S(1)} %get-tuple-element.30), kind=kLoop, calls=%fused_computation.2 | loop fusion | flops 81920 | bytes 327680 | tf_op jit(solution)/shard_map/cond/branch_1_fun/concatenate | solution.py:329
  22.2 1.2 %collective-permute-start.4 = (f32[160,256]{1,0:T(8,128)}, f32[160,256]{1,0:T(8,128)S(1)}, u32[]{:S(2)}, u32[]{:S(2)}) collective-permute-start(f32[160,256]{1,0:T(8,128)} %pad_maximum_fusion.2), channel_id=1, source_target_pairs={{0,16},{4,20},{8,24},{12,28},{16,0},{20,4},{24,8},{28,12},{1,17},{... | collective-permute-start | bytes 491528 | tf_op jit(solution)/shard_map/cond/branch_1_fun/ppermute | solution.py:330
  23.5 1.8 %branch_1_fun.8 = f32[192,256]{1,0:T(8,128)S(1)} custom-call(f32[192,256]{1,0:T(8,128)S(1)} %branch_1_fun.7.lower_ref), custom_call_target="tpu_custom_call" | custom-call | flops 1 | bytes 1 | tf_op jit(solution)/shard_map/cond/branch_1_fun/pallas_call | solution.py:266
  25.4 0.3 branch_1_fun.9.choice_ref
  25.7 2.3 %collective-permute-done.4 = f32[160,256]{1,0:T(8,128)S(1)} collective-permute-done((f32[160,256]{1,0:T(8,128)}, f32[160,256]{1,0:T(8,128)S(1)}, u32[]{:S(2)}, u32[]{:S(2)}) %collective-permute-start.4) | collective-permute-done | bytes 163872 | tf_op jit(solution)/shard_map/cond/branch_1_fun/ppermute | solution.py:330
  28.0 0.3 branch_1_fun.10.pivot_rows_ref
  28.3 0.7 %branch_1_fun.11 = f32[256,256]{1,0:T(8,128)S(1)} custom-call(f32[192,256]{1,0:T(8,128)S(1)} %broadcast_select_fusion.inverse_ref, f32[256,256]{1,0:T(8,128)S(1)} %branch_1_fun.10.pivot_rows_ref), custom_call_target="tpu_custom_call" | custom-call | flops 1 | bytes 1 | tf_op jit(solution)/shard_map/cond/branch_1_fun/pallas_call | solution.py:266
  29.1 2.0 %shard_map.40 = f32[1024,256]{1,0:T(8,128)} custom-call(s32[1,128]{1,0:T(1,128)S(1)} %get-tuple-element.44.local_ref, f32[288,256]{1,0:T(8,128)S(1)} %get-tuple-element.53.x_ref, f32[1024,256]{1,0:T(8,128)S(1)} %copy-done.1, f32[64,256]{1,0:T(8,128)S(1)} %get-tuple-element.46.refs_0_, f32[64,256]{1,0:T(8,128)S(1)} %collective-permute-done.5.refs_1_, ...), custom_call_target="tpu_custom_call" | custom-call | flops 1 | bytes 1 | tf_op jit(solution)/shard_map/pallas_call | solution.py:266
  (34 shorter events, 0.8 us)
Async XLA Ops:
  0.0 0.9 %copy-start.2 = (f32[1024,64]{0,1:T(8,128)S(1)}, f32[1024,64]{0,1:T(8,128)}, u32[]{:S(2)}) copy-start(f32[1024,64]{0,1:T(8,128)} %param.6) | copy-start | bytes 786436
  1.0 9.2 %collective-permute-start.5 = (f32[64,256]{1,0:T(8,128)S(1)}, f32[64,256]{1,0:T(8,128)S(1)}, u32[]{:S(2)}, u32[]{:S(2)}) collective-permute-start(f32[64,256]{1,0:T(8,128)S(1)} %get-tuple-element.46.refs_0_), channel_id=1, source_target_pairs={{0,1},{1,0},{2,3},{3,2},{4,5},{5,4},{6,7},{7,6},{8,9},{9,8},{10,11... | collective-permute-start | bytes 196616 | tf_op jit(solution)/shard_map/ppermute | solution.py:286
  4.1 8.9 %collective-permute-start.6 = (f32[64,256]{1,0:T(8,128)S(1)}, f32[64,256]{1,0:T(8,128)S(1)}, u32[]{:S(2)}, u32[]{:S(2)}) collective-permute-start(f32[64,256]{1,0:T(8,128)S(1)} %get-tuple-element.46.refs_0_), channel_id=1, source_target_pairs={{0,3},{1,2},{2,1},{3,0},{4,7},{5,6},{6,5},{7,4},{8,11},{9,10},{10,... | collective-permute-start | bytes 196616 | tf_op jit(solution)/shard_map/ppermute | solution.py:286
  6.6 6.6 %collective-permute-start.7 = (f32[64,256]{1,0:T(8,128)S(1)}, f32[64,256]{1,0:T(8,128)S(1)}, u32[]{:S(2)}, u32[]{:S(2)}) collective-permute-start(f32[64,256]{1,0:T(8,128)S(1)} %get-tuple-element.46.refs_0_), channel_id=1, source_target_pairs={{0,2},{1,3},{2,0},{3,1},{4,6},{5,7},{6,4},{7,5},{8,10},{9,11},{10,... | collective-permute-start | bytes 196616 | tf_op jit(solution)/shard_map/ppermute | solution.py:286
  6.7 4.4 %copy-start.3 = (s32[256]{0:T(256)S(1)}, s32[256]{0:T(256)}, u32[]{:S(2)}) copy-start(s32[256]{0:T(256)} %param.7) | copy-start | bytes 3076
  6.7 22.4 %collective-permute-start.10 = (f32[64,768]{1,0:T(8,128)S(1)}, f32[64,768]{1,0:T(8,128)S(1)}, u32[]{:S(2)}, u32[]{:S(2)}) collective-permute-start(f32[64,768]{1,0:T(8,128)S(1)} %get-tuple-element.50.refs_4_), channel_id=1, source_target_pairs={{0,1},{1,0},{2,3},{3,2},{4,5},{5,4},{6,7},{7,6},{8,9},{9,8},{10,11... | collective-permute-start | bytes 589832 | tf_op jit(solution)/shard_map/ppermute | solution.py:286
  8.5 20.6 %collective-permute-start.11 = (f32[64,768]{1,0:T(8,128)S(1)}, f32[64,768]{1,0:T(8,128)S(1)}, u32[]{:S(2)}, u32[]{:S(2)}) collective-permute-start(f32[64,768]{1,0:T(8,128)S(1)} %get-tuple-element.50.refs_4_), channel_id=1, source_target_pairs={{0,2},{1,3},{2,0},{3,1},{4,6},{5,7},{6,4},{7,5},{8,10},{9,11},{10,... | collective-permute-start | bytes 589832 | tf_op jit(solution)/shard_map/ppermute | solution.py:286
  10.2 18.9 %collective-permute-start.12 = (f32[64,768]{1,0:T(8,128)S(1)}, f32[64,768]{1,0:T(8,128)S(1)}, u32[]{:S(2)}, u32[]{:S(2)}) collective-permute-start(f32[64,768]{1,0:T(8,128)S(1)} %get-tuple-element.50.refs_4_), channel_id=1, source_target_pairs={{0,3},{1,2},{2,1},{3,0},{4,7},{5,6},{6,5},{7,4},{8,11},{9,10},{10,... | collective-permute-start | bytes 589832 | tf_op jit(solution)/shard_map/ppermute | solution.py:286
  11.1 1.2 %copy-start = (f32[1024,256]{1,0:T(8,128)S(1)}, f32[1024,256]{1,0:T(8,128)}, u32[]{:S(2)}) copy-start(f32[1024,256]{1,0:T(8,128)} %slab_ref.3) | copy-start | bytes 3145732
  13.3 1.3 %collective-permute-start.9 = (f32[32,256]{1,0:T(8,128)S(1)}, f32[32,256]{1,0:T(8,128)S(1)}, u32[]{:S(2)}, u32[]{:S(2)}) collective-permute-start(f32[32,256]{1,0:T(8,128)S(1)} %get-tuple-element.49), channel_id=1, source_target_pairs={{0,4},{4,0},{8,12},{12,8},{16,20},{20,16},{24,28},{28,24},{1,5},{5... | collective-permute-start | bytes 98312 | tf_op jit(solution)/shard_map/ppermute | solution.py:352
  13.4 1.5 %collective-permute-start.8 = (f32[128,256]{1,0:T(8,128)S(1)}, f32[128,256]{1,0:T(8,128)S(1)}, u32[]{:S(2)}, u32[]{:S(2)}) collective-permute-start(f32[128,256]{1,0:T(8,128)S(1)} %slice.37), channel_id=1, source_target_pairs={{0,4},{4,0},{8,12},{12,8},{16,20},{20,16},{24,28},{28,24},{1,5},{5... | collective-permute-start | bytes 393224 | tf_op jit(solution)/shard_map/ppermute | solution.py:355
  14.9 14.2 %copy-start.1 = (f32[1024,256]{1,0:T(8,128)S(1)}, f32[1024,256]{1,0:T(8,128)}, u32[]{:S(2)}) copy-start(f32[1024,256]{1,0:T(8,128)} %slab_ref.3) | copy-start | bytes 3145732
  14.9 4.7 %collective-permute-start = (f32[192,256]{1,0:T(8,128)S(1)}, f32[192,256]{1,0:T(8,128)S(1)}, u32[]{:S(2)}, u32[]{:S(2)}) collective-permute-start(f32[192,256]{1,0:T(8,128)S(1)} %get-tuple-element.29.held_ref), channel_id=1, source_target_pairs={{0,16},{4,0},{8,12},{12,8},{16,20},{20,4},{24,28},{28,24},{1,17},{... | collective-permute-start | bytes 589832 | tf_op jit(solution)/shard_map/cond/branch_1_fun/ppermute | solution.py:321
  16.5 5.0 %collective-permute-start.2 = (f32[128,256]{1,0:T(8,128)S(1)}, f32[128,256]{1,0:T(8,128)S(1)}, u32[]{:S(2)}, u32[]{:S(2)}) collective-permute-start(f32[128,256]{1,0:T(8,128)S(1)} %pad_maximum_fusion.3), channel_id=1, source_target_pairs={{0,8},{4,12},{8,0},{12,4},{16,24},{20,28},{24,16},{28,20},{1,9},{5... | collective-permute-start | bytes 393224 | tf_op jit(solution)/shard_map/cond/branch_1_fun/ppermute | solution.py:330
  19.6 3.8 %collective-permute-start.1 = (f32[192,256]{1,0:T(8,128)S(1)}, f32[192,256]{1,0:T(8,128)S(1)}, u32[]{:S(2)}, u32[]{:S(2)}) collective-permute-start(f32[192,256]{1,0:T(8,128)S(1)} %branch_1_fun.6.held_ref), channel_id=1, source_target_pairs={{0,8},{4,0},{8,12},{12,4},{16,24},{20,16},{24,28},{28,20},{1,9},{5... | collective-permute-start | bytes 589832 | tf_op jit(solution)/shard_map/cond/branch_1_fun/ppermute | solution.py:321
  22.2 5.7 %collective-permute-start.4 = (f32[160,256]{1,0:T(8,128)}, f32[160,256]{1,0:T(8,128)S(1)}, u32[]{:S(2)}, u32[]{:S(2)}) collective-permute-start(f32[160,256]{1,0:T(8,128)} %pad_maximum_fusion.2), channel_id=1, source_target_pairs={{0,16},{4,20},{8,24},{12,28},{16,0},{20,4},{24,8},{28,12},{1,17},{... | collective-permute-start | bytes 491528 | tf_op jit(solution)/shard_map/cond/branch_1_fun/ppermute | solution.py:330
  25.3 3.0 %collective-permute-start.3 = (f32[192,256]{1,0:T(8,128)S(1)}, f32[192,256]{1,0:T(8,128)S(1)}, u32[]{:S(2)}, u32[]{:S(2)}) collective-permute-start(f32[192,256]{1,0:T(8,128)S(1)} %branch_1_fun.8), channel_id=1, source_target_pairs={{0,4},{4,0},{8,12},{12,8},{16,20},{20,16},{24,28},{28,24},{1,5},{5... | collective-permute-start | bytes 589832 | tf_op jit(solution)/shard_map/cond/branch_1_fun/ppermute | solution.py:345

commit v15 on v14

--- a/solution.py
+++ b/solution.py
@@ -12,7 +12,7 @@
 F32 = jnp.float32
 BF16 = jnp.bfloat16
 VMEM = pl.BlockSpec(memory_space=pltpu.VMEM)
-PARAMS = pltpu.CompilerParams(vmem_limit_bytes=24 * 1024 * 1024)
+PARAMS = pltpu.CompilerParams(vmem_limit_bytes=16 * 1024 * 1024)
 
 
 def split3(x):

time: 31.3 us -> 31.3 us (level)
  no operation moved by 1% of the time
where the time goes in v15:
time: 31.3 us; the launch traced here: 31.1 us
  starting transfers between devices  13.9 us (44%)
  waiting for transfers between devices  8.03 us (26%)
  Pallas kernels  5.9 us (19%)
  local copies, waits for them, and re-layouts  2.21 us (7%)
  other arithmetic  0.81 us (3%)
    ppermute x6, starting transfers between devices, exchange(): return lax.ppermute(block, 'pcol', [(c, c ^ d) for c in range(m)])  10.1 us
    pallas_call x10, Pallas kernels, call(): pl.pallas_call(kernel, out_shape=outs, in_specs=in_specs or [VMEM] * len(...  5.9 us
    ppermute x2, waiting for transfers between devices, levels(): moved = lax.ppermute(message, 'prow', [(r, r ^ other) for r in range(n)])  4.11 us
    ppermute x2, waiting for transfers between devices, levels(): lax.ppermute(lower, 'prow', [(r, tree_partner(r, span)) for r in range(n)])  2.74 us
    unnamed x8, local copies, waits for them, and re-layouts  2.18 us
    ppermute x2, starting transfers between devices, levels(): moved = lax.ppermute(message, 'prow', [(r, r ^ other) for r in range(n)])  1.63 us
    ppermute x2, starting transfers between devices, levels(): lax.ppermute(lower, 'prow', [(r, tree_partner(r, span)) for r in range(n)])  1.54 us
    concatenate x2, other arithmetic, levels(): message = jnp.concatenate([gathered, sent], axis=0)  0.69 us
  transfers between devices with their start and end apart: 13, of which 6 were waited for; matrix products, arithmetic and copies ran while one was open for 3% of the time, Pallas kernels for 12%

profile of v15, /device:TPU:0, one launch (start us, length us, event | category | flops | bytes accessed | tf_op | source)
XLA Modules:
  0.0 31.1 jit_solution(17784129068391766974)
XLA Ops:
  0.0 0.9 %copy-done.2 = f32[1024,64]{0,1:T(8,128)S(1)} copy-done((f32[1024,64]{0,1:T(8,128)S(1)}, f32[1024,64]{0,1:T(8,128)}, u32[]{:S(2)}) %copy-start.2) | copy-done | bytes 262168
  1.0 3.1 %collective-permute-start.5 = (f32[64,256]{1,0:T(8,128)S(1)}, f32[64,256]{1,0:T(8,128)S(1)}, u32[]{:S(2)}, u32[]{:S(2)}) collective-permute-start(f32[64,256]{1,0:T(8,128)S(1)} %get-tuple-element.46.refs_0_), channel_id=1, source_target_pairs={{0,1},{1,0},{2,3},{3,2},{4,5},{5,4},{6,7},{7,6},{8,9},{9,8},{10,11... | collective-permute-start | bytes 196616 | tf_op jit(solution)/shard_map/ppermute | solution.py:286
  4.1 2.5 %collective-permute-start.6 = (f32[64,256]{1,0:T(8,128)S(1)}, f32[64,256]{1,0:T(8,128)S(1)}, u32[]{:S(2)}, u32[]{:S(2)}) collective-permute-start(f32[64,256]{1,0:T(8,128)S(1)} %get-tuple-element.46.refs_0_), channel_id=1, source_target_pairs={{0,3},{1,2},{2,1},{3,0},{4,7},{5,6},{6,5},{7,4},{8,11},{9,10},{10,... | collective-permute-start | bytes 196616 | tf_op jit(solution)/shard_map/ppermute | solution.py:286
  6.7 1.8 %collective-permute-start.10 = (f32[64,768]{1,0:T(8,128)S(1)}, f32[64,768]{1,0:T(8,128)S(1)}, u32[]{:S(2)}, u32[]{:S(2)}) collective-permute-start(f32[64,768]{1,0:T(8,128)S(1)} %get-tuple-element.50.refs_4_), channel_id=1, source_target_pairs={{0,1},{1,0},{2,3},{3,2},{4,5},{5,4},{6,7},{7,6},{8,9},{9,8},{10,11... | collective-permute-start | bytes 589832 | tf_op jit(solution)/shard_map/ppermute | solution.py:286
  8.5 1.7 %collective-permute-start.11 = (f32[64,768]{1,0:T(8,128)S(1)}, f32[64,768]{1,0:T(8,128)S(1)}, u32[]{:S(2)}, u32[]{:S(2)}) collective-permute-start(f32[64,768]{1,0:T(8,128)S(1)} %get-tuple-element.50.refs_4_), channel_id=1, source_target_pairs={{0,2},{1,3},{2,0},{3,1},{4,6},{5,7},{6,4},{7,5},{8,10},{9,11},{10,... | collective-permute-start | bytes 589832 | tf_op jit(solution)/shard_map/ppermute | solution.py:286
  10.2 0.9 %collective-permute-start.12 = (f32[64,768]{1,0:T(8,128)S(1)}, f32[64,768]{1,0:T(8,128)S(1)}, u32[]{:S(2)}, u32[]{:S(2)}) collective-permute-start(f32[64,768]{1,0:T(8,128)S(1)} %get-tuple-element.50.refs_4_), channel_id=1, source_target_pairs={{0,3},{1,2},{2,1},{3,0},{4,7},{5,6},{6,5},{7,4},{8,11},{9,10},{10,... | collective-permute-start | bytes 589832 | tf_op jit(solution)/shard_map/ppermute | solution.py:286
  11.1 1.2 %copy-done = f32[1024,256]{1,0:T(8,128)S(1)} copy-done((f32[1024,256]{1,0:T(8,128)S(1)}, f32[1024,256]{1,0:T(8,128)}, u32[]{:S(2)}) %copy-start) | copy-done | bytes 1048600
  12.3 0.7 %shard_map.37 = (f32[32,256]{1,0:T(8,128)S(1)}, f32[256,256]{1,0:T(8,128)S(1)}, s32[1,128]{1,0:T(1,128)S(1)}) custom-call(s32[1,256]{1,0:T(1,128)S(1)} %bitcast.3, f32[1024,256]{1,0:T(8,128)S(1)} %copy-done), custom_call_target="tpu_custom_call" | custom-call | flops 1 | bytes 1 | tf_op jit(solution)/shard_map/pallas_call | solution.py:266
  13.4 0.6 %collective-permute-start.8 = (f32[128,256]{1,0:T(8,128)S(1)}, f32[128,256]{1,0:T(8,128)S(1)}, u32[]{:S(2)}, u32[]{:S(2)}) collective-permute-start(f32[128,256]{1,0:T(8,128)S(1)} %slice.37), channel_id=1, source_target_pairs={{0,4},{4,0},{8,12},{12,8},{16,20},{20,16},{24,28},{28,24},{1,5},{5... | collective-permute-start | bytes 393224 | tf_op jit(solution)/shard_map/ppermute | solution.py:355
  13.9 0.6 %collective-permute-done.9 = f32[32,256]{1,0:T(8,128)S(1)} collective-permute-done((f32[32,256]{1,0:T(8,128)S(1)}, f32[32,256]{1,0:T(8,128)S(1)}, u32[]{:S(2)}, u32[]{:S(2)}) %collective-permute-start.9) | collective-permute-done | bytes 32800 | tf_op jit(solution)/shard_map/ppermute | solution.py:352
  14.6 0.4 %collective-permute-done.8 = f32[128,256]{1,0:T(8,128)S(1)} collective-permute-done((f32[128,256]{1,0:T(8,128)S(1)}, f32[128,256]{1,0:T(8,128)S(1)}, u32[]{:S(2)}, u32[]{:S(2)}) %collective-permute-start.8) | collective-permute-done | bytes 131104 | tf_op jit(solution)/shard_map/ppermute | solution.py:355
  14.9 14.1 %conditional.1 = (f32[288,256]{1,0:T(8,128)S(1)}) conditional(s32[]{:T(128)} %convert_element_type.3, () %tuple.17, (s32[]{:T(128)}, f32[192,256]{1,0:T(8,128)S(1)}, f32[256,256]{1,0:T(8,128)S(1)}, f32[128,256]{1,0:T(8,128)S(1)}, f32[64,256]{1,0:T(8,128)S(1)}, /*index=5*/s32[1,256]{1,0:T(1,128)S(1)}) %tuple.23), branch_computations={%region_0.1_spmd, %region_1.2_spmd} | conditional | flops 425996 | bytes 7110937 | solution.py:262
  14.9 1.5 %collective-permute-start = (f32[192,256]{1,0:T(8,128)S(1)}, f32[192,256]{1,0:T(8,128)S(1)}, u32[]{:S(2)}, u32[]{:S(2)}) collective-permute-start(f32[192,256]{1,0:T(8,128)S(1)} %get-tuple-element.29.held_ref), channel_id=1, source_target_pairs={{0,16},{4,0},{8,12},{12,8},{16,20},{20,4},{24,28},{28,24},{1,17},{... | collective-permute-start | bytes 589832 | tf_op jit(solution)/shard_map/cond/branch_1_fun/ppermute | solution.py:321
  16.5 0.4 %collective-permute-start.2 = (f32[128,256]{1,0:T(8,128)S(1)}, f32[128,256]{1,0:T(8,128)S(1)}, u32[]{:S(2)}, u32[]{:S(2)}) collective-permute-start(f32[128,256]{1,0:T(8,128)S(1)} %pad_maximum_fusion.3), channel_id=1, source_target_pairs={{0,8},{4,12},{8,0},{12,4},{16,24},{20,28},{24,16},{28,20},{1,9},{5... | collective-permute-start | bytes 393224 | tf_op jit(solution)/shard_map/cond/branch_1_fun/ppermute | solution.py:330
  16.9 2.7 %collective-permute-done.moved_ref = f32[192,256]{1,0:T(8,128)S(1)} collective-permute-done((f32[192,256]{1,0:T(8,128)S(1)}, f32[192,256]{1,0:T(8,128)S(1)}, u32[]{:S(2)}, u32[]{:S(2)}) %collective-permute-start) | collective-permute-done | bytes 196640 | tf_op jit(solution)/shard_map/cond/branch_1_fun/ppermute | solution.py:321
  19.7 1.9 %collective-permute-done.2 = f32[128,256]{1,0:T(8,128)S(1)} collective-permute-done((f32[128,256]{1,0:T(8,128)S(1)}, f32[128,256]{1,0:T(8,128)S(1)}, u32[]{:S(2)}, u32[]{:S(2)}) %collective-permute-start.2) | collective-permute-done | bytes 131104 | tf_op jit(solution)/shard_map/cond/branch_1_fun/ppermute | solution.py:330
  21.6 0.7 %pad_maximum_fusion.2 = f32[160,256]{1,0:T(8,128)} fusion(f32[32,256]{1,0:T(8,128)S(1)} %slice.40, f32[64,256]{1,0:T(8,128)S(1)} %get-tuple-element.51, f32[64,256]{1,0:T(8,128)S(1)} %get-tuple-element.30), kind=kLoop, calls=%fused_computation.2 | loop fusion | flops 81920 | bytes 327680 | tf_op jit(solution)/shard_map/cond/branch_1_fun/concatenate | solution.py:329
  22.2 1.2 %collective-permute-start.4 = (f32[160,256]{1,0:T(8,128)}, f32[160,256]{1,0:T(8,128)S(1)}, u32[]{:S(2)}, u32[]{:S(2)}) collective-permute-start(f32[160,256]{1,0:T(8,128)} %pad_maximum_fusion.2), channel_id=1, source_target_pairs={{0,16},{4,20},{8,24},{12,28},{16,0},{20,4},{24,8},{28,12},{1,17},{... | collective-permute-start | bytes 491528 | tf_op jit(solution)/shard_map/cond/branch_1_fun/ppermute | solution.py:330
  23.5 1.8 %branch_1_fun.8 = f32[192,256]{1,0:T(8,128)S(1)} custom-call(f32[192,256]{1,0:T(8,128)S(1)} %branch_1_fun.7.lower_ref), custom_call_target="tpu_custom_call" | custom-call | flops 1 | bytes 1 | tf_op jit(solution)/shard_map/cond/branch_1_fun/pallas_call | solution.py:266
  25.4 0.3 branch_1_fun.9.choice_ref
  25.7 2.3 %collective-permute-done.4 = f32[160,256]{1,0:T(8,128)S(1)} collective-permute-done((f32[160,256]{1,0:T(8,128)}, f32[160,256]{1,0:T(8,128)S(1)}, u32[]{:S(2)}, u32[]{:S(2)}) %collective-permute-start.4) | collective-permute-done | bytes 163872 | tf_op jit(solution)/shard_map/cond/branch_1_fun/ppermute | solution.py:330
  28.0 0.3 branch_1_fun.10.pivot_rows_ref
  28.3 0.7 %branch_1_fun.11 = f32[256,256]{1,0:T(8,128)S(1)} custom-call(f32[192,256]{1,0:T(8,128)S(1)} %broadcast_select_fusion.inverse_ref, f32[256,256]{1,0:T(8,128)S(1)} %branch_1_fun.10.pivot_rows_ref), custom_call_target="tpu_custom_call" | custom-call | flops 1 | bytes 1 | tf_op jit(solution)/shard_map/cond/branch_1_fun/pallas_call | solution.py:266
  29.1 2.0 %shard_map.40 = f32[1024,256]{1,0:T(8,128)} custom-call(s32[1,128]{1,0:T(1,128)S(1)} %get-tuple-element.44.local_ref, f32[288,256]{1,0:T(8,128)S(1)} %get-tuple-element.53.x_ref, f32[1024,256]{1,0:T(8,128)S(1)} %copy-done.1, f32[64,256]{1,0:T(8,128)S(1)} %get-tuple-element.46.refs_0_, f32[64,256]{1,0:T(8,128)S(1)} %collective-permute-done.5.refs_1_, ...), custom_call_target="tpu_custom_call" | custom-call | flops 1 | bytes 1 | tf_op jit(solution)/shard_map/pallas_call | solution.py:266
  (34 shorter events, 0.8 us)
Async XLA Ops:
  0.0 0.9 %copy-start.2 = (f32[1024,64]{0,1:T(8,128)S(1)}, f32[1024,64]{0,1:T(8,128)}, u32[]{:S(2)}) copy-start(f32[1024,64]{0,1:T(8,128)} %param.6) | copy-start | bytes 786436
  1.0 9.2 %collective-permute-start.5 = (f32[64,256]{1,0:T(8,128)S(1)}, f32[64,256]{1,0:T(8,128)S(1)}, u32[]{:S(2)}, u32[]{:S(2)}) collective-permute-start(f32[64,256]{1,0:T(8,128)S(1)} %get-tuple-element.46.refs_0_), channel_id=1, source_target_pairs={{0,1},{1,0},{2,3},{3,2},{4,5},{5,4},{6,7},{7,6},{8,9},{9,8},{10,11... | collective-permute-start | bytes 196616 | tf_op jit(solution)/shard_map/ppermute | solution.py:286
  4.1 8.9 %collective-permute-start.6 = (f32[64,256]{1,0:T(8,128)S(1)}, f32[64,256]{1,0:T(8,128)S(1)}, u32[]{:S(2)}, u32[]{:S(2)}) collective-permute-start(f32[64,256]{1,0:T(8,128)S(1)} %get-tuple-element.46.refs_0_), channel_id=1, source_target_pairs={{0,3},{1,2},{2,1},{3,0},{4,7},{5,6},{6,5},{7,4},{8,11},{9,10},{10,... | collective-permute-start | bytes 196616 | tf_op jit(solution)/shard_map/ppermute | solution.py:286
  6.6 6.6 %collective-permute-start.7 = (f32[64,256]{1,0:T(8,128)S(1)}, f32[64,256]{1,0:T(8,128)S(1)}, u32[]{:S(2)}, u32[]{:S(2)}) collective-permute-start(f32[64,256]{1,0:T(8,128)S(1)} %get-tuple-element.46.refs_0_), channel_id=1, source_target_pairs={{0,2},{1,3},{2,0},{3,1},{4,6},{5,7},{6,4},{7,5},{8,10},{9,11},{10,... | collective-permute-start | bytes 196616 | tf_op jit(solution)/shard_map/ppermute | solution.py:286
  6.7 4.4 %copy-start.3 = (s32[256]{0:T(256)S(1)}, s32[256]{0:T(256)}, u32[]{:S(2)}) copy-start(s32[256]{0:T(256)} %param.7) | copy-start | bytes 3076
  6.7 22.4 %collective-permute-start.10 = (f32[64,768]{1,0:T(8,128)S(1)}, f32[64,768]{1,0:T(8,128)S(1)}, u32[]{:S(2)}, u32[]{:S(2)}) collective-permute-start(f32[64,768]{1,0:T(8,128)S(1)} %get-tuple-element.50.refs_4_), channel_id=1, source_target_pairs={{0,1},{1,0},{2,3},{3,2},{4,5},{5,4},{6,7},{7,6},{8,9},{9,8},{10,11... | collective-permute-start | bytes 589832 | tf_op jit(solution)/shard_map/ppermute | solution.py:286
  8.5 20.6 %collective-permute-start.11 = (f32[64,768]{1,0:T(8,128)S(1)}, f32[64,768]{1,0:T(8,128)S(1)}, u32[]{:S(2)}, u32[]{:S(2)}) collective-permute-start(f32[64,768]{1,0:T(8,128)S(1)} %get-tuple-element.50.refs_4_), channel_id=1, source_target_pairs={{0,2},{1,3},{2,0},{3,1},{4,6},{5,7},{6,4},{7,5},{8,10},{9,11},{10,... | collective-permute-start | bytes 589832 | tf_op jit(solution)/shard_map/ppermute | solution.py:286
  10.2 18.9 %collective-permute-start.12 = (f32[64,768]{1,0:T(8,128)S(1)}, f32[64,768]{1,0:T(8,128)S(1)}, u32[]{:S(2)}, u32[]{:S(2)}) collective-permute-start(f32[64,768]{1,0:T(8,128)S(1)} %get-tuple-element.50.refs_4_), channel_id=1, source_target_pairs={{0,3},{1,2},{2,1},{3,0},{4,7},{5,6},{6,5},{7,4},{8,11},{9,10},{10,... | collective-permute-start | bytes 589832 | tf_op jit(solution)/shard_map/ppermute | solution.py:286
  11.1 1.2 %copy-start = (f32[1024,256]{1,0:T(8,128)S(1)}, f32[1024,256]{1,0:T(8,128)}, u32[]{:S(2)}) copy-start(f32[1024,256]{1,0:T(8,128)} %slab_ref.3) | copy-start | bytes 3145732
  13.3 1.3 %collective-permute-start.9 = (f32[32,256]{1,0:T(8,128)S(1)}, f32[32,256]{1,0:T(8,128)S(1)}, u32[]{:S(2)}, u32[]{:S(2)}) collective-permute-start(f32[32,256]{1,0:T(8,128)S(1)} %get-tuple-element.49), channel_id=1, source_target_pairs={{0,4},{4,0},{8,12},{12,8},{16,20},{20,16},{24,28},{28,24},{1,5},{5... | collective-permute-start | bytes 98312 | tf_op jit(solution)/shard_map/ppermute | solution.py:352
  13.4 1.5 %collective-permute-start.8 = (f32[128,256]{1,0:T(8,128)S(1)}, f32[128,256]{1,0:T(8,128)S(1)}, u32[]{:S(2)}, u32[]{:S(2)}) collective-permute-start(f32[128,256]{1,0:T(8,128)S(1)} %slice.37), channel_id=1, source_target_pairs={{0,4},{4,0},{8,12},{12,8},{16,20},{20,16},{24,28},{28,24},{1,5},{5... | collective-permute-start | bytes 393224 | tf_op jit(solution)/shard_map/ppermute | solution.py:355
  14.9 14.2 %copy-start.1 = (f32[1024,256]{1,0:T(8,128)S(1)}, f32[1024,256]{1,0:T(8,128)}, u32[]{:S(2)}) copy-start(f32[1024,256]{1,0:T(8,128)} %slab_ref.3) | copy-start | bytes 3145732
  14.9 4.7 %collective-permute-start = (f32[192,256]{1,0:T(8,128)S(1)}, f32[192,256]{1,0:T(8,128)S(1)}, u32[]{:S(2)}, u32[]{:S(2)}) collective-permute-start(f32[192,256]{1,0:T(8,128)S(1)} %get-tuple-element.29.held_ref), channel_id=1, source_target_pairs={{0,16},{4,0},{8,12},{12,8},{16,20},{20,4},{24,28},{28,24},{1,17},{... | collective-permute-start | bytes 589832 | tf_op jit(solution)/shard_map/cond/branch_1_fun/ppermute | solution.py:321
  16.5 5.0 %collective-permute-start.2 = (f32[128,256]{1,0:T(8,128)S(1)}, f32[128,256]{1,0:T(8,128)S(1)}, u32[]{:S(2)}, u32[]{:S(2)}) collective-permute-start(f32[128,256]{1,0:T(8,128)S(1)} %pad_maximum_fusion.3), channel_id=1, source_target_pairs={{0,8},{4,12},{8,0},{12,4},{16,24},{20,28},{24,16},{28,20},{1,9},{5... | collective-permute-start | bytes 393224 | tf_op jit(solution)/shard_map/cond/branch_1_fun/ppermute | solution.py:330
  19.6 3.8 %collective-permute-start.1 = (f32[192,256]{1,0:T(8,128)S(1)}, f32[192,256]{1,0:T(8,128)S(1)}, u32[]{:S(2)}, u32[]{:S(2)}) collective-permute-start(f32[192,256]{1,0:T(8,128)S(1)} %branch_1_fun.6.held_ref), channel_id=1, source_target_pairs={{0,8},{4,0},{8,12},{12,4},{16,24},{20,16},{24,28},{28,20},{1,9},{5... | collective-permute-start | bytes 589832 | tf_op jit(solution)/shard_map/cond/branch_1_fun/ppermute | solution.py:321
  22.2 5.7 %collective-permute-start.4 = (f32[160,256]{1,0:T(8,128)}, f32[160,256]{1,0:T(8,128)S(1)}, u32[]{:S(2)}, u32[]{:S(2)}) collective-permute-start(f32[160,256]{1,0:T(8,128)} %pad_maximum_fusion.2), channel_id=1, source_target_pairs={{0,16},{4,20},{8,24},{12,28},{16,0},{20,4},{24,8},{28,12},{1,17},{... | collective-permute-start | bytes 491528 | tf_op jit(solution)/shard_map/cond/branch_1_fun/ppermute | solution.py:330
  25.3 3.0 %collective-permute-start.3 = (f32[192,256]{1,0:T(8,128)S(1)}, f32[192,256]{1,0:T(8,128)S(1)}, u32[]{:S(2)}, u32[]{:S(2)}) collective-permute-start(f32[192,256]{1,0:T(8,128)S(1)} %branch_1_fun.8), channel_id=1, source_target_pairs={{0,4},{4,0},{8,12},{12,8},{16,20},{20,16},{24,28},{28,24},{1,5},{5... | collective-permute-start | bytes 589832 | tf_op jit(solution)/shard_map/cond/branch_1_fun/ppermute | solution.py:345

commit v16 on v13

--- a/solution.py
+++ b/solution.py
@@ -315,7 +315,7 @@
         blocks = leading.reshape(2, -1, cols)
         return blocks[0], blocks[1]
 
-    def levels(lower, gathered, leading):
+    def levels(lower, gathered, leading, choice):
         span, other, held = n // 2, 2, lower
         while span > 1:
             moved = lax.ppermute(lower, "prow", [(r, tree_partner(r, span)) for r in range(n)])
@@ -332,9 +332,6 @@
             gathered = jnp.concatenate([gathered, moved[:count]], axis=0)
             leading = jnp.where(me & other != 0, moved[count:], kept)
             span, other = span // 2, other * 2
-        choice = call(
-            functools.partial(choice_kernel, n, rows), jax.ShapeDtypeStruct((width, n * CAP), BF16), (pivot_row,)
-        )
         pivot_rows = call(order_kernel, jax.ShapeDtypeStruct((width, cols), F32), (choice, gathered))
         inverse = call(
             invert_kernel,
@@ -346,13 +343,16 @@
         inverse = jnp.where(me & 1 != 0, moved, inverse)
         return leading, call(solve_kernel, jax.ShapeDtypeStruct((width, cols), F32), (inverse, pivot_rows))
 
-    gathered, lower = lax.optimization_barrier((gathered, lower))
+    gathered, lower, pivot_row = lax.optimization_barrier((gathered, lower, pivot_row))
+    choice = call(
+        functools.partial(choice_kernel, n, rows), jax.ShapeDtypeStruct((width, n * CAP), BF16), (pivot_row,)
+    )
     twins = [(r, r ^ 1) for r in range(n)]
     moved = lax.ppermute(gathered, "prow", twins)
     gathered = jnp.concatenate([gathered, moved], axis=0)
     kept, sent = split(leading)
     leading = jnp.where(me & 1 != 0, lax.ppermute(sent, "prow", twins), kept)
-    leading, upper_rows = unit(me < n, levels, lower, gathered, leading)
+    leading, upper_rows = unit(me < n, levels, lower, gathered, leading, choice)
     return call(
         functools.partial(update_kernel, m),
         jax.ShapeDtypeStruct((rows, cols), F32),

time: 31.9 us -> 30.4 us (0.953)
  Pallas kernels: 6.65 us -> 5.91 us
  other arithmetic: 0.73 us -> 0.12 us
    pallas_call x10, Pallas kernels: 6.65 us -> 5.91 us  [call(): pl.pallas_call(kernel, out_shape=outs, in_specs=in_specs or [VMEM] * len(...]
    select_n x1, other arithmetic: 0.62 us -> 0.01 us  [levels(): leading = jnp.where(me & other != 0, moved[count:], kept)]
  transfers between devices with their start and end apart: 13 -> 13, of which waited for: 6 -> 6; matrix products, arithmetic and copies ran while one was open for 2% -> 1% of each run, Pallas kernels for 12% -> 13%
where the time goes in v16:
time: 30.4 us; the launch traced here: 30.3 us
  starting transfers between devices  14.3 us (47%)
  waiting for transfers between devices  7.54 us (25%)
  Pallas kernels  5.91 us (19%)
  local copies, waits for them, and re-layouts  2.21 us (7%)
    ppermute x6, starting transfers between devices, exchange(): return lax.ppermute(block, 'pcol', [(c, c ^ d) for c in range(m)])  10.1 us
    pallas_call x10, Pallas kernels, call(): pl.pallas_call(kernel, out_shape=outs, in_specs=in_specs or [VMEM] * len(...  5.91 us
    ppermute x2, waiting for transfers between devices, levels(): moved = lax.ppermute(message, 'prow', [(r, r ^ other) for r in range(n)])  3.93 us
    ppermute x2, waiting for transfers between devices, levels(): lax.ppermute(lower, 'prow', [(r, tree_partner(r, span)) for r in range(n)])  2.74 us
    unnamed x8, local copies, waits for them, and re-layouts  2.18 us
    ppermute x2, starting transfers between devices, levels(): moved = lax.ppermute(message, 'prow', [(r, r ^ other) for r in range(n)])  1.69 us
    ppermute x2, starting transfers between devices, levels(): lax.ppermute(lower, 'prow', [(r, tree_partner(r, span)) for r in range(n)])  1.54 us
  transfers between devices with their start and end apart: 13, of which 6 were waited for; matrix products, arithmetic and copies ran while one was open for 1% of the time, Pallas kernels for 13%

profile of v16, /device:TPU:0, one launch (start us, length us, event | category | flops | bytes accessed | tf_op | source)
XLA Modules:
  0.0 30.3 jit_solution(8007133150996545669)
XLA Ops:
  0.0 0.9 %copy-done.2 = f32[1024,64]{0,1:T(8,128)S(1)} copy-done((f32[1024,64]{0,1:T(8,128)S(1)}, f32[1024,64]{0,1:T(8,128)}, u32[]{:S(2)}) %copy-start.2) | copy-done | bytes 262168
  1.0 3.1 %collective-permute-start.6 = (f32[64,256]{1,0:T(8,128)S(1)}, f32[64,256]{1,0:T(8,128)S(1)}, u32[]{:S(2)}, u32[]{:S(2)}) collective-permute-start(f32[64,256]{1,0:T(8,128)S(1)} %get-tuple-element.47.refs_0_), channel_id=1, source_target_pairs={{0,1},{1,0},{2,3},{3,2},{4,5},{5,4},{6,7},{7,6},{8,9},{9,8},{10,11... | collective-permute-start | bytes 196616 | tf_op jit(solution)/shard_map/ppermute | solution.py:286
  4.1 2.5 %collective-permute-start.7 = (f32[64,256]{1,0:T(8,128)S(1)}, f32[64,256]{1,0:T(8,128)S(1)}, u32[]{:S(2)}, u32[]{:S(2)}) collective-permute-start(f32[64,256]{1,0:T(8,128)S(1)} %get-tuple-element.47.refs_0_), channel_id=1, source_target_pairs={{0,3},{1,2},{2,1},{3,0},{4,7},{5,6},{6,5},{7,4},{8,11},{9,10},{10,... | collective-permute-start | bytes 196616 | tf_op jit(solution)/shard_map/ppermute | solution.py:286
  6.7 1.8 %collective-permute-start.10 = (f32[64,768]{1,0:T(8,128)S(1)}, f32[64,768]{1,0:T(8,128)S(1)}, u32[]{:S(2)}, u32[]{:S(2)}) collective-permute-start(f32[64,768]{1,0:T(8,128)S(1)} %get-tuple-element.53.refs_4_), channel_id=1, source_target_pairs={{0,1},{1,0},{2,3},{3,2},{4,5},{5,4},{6,7},{7,6},{8,9},{9,8},{10,11... | collective-permute-start | bytes 589832 | tf_op jit(solution)/shard_map/ppermute | solution.py:286
  8.5 1.7 %collective-permute-start.11 = (f32[64,768]{1,0:T(8,128)S(1)}, f32[64,768]{1,0:T(8,128)S(1)}, u32[]{:S(2)}, u32[]{:S(2)}) collective-permute-start(f32[64,768]{1,0:T(8,128)S(1)} %get-tuple-element.53.refs_4_), channel_id=1, source_target_pairs={{0,2},{1,3},{2,0},{3,1},{4,6},{5,7},{6,4},{7,5},{8,10},{9,11},{10,... | collective-permute-start | bytes 589832 | tf_op jit(solution)/shard_map/ppermute | solution.py:286
  10.2 0.9 %collective-permute-start.12 = (f32[64,768]{1,0:T(8,128)S(1)}, f32[64,768]{1,0:T(8,128)S(1)}, u32[]{:S(2)}, u32[]{:S(2)}) collective-permute-start(f32[64,768]{1,0:T(8,128)S(1)} %get-tuple-element.53.refs_4_), channel_id=1, source_target_pairs={{0,3},{1,2},{2,1},{3,0},{4,7},{5,6},{6,5},{7,4},{8,11},{9,10},{10,... | collective-permute-start | bytes 589832 | tf_op jit(solution)/shard_map/ppermute | solution.py:286
  11.1 1.2 %copy-done = f32[1024,256]{1,0:T(8,128)S(1)} copy-done((f32[1024,256]{1,0:T(8,128)S(1)}, f32[1024,256]{1,0:T(8,128)}, u32[]{:S(2)}) %copy-start) | copy-done | bytes 1048600
  12.3 0.7 %shard_map.37 = (f32[32,256]{1,0:T(8,128)S(1)}, f32[256,256]{1,0:T(8,128)S(1)}, s32[1,128]{1,0:T(1,128)S(1)}) custom-call(s32[1,256]{1,0:T(1,128)S(1)} %bitcast.3, f32[1024,256]{1,0:T(8,128)S(1)} %copy-done), custom_call_target="tpu_custom_call" | custom-call | flops 1 | bytes 1 | tf_op jit(solution)/shard_map/pallas_call | solution.py:266
  13.4 0.6 %collective-permute-start.5 = (f32[128,256]{1,0:T(8,128)S(1)}, f32[128,256]{1,0:T(8,128)S(1)}, u32[]{:S(2)}, u32[]{:S(2)}) collective-permute-start(f32[128,256]{1,0:T(8,128)S(1)} %slice.37), channel_id=1, source_target_pairs={{0,4},{4,0},{8,12},{12,8},{16,20},{20,16},{24,28},{28,24},{1,5},{5... | collective-permute-start | bytes 393224 | tf_op jit(solution)/shard_map/ppermute | solution.py:354
  13.9 0.3 shard_map.40
  14.2 0.3 %collective-permute-done.9 = f32[32,256]{1,0:T(8,128)S(1)} collective-permute-done((f32[32,256]{1,0:T(8,128)S(1)}, f32[32,256]{1,0:T(8,128)S(1)}, u32[]{:S(2)}, u32[]{:S(2)}) %collective-permute-start.9) | collective-permute-done | bytes 32800 | tf_op jit(solution)/shard_map/ppermute | solution.py:351
  14.6 0.4 %collective-permute-done.5 = f32[128,256]{1,0:T(8,128)S(1)} collective-permute-done((f32[128,256]{1,0:T(8,128)S(1)}, f32[128,256]{1,0:T(8,128)S(1)}, u32[]{:S(2)}, u32[]{:S(2)}) %collective-permute-start.5) | collective-permute-done | bytes 131104 | tf_op jit(solution)/shard_map/ppermute | solution.py:354
  14.9 13.3 %conditional.1 = (f32[32,256]{1,0:T(8,128)S(1)}, f32[256,256]{1,0:T(8,128)S(1)}) conditional(s32[]{:T(128)} %convert_element_type.3, () %tuple.19, (s32[]{:T(128)}, f32[256,256]{1,0:T(8,128)S(1)}, f32[128,256]{1,0:T(8,128)S(1)}, f32[64,256]{1,0:T(8,128)S(1)}, f32[192,256]{1,0:T(8,128)S(1)}, /*index=5*/bf16[256,256]{1,0:T(8,128)(2,1)S(1)}) %tuple.21), branch_computations={%region_0.1_spmd, %region_1.2_spmd} | conditional | flops 352267 | bytes 6521120 | solution.py:262
  14.9 1.5 %collective-permute-start.1 = (f32[192,256]{1,0:T(8,128)S(1)}, f32[192,256]{1,0:T(8,128)S(1)}, u32[]{:S(2)}, u32[]{:S(2)}) collective-permute-start(f32[192,256]{1,0:T(8,128)S(1)} %get-tuple-element.29.held_ref), channel_id=1, source_target_pairs={{0,16},{4,0},{8,12},{12,8},{16,20},{20,4},{24,28},{28,24},{1,17},{... | collective-permute-start | bytes 589832 | tf_op jit(solution)/shard_map/cond/branch_1_fun/ppermute | solution.py:321
  16.5 0.4 %collective-permute-start = (f32[128,256]{1,0:T(8,128)S(1)}, f32[128,256]{1,0:T(8,128)S(1)}, u32[]{:S(2)}, u32[]{:S(2)}) collective-permute-start(f32[128,256]{1,0:T(8,128)S(1)} %pad_maximum_fusion.2), channel_id=1, source_target_pairs={{0,8},{4,12},{8,0},{12,4},{16,24},{20,28},{24,16},{28,20},{1,9},{5... | collective-permute-start | bytes 393224 | tf_op jit(solution)/shard_map/cond/branch_1_fun/ppermute | solution.py:330
  16.9 2.7 %collective-permute-done.1.moved_ref = f32[192,256]{1,0:T(8,128)S(1)} collective-permute-done((f32[192,256]{1,0:T(8,128)S(1)}, f32[192,256]{1,0:T(8,128)S(1)}, u32[]{:S(2)}, u32[]{:S(2)}) %collective-permute-start.1) | collective-permute-done | bytes 196640 | tf_op jit(solution)/shard_map/cond/branch_1_fun/ppermute | solution.py:321
  19.7 1.9 %collective-permute-done = f32[128,256]{1,0:T(8,128)S(1)} collective-permute-done((f32[128,256]{1,0:T(8,128)S(1)}, f32[128,256]{1,0:T(8,128)S(1)}, u32[]{:S(2)}, u32[]{:S(2)}) %collective-permute-start) | collective-permute-done | bytes 131104 | tf_op jit(solution)/shard_map/cond/branch_1_fun/ppermute | solution.py:330
  21.6 1.3 %collective-permute-start.2 = (f32[160,256]{1,0:T(8,128)S(1)}, f32[160,256]{1,0:T(8,128)S(1)}, u32[]{:S(2)}, u32[]{:S(2)}) collective-permute-start(f32[160,256]{1,0:T(8,128)S(1)} %pad_maximum_fusion.1), channel_id=1, source_target_pairs={{0,16},{4,20},{8,24},{12,28},{16,0},{20,4},{24,8},{28,12},{1,17},{... | collective-permute-start | bytes 491528 | tf_op jit(solution)/shard_map/cond/branch_1_fun/ppermute | solution.py:330
  22.9 1.8 %branch_1_fun.7 = f32[192,256]{1,0:T(8,128)S(1)} custom-call(f32[192,256]{1,0:T(8,128)S(1)} %branch_1_fun.6.lower_ref), custom_call_target="tpu_custom_call" | custom-call | flops 1 | bytes 1 | tf_op jit(solution)/shard_map/cond/branch_1_fun/pallas_call | solution.py:266
  24.7 0.4 %collective-permute-start.4 = (f32[192,256]{1,0:T(8,128)S(1)}, f32[192,256]{1,0:T(8,128)S(1)}, u32[]{:S(2)}, u32[]{:S(2)}) collective-permute-start(f32[192,256]{1,0:T(8,128)S(1)} %branch_1_fun.7), channel_id=1, source_target_pairs={{0,4},{4,0},{8,12},{12,8},{16,20},{20,16},{24,28},{28,24},{1,5},{5... | collective-permute-start | bytes 589832 | tf_op jit(solution)/shard_map/cond/branch_1_fun/ppermute | solution.py:342
  25.1 2.1 %collective-permute-done.2 = f32[160,256]{1,0:T(8,128)S(1)} collective-permute-done((f32[160,256]{1,0:T(8,128)S(1)}, f32[160,256]{1,0:T(8,128)S(1)}, u32[]{:S(2)}, u32[]{:S(2)}) %collective-permute-start.2) | collective-permute-done | bytes 163872 | tf_op jit(solution)/shard_map/cond/branch_1_fun/ppermute | solution.py:330
  27.2 0.3 branch_1_fun.8.pivot_rows_ref
  27.5 0.7 %branch_1_fun.9 = f32[256,256]{1,0:T(8,128)S(1)} custom-call(f32[192,256]{1,0:T(8,128)S(1)} %broadcast_select_fusion.inverse_ref, f32[256,256]{1,0:T(8,128)S(1)} %branch_1_fun.8.pivot_rows_ref), custom_call_target="tpu_custom_call" | custom-call | flops 1 | bytes 1 | tf_op jit(solution)/shard_map/cond/branch_1_fun/pallas_call | solution.py:266
  28.3 2.0 %shard_map.41 = f32[1024,256]{1,0:T(8,128)} custom-call(s32[1,128]{1,0:T(1,128)S(1)} %get-tuple-element.44.local_ref, f32[32,256]{1,0:T(8,128)S(1)} %get-tuple-element.51.lead_ref, f32[256,256]{1,0:T(8,128)S(1)} %get-tuple-element.52.x_ref, f32[1024,256]{1,0:T(8,128)S(1)} %copy-done.1, f32[64,256]{1,0:T(8,128)S(1)} %get-tuple-element.47.refs_0_, ...), custom_call_target="tpu_custom_call" | custom-call | flops 1 | bytes 1 | tf_op jit(solution)/shard_map/pallas_call | solution.py:266
  (33 shorter events, 0.7 us)
Async XLA Ops:
  0.0 0.9 %copy-start.2 = (f32[1024,64]{0,1:T(8,128)S(1)}, f32[1024,64]{0,1:T(8,128)}, u32[]{:S(2)}) copy-start(f32[1024,64]{0,1:T(8,128)} %param.6) | copy-start | bytes 786436
  1.0 9.2 %collective-permute-start.6 = (f32[64,256]{1,0:T(8,128)S(1)}, f32[64,256]{1,0:T(8,128)S(1)}, u32[]{:S(2)}, u32[]{:S(2)}) collective-permute-start(f32[64,256]{1,0:T(8,128)S(1)} %get-tuple-element.47.refs_0_), channel_id=1, source_target_pairs={{0,1},{1,0},{2,3},{3,2},{4,5},{5,4},{6,7},{7,6},{8,9},{9,8},{10,11... | collective-permute-start | bytes 196616 | tf_op jit(solution)/shard_map/ppermute | solution.py:286
  4.1 8.9 %collective-permute-start.7 = (f32[64,256]{1,0:T(8,128)S(1)}, f32[64,256]{1,0:T(8,128)S(1)}, u32[]{:S(2)}, u32[]{:S(2)}) collective-permute-start(f32[64,256]{1,0:T(8,128)S(1)} %get-tuple-element.47.refs_0_), channel_id=1, source_target_pairs={{0,3},{1,2},{2,1},{3,0},{4,7},{5,6},{6,5},{7,4},{8,11},{9,10},{10,... | collective-permute-start | bytes 196616 | tf_op jit(solution)/shard_map/ppermute | solution.py:286
  6.6 6.6 %collective-permute-start.8 = (f32[64,256]{1,0:T(8,128)S(1)}, f32[64,256]{1,0:T(8,128)S(1)}, u32[]{:S(2)}, u32[]{:S(2)}) collective-permute-start(f32[64,256]{1,0:T(8,128)S(1)} %get-tuple-element.47.refs_0_), channel_id=1, source_target_pairs={{0,2},{1,3},{2,0},{3,1},{4,6},{5,7},{6,4},{7,5},{8,10},{9,11},{10,... | collective-permute-start | bytes 196616 | tf_op jit(solution)/shard_map/ppermute | solution.py:286
  6.7 4.4 %copy-start.3 = (s32[256]{0:T(256)S(1)}, s32[256]{0:T(256)}, u32[]{:S(2)}) copy-start(s32[256]{0:T(256)} %param.7) | copy-start | bytes 3076
  6.7 21.5 %collective-permute-start.10 = (f32[64,768]{1,0:T(8,128)S(1)}, f32[64,768]{1,0:T(8,128)S(1)}, u32[]{:S(2)}, u32[]{:S(2)}) collective-permute-start(f32[64,768]{1,0:T(8,128)S(1)} %get-tuple-element.53.refs_4_), channel_id=1, source_target_pairs={{0,1},{1,0},{2,3},{3,2},{4,5},{5,4},{6,7},{7,6},{8,9},{9,8},{10,11... | collective-permute-start | bytes 589832 | tf_op jit(solution)/shard_map/ppermute | solution.py:286
  8.5 19.7 %collective-permute-start.11 = (f32[64,768]{1,0:T(8,128)S(1)}, f32[64,768]{1,0:T(8,128)S(1)}, u32[]{:S(2)}, u32[]{:S(2)}) collective-permute-start(f32[64,768]{1,0:T(8,128)S(1)} %get-tuple-element.53.refs_4_), channel_id=1, source_target_pairs={{0,2},{1,3},{2,0},{3,1},{4,6},{5,7},{6,4},{7,5},{8,10},{9,11},{10,... | collective-permute-start | bytes 589832 | tf_op jit(solution)/shard_map/ppermute | solution.py:286
  10.2 18.1 %collective-permute-start.12 = (f32[64,768]{1,0:T(8,128)S(1)}, f32[64,768]{1,0:T(8,128)S(1)}, u32[]{:S(2)}, u32[]{:S(2)}) collective-permute-start(f32[64,768]{1,0:T(8,128)S(1)} %get-tuple-element.53.refs_4_), channel_id=1, source_target_pairs={{0,3},{1,2},{2,1},{3,0},{4,7},{5,6},{6,5},{7,4},{8,11},{9,10},{10,... | collective-permute-start | bytes 589832 | tf_op jit(solution)/shard_map/ppermute | solution.py:286
  11.1 1.2 %copy-start = (f32[1024,256]{1,0:T(8,128)S(1)}, f32[1024,256]{1,0:T(8,128)}, u32[]{:S(2)}) copy-start(f32[1024,256]{1,0:T(8,128)} %slab_ref.3) | copy-start | bytes 3145732
  13.3 1.3 %collective-permute-start.9 = (f32[32,256]{1,0:T(8,128)S(1)}, f32[32,256]{1,0:T(8,128)S(1)}, u32[]{:S(2)}, u32[]{:S(2)}) collective-permute-start(f32[32,256]{1,0:T(8,128)S(1)} %get-tuple-element.48), channel_id=1, source_target_pairs={{0,4},{4,0},{8,12},{12,8},{16,20},{20,16},{24,28},{28,24},{1,5},{5... | collective-permute-start | bytes 98312 | tf_op jit(solution)/shard_map/ppermute | solution.py:351
  13.4 1.5 %collective-permute-start.5 = (f32[128,256]{1,0:T(8,128)S(1)}, f32[128,256]{1,0:T(8,128)S(1)}, u32[]{:S(2)}, u32[]{:S(2)}) collective-permute-start(f32[128,256]{1,0:T(8,128)S(1)} %slice.37), channel_id=1, source_target_pairs={{0,4},{4,0},{8,12},{12,8},{16,20},{20,16},{24,28},{28,24},{1,5},{5... | collective-permute-start | bytes 393224 | tf_op jit(solution)/shard_map/ppermute | solution.py:354
  14.9 13.4 %copy-start.1 = (f32[1024,256]{1,0:T(8,128)S(1)}, f32[1024,256]{1,0:T(8,128)}, u32[]{:S(2)}) copy-start(f32[1024,256]{1,0:T(8,128)} %slab_ref.3) | copy-start | bytes 3145732
  14.9 4.7 %collective-permute-start.1 = (f32[192,256]{1,0:T(8,128)S(1)}, f32[192,256]{1,0:T(8,128)S(1)}, u32[]{:S(2)}, u32[]{:S(2)}) collective-permute-start(f32[192,256]{1,0:T(8,128)S(1)} %get-tuple-element.29.held_ref), channel_id=1, source_target_pairs={{0,16},{4,0},{8,12},{12,8},{16,20},{20,4},{24,28},{28,24},{1,17},{... | collective-permute-start | bytes 589832 | tf_op jit(solution)/shard_map/cond/branch_1_fun/ppermute | solution.py:321
  16.5 5.0 %collective-permute-start = (f32[128,256]{1,0:T(8,128)S(1)}, f32[128,256]{1,0:T(8,128)S(1)}, u32[]{:S(2)}, u32[]{:S(2)}) collective-permute-start(f32[128,256]{1,0:T(8,128)S(1)} %pad_maximum_fusion.2), channel_id=1, source_target_pairs={{0,8},{4,12},{8,0},{12,4},{16,24},{20,28},{24,16},{28,20},{1,9},{5... | collective-permute-start | bytes 393224 | tf_op jit(solution)/shard_map/cond/branch_1_fun/ppermute | solution.py:330
  19.6 3.2 %collective-permute-start.3 = (f32[192,256]{1,0:T(8,128)S(1)}, f32[192,256]{1,0:T(8,128)S(1)}, u32[]{:S(2)}, u32[]{:S(2)}) collective-permute-start(f32[192,256]{1,0:T(8,128)S(1)} %branch_1_fun.5.held_ref), channel_id=1, source_target_pairs={{0,8},{4,0},{8,12},{12,4},{16,24},{20,16},{24,28},{28,20},{1,9},{5... | collective-permute-start | bytes 589832 | tf_op jit(solution)/shard_map/cond/branch_1_fun/ppermute | solution.py:321
  21.6 5.6 %collective-permute-start.2 = (f32[160,256]{1,0:T(8,128)S(1)}, f32[160,256]{1,0:T(8,128)S(1)}, u32[]{:S(2)}, u32[]{:S(2)}) collective-permute-start(f32[160,256]{1,0:T(8,128)S(1)} %pad_maximum_fusion.1), channel_id=1, source_target_pairs={{0,16},{4,20},{8,24},{12,28},{16,0},{20,4},{24,8},{28,12},{1,17},{... | collective-permute-start | bytes 491528 | tf_op jit(solution)/shard_map/cond/branch_1_fun/ppermute | solution.py:330
  24.7 2.8 %collective-permute-start.4 = (f32[192,256]{1,0:T(8,128)S(1)}, f32[192,256]{1,0:T(8,128)S(1)}, u32[]{:S(2)}, u32[]{:S(2)}) collective-permute-start(f32[192,256]{1,0:T(8,128)S(1)} %branch_1_fun.7), channel_id=1, source_target_pairs={{0,4},{4,0},{8,12},{12,8},{16,20},{20,16},{24,28},{28,24},{1,5},{5... | collective-permute-start | bytes 589832 | tf_op jit(solution)/shard_map/cond/branch_1_fun/ppermute | solution.py:342

commit v17 on v16

--- a/solution.py
+++ b/solution.py
@@ -191,16 +191,18 @@
                 inv = inv - dot_full(dot_full(inv, jnp.where(off, corner, 0.0)), inv)
                 size *= 2
             out_ref[:half, h * half : (h + 1) * half] = inv
-        out_ref[half:, :half] = lower[half : half + half // 2, :half]
-        out_ref[half:, half:] = lower[half + half // 2 :, :half]
+        first, second = out_ref[:half, :half], out_ref[:half, half:]
+        quarter = -dot_full(dot_full(second, lower[half:, :half]), first)
+        out_ref[half:, :half] = quarter[: half // 2]
+        out_ref[half:, half:] = quarter[half // 2 :]
 
 
 def solve_kernel(inverse_ref, pivot_rows_ref, x_ref):
     half = pivot_rows_ref.shape[0] // 2
     quarter = jnp.concatenate([inverse_ref[half:, :half], inverse_ref[half:, half:]], axis=0)
-    first = dot_full(inverse_ref[:half, :half], pivot_rows_ref[:half, :])
-    x_ref[:half, :] = first
-    x_ref[half:, :] = dot_full(inverse_ref[:half, half:], pivot_rows_ref[half:, :] - dot_full(quarter, first))
+    lower_half = jnp.concatenate([quarter, inverse_ref[:half, half:]], axis=1)
+    x_ref[:half, :] = dot_full(inverse_ref[:half, :half], pivot_rows_ref[:half, :])
+    x_ref[half:, :] = dot_full(lower_half, pivot_rows_ref[...])
 
 
 def product(pieces, upper):

time: 30.4 us -> 30.1 us (level)
  no operation moved by 1% of the time
where the time goes in v17:
time: 30.1 us; the launch traced here: 29.9 us
  starting transfers between devices  14 us (47%)
  waiting for transfers between devices  7.44 us (25%)
  Pallas kernels  5.91 us (20%)
  local copies, waits for them, and re-layouts  2.21 us (7%)
    ppermute x6, starting transfers between devices, exchange(): return lax.ppermute(block, 'pcol', [(c, c ^ d) for c in range(m)])  10.1 us
    pallas_call x10, Pallas kernels, call(): pl.pallas_call(kernel, out_shape=outs, in_specs=in_specs or [VMEM] * len(...  5.91 us
    ppermute x2, waiting for transfers between devices, levels(): moved = lax.ppermute(message, 'prow', [(r, r ^ other) for r in range(n)])  3.83 us
    ppermute x2, waiting for transfers between devices, levels(): lax.ppermute(lower, 'prow', [(r, tree_partner(r, span)) for r in range(n)])  2.74 us
    unnamed x8, local copies, waits for them, and re-layouts  2.18 us
    ppermute x2, starting transfers between devices, levels(): moved = lax.ppermute(message, 'prow', [(r, r ^ other) for r in range(n)])  1.69 us
    ppermute x2, starting transfers between devices, levels(): lax.ppermute(lower, 'prow', [(r, tree_partner(r, span)) for r in range(n)])  1.54 us
  transfers between devices with their start and end apart: 13, of which 6 were waited for; matrix products, arithmetic and copies ran while one was open for 1% of the time, Pallas kernels for 13%

profile of v17, /device:TPU:0, one launch (start us, length us, event | category | flops | bytes accessed | tf_op | source)
XLA Modules:
  0.0 29.9 jit_solution(8852864133231461112)
XLA Ops:
  0.0 0.9 %copy-done.2 = f32[1024,64]{0,1:T(8,128)S(1)} copy-done((f32[1024,64]{0,1:T(8,128)S(1)}, f32[1024,64]{0,1:T(8,128)}, u32[]{:S(2)}) %copy-start.2) | copy-done | bytes 262168
  1.0 3.1 %collective-permute-start.6 = (f32[64,256]{1,0:T(8,128)S(1)}, f32[64,256]{1,0:T(8,128)S(1)}, u32[]{:S(2)}, u32[]{:S(2)}) collective-permute-start(f32[64,256]{1,0:T(8,128)S(1)} %get-tuple-element.47.refs_0_), channel_id=1, source_target_pairs={{0,1},{1,0},{2,3},{3,2},{4,5},{5,4},{6,7},{7,6},{8,9},{9,8},{10,11... | collective-permute-start | bytes 196616 | tf_op jit(solution)/shard_map/ppermute | solution.py:288
  4.1 2.5 %collective-permute-start.7 = (f32[64,256]{1,0:T(8,128)S(1)}, f32[64,256]{1,0:T(8,128)S(1)}, u32[]{:S(2)}, u32[]{:S(2)}) collective-permute-start(f32[64,256]{1,0:T(8,128)S(1)} %get-tuple-element.47.refs_0_), channel_id=1, source_target_pairs={{0,3},{1,2},{2,1},{3,0},{4,7},{5,6},{6,5},{7,4},{8,11},{9,10},{10,... | collective-permute-start | bytes 196616 | tf_op jit(solution)/shard_map/ppermute | solution.py:288
  6.7 1.8 %collective-permute-start.10 = (f32[64,768]{1,0:T(8,128)S(1)}, f32[64,768]{1,0:T(8,128)S(1)}, u32[]{:S(2)}, u32[]{:S(2)}) collective-permute-start(f32[64,768]{1,0:T(8,128)S(1)} %get-tuple-element.53.refs_4_), channel_id=1, source_target_pairs={{0,1},{1,0},{2,3},{3,2},{4,5},{5,4},{6,7},{7,6},{8,9},{9,8},{10,11... | collective-permute-start | bytes 589832 | tf_op jit(solution)/shard_map/ppermute | solution.py:288
  8.5 1.7 %collective-permute-start.11 = (f32[64,768]{1,0:T(8,128)S(1)}, f32[64,768]{1,0:T(8,128)S(1)}, u32[]{:S(2)}, u32[]{:S(2)}) collective-permute-start(f32[64,768]{1,0:T(8,128)S(1)} %get-tuple-element.53.refs_4_), channel_id=1, source_target_pairs={{0,2},{1,3},{2,0},{3,1},{4,6},{5,7},{6,4},{7,5},{8,10},{9,11},{10,... | collective-permute-start | bytes 589832 | tf_op jit(solution)/shard_map/ppermute | solution.py:288
  10.2 0.9 %collective-permute-start.12 = (f32[64,768]{1,0:T(8,128)S(1)}, f32[64,768]{1,0:T(8,128)S(1)}, u32[]{:S(2)}, u32[]{:S(2)}) collective-permute-start(f32[64,768]{1,0:T(8,128)S(1)} %get-tuple-element.53.refs_4_), channel_id=1, source_target_pairs={{0,3},{1,2},{2,1},{3,0},{4,7},{5,6},{6,5},{7,4},{8,11},{9,10},{10,... | collective-permute-start | bytes 589832 | tf_op jit(solution)/shard_map/ppermute | solution.py:288
  11.1 1.2 %copy-done = f32[1024,256]{1,0:T(8,128)S(1)} copy-done((f32[1024,256]{1,0:T(8,128)S(1)}, f32[1024,256]{1,0:T(8,128)}, u32[]{:S(2)}) %copy-start) | copy-done | bytes 1048600
  12.3 0.7 %shard_map.37 = (f32[32,256]{1,0:T(8,128)S(1)}, f32[256,256]{1,0:T(8,128)S(1)}, s32[1,128]{1,0:T(1,128)S(1)}) custom-call(s32[1,256]{1,0:T(1,128)S(1)} %bitcast.3, f32[1024,256]{1,0:T(8,128)S(1)} %copy-done), custom_call_target="tpu_custom_call" | custom-call | flops 1 | bytes 1 | tf_op jit(solution)/shard_map/pallas_call | solution.py:268
  13.1 0.2 collective-permute-done.8.refs_3_
  13.4 0.6 %collective-permute-start.5 = (f32[128,256]{1,0:T(8,128)S(1)}, f32[128,256]{1,0:T(8,128)S(1)}, u32[]{:S(2)}, u32[]{:S(2)}) collective-permute-start(f32[128,256]{1,0:T(8,128)S(1)} %slice.37), channel_id=1, source_target_pairs={{0,4},{4,0},{8,12},{12,8},{16,20},{20,16},{24,28},{28,24},{1,5},{5... | collective-permute-start | bytes 393224 | tf_op jit(solution)/shard_map/ppermute | solution.py:356
  13.9 0.3 shard_map.40
  14.2 0.3 %collective-permute-done.9 = f32[32,256]{1,0:T(8,128)S(1)} collective-permute-done((f32[32,256]{1,0:T(8,128)S(1)}, f32[32,256]{1,0:T(8,128)S(1)}, u32[]{:S(2)}, u32[]{:S(2)}) %collective-permute-start.9) | collective-permute-done | bytes 32800 | tf_op jit(solution)/shard_map/ppermute | solution.py:353
  14.6 0.4 %collective-permute-done.5 = f32[128,256]{1,0:T(8,128)S(1)} collective-permute-done((f32[128,256]{1,0:T(8,128)S(1)}, f32[128,256]{1,0:T(8,128)S(1)}, u32[]{:S(2)}, u32[]{:S(2)}) %collective-permute-start.5) | collective-permute-done | bytes 131104 | tf_op jit(solution)/shard_map/ppermute | solution.py:356
  14.9 12.9 %conditional.1 = (f32[32,256]{1,0:T(8,128)S(1)}, f32[256,256]{1,0:T(8,128)S(1)}) conditional(s32[]{:T(128)} %convert_element_type.3, () %tuple.19, (s32[]{:T(128)}, f32[256,256]{1,0:T(8,128)S(1)}, f32[128,256]{1,0:T(8,128)S(1)}, f32[64,256]{1,0:T(8,128)S(1)}, f32[192,256]{1,0:T(8,128)S(1)}, /*index=5*/bf16[256,256]{1,0:T(8,128)(2,1)S(1)}) %tuple.21), branch_computations={%region_0.1_spmd, %region_1.2_spmd} | conditional | flops 352267 | bytes 6521120 | solution.py:264
  14.9 1.5 %collective-permute-start.1 = (f32[192,256]{1,0:T(8,128)S(1)}, f32[192,256]{1,0:T(8,128)S(1)}, u32[]{:S(2)}, u32[]{:S(2)}) collective-permute-start(f32[192,256]{1,0:T(8,128)S(1)} %get-tuple-element.29.held_ref), channel_id=1, source_target_pairs={{0,16},{4,0},{8,12},{12,8},{16,20},{20,4},{24,28},{28,24},{1,17},{... | collective-permute-start | bytes 589832 | tf_op jit(solution)/shard_map/cond/branch_1_fun/ppermute | solution.py:323
  16.5 0.4 %collective-permute-start = (f32[128,256]{1,0:T(8,128)S(1)}, f32[128,256]{1,0:T(8,128)S(1)}, u32[]{:S(2)}, u32[]{:S(2)}) collective-permute-start(f32[128,256]{1,0:T(8,128)S(1)} %pad_maximum_fusion.2), channel_id=1, source_target_pairs={{0,8},{4,12},{8,0},{12,4},{16,24},{20,28},{24,16},{28,20},{1,9},{5... | collective-permute-start | bytes 393224 | tf_op jit(solution)/shard_map/cond/branch_1_fun/ppermute | solution.py:332
  16.9 2.7 %collective-permute-done.1.moved_ref = f32[192,256]{1,0:T(8,128)S(1)} collective-permute-done((f32[192,256]{1,0:T(8,128)S(1)}, f32[192,256]{1,0:T(8,128)S(1)}, u32[]{:S(2)}, u32[]{:S(2)}) %collective-permute-start.1) | collective-permute-done | bytes 196640 | tf_op jit(solution)/shard_map/cond/branch_1_fun/ppermute | solution.py:323
  19.7 1.9 %collective-permute-done = f32[128,256]{1,0:T(8,128)S(1)} collective-permute-done((f32[128,256]{1,0:T(8,128)S(1)}, f32[128,256]{1,0:T(8,128)S(1)}, u32[]{:S(2)}, u32[]{:S(2)}) %collective-permute-start) | collective-permute-done | bytes 131104 | tf_op jit(solution)/shard_map/cond/branch_1_fun/ppermute | solution.py:332
  21.6 1.3 %collective-permute-start.2 = (f32[160,256]{1,0:T(8,128)S(1)}, f32[160,256]{1,0:T(8,128)S(1)}, u32[]{:S(2)}, u32[]{:S(2)}) collective-permute-start(f32[160,256]{1,0:T(8,128)S(1)} %pad_maximum_fusion.1), channel_id=1, source_target_pairs={{0,16},{4,20},{8,24},{12,28},{16,0},{20,4},{24,8},{28,12},{1,17},{... | collective-permute-start | bytes 491528 | tf_op jit(solution)/shard_map/cond/branch_1_fun/ppermute | solution.py:332
  22.9 2.2 %branch_1_fun.7 = f32[192,256]{1,0:T(8,128)S(1)} custom-call(f32[192,256]{1,0:T(8,128)S(1)} %branch_1_fun.6.lower_ref), custom_call_target="tpu_custom_call" | custom-call | flops 1 | bytes 1 | tf_op jit(solution)/shard_map/cond/branch_1_fun/pallas_call | solution.py:268
  25.2 2.0 %collective-permute-done.2 = f32[160,256]{1,0:T(8,128)S(1)} collective-permute-done((f32[160,256]{1,0:T(8,128)S(1)}, f32[160,256]{1,0:T(8,128)S(1)}, u32[]{:S(2)}, u32[]{:S(2)}) %collective-permute-start.2) | collective-permute-done | bytes 163872 | tf_op jit(solution)/shard_map/cond/branch_1_fun/ppermute | solution.py:332
  27.2 0.3 branch_1_fun.8.pivot_rows_ref
  27.5 0.3 %branch_1_fun.9 = f32[256,256]{1,0:T(8,128)S(1)} custom-call(f32[192,256]{1,0:T(8,128)S(1)} %broadcast_select_fusion.inverse_ref, f32[256,256]{1,0:T(8,128)S(1)} %branch_1_fun.8.pivot_rows_ref), custom_call_target="tpu_custom_call" | custom-call | flops 1 | bytes 1 | tf_op jit(solution)/shard_map/cond/branch_1_fun/pallas_call | solution.py:268
  27.9 2.0 %shard_map.41 = f32[1024,256]{1,0:T(8,128)} custom-call(s32[1,128]{1,0:T(1,128)S(1)} %get-tuple-element.44.local_ref, f32[32,256]{1,0:T(8,128)S(1)} %get-tuple-element.51.lead_ref, f32[256,256]{1,0:T(8,128)S(1)} %get-tuple-element.52.x_ref, f32[1024,256]{1,0:T(8,128)S(1)} %copy-done.1, f32[64,256]{1,0:T(8,128)S(1)} %get-tuple-element.47.refs_0_, ...), custom_call_target="tpu_custom_call" | custom-call | flops 1 | bytes 1 | tf_op jit(solution)/shard_map/pallas_call | solution.py:268
  (33 shorter events, 0.6 us)
Async XLA Ops:
  0.0 0.9 %copy-start.2 = (f32[1024,64]{0,1:T(8,128)S(1)}, f32[1024,64]{0,1:T(8,128)}, u32[]{:S(2)}) copy-start(f32[1024,64]{0,1:T(8,128)} %param.6) | copy-start | bytes 786436
  1.0 9.2 %collective-permute-start.6 = (f32[64,256]{1,0:T(8,128)S(1)}, f32[64,256]{1,0:T(8,128)S(1)}, u32[]{:S(2)}, u32[]{:S(2)}) collective-permute-start(f32[64,256]{1,0:T(8,128)S(1)} %get-tuple-element.47.refs_0_), channel_id=1, source_target_pairs={{0,1},{1,0},{2,3},{3,2},{4,5},{5,4},{6,7},{7,6},{8,9},{9,8},{10,11... | collective-permute-start | bytes 196616 | tf_op jit(solution)/shard_map/ppermute | solution.py:288
  4.1 8.9 %collective-permute-start.7 = (f32[64,256]{1,0:T(8,128)S(1)}, f32[64,256]{1,0:T(8,128)S(1)}, u32[]{:S(2)}, u32[]{:S(2)}) collective-permute-start(f32[64,256]{1,0:T(8,128)S(1)} %get-tuple-element.47.refs_0_), channel_id=1, source_target_pairs={{0,3},{1,2},{2,1},{3,0},{4,7},{5,6},{6,5},{7,4},{8,11},{9,10},{10,... | collective-permute-start | bytes 196616 | tf_op jit(solution)/shard_map/ppermute | solution.py:288
  6.6 6.6 %collective-permute-start.8 = (f32[64,256]{1,0:T(8,128)S(1)}, f32[64,256]{1,0:T(8,128)S(1)}, u32[]{:S(2)}, u32[]{:S(2)}) collective-permute-start(f32[64,256]{1,0:T(8,128)S(1)} %get-tuple-element.47.refs_0_), channel_id=1, source_target_pairs={{0,2},{1,3},{2,0},{3,1},{4,6},{5,7},{6,4},{7,5},{8,10},{9,11},{10,... | collective-permute-start | bytes 196616 | tf_op jit(solution)/shard_map/ppermute | solution.py:288
  6.7 4.4 %copy-start.3 = (s32[256]{0:T(256)S(1)}, s32[256]{0:T(256)}, u32[]{:S(2)}) copy-start(s32[256]{0:T(256)} %param.7) | copy-start | bytes 3076
  6.7 21.2 %collective-permute-start.10 = (f32[64,768]{1,0:T(8,128)S(1)}, f32[64,768]{1,0:T(8,128)S(1)}, u32[]{:S(2)}, u32[]{:S(2)}) collective-permute-start(f32[64,768]{1,0:T(8,128)S(1)} %get-tuple-element.53.refs_4_), channel_id=1, source_target_pairs={{0,1},{1,0},{2,3},{3,2},{4,5},{5,4},{6,7},{7,6},{8,9},{9,8},{10,11... | collective-permute-start | bytes 589832 | tf_op jit(solution)/shard_map/ppermute | solution.py:288
  8.5 19.4 %collective-permute-start.11 = (f32[64,768]{1,0:T(8,128)S(1)}, f32[64,768]{1,0:T(8,128)S(1)}, u32[]{:S(2)}, u32[]{:S(2)}) collective-permute-start(f32[64,768]{1,0:T(8,128)S(1)} %get-tuple-element.53.refs_4_), channel_id=1, source_target_pairs={{0,2},{1,3},{2,0},{3,1},{4,6},{5,7},{6,4},{7,5},{8,10},{9,11},{10,... | collective-permute-start | bytes 589832 | tf_op jit(solution)/shard_map/ppermute | solution.py:288
  10.2 17.7 %collective-permute-start.12 = (f32[64,768]{1,0:T(8,128)S(1)}, f32[64,768]{1,0:T(8,128)S(1)}, u32[]{:S(2)}, u32[]{:S(2)}) collective-permute-start(f32[64,768]{1,0:T(8,128)S(1)} %get-tuple-element.53.refs_4_), channel_id=1, source_target_pairs={{0,3},{1,2},{2,1},{3,0},{4,7},{5,6},{6,5},{7,4},{8,11},{9,10},{10,... | collective-permute-start | bytes 589832 | tf_op jit(solution)/shard_map/ppermute | solution.py:288
  11.1 1.2 %copy-start = (f32[1024,256]{1,0:T(8,128)S(1)}, f32[1024,256]{1,0:T(8,128)}, u32[]{:S(2)}) copy-start(f32[1024,256]{1,0:T(8,128)} %slab_ref.3) | copy-start | bytes 3145732
  13.3 1.3 %collective-permute-start.9 = (f32[32,256]{1,0:T(8,128)S(1)}, f32[32,256]{1,0:T(8,128)S(1)}, u32[]{:S(2)}, u32[]{:S(2)}) collective-permute-start(f32[32,256]{1,0:T(8,128)S(1)} %get-tuple-element.48), channel_id=1, source_target_pairs={{0,4},{4,0},{8,12},{12,8},{16,20},{20,16},{24,28},{28,24},{1,5},{5... | collective-permute-start | bytes 98312 | tf_op jit(solution)/shard_map/ppermute | solution.py:353
  13.4 1.5 %collective-permute-start.5 = (f32[128,256]{1,0:T(8,128)S(1)}, f32[128,256]{1,0:T(8,128)S(1)}, u32[]{:S(2)}, u32[]{:S(2)}) collective-permute-start(f32[128,256]{1,0:T(8,128)S(1)} %slice.37), channel_id=1, source_target_pairs={{0,4},{4,0},{8,12},{12,8},{16,20},{20,16},{24,28},{28,24},{1,5},{5... | collective-permute-start | bytes 393224 | tf_op jit(solution)/shard_map/ppermute | solution.py:356
  14.9 13.0 %copy-start.1 = (f32[1024,256]{1,0:T(8,128)S(1)}, f32[1024,256]{1,0:T(8,128)}, u32[]{:S(2)}) copy-start(f32[1024,256]{1,0:T(8,128)} %slab_ref.3) | copy-start | bytes 3145732
  14.9 4.7 %collective-permute-start.1 = (f32[192,256]{1,0:T(8,128)S(1)}, f32[192,256]{1,0:T(8,128)S(1)}, u32[]{:S(2)}, u32[]{:S(2)}) collective-permute-start(f32[192,256]{1,0:T(8,128)S(1)} %get-tuple-element.29.held_ref), channel_id=1, source_target_pairs={{0,16},{4,0},{8,12},{12,8},{16,20},{20,4},{24,28},{28,24},{1,17},{... | collective-permute-start | bytes 589832 | tf_op jit(solution)/shard_map/cond/branch_1_fun/ppermute | solution.py:323
  16.5 5.0 %collective-permute-start = (f32[128,256]{1,0:T(8,128)S(1)}, f32[128,256]{1,0:T(8,128)S(1)}, u32[]{:S(2)}, u32[]{:S(2)}) collective-permute-start(f32[128,256]{1,0:T(8,128)S(1)} %pad_maximum_fusion.2), channel_id=1, source_target_pairs={{0,8},{4,12},{8,0},{12,4},{16,24},{20,28},{24,16},{28,20},{1,9},{5... | collective-permute-start | bytes 393224 | tf_op jit(solution)/shard_map/cond/branch_1_fun/ppermute | solution.py:332
  19.6 3.2 %collective-permute-start.3 = (f32[192,256]{1,0:T(8,128)S(1)}, f32[192,256]{1,0:T(8,128)S(1)}, u32[]{:S(2)}, u32[]{:S(2)}) collective-permute-start(f32[192,256]{1,0:T(8,128)S(1)} %branch_1_fun.5.held_ref), channel_id=1, source_target_pairs={{0,8},{4,0},{8,12},{12,4},{16,24},{20,16},{24,28},{28,20},{1,9},{5... | collective-permute-start | bytes 589832 | tf_op jit(solution)/shard_map/cond/branch_1_fun/ppermute | solution.py:323
  21.6 5.6 %collective-permute-start.2 = (f32[160,256]{1,0:T(8,128)S(1)}, f32[160,256]{1,0:T(8,128)S(1)}, u32[]{:S(2)}, u32[]{:S(2)}) collective-permute-start(f32[160,256]{1,0:T(8,128)S(1)} %pad_maximum_fusion.1), channel_id=1, source_target_pairs={{0,16},{4,20},{8,24},{12,28},{16,0},{20,4},{24,8},{28,12},{1,17},{... | collective-permute-start | bytes 491528 | tf_op jit(solution)/shard_map/cond/branch_1_fun/ppermute | solution.py:332
  25.1 2.4 %collective-permute-start.4 = (f32[192,256]{1,0:T(8,128)S(1)}, f32[192,256]{1,0:T(8,128)S(1)}, u32[]{:S(2)}, u32[]{:S(2)}) collective-permute-start(f32[192,256]{1,0:T(8,128)S(1)} %branch_1_fun.7), channel_id=1, source_target_pairs={{0,4},{4,0},{8,12},{12,8},{16,20},{20,16},{24,28},{28,24},{1,5},{5... | collective-permute-start | bytes 589832 | tf_op jit(solution)/shard_map/cond/branch_1_fun/ppermute | solution.py:344

commit v18 on v17

--- a/solution.py
+++ b/solution.py
@@ -230,16 +230,17 @@
     rows = slab_ref.shape[0]
     width = x_ref.shape[0]
     blocks = rows // width
-    fetch = pltpu.make_async_copy(local_ref, swaps, sems.at[blocks])
+    fetch = pltpu.make_async_copy(local_ref, swaps, sems.at[blocks + 1])
     fetch.start()
     result[:rows, :] = slab_ref[...]
     top_upper = split2(jnp.concatenate([piece_rows(x_ref, m, d) for d in top_order(m)], axis=0))
     upper = split2(jnp.concatenate([piece_rows(x_ref, m, d) for d in range(m)], axis=0))
     copies = []
-    for c in range(blocks):
-        part = pl.ds(c * width, width)
+    starts = [*range(0, rows, width), rows - width // 2, rows]
+    for c, (start, stop) in enumerate(zip(starts, starts[1:])):
+        part = pl.ds(start, stop - start)
         if c:
-            total = product([rest[:, (c - 1) * width : c * width] for rest in rests], upper)
+            total = product([rest[:, start - width : stop - width] for rest in rests], upper)
         else:
             total = product([top[...] for top in tops], top_upper)
             fetch.wait()
@@ -364,7 +365,7 @@
         scratch=[
             pltpu.VMEM((rows + 8, cols), F32),
             pltpu.SMEM((1, 128), jnp.int32),
-            pltpu.SemaphoreType.DMA((rows // width + 1,)),
+            pltpu.SemaphoreType.DMA((rows // width + 2,)),
         ],
     )
 

time: 30.1 us -> 30.1 us (level)
  no operation moved by 1% of the time
where the time goes in v18:
time: 30.1 us; the launch traced here: 29.9 us
  starting transfers between devices  14 us (47%)
  waiting for transfers between devices  7.44 us (25%)
  Pallas kernels  5.88 us (20%)
  local copies, waits for them, and re-layouts  2.21 us (7%)
    ppermute x6, starting transfers between devices, exchange(): return lax.ppermute(block, 'pcol', [(c, c ^ d) for c in range(m)])  10.1 us
    pallas_call x10, Pallas kernels, call(): pl.pallas_call(kernel, out_shape=outs, in_specs=in_specs or [VMEM] * len(...  5.88 us
    ppermute x2, waiting for transfers between devices, levels(): moved = lax.ppermute(message, 'prow', [(r, r ^ other) for r in range(n)])  3.83 us
    ppermute x2, waiting for transfers between devices, levels(): lax.ppermute(lower, 'prow', [(r, tree_partner(r, span)) for r in range(n)])  2.74 us
    unnamed x8, local copies, waits for them, and re-layouts  2.18 us
    ppermute x2, starting transfers between devices, levels(): moved = lax.ppermute(message, 'prow', [(r, r ^ other) for r in range(n)])  1.69 us
    ppermute x2, starting transfers between devices, levels(): lax.ppermute(lower, 'prow', [(r, tree_partner(r, span)) for r in range(n)])  1.54 us
  transfers between devices with their start and end apart: 13, of which 6 were waited for; matrix products, arithmetic and copies ran while one was open for 1% of the time, Pallas kernels for 13%

profile of v18, /device:TPU:0, one launch (start us, length us, event | category | flops | bytes accessed | tf_op | source)
XLA Modules:
  0.0 29.9 jit_solution(4222286814697975060)
XLA Ops:
  0.0 0.9 %copy-done.2 = f32[1024,64]{0,1:T(8,128)S(1)} copy-done((f32[1024,64]{0,1:T(8,128)S(1)}, f32[1024,64]{0,1:T(8,128)}, u32[]{:S(2)}) %copy-start.2) | copy-done | bytes 262168
  1.0 3.1 %collective-permute-start.6 = (f32[64,256]{1,0:T(8,128)S(1)}, f32[64,256]{1,0:T(8,128)S(1)}, u32[]{:S(2)}, u32[]{:S(2)}) collective-permute-start(f32[64,256]{1,0:T(8,128)S(1)} %get-tuple-element.47.refs_0_), channel_id=1, source_target_pairs={{0,1},{1,0},{2,3},{3,2},{4,5},{5,4},{6,7},{7,6},{8,9},{9,8},{10,11... | collective-permute-start | bytes 196616 | tf_op jit(solution)/shard_map/ppermute | solution.py:289
  4.1 2.5 %collective-permute-start.7 = (f32[64,256]{1,0:T(8,128)S(1)}, f32[64,256]{1,0:T(8,128)S(1)}, u32[]{:S(2)}, u32[]{:S(2)}) collective-permute-start(f32[64,256]{1,0:T(8,128)S(1)} %get-tuple-element.47.refs_0_), channel_id=1, source_target_pairs={{0,3},{1,2},{2,1},{3,0},{4,7},{5,6},{6,5},{7,4},{8,11},{9,10},{10,... | collective-permute-start | bytes 196616 | tf_op jit(solution)/shard_map/ppermute | solution.py:289
  6.7 1.8 %collective-permute-start.10 = (f32[64,768]{1,0:T(8,128)S(1)}, f32[64,768]{1,0:T(8,128)S(1)}, u32[]{:S(2)}, u32[]{:S(2)}) collective-permute-start(f32[64,768]{1,0:T(8,128)S(1)} %get-tuple-element.53.refs_4_), channel_id=1, source_target_pairs={{0,1},{1,0},{2,3},{3,2},{4,5},{5,4},{6,7},{7,6},{8,9},{9,8},{10,11... | collective-permute-start | bytes 589832 | tf_op jit(solution)/shard_map/ppermute | solution.py:289
  8.5 1.7 %collective-permute-start.11 = (f32[64,768]{1,0:T(8,128)S(1)}, f32[64,768]{1,0:T(8,128)S(1)}, u32[]{:S(2)}, u32[]{:S(2)}) collective-permute-start(f32[64,768]{1,0:T(8,128)S(1)} %get-tuple-element.53.refs_4_), channel_id=1, source_target_pairs={{0,2},{1,3},{2,0},{3,1},{4,6},{5,7},{6,4},{7,5},{8,10},{9,11},{10,... | collective-permute-start | bytes 589832 | tf_op jit(solution)/shard_map/ppermute | solution.py:289
  10.2 0.9 %collective-permute-start.12 = (f32[64,768]{1,0:T(8,128)S(1)}, f32[64,768]{1,0:T(8,128)S(1)}, u32[]{:S(2)}, u32[]{:S(2)}) collective-permute-start(f32[64,768]{1,0:T(8,128)S(1)} %get-tuple-element.53.refs_4_), channel_id=1, source_target_pairs={{0,3},{1,2},{2,1},{3,0},{4,7},{5,6},{6,5},{7,4},{8,11},{9,10},{10,... | collective-permute-start | bytes 589832 | tf_op jit(solution)/shard_map/ppermute | solution.py:289
  11.1 1.2 %copy-done = f32[1024,256]{1,0:T(8,128)S(1)} copy-done((f32[1024,256]{1,0:T(8,128)S(1)}, f32[1024,256]{1,0:T(8,128)}, u32[]{:S(2)}) %copy-start) | copy-done | bytes 1048600
  12.3 0.7 %shard_map.37 = (f32[32,256]{1,0:T(8,128)S(1)}, f32[256,256]{1,0:T(8,128)S(1)}, s32[1,128]{1,0:T(1,128)S(1)}) custom-call(s32[1,256]{1,0:T(1,128)S(1)} %bitcast.3, f32[1024,256]{1,0:T(8,128)S(1)} %copy-done), custom_call_target="tpu_custom_call" | custom-call | flops 1 | bytes 1 | tf_op jit(solution)/shard_map/pallas_call | solution.py:269
  13.1 0.2 collective-permute-done.8.refs_3_
  13.4 0.6 %collective-permute-start.5 = (f32[128,256]{1,0:T(8,128)S(1)}, f32[128,256]{1,0:T(8,128)S(1)}, u32[]{:S(2)}, u32[]{:S(2)}) collective-permute-start(f32[128,256]{1,0:T(8,128)S(1)} %slice.37), channel_id=1, source_target_pairs={{0,4},{4,0},{8,12},{12,8},{16,20},{20,16},{24,28},{28,24},{1,5},{5... | collective-permute-start | bytes 393224 | tf_op jit(solution)/shard_map/ppermute | solution.py:357
  13.9 0.3 shard_map.40
  14.2 0.3 %collective-permute-done.9 = f32[32,256]{1,0:T(8,128)S(1)} collective-permute-done((f32[32,256]{1,0:T(8,128)S(1)}, f32[32,256]{1,0:T(8,128)S(1)}, u32[]{:S(2)}, u32[]{:S(2)}) %collective-permute-start.9) | collective-permute-done | bytes 32800 | tf_op jit(solution)/shard_map/ppermute | solution.py:354
  14.6 0.4 %collective-permute-done.5 = f32[128,256]{1,0:T(8,128)S(1)} collective-permute-done((f32[128,256]{1,0:T(8,128)S(1)}, f32[128,256]{1,0:T(8,128)S(1)}, u32[]{:S(2)}, u32[]{:S(2)}) %collective-permute-start.5) | collective-permute-done | bytes 131104 | tf_op jit(solution)/shard_map/ppermute | solution.py:357
  14.9 12.9 %conditional.1 = (f32[32,256]{1,0:T(8,128)S(1)}, f32[256,256]{1,0:T(8,128)S(1)}) conditional(s32[]{:T(128)} %convert_element_type.3, () %tuple.19, (s32[]{:T(128)}, f32[256,256]{1,0:T(8,128)S(1)}, f32[128,256]{1,0:T(8,128)S(1)}, f32[64,256]{1,0:T(8,128)S(1)}, f32[192,256]{1,0:T(8,128)S(1)}, /*index=5*/bf16[256,256]{1,0:T(8,128)(2,1)S(1)}) %tuple.21), branch_computations={%region_0.1_spmd, %region_1.2_spmd} | conditional | flops 352267 | bytes 6521120 | solution.py:265
  14.9 1.5 %collective-permute-start.1 = (f32[192,256]{1,0:T(8,128)S(1)}, f32[192,256]{1,0:T(8,128)S(1)}, u32[]{:S(2)}, u32[]{:S(2)}) collective-permute-start(f32[192,256]{1,0:T(8,128)S(1)} %get-tuple-element.29.held_ref), channel_id=1, source_target_pairs={{0,16},{4,0},{8,12},{12,8},{16,20},{20,4},{24,28},{28,24},{1,17},{... | collective-permute-start | bytes 589832 | tf_op jit(solution)/shard_map/cond/branch_1_fun/ppermute | solution.py:324
  16.5 0.4 %collective-permute-start = (f32[128,256]{1,0:T(8,128)S(1)}, f32[128,256]{1,0:T(8,128)S(1)}, u32[]{:S(2)}, u32[]{:S(2)}) collective-permute-start(f32[128,256]{1,0:T(8,128)S(1)} %pad_maximum_fusion.2), channel_id=1, source_target_pairs={{0,8},{4,12},{8,0},{12,4},{16,24},{20,28},{24,16},{28,20},{1,9},{5... | collective-permute-start | bytes 393224 | tf_op jit(solution)/shard_map/cond/branch_1_fun/ppermute | solution.py:333
  16.9 2.7 %collective-permute-done.1.moved_ref = f32[192,256]{1,0:T(8,128)S(1)} collective-permute-done((f32[192,256]{1,0:T(8,128)S(1)}, f32[192,256]{1,0:T(8,128)S(1)}, u32[]{:S(2)}, u32[]{:S(2)}) %collective-permute-start.1) | collective-permute-done | bytes 196640 | tf_op jit(solution)/shard_map/cond/branch_1_fun/ppermute | solution.py:324
  19.7 1.9 %collective-permute-done = f32[128,256]{1,0:T(8,128)S(1)} collective-permute-done((f32[128,256]{1,0:T(8,128)S(1)}, f32[128,256]{1,0:T(8,128)S(1)}, u32[]{:S(2)}, u32[]{:S(2)}) %collective-permute-start) | collective-permute-done | bytes 131104 | tf_op jit(solution)/shard_map/cond/branch_1_fun/ppermute | solution.py:333
  21.6 1.3 %collective-permute-start.2 = (f32[160,256]{1,0:T(8,128)S(1)}, f32[160,256]{1,0:T(8,128)S(1)}, u32[]{:S(2)}, u32[]{:S(2)}) collective-permute-start(f32[160,256]{1,0:T(8,128)S(1)} %pad_maximum_fusion.1), channel_id=1, source_target_pairs={{0,16},{4,20},{8,24},{12,28},{16,0},{20,4},{24,8},{28,12},{1,17},{... | collective-permute-start | bytes 491528 | tf_op jit(solution)/shard_map/cond/branch_1_fun/ppermute | solution.py:333
  22.9 2.2 %branch_1_fun.7 = f32[192,256]{1,0:T(8,128)S(1)} custom-call(f32[192,256]{1,0:T(8,128)S(1)} %branch_1_fun.6.lower_ref), custom_call_target="tpu_custom_call" | custom-call | flops 1 | bytes 1 | tf_op jit(solution)/shard_map/cond/branch_1_fun/pallas_call | solution.py:269
  25.2 2.0 %collective-permute-done.2 = f32[160,256]{1,0:T(8,128)S(1)} collective-permute-done((f32[160,256]{1,0:T(8,128)S(1)}, f32[160,256]{1,0:T(8,128)S(1)}, u32[]{:S(2)}, u32[]{:S(2)}) %collective-permute-start.2) | collective-permute-done | bytes 163872 | tf_op jit(solution)/shard_map/cond/branch_1_fun/ppermute | solution.py:333
  27.2 0.3 branch_1_fun.8.pivot_rows_ref
  27.5 0.3 %branch_1_fun.9 = f32[256,256]{1,0:T(8,128)S(1)} custom-call(f32[192,256]{1,0:T(8,128)S(1)} %broadcast_select_fusion.inverse_ref, f32[256,256]{1,0:T(8,128)S(1)} %branch_1_fun.8.pivot_rows_ref), custom_call_target="tpu_custom_call" | custom-call | flops 1 | bytes 1 | tf_op jit(solution)/shard_map/cond/branch_1_fun/pallas_call | solution.py:269
  27.9 2.0 %shard_map.41 = f32[1024,256]{1,0:T(8,128)} custom-call(s32[1,128]{1,0:T(1,128)S(1)} %get-tuple-element.44.local_ref, f32[32,256]{1,0:T(8,128)S(1)} %get-tuple-element.51.lead_ref, f32[256,256]{1,0:T(8,128)S(1)} %get-tuple-element.52.x_ref, f32[1024,256]{1,0:T(8,128)S(1)} %copy-done.1, f32[64,256]{1,0:T(8,128)S(1)} %get-tuple-element.47.refs_0_, ...), custom_call_target="tpu_custom_call" | custom-call | flops 1 | bytes 1 | tf_op jit(solution)/shard_map/pallas_call | solution.py:269
  (33 shorter events, 0.6 us)
Async XLA Ops:
  0.0 0.9 %copy-start.2 = (f32[1024,64]{0,1:T(8,128)S(1)}, f32[1024,64]{0,1:T(8,128)}, u32[]{:S(2)}) copy-start(f32[1024,64]{0,1:T(8,128)} %param.6) | copy-start | bytes 786436
  1.0 9.2 %collective-permute-start.6 = (f32[64,256]{1,0:T(8,128)S(1)}, f32[64,256]{1,0:T(8,128)S(1)}, u32[]{:S(2)}, u32[]{:S(2)}) collective-permute-start(f32[64,256]{1,0:T(8,128)S(1)} %get-tuple-element.47.refs_0_), channel_id=1, source_target_pairs={{0,1},{1,0},{2,3},{3,2},{4,5},{5,4},{6,7},{7,6},{8,9},{9,8},{10,11... | collective-permute-start | bytes 196616 | tf_op jit(solution)/shard_map/ppermute | solution.py:289
  4.1 8.9 %collective-permute-start.7 = (f32[64,256]{1,0:T(8,128)S(1)}, f32[64,256]{1,0:T(8,128)S(1)}, u32[]{:S(2)}, u32[]{:S(2)}) collective-permute-start(f32[64,256]{1,0:T(8,128)S(1)} %get-tuple-element.47.refs_0_), channel_id=1, source_target_pairs={{0,3},{1,2},{2,1},{3,0},{4,7},{5,6},{6,5},{7,4},{8,11},{9,10},{10,... | collective-permute-start | bytes 196616 | tf_op jit(solution)/shard_map/ppermute | solution.py:289
  6.6 6.6 %collective-permute-start.8 = (f32[64,256]{1,0:T(8,128)S(1)}, f32[64,256]{1,0:T(8,128)S(1)}, u32[]{:S(2)}, u32[]{:S(2)}) collective-permute-start(f32[64,256]{1,0:T(8,128)S(1)} %get-tuple-element.47.refs_0_), channel_id=1, source_target_pairs={{0,2},{1,3},{2,0},{3,1},{4,6},{5,7},{6,4},{7,5},{8,10},{9,11},{10,... | collective-permute-start | bytes 196616 | tf_op jit(solution)/shard_map/ppermute | solution.py:289
  6.7 4.4 %copy-start.3 = (s32[256]{0:T(256)S(1)}, s32[256]{0:T(256)}, u32[]{:S(2)}) copy-start(s32[256]{0:T(256)} %param.7) | copy-start | bytes 3076
  6.7 21.2 %collective-permute-start.10 = (f32[64,768]{1,0:T(8,128)S(1)}, f32[64,768]{1,0:T(8,128)S(1)}, u32[]{:S(2)}, u32[]{:S(2)}) collective-permute-start(f32[64,768]{1,0:T(8,128)S(1)} %get-tuple-element.53.refs_4_), channel_id=1, source_target_pairs={{0,1},{1,0},{2,3},{3,2},{4,5},{5,4},{6,7},{7,6},{8,9},{9,8},{10,11... | collective-permute-start | bytes 589832 | tf_op jit(solution)/shard_map/ppermute | solution.py:289
  8.5 19.4 %collective-permute-start.11 = (f32[64,768]{1,0:T(8,128)S(1)}, f32[64,768]{1,0:T(8,128)S(1)}, u32[]{:S(2)}, u32[]{:S(2)}) collective-permute-start(f32[64,768]{1,0:T(8,128)S(1)} %get-tuple-element.53.refs_4_), channel_id=1, source_target_pairs={{0,2},{1,3},{2,0},{3,1},{4,6},{5,7},{6,4},{7,5},{8,10},{9,11},{10,... | collective-permute-start | bytes 589832 | tf_op jit(solution)/shard_map/ppermute | solution.py:289
  10.2 17.7 %collective-permute-start.12 = (f32[64,768]{1,0:T(8,128)S(1)}, f32[64,768]{1,0:T(8,128)S(1)}, u32[]{:S(2)}, u32[]{:S(2)}) collective-permute-start(f32[64,768]{1,0:T(8,128)S(1)} %get-tuple-element.53.refs_4_), channel_id=1, source_target_pairs={{0,3},{1,2},{2,1},{3,0},{4,7},{5,6},{6,5},{7,4},{8,11},{9,10},{10,... | collective-permute-start | bytes 589832 | tf_op jit(solution)/shard_map/ppermute | solution.py:289
  11.1 1.2 %copy-start = (f32[1024,256]{1,0:T(8,128)S(1)}, f32[1024,256]{1,0:T(8,128)}, u32[]{:S(2)}) copy-start(f32[1024,256]{1,0:T(8,128)} %slab_ref.3) | copy-start | bytes 3145732
  13.3 1.3 %collective-permute-start.9 = (f32[32,256]{1,0:T(8,128)S(1)}, f32[32,256]{1,0:T(8,128)S(1)}, u32[]{:S(2)}, u32[]{:S(2)}) collective-permute-start(f32[32,256]{1,0:T(8,128)S(1)} %get-tuple-element.48), channel_id=1, source_target_pairs={{0,4},{4,0},{8,12},{12,8},{16,20},{20,16},{24,28},{28,24},{1,5},{5... | collective-permute-start | bytes 98312 | tf_op jit(solution)/shard_map/ppermute | solution.py:354
  13.4 1.5 %collective-permute-start.5 = (f32[128,256]{1,0:T(8,128)S(1)}, f32[128,256]{1,0:T(8,128)S(1)}, u32[]{:S(2)}, u32[]{:S(2)}) collective-permute-start(f32[128,256]{1,0:T(8,128)S(1)} %slice.37), channel_id=1, source_target_pairs={{0,4},{4,0},{8,12},{12,8},{16,20},{20,16},{24,28},{28,24},{1,5},{5... | collective-permute-start | bytes 393224 | tf_op jit(solution)/shard_map/ppermute | solution.py:357
  14.9 13.0 %copy-start.1 = (f32[1024,256]{1,0:T(8,128)S(1)}, f32[1024,256]{1,0:T(8,128)}, u32[]{:S(2)}) copy-start(f32[1024,256]{1,0:T(8,128)} %slab_ref.3) | copy-start | bytes 3145732
  14.9 4.7 %collective-permute-start.1 = (f32[192,256]{1,0:T(8,128)S(1)}, f32[192,256]{1,0:T(8,128)S(1)}, u32[]{:S(2)}, u32[]{:S(2)}) collective-permute-start(f32[192,256]{1,0:T(8,128)S(1)} %get-tuple-element.29.held_ref), channel_id=1, source_target_pairs={{0,16},{4,0},{8,12},{12,8},{16,20},{20,4},{24,28},{28,24},{1,17},{... | collective-permute-start | bytes 589832 | tf_op jit(solution)/shard_map/cond/branch_1_fun/ppermute | solution.py:324
  16.5 5.0 %collective-permute-start = (f32[128,256]{1,0:T(8,128)S(1)}, f32[128,256]{1,0:T(8,128)S(1)}, u32[]{:S(2)}, u32[]{:S(2)}) collective-permute-start(f32[128,256]{1,0:T(8,128)S(1)} %pad_maximum_fusion.2), channel_id=1, source_target_pairs={{0,8},{4,12},{8,0},{12,4},{16,24},{20,28},{24,16},{28,20},{1,9},{5... | collective-permute-start | bytes 393224 | tf_op jit(solution)/shard_map/cond/branch_1_fun/ppermute | solution.py:333
  19.6 3.2 %collective-permute-start.3 = (f32[192,256]{1,0:T(8,128)S(1)}, f32[192,256]{1,0:T(8,128)S(1)}, u32[]{:S(2)}, u32[]{:S(2)}) collective-permute-start(f32[192,256]{1,0:T(8,128)S(1)} %branch_1_fun.5.held_ref), channel_id=1, source_target_pairs={{0,8},{4,0},{8,12},{12,4},{16,24},{20,16},{24,28},{28,20},{1,9},{5... | collective-permute-start | bytes 589832 | tf_op jit(solution)/shard_map/cond/branch_1_fun/ppermute | solution.py:324
  21.6 5.6 %collective-permute-start.2 = (f32[160,256]{1,0:T(8,128)S(1)}, f32[160,256]{1,0:T(8,128)S(1)}, u32[]{:S(2)}, u32[]{:S(2)}) collective-permute-start(f32[160,256]{1,0:T(8,128)S(1)} %pad_maximum_fusion.1), channel_id=1, source_target_pairs={{0,16},{4,20},{8,24},{12,28},{16,0},{20,4},{24,8},{28,12},{1,17},{... | collective-permute-start | bytes 491528 | tf_op jit(solution)/shard_map/cond/branch_1_fun/ppermute | solution.py:333
  25.1 2.4 %collective-permute-start.4 = (f32[192,256]{1,0:T(8,128)S(1)}, f32[192,256]{1,0:T(8,128)S(1)}, u32[]{:S(2)}, u32[]{:S(2)}) collective-permute-start(f32[192,256]{1,0:T(8,128)S(1)} %branch_1_fun.7), channel_id=1, source_target_pairs={{0,4},{4,0},{8,12},{12,8},{16,20},{20,16},{24,28},{28,24},{1,5},{5... | collective-permute-start | bytes 589832 | tf_op jit(solution)/shard_map/cond/branch_1_fun/ppermute | solution.py:345

commit v19 on v17

--- a/solution.py
+++ b/solution.py
@@ -124,7 +124,8 @@
 
 
 def top_order(m):
-    return [0, 1, *range(m - 1, 1, -1)]
+    even = [0, 1, *range(m - 1, 1, -1)]
+    return list(zip(even, [0, even[-1], *even[1:-1]]))
 
 
 def cut_kernel(panel_ref, top_ref, rest_ref, sems):
@@ -144,7 +145,7 @@
     piece = width // m
     half = width // 2
     z = lax.axis_index("pcol")
-    for d, ref in zip(top_order(m), pieces):
+    for (d, _), ref in zip(top_order(m), pieces):
         lower_t[pl.ds(pl.multiple_of(jnp.bitwise_xor(z, d) * piece, piece), piece), :] = ref[...]
     out_ref[:half, :] = lower_t[:half, :]
     out_ref[half:, :half] = lower_t[half : half + half // 2, half:]
@@ -233,7 +234,10 @@
     fetch = pltpu.make_async_copy(local_ref, swaps, sems.at[blocks])
     fetch.start()
     result[:rows, :] = slab_ref[...]
-    top_upper = split2(jnp.concatenate([piece_rows(x_ref, m, d) for d in top_order(m)], axis=0))
+    odd = lax.axis_index("prow") & 1 != 0
+    top_upper = split2(
+        jnp.concatenate([piece_rows(x_ref, m, jnp.where(odd, d, e)) for e, d in top_order(m)], axis=0)
+    )
     upper = split2(jnp.concatenate([piece_rows(x_ref, m, d) for d in range(m)], axis=0))
     copies = []
     for c in range(blocks):
@@ -294,7 +298,10 @@
         in_specs=[pl.BlockSpec(memory_space=pl.ANY)],
         scratch=[pltpu.SemaphoreType.DMA((rows // width,))],
     )
-    tops = [top] + [exchange(top, d) for d in top_order(m)[1:]]
+    tops = [top]
+    for by_parity in top_order(m)[1:]:
+        pairs = [(r * m + c, r * m + (c ^ by_parity[r & 1])) for r in range(n) for c in range(m)]
+        tops.append(lax.ppermute(top, ("prow", "pcol"), pairs))
     rests = [rest] + [exchange(rest, d) for d in range(1, m)]
 
     gathered, leading, local_rows = call(

time: 30.1 us -> 30.1 us (level)
    ppermute x0 -> x3, starting transfers between devices: none -> 5.68 us  [local(): tops.append(lax.ppermute(top, ('prow', 'pcol'), pairs))]
    ppermute x6 -> x3, starting transfers between devices: 10.1 us -> 4.39 us  [exchange(): return lax.ppermute(block, 'pcol', [(c, c ^ d) for c in range(m)])]
where the time goes in v19:
time: 30.1 us; the launch traced here: 29.9 us
  starting transfers between devices  14 us (47%)
  waiting for transfers between devices  7.45 us (25%)
  Pallas kernels  5.91 us (20%)
  local copies, waits for them, and re-layouts  2.21 us (7%)
    pallas_call x10, Pallas kernels, call(): pl.pallas_call(kernel, out_shape=outs, in_specs=in_specs or [VMEM] * len(...  5.91 us
    ppermute x3, starting transfers between devices, local(): tops.append(lax.ppermute(top, ('prow', 'pcol'), pairs))  5.68 us
    ppermute x3, starting transfers between devices, exchange(): return lax.ppermute(block, 'pcol', [(c, c ^ d) for c in range(m)])  4.39 us
    ppermute x2, waiting for transfers between devices, levels(): moved = lax.ppermute(message, 'prow', [(r, r ^ other) for r in range(n)])  3.83 us
    ppermute x2, waiting for transfers between devices, levels(): lax.ppermute(lower, 'prow', [(r, tree_partner(r, span)) for r in range(n)])  2.74 us
    unnamed x8, local copies, waits for them, and re-layouts  2.18 us
    ppermute x2, starting transfers between devices, levels(): moved = lax.ppermute(message, 'prow', [(r, r ^ other) for r in range(n)])  1.69 us
    ppermute x2, starting transfers between devices, levels(): lax.ppermute(lower, 'prow', [(r, tree_partner(r, span)) for r in range(n)])  1.54 us
  transfers between devices with their start and end apart: 13, of which 6 were waited for; matrix products, arithmetic and copies ran while one was open for 1% of the time, Pallas kernels for 13%

profile of v19, /device:TPU:0, one launch (start us, length us, event | category | flops | bytes accessed | tf_op | source)
XLA Modules:
  0.0 29.9 jit_solution(16958799973509208311)
XLA Ops:
  0.0 0.9 %copy-done.2 = f32[1024,64]{0,1:T(8,128)S(1)} copy-done((f32[1024,64]{0,1:T(8,128)S(1)}, f32[1024,64]{0,1:T(8,128)}, u32[]{:S(2)}) %copy-start.2) | copy-done | bytes 262168
  1.0 3.1 %collective-permute-start.6 = (f32[64,256]{1,0:T(8,128)S(1)}, f32[64,256]{1,0:T(8,128)S(1)}, u32[]{:S(2)}, u32[]{:S(2)}) collective-permute-start(f32[64,256]{1,0:T(8,128)S(1)} %get-tuple-element.47.refs_0_), channel_id=1, source_target_pairs={{0,1},{1,0},{2,3},{3,2},{4,6},{5,7},{6,4},{7,5},{8,9},{9,8},{10,11... | collective-permute-start | bytes 196616 | tf_op jit(solution)/shard_map/ppermute | solution.py:304
  4.1 2.5 %collective-permute-start.7 = (f32[64,256]{1,0:T(8,128)S(1)}, f32[64,256]{1,0:T(8,128)S(1)}, u32[]{:S(2)}, u32[]{:S(2)}) collective-permute-start(f32[64,256]{1,0:T(8,128)S(1)} %get-tuple-element.47.refs_0_), channel_id=1, source_target_pairs={{0,3},{1,2},{2,1},{3,0},{4,5},{5,4},{6,7},{7,6},{8,11},{9,10},{10,... | collective-permute-start | bytes 196616 | tf_op jit(solution)/shard_map/ppermute | solution.py:304
  6.7 1.8 %collective-permute-start.10 = (f32[64,768]{1,0:T(8,128)S(1)}, f32[64,768]{1,0:T(8,128)S(1)}, u32[]{:S(2)}, u32[]{:S(2)}) collective-permute-start(f32[64,768]{1,0:T(8,128)S(1)} %get-tuple-element.53.refs_4_), channel_id=1, source_target_pairs={{0,1},{1,0},{2,3},{3,2},{4,5},{5,4},{6,7},{7,6},{8,9},{9,8},{10,11... | collective-permute-start | bytes 589832 | tf_op jit(solution)/shard_map/ppermute | solution.py:292
  8.5 1.7 %collective-permute-start.11 = (f32[64,768]{1,0:T(8,128)S(1)}, f32[64,768]{1,0:T(8,128)S(1)}, u32[]{:S(2)}, u32[]{:S(2)}) collective-permute-start(f32[64,768]{1,0:T(8,128)S(1)} %get-tuple-element.53.refs_4_), channel_id=1, source_target_pairs={{0,2},{1,3},{2,0},{3,1},{4,6},{5,7},{6,4},{7,5},{8,10},{9,11},{10,... | collective-permute-start | bytes 589832 | tf_op jit(solution)/shard_map/ppermute | solution.py:292
  10.2 0.9 %collective-permute-start.12 = (f32[64,768]{1,0:T(8,128)S(1)}, f32[64,768]{1,0:T(8,128)S(1)}, u32[]{:S(2)}, u32[]{:S(2)}) collective-permute-start(f32[64,768]{1,0:T(8,128)S(1)} %get-tuple-element.53.refs_4_), channel_id=1, source_target_pairs={{0,3},{1,2},{2,1},{3,0},{4,7},{5,6},{6,5},{7,4},{8,11},{9,10},{10,... | collective-permute-start | bytes 589832 | tf_op jit(solution)/shard_map/ppermute | solution.py:292
  11.1 1.2 %copy-done = f32[1024,256]{1,0:T(8,128)S(1)} copy-done((f32[1024,256]{1,0:T(8,128)S(1)}, f32[1024,256]{1,0:T(8,128)}, u32[]{:S(2)}) %copy-start) | copy-done | bytes 1048600
  12.3 0.7 %shard_map.37 = (f32[32,256]{1,0:T(8,128)S(1)}, f32[256,256]{1,0:T(8,128)S(1)}, s32[1,128]{1,0:T(1,128)S(1)}) custom-call(s32[1,256]{1,0:T(1,128)S(1)} %bitcast.3, f32[1024,256]{1,0:T(8,128)S(1)} %copy-done), custom_call_target="tpu_custom_call" | custom-call | flops 1 | bytes 1 | tf_op jit(solution)/shard_map/pallas_call | solution.py:272
  13.1 0.2 collective-permute-done.8.refs_3_
  13.4 0.6 %collective-permute-start.5 = (f32[128,256]{1,0:T(8,128)S(1)}, f32[128,256]{1,0:T(8,128)S(1)}, u32[]{:S(2)}, u32[]{:S(2)}) collective-permute-start(f32[128,256]{1,0:T(8,128)S(1)} %slice.37), channel_id=1, source_target_pairs={{0,4},{4,0},{8,12},{12,8},{16,20},{20,16},{24,28},{28,24},{1,5},{5... | collective-permute-start | bytes 393224 | tf_op jit(solution)/shard_map/ppermute | solution.py:363
  13.9 0.3 shard_map.40
  14.2 0.3 %collective-permute-done.9 = f32[32,256]{1,0:T(8,128)S(1)} collective-permute-done((f32[32,256]{1,0:T(8,128)S(1)}, f32[32,256]{1,0:T(8,128)S(1)}, u32[]{:S(2)}, u32[]{:S(2)}) %collective-permute-start.9) | collective-permute-done | bytes 32800 | tf_op jit(solution)/shard_map/ppermute | solution.py:360
  14.6 0.4 %collective-permute-done.5 = f32[128,256]{1,0:T(8,128)S(1)} collective-permute-done((f32[128,256]{1,0:T(8,128)S(1)}, f32[128,256]{1,0:T(8,128)S(1)}, u32[]{:S(2)}, u32[]{:S(2)}) %collective-permute-start.5) | collective-permute-done | bytes 131104 | tf_op jit(solution)/shard_map/ppermute | solution.py:363
  14.9 12.9 %conditional.1 = (f32[32,256]{1,0:T(8,128)S(1)}, f32[256,256]{1,0:T(8,128)S(1)}) conditional(s32[]{:T(128)} %convert_element_type.3, () %tuple.19, (s32[]{:T(128)}, f32[256,256]{1,0:T(8,128)S(1)}, f32[128,256]{1,0:T(8,128)S(1)}, f32[64,256]{1,0:T(8,128)S(1)}, f32[192,256]{1,0:T(8,128)S(1)}, /*index=5*/bf16[256,256]{1,0:T(8,128)(2,1)S(1)}) %tuple.21), branch_computations={%region_0.1_spmd, %region_1.2_spmd} | conditional | flops 352267 | bytes 6521120 | solution.py:268
  14.9 1.5 %collective-permute-start.1 = (f32[192,256]{1,0:T(8,128)S(1)}, f32[192,256]{1,0:T(8,128)S(1)}, u32[]{:S(2)}, u32[]{:S(2)}) collective-permute-start(f32[192,256]{1,0:T(8,128)S(1)} %get-tuple-element.29.held_ref), channel_id=1, source_target_pairs={{0,16},{4,0},{8,12},{12,8},{16,20},{20,4},{24,28},{28,24},{1,17},{... | collective-permute-start | bytes 589832 | tf_op jit(solution)/shard_map/cond/branch_1_fun/ppermute | solution.py:330
  16.5 0.4 %collective-permute-start = (f32[128,256]{1,0:T(8,128)S(1)}, f32[128,256]{1,0:T(8,128)S(1)}, u32[]{:S(2)}, u32[]{:S(2)}) collective-permute-start(f32[128,256]{1,0:T(8,128)S(1)} %pad_maximum_fusion.2), channel_id=1, source_target_pairs={{0,8},{4,12},{8,0},{12,4},{16,24},{20,28},{24,16},{28,20},{1,9},{5... | collective-permute-start | bytes 393224 | tf_op jit(solution)/shard_map/cond/branch_1_fun/ppermute | solution.py:339
  16.9 2.7 %collective-permute-done.1.moved_ref = f32[192,256]{1,0:T(8,128)S(1)} collective-permute-done((f32[192,256]{1,0:T(8,128)S(1)}, f32[192,256]{1,0:T(8,128)S(1)}, u32[]{:S(2)}, u32[]{:S(2)}) %collective-permute-start.1) | collective-permute-done | bytes 196640 | tf_op jit(solution)/shard_map/cond/branch_1_fun/ppermute | solution.py:330
  19.7 1.9 %collective-permute-done = f32[128,256]{1,0:T(8,128)S(1)} collective-permute-done((f32[128,256]{1,0:T(8,128)S(1)}, f32[128,256]{1,0:T(8,128)S(1)}, u32[]{:S(2)}, u32[]{:S(2)}) %collective-permute-start) | collective-permute-done | bytes 131104 | tf_op jit(solution)/shard_map/cond/branch_1_fun/ppermute | solution.py:339
  21.6 1.3 %collective-permute-start.2 = (f32[160,256]{1,0:T(8,128)S(1)}, f32[160,256]{1,0:T(8,128)S(1)}, u32[]{:S(2)}, u32[]{:S(2)}) collective-permute-start(f32[160,256]{1,0:T(8,128)S(1)} %pad_maximum_fusion.1), channel_id=1, source_target_pairs={{0,16},{4,20},{8,24},{12,28},{16,0},{20,4},{24,8},{28,12},{1,17},{... | collective-permute-start | bytes 491528 | tf_op jit(solution)/shard_map/cond/branch_1_fun/ppermute | solution.py:339
  22.9 2.2 %branch_1_fun.7 = f32[192,256]{1,0:T(8,128)S(1)} custom-call(f32[192,256]{1,0:T(8,128)S(1)} %branch_1_fun.6.lower_ref), custom_call_target="tpu_custom_call" | custom-call | flops 1 | bytes 1 | tf_op jit(solution)/shard_map/cond/branch_1_fun/pallas_call | solution.py:272
  25.2 2.0 %collective-permute-done.2 = f32[160,256]{1,0:T(8,128)S(1)} collective-permute-done((f32[160,256]{1,0:T(8,128)S(1)}, f32[160,256]{1,0:T(8,128)S(1)}, u32[]{:S(2)}, u32[]{:S(2)}) %collective-permute-start.2) | collective-permute-done | bytes 163872 | tf_op jit(solution)/shard_map/cond/branch_1_fun/ppermute | solution.py:339
  27.2 0.3 branch_1_fun.8.pivot_rows_ref
  27.5 0.3 %branch_1_fun.9 = f32[256,256]{1,0:T(8,128)S(1)} custom-call(f32[192,256]{1,0:T(8,128)S(1)} %broadcast_select_fusion.inverse_ref, f32[256,256]{1,0:T(8,128)S(1)} %branch_1_fun.8.pivot_rows_ref), custom_call_target="tpu_custom_call" | custom-call | flops 1 | bytes 1 | tf_op jit(solution)/shard_map/cond/branch_1_fun/pallas_call | solution.py:272
  27.9 2.0 %shard_map.41 = f32[1024,256]{1,0:T(8,128)} custom-call(s32[1,128]{1,0:T(1,128)S(1)} %get-tuple-element.44.local_ref, f32[32,256]{1,0:T(8,128)S(1)} %get-tuple-element.51.lead_ref, f32[256,256]{1,0:T(8,128)S(1)} %get-tuple-element.52.x_ref, f32[1024,256]{1,0:T(8,128)S(1)} %copy-done.1, f32[64,256]{1,0:T(8,128)S(1)} %get-tuple-element.47.refs_0_, ...), custom_call_target="tpu_custom_call" | custom-call | flops 1 | bytes 1 | tf_op jit(solution)/shard_map/pallas_call | solution.py:272
  (33 shorter events, 0.6 us)
Async XLA Ops:
  0.0 0.9 %copy-start.2 = (f32[1024,64]{0,1:T(8,128)S(1)}, f32[1024,64]{0,1:T(8,128)}, u32[]{:S(2)}) copy-start(f32[1024,64]{0,1:T(8,128)} %param.6) | copy-start | bytes 786436
  1.0 9.2 %collective-permute-start.6 = (f32[64,256]{1,0:T(8,128)S(1)}, f32[64,256]{1,0:T(8,128)S(1)}, u32[]{:S(2)}, u32[]{:S(2)}) collective-permute-start(f32[64,256]{1,0:T(8,128)S(1)} %get-tuple-element.47.refs_0_), channel_id=1, source_target_pairs={{0,1},{1,0},{2,3},{3,2},{4,6},{5,7},{6,4},{7,5},{8,9},{9,8},{10,11... | collective-permute-start | bytes 196616 | tf_op jit(solution)/shard_map/ppermute | solution.py:304
  4.1 8.9 %collective-permute-start.7 = (f32[64,256]{1,0:T(8,128)S(1)}, f32[64,256]{1,0:T(8,128)S(1)}, u32[]{:S(2)}, u32[]{:S(2)}) collective-permute-start(f32[64,256]{1,0:T(8,128)S(1)} %get-tuple-element.47.refs_0_), channel_id=1, source_target_pairs={{0,3},{1,2},{2,1},{3,0},{4,5},{5,4},{6,7},{7,6},{8,11},{9,10},{10,... | collective-permute-start | bytes 196616 | tf_op jit(solution)/shard_map/ppermute | solution.py:304
  6.6 6.6 %collective-permute-start.8 = (f32[64,256]{1,0:T(8,128)S(1)}, f32[64,256]{1,0:T(8,128)S(1)}, u32[]{:S(2)}, u32[]{:S(2)}) collective-permute-start(f32[64,256]{1,0:T(8,128)S(1)} %get-tuple-element.47.refs_0_), channel_id=1, source_target_pairs={{0,2},{1,3},{2,0},{3,1},{4,7},{5,6},{6,5},{7,4},{8,10},{9,11},{10,... | collective-permute-start | bytes 196616 | tf_op jit(solution)/shard_map/ppermute | solution.py:304
  6.7 4.4 %copy-start.3 = (s32[256]{0:T(256)S(1)}, s32[256]{0:T(256)}, u32[]{:S(2)}) copy-start(s32[256]{0:T(256)} %param.7) | copy-start | bytes 3076
  6.7 21.2 %collective-permute-start.10 = (f32[64,768]{1,0:T(8,128)S(1)}, f32[64,768]{1,0:T(8,128)S(1)}, u32[]{:S(2)}, u32[]{:S(2)}) collective-permute-start(f32[64,768]{1,0:T(8,128)S(1)} %get-tuple-element.53.refs_4_), channel_id=1, source_target_pairs={{0,1},{1,0},{2,3},{3,2},{4,5},{5,4},{6,7},{7,6},{8,9},{9,8},{10,11... | collective-permute-start | bytes 589832 | tf_op jit(solution)/shard_map/ppermute | solution.py:292
  8.5 19.4 %collective-permute-start.11 = (f32[64,768]{1,0:T(8,128)S(1)}, f32[64,768]{1,0:T(8,128)S(1)}, u32[]{:S(2)}, u32[]{:S(2)}) collective-permute-start(f32[64,768]{1,0:T(8,128)S(1)} %get-tuple-element.53.refs_4_), channel_id=1, source_target_pairs={{0,2},{1,3},{2,0},{3,1},{4,6},{5,7},{6,4},{7,5},{8,10},{9,11},{10,... | collective-permute-start | bytes 589832 | tf_op jit(solution)/shard_map/ppermute | solution.py:292
  10.2 17.7 %collective-permute-start.12 = (f32[64,768]{1,0:T(8,128)S(1)}, f32[64,768]{1,0:T(8,128)S(1)}, u32[]{:S(2)}, u32[]{:S(2)}) collective-permute-start(f32[64,768]{1,0:T(8,128)S(1)} %get-tuple-element.53.refs_4_), channel_id=1, source_target_pairs={{0,3},{1,2},{2,1},{3,0},{4,7},{5,6},{6,5},{7,4},{8,11},{9,10},{10,... | collective-permute-start | bytes 589832 | tf_op jit(solution)/shard_map/ppermute | solution.py:292
  11.1 1.2 %copy-start = (f32[1024,256]{1,0:T(8,128)S(1)}, f32[1024,256]{1,0:T(8,128)}, u32[]{:S(2)}) copy-start(f32[1024,256]{1,0:T(8,128)} %slab_ref.3) | copy-start | bytes 3145732
  13.3 1.3 %collective-permute-start.9 = (f32[32,256]{1,0:T(8,128)S(1)}, f32[32,256]{1,0:T(8,128)S(1)}, u32[]{:S(2)}, u32[]{:S(2)}) collective-permute-start(f32[32,256]{1,0:T(8,128)S(1)} %get-tuple-element.48), channel_id=1, source_target_pairs={{0,4},{4,0},{8,12},{12,8},{16,20},{20,16},{24,28},{28,24},{1,5},{5... | collective-permute-start | bytes 98312 | tf_op jit(solution)/shard_map/ppermute | solution.py:360
  13.4 1.5 %collective-permute-start.5 = (f32[128,256]{1,0:T(8,128)S(1)}, f32[128,256]{1,0:T(8,128)S(1)}, u32[]{:S(2)}, u32[]{:S(2)}) collective-permute-start(f32[128,256]{1,0:T(8,128)S(1)} %slice.37), channel_id=1, source_target_pairs={{0,4},{4,0},{8,12},{12,8},{16,20},{20,16},{24,28},{28,24},{1,5},{5... | collective-permute-start | bytes 393224 | tf_op jit(solution)/shard_map/ppermute | solution.py:363
  14.9 13.0 %copy-start.1 = (f32[1024,256]{1,0:T(8,128)S(1)}, f32[1024,256]{1,0:T(8,128)}, u32[]{:S(2)}) copy-start(f32[1024,256]{1,0:T(8,128)} %slab_ref.3) | copy-start | bytes 3145732
  14.9 4.7 %collective-permute-start.1 = (f32[192,256]{1,0:T(8,128)S(1)}, f32[192,256]{1,0:T(8,128)S(1)}, u32[]{:S(2)}, u32[]{:S(2)}) collective-permute-start(f32[192,256]{1,0:T(8,128)S(1)} %get-tuple-element.29.held_ref), channel_id=1, source_target_pairs={{0,16},{4,0},{8,12},{12,8},{16,20},{20,4},{24,28},{28,24},{1,17},{... | collective-permute-start | bytes 589832 | tf_op jit(solution)/shard_map/cond/branch_1_fun/ppermute | solution.py:330
  16.5 5.0 %collective-permute-start = (f32[128,256]{1,0:T(8,128)S(1)}, f32[128,256]{1,0:T(8,128)S(1)}, u32[]{:S(2)}, u32[]{:S(2)}) collective-permute-start(f32[128,256]{1,0:T(8,128)S(1)} %pad_maximum_fusion.2), channel_id=1, source_target_pairs={{0,8},{4,12},{8,0},{12,4},{16,24},{20,28},{24,16},{28,20},{1,9},{5... | collective-permute-start | bytes 393224 | tf_op jit(solution)/shard_map/cond/branch_1_fun/ppermute | solution.py:339
  19.7 3.2 %collective-permute-start.3 = (f32[192,256]{1,0:T(8,128)S(1)}, f32[192,256]{1,0:T(8,128)S(1)}, u32[]{:S(2)}, u32[]{:S(2)}) collective-permute-start(f32[192,256]{1,0:T(8,128)S(1)} %branch_1_fun.5.held_ref), channel_id=1, source_target_pairs={{0,8},{4,0},{8,12},{12,4},{16,24},{20,16},{24,28},{28,20},{1,9},{5... | collective-permute-start | bytes 589832 | tf_op jit(solution)/shard_map/cond/branch_1_fun/ppermute | solution.py:330
  21.6 5.6 %collective-permute-start.2 = (f32[160,256]{1,0:T(8,128)S(1)}, f32[160,256]{1,0:T(8,128)S(1)}, u32[]{:S(2)}, u32[]{:S(2)}) collective-permute-start(f32[160,256]{1,0:T(8,128)S(1)} %pad_maximum_fusion.1), channel_id=1, source_target_pairs={{0,16},{4,20},{8,24},{12,28},{16,0},{20,4},{24,8},{28,12},{1,17},{... | collective-permute-start | bytes 491528 | tf_op jit(solution)/shard_map/cond/branch_1_fun/ppermute | solution.py:339
  25.1 2.4 %collective-permute-start.4 = (f32[192,256]{1,0:T(8,128)S(1)}, f32[192,256]{1,0:T(8,128)S(1)}, u32[]{:S(2)}, u32[]{:S(2)}) collective-permute-start(f32[192,256]{1,0:T(8,128)S(1)} %branch_1_fun.7), channel_id=1, source_target_pairs={{0,4},{4,0},{8,12},{12,8},{16,20},{20,16},{24,28},{28,24},{1,5},{5... | collective-permute-start | bytes 589832 | tf_op jit(solution)/shard_map/cond/branch_1_fun/ppermute | solution.py:351

commit v20 on v17

--- a/solution.py
+++ b/solution.py
@@ -101,16 +101,19 @@
         diag = jnp.where(block == b, lower[b * BLOCK : (b + 1) * BLOCK], diag)
     diag = jnp.where(within < sub, diag, 0.0)
     inv = jnp.where(within == sub, 1.0, 0.0).astype(F32)
-    half = 128
-    first = (lax.broadcasted_iota(jnp.int32, (BLOCK, half), 1) // BLOCK) * BLOCK
-    outs = []
-    for h in range(0, width, half):
-        d, x = diag[:, h : h + half], inv[:, h : h + half]
-        for k in range(BLOCK - 1):
-            column = jnp.take_along_axis(d, first + k, axis=1)
-            x = x - column * x[k : k + 1, :]
-        outs.append(x)
-    return outs
+    half, tile = 128, 8
+    first = (lax.broadcasted_iota(jnp.int32, (tile, half), 1) // BLOCK) * BLOCK
+    starts = range(0, width, half)
+    tops = range(0, BLOCK, tile)
+    d = [[diag[t : t + tile, h : h + half] for t in tops] for h in starts]
+    x = [[inv[t : t + tile, h : h + half] for t in tops] for h in starts]
+    for k in range(BLOCK - 1):
+        for h in range(len(starts)):
+            row = x[h][k // tile][k % tile : k % tile + 1, :]
+            for t in range((k + 1) // tile, len(tops)):
+                column = jnp.take_along_axis(d[h][t], first + k, axis=1)
+                x[h][t] = x[h][t] - column * row
+    return [jnp.concatenate(tiles, axis=0) for tiles in x]
 
 
 def choice_kernel(n, rows, pivot_ref, out_ref):

time: 30.1 us -> 30.1 us (level)
  transfers between devices with their start and end apart: 13 -> 13, of which waited for: 6 -> 6; matrix products, arithmetic and copies ran while one was open for 1% -> 1% of each run, Pallas kernels for 13% -> 12%
where the time goes in v20:
time: 30.1 us; the launch traced here: 29.9 us
  starting transfers between devices  14 us (47%)
  waiting for transfers between devices  7.54 us (25%)
  Pallas kernels  5.8 us (19%)
  local copies, waits for them, and re-layouts  2.21 us (7%)
    ppermute x6, starting transfers between devices, exchange(): return lax.ppermute(block, 'pcol', [(c, c ^ d) for c in range(m)])  10.1 us
    pallas_call x10, Pallas kernels, call(): pl.pallas_call(kernel, out_shape=outs, in_specs=in_specs or [VMEM] * len(...  5.8 us
    ppermute x2, waiting for transfers between devices, levels(): moved = lax.ppermute(message, 'prow', [(r, r ^ other) for r in range(n)])  3.93 us
    ppermute x2, waiting for transfers between devices, levels(): lax.ppermute(lower, 'prow', [(r, tree_partner(r, span)) for r in range(n)])  2.74 us
    unnamed x8, local copies, waits for them, and re-layouts  2.18 us
    ppermute x2, starting transfers between devices, levels(): moved = lax.ppermute(message, 'prow', [(r, r ^ other) for r in range(n)])  1.69 us
    ppermute x2, starting transfers between devices, levels(): lax.ppermute(lower, 'prow', [(r, tree_partner(r, span)) for r in range(n)])  1.54 us
  transfers between devices with their start and end apart: 13, of which 6 were waited for; matrix products, arithmetic and copies ran while one was open for 1% of the time, Pallas kernels for 12%

profile of v20, /device:TPU:0, one launch (start us, length us, event | category | flops | bytes accessed | tf_op | source)
XLA Modules:
  0.0 29.9 jit_solution(7541832522655991485)
XLA Ops:
  0.0 0.9 %copy-done.2 = f32[1024,64]{0,1:T(8,128)S(1)} copy-done((f32[1024,64]{0,1:T(8,128)S(1)}, f32[1024,64]{0,1:T(8,128)}, u32[]{:S(2)}) %copy-start.2) | copy-done | bytes 262168
  1.0 3.1 %collective-permute-start.6 = (f32[64,256]{1,0:T(8,128)S(1)}, f32[64,256]{1,0:T(8,128)S(1)}, u32[]{:S(2)}, u32[]{:S(2)}) collective-permute-start(f32[64,256]{1,0:T(8,128)S(1)} %get-tuple-element.47.refs_0_), channel_id=1, source_target_pairs={{0,1},{1,0},{2,3},{3,2},{4,5},{5,4},{6,7},{7,6},{8,9},{9,8},{10,11... | collective-permute-start | bytes 196616 | tf_op jit(solution)/shard_map/ppermute | solution.py:291
  4.1 2.5 %collective-permute-start.7 = (f32[64,256]{1,0:T(8,128)S(1)}, f32[64,256]{1,0:T(8,128)S(1)}, u32[]{:S(2)}, u32[]{:S(2)}) collective-permute-start(f32[64,256]{1,0:T(8,128)S(1)} %get-tuple-element.47.refs_0_), channel_id=1, source_target_pairs={{0,3},{1,2},{2,1},{3,0},{4,7},{5,6},{6,5},{7,4},{8,11},{9,10},{10,... | collective-permute-start | bytes 196616 | tf_op jit(solution)/shard_map/ppermute | solution.py:291
  6.7 1.8 %collective-permute-start.10 = (f32[64,768]{1,0:T(8,128)S(1)}, f32[64,768]{1,0:T(8,128)S(1)}, u32[]{:S(2)}, u32[]{:S(2)}) collective-permute-start(f32[64,768]{1,0:T(8,128)S(1)} %get-tuple-element.53.refs_4_), channel_id=1, source_target_pairs={{0,1},{1,0},{2,3},{3,2},{4,5},{5,4},{6,7},{7,6},{8,9},{9,8},{10,11... | collective-permute-start | bytes 589832 | tf_op jit(solution)/shard_map/ppermute | solution.py:291
  8.5 1.7 %collective-permute-start.11 = (f32[64,768]{1,0:T(8,128)S(1)}, f32[64,768]{1,0:T(8,128)S(1)}, u32[]{:S(2)}, u32[]{:S(2)}) collective-permute-start(f32[64,768]{1,0:T(8,128)S(1)} %get-tuple-element.53.refs_4_), channel_id=1, source_target_pairs={{0,2},{1,3},{2,0},{3,1},{4,6},{5,7},{6,4},{7,5},{8,10},{9,11},{10,... | collective-permute-start | bytes 589832 | tf_op jit(solution)/shard_map/ppermute | solution.py:291
  10.2 0.9 %collective-permute-start.12 = (f32[64,768]{1,0:T(8,128)S(1)}, f32[64,768]{1,0:T(8,128)S(1)}, u32[]{:S(2)}, u32[]{:S(2)}) collective-permute-start(f32[64,768]{1,0:T(8,128)S(1)} %get-tuple-element.53.refs_4_), channel_id=1, source_target_pairs={{0,3},{1,2},{2,1},{3,0},{4,7},{5,6},{6,5},{7,4},{8,11},{9,10},{10,... | collective-permute-start | bytes 589832 | tf_op jit(solution)/shard_map/ppermute | solution.py:291
  11.1 1.2 %copy-done = f32[1024,256]{1,0:T(8,128)S(1)} copy-done((f32[1024,256]{1,0:T(8,128)S(1)}, f32[1024,256]{1,0:T(8,128)}, u32[]{:S(2)}) %copy-start) | copy-done | bytes 1048600
  12.3 0.7 %shard_map.37 = (f32[32,256]{1,0:T(8,128)S(1)}, f32[256,256]{1,0:T(8,128)S(1)}, s32[1,128]{1,0:T(1,128)S(1)}) custom-call(s32[1,256]{1,0:T(1,128)S(1)} %bitcast.3, f32[1024,256]{1,0:T(8,128)S(1)} %copy-done), custom_call_target="tpu_custom_call" | custom-call | flops 1 | bytes 1 | tf_op jit(solution)/shard_map/pallas_call | solution.py:271
  13.1 0.2 collective-permute-done.8.refs_3_
  13.4 0.6 %collective-permute-start.5 = (f32[128,256]{1,0:T(8,128)S(1)}, f32[128,256]{1,0:T(8,128)S(1)}, u32[]{:S(2)}, u32[]{:S(2)}) collective-permute-start(f32[128,256]{1,0:T(8,128)S(1)} %slice.37), channel_id=1, source_target_pairs={{0,4},{4,0},{8,12},{12,8},{16,20},{20,16},{24,28},{28,24},{1,5},{5... | collective-permute-start | bytes 393224 | tf_op jit(solution)/shard_map/ppermute | solution.py:359
  13.9 0.3 shard_map.40
  14.2 0.3 %collective-permute-done.9 = f32[32,256]{1,0:T(8,128)S(1)} collective-permute-done((f32[32,256]{1,0:T(8,128)S(1)}, f32[32,256]{1,0:T(8,128)S(1)}, u32[]{:S(2)}, u32[]{:S(2)}) %collective-permute-start.9) | collective-permute-done | bytes 32800 | tf_op jit(solution)/shard_map/ppermute | solution.py:356
  14.6 0.4 %collective-permute-done.5 = f32[128,256]{1,0:T(8,128)S(1)} collective-permute-done((f32[128,256]{1,0:T(8,128)S(1)}, f32[128,256]{1,0:T(8,128)S(1)}, u32[]{:S(2)}, u32[]{:S(2)}) %collective-permute-start.5) | collective-permute-done | bytes 131104 | tf_op jit(solution)/shard_map/ppermute | solution.py:359
  14.9 12.9 %conditional.1 = (f32[32,256]{1,0:T(8,128)S(1)}, f32[256,256]{1,0:T(8,128)S(1)}) conditional(s32[]{:T(128)} %convert_element_type.3, () %tuple.19, (s32[]{:T(128)}, f32[256,256]{1,0:T(8,128)S(1)}, f32[128,256]{1,0:T(8,128)S(1)}, f32[64,256]{1,0:T(8,128)S(1)}, f32[192,256]{1,0:T(8,128)S(1)}, /*index=5*/bf16[256,256]{1,0:T(8,128)(2,1)S(1)}) %tuple.21), branch_computations={%region_0.1_spmd, %region_1.2_spmd} | conditional | flops 352267 | bytes 6521120 | solution.py:267
  14.9 1.5 %collective-permute-start.1 = (f32[192,256]{1,0:T(8,128)S(1)}, f32[192,256]{1,0:T(8,128)S(1)}, u32[]{:S(2)}, u32[]{:S(2)}) collective-permute-start(f32[192,256]{1,0:T(8,128)S(1)} %get-tuple-element.29.held_ref), channel_id=1, source_target_pairs={{0,16},{4,0},{8,12},{12,8},{16,20},{20,4},{24,28},{28,24},{1,17},{... | collective-permute-start | bytes 589832 | tf_op jit(solution)/shard_map/cond/branch_1_fun/ppermute | solution.py:326
  16.5 0.4 %collective-permute-start = (f32[128,256]{1,0:T(8,128)S(1)}, f32[128,256]{1,0:T(8,128)S(1)}, u32[]{:S(2)}, u32[]{:S(2)}) collective-permute-start(f32[128,256]{1,0:T(8,128)S(1)} %pad_maximum_fusion.2), channel_id=1, source_target_pairs={{0,8},{4,12},{8,0},{12,4},{16,24},{20,28},{24,16},{28,20},{1,9},{5... | collective-permute-start | bytes 393224 | tf_op jit(solution)/shard_map/cond/branch_1_fun/ppermute | solution.py:335
  16.9 2.7 %collective-permute-done.1.moved_ref = f32[192,256]{1,0:T(8,128)S(1)} collective-permute-done((f32[192,256]{1,0:T(8,128)S(1)}, f32[192,256]{1,0:T(8,128)S(1)}, u32[]{:S(2)}, u32[]{:S(2)}) %collective-permute-start.1) | collective-permute-done | bytes 196640 | tf_op jit(solution)/shard_map/cond/branch_1_fun/ppermute | solution.py:326
  19.7 1.9 %collective-permute-done = f32[128,256]{1,0:T(8,128)S(1)} collective-permute-done((f32[128,256]{1,0:T(8,128)S(1)}, f32[128,256]{1,0:T(8,128)S(1)}, u32[]{:S(2)}, u32[]{:S(2)}) %collective-permute-start) | collective-permute-done | bytes 131104 | tf_op jit(solution)/shard_map/cond/branch_1_fun/ppermute | solution.py:335
  21.6 1.3 %collective-permute-start.2 = (f32[160,256]{1,0:T(8,128)S(1)}, f32[160,256]{1,0:T(8,128)S(1)}, u32[]{:S(2)}, u32[]{:S(2)}) collective-permute-start(f32[160,256]{1,0:T(8,128)S(1)} %pad_maximum_fusion.1), channel_id=1, source_target_pairs={{0,16},{4,20},{8,24},{12,28},{16,0},{20,4},{24,8},{28,12},{1,17},{... | collective-permute-start | bytes 491528 | tf_op jit(solution)/shard_map/cond/branch_1_fun/ppermute | solution.py:335
  22.9 2.1 %branch_1_fun.7 = f32[192,256]{1,0:T(8,128)S(1)} custom-call(f32[192,256]{1,0:T(8,128)S(1)} %branch_1_fun.6.lower_ref), custom_call_target="tpu_custom_call" | custom-call | flops 1 | bytes 1 | tf_op jit(solution)/shard_map/cond/branch_1_fun/pallas_call | solution.py:271
  25.1 2.1 %collective-permute-done.2 = f32[160,256]{1,0:T(8,128)S(1)} collective-permute-done((f32[160,256]{1,0:T(8,128)S(1)}, f32[160,256]{1,0:T(8,128)S(1)}, u32[]{:S(2)}, u32[]{:S(2)}) %collective-permute-start.2) | collective-permute-done | bytes 163872 | tf_op jit(solution)/shard_map/cond/branch_1_fun/ppermute | solution.py:335
  27.2 0.3 branch_1_fun.8.pivot_rows_ref
  27.5 0.3 %branch_1_fun.9 = f32[256,256]{1,0:T(8,128)S(1)} custom-call(f32[192,256]{1,0:T(8,128)S(1)} %broadcast_select_fusion.inverse_ref, f32[256,256]{1,0:T(8,128)S(1)} %branch_1_fun.8.pivot_rows_ref), custom_call_target="tpu_custom_call" | custom-call | flops 1 | bytes 1 | tf_op jit(solution)/shard_map/cond/branch_1_fun/pallas_call | solution.py:271
  27.9 2.0 %shard_map.41 = f32[1024,256]{1,0:T(8,128)} custom-call(s32[1,128]{1,0:T(1,128)S(1)} %get-tuple-element.44.local_ref, f32[32,256]{1,0:T(8,128)S(1)} %get-tuple-element.51.lead_ref, f32[256,256]{1,0:T(8,128)S(1)} %get-tuple-element.52.x_ref, f32[1024,256]{1,0:T(8,128)S(1)} %copy-done.1, f32[64,256]{1,0:T(8,128)S(1)} %get-tuple-element.47.refs_0_, ...), custom_call_target="tpu_custom_call" | custom-call | flops 1 | bytes 1 | tf_op jit(solution)/shard_map/pallas_call | solution.py:271
  (33 shorter events, 0.6 us)
Async XLA Ops:
  0.0 0.9 %copy-start.2 = (f32[1024,64]{0,1:T(8,128)S(1)}, f32[1024,64]{0,1:T(8,128)}, u32[]{:S(2)}) copy-start(f32[1024,64]{0,1:T(8,128)} %param.6) | copy-start | bytes 786436
  1.0 9.2 %collective-permute-start.6 = (f32[64,256]{1,0:T(8,128)S(1)}, f32[64,256]{1,0:T(8,128)S(1)}, u32[]{:S(2)}, u32[]{:S(2)}) collective-permute-start(f32[64,256]{1,0:T(8,128)S(1)} %get-tuple-element.47.refs_0_), channel_id=1, source_target_pairs={{0,1},{1,0},{2,3},{3,2},{4,5},{5,4},{6,7},{7,6},{8,9},{9,8},{10,11... | collective-permute-start | bytes 196616 | tf_op jit(solution)/shard_map/ppermute | solution.py:291
  4.1 8.9 %collective-permute-start.7 = (f32[64,256]{1,0:T(8,128)S(1)}, f32[64,256]{1,0:T(8,128)S(1)}, u32[]{:S(2)}, u32[]{:S(2)}) collective-permute-start(f32[64,256]{1,0:T(8,128)S(1)} %get-tuple-element.47.refs_0_), channel_id=1, source_target_pairs={{0,3},{1,2},{2,1},{3,0},{4,7},{5,6},{6,5},{7,4},{8,11},{9,10},{10,... | collective-permute-start | bytes 196616 | tf_op jit(solution)/shard_map/ppermute | solution.py:291
  6.6 6.6 %collective-permute-start.8 = (f32[64,256]{1,0:T(8,128)S(1)}, f32[64,256]{1,0:T(8,128)S(1)}, u32[]{:S(2)}, u32[]{:S(2)}) collective-permute-start(f32[64,256]{1,0:T(8,128)S(1)} %get-tuple-element.47.refs_0_), channel_id=1, source_target_pairs={{0,2},{1,3},{2,0},{3,1},{4,6},{5,7},{6,4},{7,5},{8,10},{9,11},{10,... | collective-permute-start | bytes 196616 | tf_op jit(solution)/shard_map/ppermute | solution.py:291
  6.7 4.4 %copy-start.3 = (s32[256]{0:T(256)S(1)}, s32[256]{0:T(256)}, u32[]{:S(2)}) copy-start(s32[256]{0:T(256)} %param.7) | copy-start | bytes 3076
  6.7 21.2 %collective-permute-start.10 = (f32[64,768]{1,0:T(8,128)S(1)}, f32[64,768]{1,0:T(8,128)S(1)}, u32[]{:S(2)}, u32[]{:S(2)}) collective-permute-start(f32[64,768]{1,0:T(8,128)S(1)} %get-tuple-element.53.refs_4_), channel_id=1, source_target_pairs={{0,1},{1,0},{2,3},{3,2},{4,5},{5,4},{6,7},{7,6},{8,9},{9,8},{10,11... | collective-permute-start | bytes 589832 | tf_op jit(solution)/shard_map/ppermute | solution.py:291
  8.5 19.4 %collective-permute-start.11 = (f32[64,768]{1,0:T(8,128)S(1)}, f32[64,768]{1,0:T(8,128)S(1)}, u32[]{:S(2)}, u32[]{:S(2)}) collective-permute-start(f32[64,768]{1,0:T(8,128)S(1)} %get-tuple-element.53.refs_4_), channel_id=1, source_target_pairs={{0,2},{1,3},{2,0},{3,1},{4,6},{5,7},{6,4},{7,5},{8,10},{9,11},{10,... | collective-permute-start | bytes 589832 | tf_op jit(solution)/shard_map/ppermute | solution.py:291
  10.2 17.7 %collective-permute-start.12 = (f32[64,768]{1,0:T(8,128)S(1)}, f32[64,768]{1,0:T(8,128)S(1)}, u32[]{:S(2)}, u32[]{:S(2)}) collective-permute-start(f32[64,768]{1,0:T(8,128)S(1)} %get-tuple-element.53.refs_4_), channel_id=1, source_target_pairs={{0,3},{1,2},{2,1},{3,0},{4,7},{5,6},{6,5},{7,4},{8,11},{9,10},{10,... | collective-permute-start | bytes 589832 | tf_op jit(solution)/shard_map/ppermute | solution.py:291
  11.1 1.2 %copy-start = (f32[1024,256]{1,0:T(8,128)S(1)}, f32[1024,256]{1,0:T(8,128)}, u32[]{:S(2)}) copy-start(f32[1024,256]{1,0:T(8,128)} %slab_ref.3) | copy-start | bytes 3145732
  13.3 1.3 %collective-permute-start.9 = (f32[32,256]{1,0:T(8,128)S(1)}, f32[32,256]{1,0:T(8,128)S(1)}, u32[]{:S(2)}, u32[]{:S(2)}) collective-permute-start(f32[32,256]{1,0:T(8,128)S(1)} %get-tuple-element.48), channel_id=1, source_target_pairs={{0,4},{4,0},{8,12},{12,8},{16,20},{20,16},{24,28},{28,24},{1,5},{5... | collective-permute-start | bytes 98312 | tf_op jit(solution)/shard_map/ppermute | solution.py:356
  13.4 1.5 %collective-permute-start.5 = (f32[128,256]{1,0:T(8,128)S(1)}, f32[128,256]{1,0:T(8,128)S(1)}, u32[]{:S(2)}, u32[]{:S(2)}) collective-permute-start(f32[128,256]{1,0:T(8,128)S(1)} %slice.37), channel_id=1, source_target_pairs={{0,4},{4,0},{8,12},{12,8},{16,20},{20,16},{24,28},{28,24},{1,5},{5... | collective-permute-start | bytes 393224 | tf_op jit(solution)/shard_map/ppermute | solution.py:359
  14.9 13.0 %copy-start.1 = (f32[1024,256]{1,0:T(8,128)S(1)}, f32[1024,256]{1,0:T(8,128)}, u32[]{:S(2)}) copy-start(f32[1024,256]{1,0:T(8,128)} %slab_ref.3) | copy-start | bytes 3145732
  14.9 4.7 %collective-permute-start.1 = (f32[192,256]{1,0:T(8,128)S(1)}, f32[192,256]{1,0:T(8,128)S(1)}, u32[]{:S(2)}, u32[]{:S(2)}) collective-permute-start(f32[192,256]{1,0:T(8,128)S(1)} %get-tuple-element.29.held_ref), channel_id=1, source_target_pairs={{0,16},{4,0},{8,12},{12,8},{16,20},{20,4},{24,28},{28,24},{1,17},{... | collective-permute-start | bytes 589832 | tf_op jit(solution)/shard_map/cond/branch_1_fun/ppermute | solution.py:326
  16.5 5.0 %collective-permute-start = (f32[128,256]{1,0:T(8,128)S(1)}, f32[128,256]{1,0:T(8,128)S(1)}, u32[]{:S(2)}, u32[]{:S(2)}) collective-permute-start(f32[128,256]{1,0:T(8,128)S(1)} %pad_maximum_fusion.2), channel_id=1, source_target_pairs={{0,8},{4,12},{8,0},{12,4},{16,24},{20,28},{24,16},{28,20},{1,9},{5... | collective-permute-start | bytes 393224 | tf_op jit(solution)/shard_map/cond/branch_1_fun/ppermute | solution.py:335
  19.6 3.2 %collective-permute-start.3 = (f32[192,256]{1,0:T(8,128)S(1)}, f32[192,256]{1,0:T(8,128)S(1)}, u32[]{:S(2)}, u32[]{:S(2)}) collective-permute-start(f32[192,256]{1,0:T(8,128)S(1)} %branch_1_fun.5.held_ref), channel_id=1, source_target_pairs={{0,8},{4,0},{8,12},{12,4},{16,24},{20,16},{24,28},{28,20},{1,9},{5... | collective-permute-start | bytes 589832 | tf_op jit(solution)/shard_map/cond/branch_1_fun/ppermute | solution.py:326
  21.6 5.6 %collective-permute-start.2 = (f32[160,256]{1,0:T(8,128)S(1)}, f32[160,256]{1,0:T(8,128)S(1)}, u32[]{:S(2)}, u32[]{:S(2)}) collective-permute-start(f32[160,256]{1,0:T(8,128)S(1)} %pad_maximum_fusion.1), channel_id=1, source_target_pairs={{0,16},{4,20},{8,24},{12,28},{16,0},{20,4},{24,8},{28,12},{1,17},{... | collective-permute-start | bytes 491528 | tf_op jit(solution)/shard_map/cond/branch_1_fun/ppermute | solution.py:335
  25.0 2.5 %collective-permute-start.4 = (f32[192,256]{1,0:T(8,128)S(1)}, f32[192,256]{1,0:T(8,128)S(1)}, u32[]{:S(2)}, u32[]{:S(2)}) collective-permute-start(f32[192,256]{1,0:T(8,128)S(1)} %branch_1_fun.7), channel_id=1, source_target_pairs={{0,4},{4,0},{8,12},{12,8},{16,20},{20,16},{24,28},{28,24},{1,5},{5... | collective-permute-start | bytes 589832 | tf_op jit(solution)/shard_map/cond/branch_1_fun/ppermute | solution.py:347
